TPU v7x, 512 devices: a whole 4x8x8 slice. The times are simulated.
512 devices in a mesh: row: 32 (over x_lo, z, core), col: 16 (over y, x_hi).
Axes of the slice: x: 4 (x_hi: 2, x_lo: 2; x = x_hi * 2 + x_lo), y: 8, z: 8, core: 2. Of those that a mesh axis runs over, the one named last changes fastest.
Arguments:
- inputs: bfloat16 [4096, 8192], P('col', 'row'), may hold values from -4 to 4
- out_grad: bfloat16 [4096, 10240], P('row', 'col'), may hold values from -6 to 6
- weight: bfloat16 [8192, 10240], P('row', 'col'), may hold values from -0.0625 to 0.0625
Outputs:
- w_grad: float32 [8192, 10240], P('row', 'col')
- input_grad: bfloat16 [4096, 8192], P('col', 'row')
All inputs are finite; a program needn't handle non-finite values.
Results may differ from a plain program's by a relative error of at most 0.019.
Values may be sent and summed in bfloat16 or wider, within the bound.
No kernel may reach another device: no remote copies, remote signals or barrier semaphores. Data moves between devices by JAX's collectives and lax.ppermute only.
A program may use at most 64 MiB of HBM per device.

v0:
```python
import jax
import jax.numpy as jnp
from jax import lax
from jax.sharding import PartitionSpec as P


def per_device(inputs, out_grad, weight):
    grad_panel = lax.all_gather(out_grad, "row", axis=0, tiled=True)
    input_grad = lax.psum_scatter(
        lax.dot_general(
            grad_panel, weight, (((1,), (1,)), ((), ())), preferred_element_type=jnp.float32
        ).astype(jnp.bfloat16),
        "col",
        scatter_dimension=0,
        tiled=True,
    )
    act_panel = lax.all_gather(inputs, "col", axis=0, tiled=True)
    w_grad = lax.dot_general(
        act_panel, grad_panel, (((0,), (0,)), ((), ())), preferred_element_type=jnp.float32
    )
    return (w_grad, input_grad)


def solution(mesh):
    placed = (P("col", "row"), P("row", "col"), P("row", "col"))
    return jax.shard_map(
        per_device,
        mesh=mesh,
        in_specs=placed,
        out_specs=(P("row", "col"), P("col", "row")),
        check_vma=False,
    )
```

profile of v0, /device:TPU:1, one launch (start us, length us, event | category | flops | bytes accessed | tf_op | source)
XLA Modules:
  0.0 398.0 jit_solution(6190268982631196199)
XLA Ops:
  7.2 0.0 copy-start
  7.2 0.0 all-gather.5.cloned.1.call-start
  7.2 0.7 all-gather.5.cloned.1.call-update
  7.9 0.0 all-gather.3.cloned.1.call-start
  8.0 0.7 all-gather.3.cloned.1.call-update
  8.7 0.0 reduce-scatter.2.cloned.1.call-start
  8.7 79.2 %all-gather.5.cloned.1.call-done = bf16[4096,640]{1,0:T(8,128)(2,1)} async-done(((bf16[128,640]{1,0:T(8,128)(2,1)}), bf16[4096,640]{1,0:T(8,128)(2,1)}) %all-gather.5.cloned.1.call-update) | async-done | bytes 5242896 | tf_op jit(solution)/shard_map/all_gather | solution.py:8
  87.9 0.0 copy-done
  87.9 5.7 %convolution_convert_fusion = bf16[4096,256]{1,0:T(8,128)(2,1)} fusion(bf16[4096,640]{1,0:T(8,128)(2,1)} %all-gather.5.cloned.1.call-done, bf16[256,640]{1,0:T(8,128)(2,1)S(1)} %copy-done), kind=kOutput, calls=%fused_computation | convolution fusion | flops 1343225856 | bytes 7667712 | tf_op jit(solution)/shard_map/dot_general | solution.py:10
  93.6 0.0 reduce-scatter.2.cloned.1.call-update
  93.6 83.7 %all-gather.3.cloned.1.call-done = bf16[4096,256]{1,0:T(8,128)(2,1)} async-done(((bf16[256,256]{1,0:T(8,128)(2,1)}), bf16[4096,256]{1,0:T(8,128)(2,1)}) %all-gather.3.cloned.1.call-update) | async-done | bytes 2097168 | tf_op jit(solution)/shard_map/all_gather | solution.py:17
  177.3 5.8 %fusion = f32[256,640]{1,0:T(8,128)} fusion(bf16[4096,256]{1,0:T(8,128)(2,1)} %all-gather.3.cloned.1.call-done, bf16[4096,640]{1,0:T(8,128)(2,1)} %all-gather.5.cloned.1.call-done), kind=kOutput, calls=%fused_computation.1 | convolution fusion | flops 1342177280 | bytes 7995392 | tf_op jit(solution)/shard_map/dot_general | solution.py:18
  183.1 208.3 %reduce-scatter.2.cloned.1.call-done = bf16[256,256]{1,0:T(8,128)(2,1)} async-done(((bf16[4096,256]{1,0:T(8,128)(2,1)}), bf16[256,256]{1,0:T(8,128)(2,1)}) %reduce-scatter.2.cloned.1.call-update) | async-done | bytes 131088 | tf_op jit(solution)/shard_map/reduce_scatter | solution.py:9
Async XLA Ops:
  7.2 80.7 %copy-start = (bf16[256,640]{1,0:T(8,128)(2,1)S(1)}, bf16[256,640]{1,0:T(8,128)(2,1)}, u32[]{:S(2)}) copy-start(bf16[256,640]{1,0:T(8,128)(2,1)} %param.5) | copy-start | bytes 983044
  7.2 80.7 %all-gather.5.cloned.1.call-start = ((), (), s32[]{:S(2)}) async-start(), calls=%async_computation.2 | async-start | bytes 5406720 | tf_op jit(solution)/shard_map/all_gather | solution.py:8
  7.9 169.4 %all-gather.3.cloned.1.call-start = ((), (), s32[]{:S(2)}) async-start(), calls=%async_computation.1 | async-start | bytes 2228224 | tf_op jit(solution)/shard_map/all_gather | solution.py:17
  8.7 382.8 %reduce-scatter.2.cloned.1.call-start = ((), (), s32[]{:S(2)}) async-start(), calls=%async_computation.3 | async-start | bytes 2228224 | tf_op jit(solution)/shard_map/reduce_scatter | solution.py:9
Sparse Core Ops, SparseCore 0:
  10.2 77.6 all-gather.4
  91.0 86.2 all-gather.2
  182.4 209.0 reduce-scatter.1
where the time goes:
time: 401 us; the launch traced here: 398 us
  waiting for transfers between devices  373 us (93%)
  between operations  13.8 us (3%)
  matrix products  11.5 us (3%)
    reduce_scatter x1, waiting for transfers between devices, per_device(): lax.psum_scatter(lax.dot_general(grad_panel, weight, (((1,), (1,)), ((),...  208 us
    all_gather x1, waiting for transfers between devices, per_device(): act_panel = lax.all_gather(inputs, 'col', axis=0, tiled=True)  83.7 us
    all_gather x1, waiting for transfers between devices, per_device(): grad_panel = lax.all_gather(out_grad, 'row', axis=0, tiled=True)  79.2 us
  transfers between devices with their start and end apart: 3, of which 3 were waited for; matrix products, arithmetic and copies ran while one was open for 3% of the time, Pallas kernels for 0%

commit v1 on v0

v1 whole, which is shorter than its diff:
```python
import jax
import jax.numpy as jnp
from jax import lax
from jax.sharding import Mesh, PartitionSpec as P

SWAP = ((0, 1), (1, 0))


def swap(block, axis):
    return lax.ppermute(block, axis, SWAP)


def keep_and_give(block, own, axis):
    half = block.shape[axis] // 2
    kept = lax.dynamic_slice_in_dim(block, own * half, half, axis)
    given = lax.dynamic_slice_in_dim(block, (1 - own) * half, half, axis)
    return kept, given


def in_order(own, kept, got, axis):
    return jnp.concatenate(
        [jnp.where(own == 0, kept, got), jnp.where(own == 0, got, kept)], axis=axis
    )


def ring_gather(block, axis):
    size = lax.axis_size(axis)
    me = lax.axis_index(axis)
    rows = block.shape[0]
    up = [(i, (i + 1) % size) for i in range(size)]
    down = [(i, (i - 1) % size) for i in range(size)]
    panel = jnp.zeros((size * rows,) + block.shape[1:], block.dtype)

    def put(panel, block, owner):
        return lax.dynamic_update_slice_in_dim(panel, block, lax.rem(owner + size, size) * rows, 0)

    panel = put(panel, block, me)
    rising = falling = block
    for step in range(1, size // 2 + 1):
        rising = lax.ppermute(rising, axis, up)
        panel = put(panel, rising, me - step)
        if 2 * step < size:
            falling = lax.ppermute(falling, axis, down)
            panel = put(panel, falling, me + step)
    return panel


def per_device(inputs, out_grad, weight):
    core = lax.axis_index("core")
    half = lax.axis_index("xh")

    kept, given = keep_and_give(out_grad, half, 0)
    grads = jnp.concatenate([kept, swap(given, "xh")], axis=1)
    grads, inputs, weight = lax.optimization_barrier((grads, inputs, weight))
    grads = lax.all_gather(grads, ("xl", "z"), axis=0, tiled=True)

    kept, given = keep_and_give(inputs, core, 0)
    acts = jnp.concatenate([kept, swap(given, "core")], axis=1)
    kept, given = keep_and_give(acts, half, 0)
    acts = in_order(half, kept, swap(given, "xh"), 0)
    acts = ring_gather(acts, "y")

    weights = jnp.concatenate([weight, swap(weight, "xh")], axis=1)
    weights = jnp.concatenate([weights, swap(weights, "core")], axis=0)

    grads, acts, weights = lax.optimization_barrier((grads, acts, weights))
    partial = lax.dot_general(
        grads, weights, (((1,), (1,)), ((), ())), preferred_element_type=jnp.float32
    ).astype(jnp.bfloat16)
    partial, grads, acts = lax.optimization_barrier((partial, grads, acts))
    share = lax.psum_scatter(partial, "y", scatter_dimension=0, tiled=True)
    w_part = lax.dot_general(
        acts, grads, (((0,), (0,)), ((), ())), preferred_element_type=jnp.float32
    )
    rows, columns = weight.shape
    w_part = w_part[:rows] + swap(w_part[rows:].astype(jnp.bfloat16), "core")
    w_grad = w_part[:, :columns] + swap(w_part[:, columns:].astype(jnp.bfloat16), "xh")

    share, w_grad = lax.optimization_barrier((share, w_grad))
    kept, given = keep_and_give(share, half, 0)
    share = in_order(half, kept, swap(given, "xh"), 0)
    features = share.shape[1] // 2
    input_grad = in_order(core, share[:, :features], swap(share[:, features:], "core"), 0)
    return (w_grad, input_grad)


def solution(mesh):
    rows, cols = mesh.devices.shape
    split = Mesh(
        mesh.devices.reshape(2, rows // 4, 2, cols // 2, 2), ("xl", "z", "core", "y", "xh")
    )
    row, col = ("xl", "z", "core"), ("y", "xh")
    return jax.shard_map(
        per_device,
        mesh=split,
        in_specs=(P(col, row), P(row, col), P(row, col)),
        out_specs=(P(row, col), P(col, row)),
        check_vma=False,
    )
```

time: 401 us -> 163 us (0.41)
  waiting for transfers between devices: 373 us -> 57.6 us
  starting transfers between devices: 0.11 us -> 75.8 us
    reduce_scatter x1, waiting for transfers between devices: 208 us -> 13.1 us  [per_device(): share = lax.psum_scatter(partial, 'y', scatter_dimension=0, tiled=True)]
    all_gather x2 -> x1, waiting for transfers between devices: 163 us -> 21.1 us  [per_device(): grads = lax.all_gather(grads, ('xl', 'z'), axis=0, tiled=True)]
    ppermute x0 -> x16, starting transfers between devices: none -> 75.7 us  [the longest x9 54.2 us: swap(): return lax.ppermute(block, axis, SWAP)]
    ppermute x0 -> x16, waiting for transfers between devices: none -> 23.3 us  [the longest x9 15.7 us: swap(): return lax.ppermute(block, axis, SWAP)]
  transfers between devices with their start and end apart: 3 -> 18, of which waited for: 3 -> 11; matrix products, arithmetic and copies ran while one was open for 3% -> 4% of each run, Pallas kernels for 0% -> 0%
where the time goes in v1:
time: 163 us; the launch traced here: 162 us
  starting transfers between devices  75.8 us (47%)
  waiting for transfers between devices  57.6 us (35%)
  between operations  14.5 us (9%)
  matrix products  7.57 us (5%)
  other arithmetic  3.39 us (2%)
  local copies, waits for them, and re-layouts  3.08 us (2%)
    ppermute x9, starting transfers between devices, swap(): return lax.ppermute(block, axis, SWAP)  54.2 us
    all_gather x1, waiting for transfers between devices, per_device(): grads = lax.all_gather(grads, ('xl', 'z'), axis=0, tiled=True)  21.1 us
    ppermute x9, waiting for transfers between devices, swap(): return lax.ppermute(block, axis, SWAP)  15.7 us
    ppermute x3, starting transfers between devices, ring_gather(): falling = lax.ppermute(falling, axis, down)  13.8 us
    reduce_scatter x1, waiting for transfers between devices, per_device(): share = lax.psum_scatter(partial, 'y', scatter_dimension=0, tiled=True)  13.1 us
    ppermute x4, starting transfers between devices, ring_gather(): rising = lax.ppermute(rising, axis, up)  7.66 us
    ppermute x4, waiting for transfers between devices, ring_gather(): rising = lax.ppermute(rising, axis, up)  7.61 us
    dot_general x1, matrix products, per_device(): lax.dot_general(grads, weights, (((1,), (1,)), ((), ())), preferred_eleme...  4.27 us
  transfers between devices with their start and end apart: 18, of which 11 were waited for; matrix products, arithmetic and copies ran while one was open for 4% of the time, Pallas kernels for 0%

profile of v1, /device:TPU:1, one launch (start us, length us, event | category | flops | bytes accessed | tf_op | source)
XLA Modules:
  0.0 161.8 jit_solution(10606411880688559368)
XLA Ops:
  7.2 0.0 copy-start
  7.2 0.0 all-gather.2.cloned.1.call-start
  7.2 1.0 constant_dynamic-slice_fusion.4
  8.2 5.5 %collective-permute-start = (bf16[64,640]{1,0:T(8,128)(2,1)S(1)}, bf16[64,640]{1,0:T(8,128)(2,1)S(1)}, u32[]{:S(2)}, u32[]{:S(2)}) collective-permute-start(bf16[64,640]{1,0:T(8,128)(2,1)S(1)} %get-tuple-element.31), channel_id=1, source_target_pairs={{0,1},{1,0},{2,3},{3,2},{4,5},{5,4},{6,7},{7,6},{8,9},{9,8},{10,11... | collective-permute-start | bytes 245768 | tf_op jit(solution)/shard_map/ppermute | solution.py:10
  13.7 1.8 %collective-permute-done = bf16[64,640]{1,0:T(8,128)(2,1)S(1)} collective-permute-done((bf16[64,640]{1,0:T(8,128)(2,1)S(1)}, bf16[64,640]{1,0:T(8,128)(2,1)S(1)}, u32[]{:S(2)}, u32[]{:S(2)}) %collective-permute-start) | collective-permute-done | bytes 81952 | tf_op jit(solution)/shard_map/ppermute | solution.py:10
  15.5 0.7 pad_maximum_fusion.1
  16.2 0.0 all-gather.2.cloned.1.call-update
  16.2 0.0 reduce-scatter.2.cloned.1.call-start
  16.3 0.9 constant_dynamic-slice_fusion.1
  17.2 9.3 %collective-permute-start.1 = (bf16[128,256]{1,0:T(8,128)(2,1)S(1)}, bf16[128,256]{1,0:T(8,128)(2,1)S(1)}, u32[]{:S(2)}, u32[]{:S(2)}) collective-permute-start(bf16[128,256]{1,0:T(8,128)(2,1)S(1)} %get-tuple-element.34), channel_id=1, source_target_pairs={{0,16},{16,0},{1,17},{17,1},{2,18},{18,2},{3,19},{19,3},{4,20},{20... | collective-permute-start | bytes 196616 | tf_op jit(solution)/shard_map/ppermute | solution.py:10
  26.5 0.9 collective-permute-done.1
  27.4 1.9 %collective-permute-start.2 = (bf16[64,512]{1,0:T(8,128)(2,1)S(1)}, bf16[64,512]{1,0:T(8,128)(2,1)S(1)}, u32[]{:S(2)}, u32[]{:S(2)}) collective-permute-start(bf16[64,512]{1,0:T(8,128)(2,1)S(1)} %fusion.1), channel_id=1, source_target_pairs={{0,1},{1,0},{2,3},{3,2},{4,5},{5,4},{6,7},{7,6},{8,9},{9,8},{10,11... | collective-permute-start | bytes 196616 | tf_op jit(solution)/shard_map/ppermute | solution.py:10
  29.3 4.9 %collective-permute-start.10 = (bf16[256,640]{1,0:T(8,128)(2,1)}, bf16[256,640]{1,0:T(8,128)(2,1)S(1)}, u32[]{:S(2)}, u32[]{:S(2)}) collective-permute-start(bf16[256,640]{1,0:T(8,128)(2,1)} %param.5), channel_id=1, source_target_pairs={{0,1},{1,0},{2,3},{3,2},{4,5},{5,4},{6,7},{7,6},{8,9},{9,8},{10,11... | collective-permute-start | bytes 983048 | tf_op jit(solution)/shard_map/ppermute | solution.py:10
  34.2 0.0 collective-permute-done.2
  34.2 0.1 broadcast_in_dim.3
  34.3 1.9 %collective-permute-start.3 = (bf16[128,512]{1,0:T(8,128)(2,1)S(1)}, bf16[128,512]{1,0:T(8,128)(2,1)S(1)}, u32[]{:S(2)}, u32[]{:S(2)}) collective-permute-start(bf16[128,512]{1,0:T(8,128)(2,1)S(1)} %get-tuple-element.32), channel_id=1, source_target_pairs={{0,2},{2,4},{4,6},{6,8},{8,10},{10,12},{12,14},{14,0},{1,3},{3,5},... | collective-permute-start | bytes 393224 | tf_op jit(solution)/shard_map/ppermute | solution.py:40
  36.3 4.6 %collective-permute-start.4 = (bf16[128,512]{1,0:T(8,128)(2,1)S(1)}, bf16[128,512]{1,0:T(8,128)(2,1)S(1)}, u32[]{:S(2)}, u32[]{:S(2)}) collective-permute-start(bf16[128,512]{1,0:T(8,128)(2,1)S(1)} %get-tuple-element.32), channel_id=1, source_target_pairs={{0,14},{2,0},{4,2},{6,4},{8,6},{10,8},{12,10},{14,12},{1,15},{3,1}... | collective-permute-start | bytes 393224 | tf_op jit(solution)/shard_map/ppermute | solution.py:43
  40.9 0.0 copy-done
  41.0 0.6 collective-permute-done.3
  41.6 1.9 %collective-permute-start.5 = (bf16[128,512]{1,0:T(8,128)(2,1)S(1)}, bf16[128,512]{1,0:T(8,128)(2,1)S(1)}, u32[]{:S(2)}, u32[]{:S(2)}) collective-permute-start(bf16[128,512]{1,0:T(8,128)(2,1)S(1)} %collective-permute-done.3), channel_id=1, source_target_pairs={{0,2},{2,4},{4,6},{6,8},{8,10},{10,12},{12,14},{14,0},{1,3},{3,5},... | collective-permute-start | bytes 393224 | tf_op jit(solution)/shard_map/ppermute | solution.py:40
  43.5 0.0 collective-permute-done.4
  43.5 4.7 %collective-permute-start.6 = (bf16[128,512]{1,0:T(8,128)(2,1)S(1)}, bf16[128,512]{1,0:T(8,128)(2,1)S(1)}, u32[]{:S(2)}, u32[]{:S(2)}) collective-permute-start(bf16[128,512]{1,0:T(8,128)(2,1)S(1)} %collective-permute-done.4), channel_id=1, source_target_pairs={{0,14},{2,0},{4,2},{6,4},{8,6},{10,8},{12,10},{14,12},{1,15},{3,1}... | collective-permute-start | bytes 393224 | tf_op jit(solution)/shard_map/ppermute | solution.py:43
  48.2 0.0 collective-permute-done.10
  48.3 4.4 %collective-permute-start.11 = (bf16[256,1280]{1,0:T(8,128)(2,1)S(1)}, bf16[256,1280]{1,0:T(8,128)(2,1)S(1)}, u32[]{:S(2)}, u32[]{:S(2)}) collective-permute-start(bf16[256,1280]{1,0:T(8,128)(2,1)S(1)} %constant_dynamic-update-slice_fusion), channel_id=1, source_target_pairs={{0,16},{16,0},{1,17},{17,1},{2,18},{18,2},{3,19},{19,3},{4,20},{20... | collective-permute-start | bytes 1966088 | tf_op jit(solution)/shard_map/ppermute | solution.py:10
  52.7 0.0 collective-permute-done.5
  52.7 1.9 %collective-permute-start.7 = (bf16[128,512]{1,0:T(8,128)(2,1)S(1)}, bf16[128,512]{1,0:T(8,128)(2,1)S(1)}, u32[]{:S(2)}, u32[]{:S(2)}) collective-permute-start(bf16[128,512]{1,0:T(8,128)(2,1)S(1)} %collective-permute-done.5), channel_id=1, source_target_pairs={{0,2},{2,4},{4,6},{6,8},{8,10},{10,12},{12,14},{14,0},{1,3},{3,5},... | collective-permute-start | bytes 393224 | tf_op jit(solution)/shard_map/ppermute | solution.py:40
  54.6 0.0 collective-permute-done.6
  54.6 4.6 %collective-permute-start.8 = (bf16[128,512]{1,0:T(8,128)(2,1)S(1)}, bf16[128,512]{1,0:T(8,128)(2,1)S(1)}, u32[]{:S(2)}, u32[]{:S(2)}) collective-permute-start(bf16[128,512]{1,0:T(8,128)(2,1)S(1)} %collective-permute-done.6), channel_id=1, source_target_pairs={{0,14},{2,0},{4,2},{6,4},{8,6},{10,8},{12,10},{14,12},{1,15},{3,1}... | collective-permute-start | bytes 393224 | tf_op jit(solution)/shard_map/ppermute | solution.py:43
  59.3 1.7 %collective-permute-done.7 = bf16[128,512]{1,0:T(8,128)(2,1)S(1)} collective-permute-done((bf16[128,512]{1,0:T(8,128)(2,1)S(1)}, bf16[128,512]{1,0:T(8,128)(2,1)S(1)}, u32[]{:S(2)}, u32[]{:S(2)}) %collective-permute-start.7) | collective-permute-done | bytes 131104 | tf_op jit(solution)/shard_map/ppermute | solution.py:40
  60.9 1.9 %collective-permute-start.9 = (bf16[128,512]{1,0:T(8,128)(2,1)S(1)}, bf16[128,512]{1,0:T(8,128)(2,1)S(1)}, u32[]{:S(2)}, u32[]{:S(2)}) collective-permute-start(bf16[128,512]{1,0:T(8,128)(2,1)S(1)} %collective-permute-done.7), channel_id=1, source_target_pairs={{0,2},{2,4},{4,6},{6,8},{8,10},{10,12},{12,14},{14,0},{1,3},{3,5},... | collective-permute-start | bytes 393224 | tf_op jit(solution)/shard_map/ppermute | solution.py:40
  62.9 0.0 collective-permute-done.8
  62.9 5.3 %collective-permute-done.9 = bf16[128,512]{1,0:T(8,128)(2,1)S(1)} collective-permute-done((bf16[128,512]{1,0:T(8,128)(2,1)S(1)}, bf16[128,512]{1,0:T(8,128)(2,1)S(1)}, u32[]{:S(2)}, u32[]{:S(2)}) %collective-permute-start.9) | collective-permute-done | bytes 131104 | tf_op jit(solution)/shard_map/ppermute | solution.py:40
  68.3 0.0 collective-permute-done.11
  68.3 0.1 pad_maximum_fusion
  68.4 21.1 %all-gather.2.cloned.1.call-done = bf16[1024,1280]{1,0:T(8,128)(2,1)} async-done(((bf16[64,1280]{1,0:T(8,128)(2,1)}), bf16[1024,1280]{1,0:T(8,128)(2,1)}) %all-gather.2.cloned.1.call-update) | async-done | bytes 2621456 | tf_op jit(solution)/shard_map/all_gather | solution.py:55
  89.5 4.3 %convolution_convert_fusion = bf16[1024,512]{1,0:T(8,128)(2,1)} fusion(bf16[1024,1280]{1,0:T(8,128)(2,1)} %all-gather.2.cloned.1.call-done, bf16[512,1280]{1,0:T(8,128)(2,1)S(1)} %pad_maximum_fusion), kind=kOutput, calls=%fused_computation | convolution fusion | flops 1342701568 | bytes 4980736 | tf_op jit(solution)/shard_map/dot_general | solution.py:67
  93.8 0.0 reduce-scatter.2.cloned.1.call-update
  93.8 3.3 %fusion.3 = f32[512,1280]{1,0:T(8,128)S(1)} fusion(bf16[1024,512]{1,0:T(8,128)(2,1)S(1)} %constant_dynamic-update-slice_fusion.2, bf16[1024,1280]{1,0:T(8,128)(2,1)} %all-gather.2.cloned.1.call-done), kind=kOutput, calls=%fused_computation.40 | convolution fusion | flops 1342177280 | bytes 6291456 | tf_op jit(solution)/shard_map/dot_general | solution.py:72
  97.1 0.1 slice.50
  97.2 12.0 %collective-permute-start.12 = (bf16[256,1280]{1,0:T(8,128)(2,1)S(1)}, bf16[256,1280]{1,0:T(8,128)(2,1)S(1)}, u32[]{:S(2)}, u32[]{:S(2)}) collective-permute-start(bf16[256,1280]{1,0:T(8,128)(2,1)S(1)} %slice.50), channel_id=1, source_target_pairs={{0,16},{16,0},{1,17},{17,1},{2,18},{18,2},{3,19},{19,3},{4,20},{20... | collective-permute-start | bytes 1966088 | tf_op jit(solution)/shard_map/ppermute | solution.py:10
  109.3 1.7 %collective-permute-done.12 = bf16[256,1280]{1,0:T(8,128)(2,1)S(1)} collective-permute-done((bf16[256,1280]{1,0:T(8,128)(2,1)S(1)}, bf16[256,1280]{1,0:T(8,128)(2,1)S(1)}, u32[]{:S(2)}, u32[]{:S(2)}) %collective-permute-start.12) | collective-permute-done | bytes 655392 | tf_op jit(solution)/shard_map/ppermute | solution.py:10
  111.0 0.1 slice_add_fusion
  111.1 4.0 %collective-permute-start.13 = (bf16[256,640]{1,0:T(8,128)(2,1)S(1)}, bf16[256,640]{1,0:T(8,128)(2,1)S(1)}, u32[]{:S(2)}, u32[]{:S(2)}) collective-permute-start(bf16[256,640]{1,0:T(8,128)(2,1)S(1)} %slice.51), channel_id=1, source_target_pairs={{0,1},{1,0},{2,3},{3,2},{4,5},{5,4},{6,7},{7,6},{8,9},{9,8},{10,11... | collective-permute-start | bytes 983048 | tf_op jit(solution)/shard_map/ppermute | solution.py:10
  115.2 8.3 %collective-permute-done.13 = bf16[256,640]{1,0:T(8,128)(2,1)S(1)} collective-permute-done((bf16[256,640]{1,0:T(8,128)(2,1)S(1)}, bf16[256,640]{1,0:T(8,128)(2,1)S(1)}, u32[]{:S(2)}, u32[]{:S(2)}) %collective-permute-start.13) | collective-permute-done | bytes 327712 | tf_op jit(solution)/shard_map/ppermute | solution.py:10
  123.4 0.9 slice_add_fusion.1
  124.3 13.1 %reduce-scatter.2.cloned.1.call-done = bf16[128,512]{1,0:T(8,128)(2,1)} async-done(((bf16[1024,512]{1,0:T(8,128)(2,1)}), bf16[128,512]{1,0:T(8,128)(2,1)}) %reduce-scatter.2.cloned.1.call-update) | async-done | bytes 131088 | tf_op jit(solution)/shard_map/reduce_scatter | solution.py:71
  137.4 0.8 constant_dynamic-slice_fusion
  138.2 4.3 %collective-permute-start.14 = (bf16[64,512]{1,0:T(8,128)(2,1)S(1)}, bf16[64,512]{1,0:T(8,128)(2,1)S(1)}, u32[]{:S(2)}, u32[]{:S(2)}) collective-permute-start(bf16[64,512]{1,0:T(8,128)(2,1)S(1)} %constant_dynamic-slice_fusion), channel_id=1, source_target_pairs={{0,1},{1,0},{2,3},{3,2},{4,5},{5,4},{6,7},{7,6},{8,9},{9,8},{10,11... | collective-permute-start | bytes 196616 | tf_op jit(solution)/shard_map/ppermute | solution.py:10
  142.6 2.2 %collective-permute-done.14 = bf16[64,512]{1,0:T(8,128)(2,1)S(1)} collective-permute-done((bf16[64,512]{1,0:T(8,128)(2,1)S(1)}, bf16[64,512]{1,0:T(8,128)(2,1)S(1)}, u32[]{:S(2)}, u32[]{:S(2)}) %collective-permute-start.14) | collective-permute-done | bytes 65568 | tf_op jit(solution)/shard_map/ppermute | solution.py:10
  144.7 0.9 broadcast_select_fusion.3
  145.6 7.8 %collective-permute-start.15 = (bf16[128,256]{1,0:T(8,128)(2,1)S(1)}, bf16[128,256]{1,0:T(8,128)(2,1)S(1)}, u32[]{:S(2)}, u32[]{:S(2)}) collective-permute-start(bf16[128,256]{1,0:T(8,128)(2,1)S(1)} %pad_maximum_fusion.4), channel_id=1, source_target_pairs={{0,16},{16,0},{1,17},{17,1},{2,18},{18,2},{3,19},{19,3},{4,20},{20... | collective-permute-start | bytes 196616 | tf_op jit(solution)/shard_map/ppermute | solution.py:10
  153.4 0.9 collective-permute-done.15
  154.3 0.7 pad_maximum_fusion.3
  (15 shorter events, 0.3 us)
Async XLA Ops:
  7.2 33.7 %copy-start = (bf16[256,640]{1,0:T(8,128)(2,1)S(1)}, bf16[256,640]{1,0:T(8,128)(2,1)}, u32[]{:S(2)}) copy-start(bf16[256,640]{1,0:T(8,128)(2,1)} %param.5) | copy-start | bytes 983044
  7.2 82.3 %all-gather.2.cloned.1.call-start = ((), (), s32[]{:S(2)}) async-start(), calls=%async_computation.1 | async-start | bytes 2785280 | tf_op jit(solution)/shard_map/all_gather | solution.py:55
  8.2 7.3 %collective-permute-start = (bf16[64,640]{1,0:T(8,128)(2,1)S(1)}, bf16[64,640]{1,0:T(8,128)(2,1)S(1)}, u32[]{:S(2)}, u32[]{:S(2)}) collective-permute-start(bf16[64,640]{1,0:T(8,128)(2,1)S(1)} %get-tuple-element.31), channel_id=1, source_target_pairs={{0,1},{1,0},{2,3},{3,2},{4,5},{5,4},{6,7},{7,6},{8,9},{9,8},{10,11... | collective-permute-start | bytes 245768 | tf_op jit(solution)/shard_map/ppermute | solution.py:10
  16.2 121.2 %reduce-scatter.2.cloned.1.call-start = ((), (), s32[]{:S(2)}) async-start(), calls=%async_computation.2 | async-start | bytes 1179648 | tf_op jit(solution)/shard_map/reduce_scatter | solution.py:71
  17.2 10.2 %collective-permute-start.1 = (bf16[128,256]{1,0:T(8,128)(2,1)S(1)}, bf16[128,256]{1,0:T(8,128)(2,1)S(1)}, u32[]{:S(2)}, u32[]{:S(2)}) collective-permute-start(bf16[128,256]{1,0:T(8,128)(2,1)S(1)} %get-tuple-element.34), channel_id=1, source_target_pairs={{0,16},{16,0},{1,17},{17,1},{2,18},{18,2},{3,19},{19,3},{4,20},{20... | collective-permute-start | bytes 196616 | tf_op jit(solution)/shard_map/ppermute | solution.py:10
  27.4 6.8 %collective-permute-start.2 = (bf16[64,512]{1,0:T(8,128)(2,1)S(1)}, bf16[64,512]{1,0:T(8,128)(2,1)S(1)}, u32[]{:S(2)}, u32[]{:S(2)}) collective-permute-start(bf16[64,512]{1,0:T(8,128)(2,1)S(1)} %fusion.1), channel_id=1, source_target_pairs={{0,1},{1,0},{2,3},{3,2},{4,5},{5,4},{6,7},{7,6},{8,9},{9,8},{10,11... | collective-permute-start | bytes 196616 | tf_op jit(solution)/shard_map/ppermute | solution.py:10
  29.3 18.9 %collective-permute-start.10 = (bf16[256,640]{1,0:T(8,128)(2,1)}, bf16[256,640]{1,0:T(8,128)(2,1)S(1)}, u32[]{:S(2)}, u32[]{:S(2)}) collective-permute-start(bf16[256,640]{1,0:T(8,128)(2,1)} %param.5), channel_id=1, source_target_pairs={{0,1},{1,0},{2,3},{3,2},{4,5},{5,4},{6,7},{7,6},{8,9},{9,8},{10,11... | collective-permute-start | bytes 983048 | tf_op jit(solution)/shard_map/ppermute | solution.py:10
  34.3 7.2 %collective-permute-start.3 = (bf16[128,512]{1,0:T(8,128)(2,1)S(1)}, bf16[128,512]{1,0:T(8,128)(2,1)S(1)}, u32[]{:S(2)}, u32[]{:S(2)}) collective-permute-start(bf16[128,512]{1,0:T(8,128)(2,1)S(1)} %get-tuple-element.32), channel_id=1, source_target_pairs={{0,2},{2,4},{4,6},{6,8},{8,10},{10,12},{12,14},{14,0},{1,3},{3,5},... | collective-permute-start | bytes 393224 | tf_op jit(solution)/shard_map/ppermute | solution.py:40
  36.3 7.2 %collective-permute-start.4 = (bf16[128,512]{1,0:T(8,128)(2,1)S(1)}, bf16[128,512]{1,0:T(8,128)(2,1)S(1)}, u32[]{:S(2)}, u32[]{:S(2)}) collective-permute-start(bf16[128,512]{1,0:T(8,128)(2,1)S(1)} %get-tuple-element.32), channel_id=1, source_target_pairs={{0,14},{2,0},{4,2},{6,4},{8,6},{10,8},{12,10},{14,12},{1,15},{3,1}... | collective-permute-start | bytes 393224 | tf_op jit(solution)/shard_map/ppermute | solution.py:43
  41.6 11.1 %collective-permute-start.5 = (bf16[128,512]{1,0:T(8,128)(2,1)S(1)}, bf16[128,512]{1,0:T(8,128)(2,1)S(1)}, u32[]{:S(2)}, u32[]{:S(2)}) collective-permute-start(bf16[128,512]{1,0:T(8,128)(2,1)S(1)} %collective-permute-done.3), channel_id=1, source_target_pairs={{0,2},{2,4},{4,6},{6,8},{8,10},{10,12},{12,14},{14,0},{1,3},{3,5},... | collective-permute-start | bytes 393224 | tf_op jit(solution)/shard_map/ppermute | solution.py:40
  43.5 11.1 %collective-permute-start.6 = (bf16[128,512]{1,0:T(8,128)(2,1)S(1)}, bf16[128,512]{1,0:T(8,128)(2,1)S(1)}, u32[]{:S(2)}, u32[]{:S(2)}) collective-permute-start(bf16[128,512]{1,0:T(8,128)(2,1)S(1)} %collective-permute-done.4), channel_id=1, source_target_pairs={{0,14},{2,0},{4,2},{6,4},{8,6},{10,8},{12,10},{14,12},{1,15},{3,1}... | collective-permute-start | bytes 393224 | tf_op jit(solution)/shard_map/ppermute | solution.py:43
  48.3 20.0 %collective-permute-start.11 = (bf16[256,1280]{1,0:T(8,128)(2,1)S(1)}, bf16[256,1280]{1,0:T(8,128)(2,1)S(1)}, u32[]{:S(2)}, u32[]{:S(2)}) collective-permute-start(bf16[256,1280]{1,0:T(8,128)(2,1)S(1)} %constant_dynamic-update-slice_fusion), channel_id=1, source_target_pairs={{0,16},{16,0},{1,17},{17,1},{2,18},{18,2},{3,19},{19,3},{4,20},{20... | collective-permute-start | bytes 1966088 | tf_op jit(solution)/shard_map/ppermute | solution.py:10
  52.7 8.2 %collective-permute-start.7 = (bf16[128,512]{1,0:T(8,128)(2,1)S(1)}, bf16[128,512]{1,0:T(8,128)(2,1)S(1)}, u32[]{:S(2)}, u32[]{:S(2)}) collective-permute-start(bf16[128,512]{1,0:T(8,128)(2,1)S(1)} %collective-permute-done.5), channel_id=1, source_target_pairs={{0,2},{2,4},{4,6},{6,8},{8,10},{10,12},{12,14},{14,0},{1,3},{3,5},... | collective-permute-start | bytes 393224 | tf_op jit(solution)/shard_map/ppermute | solution.py:40
  54.6 8.2 %collective-permute-start.8 = (bf16[128,512]{1,0:T(8,128)(2,1)S(1)}, bf16[128,512]{1,0:T(8,128)(2,1)S(1)}, u32[]{:S(2)}, u32[]{:S(2)}) collective-permute-start(bf16[128,512]{1,0:T(8,128)(2,1)S(1)} %collective-permute-done.6), channel_id=1, source_target_pairs={{0,14},{2,0},{4,2},{6,4},{8,6},{10,8},{12,10},{14,12},{1,15},{3,1}... | collective-permute-start | bytes 393224 | tf_op jit(solution)/shard_map/ppermute | solution.py:43
  60.9 7.3 %collective-permute-start.9 = (bf16[128,512]{1,0:T(8,128)(2,1)S(1)}, bf16[128,512]{1,0:T(8,128)(2,1)S(1)}, u32[]{:S(2)}, u32[]{:S(2)}) collective-permute-start(bf16[128,512]{1,0:T(8,128)(2,1)S(1)} %collective-permute-done.7), channel_id=1, source_target_pairs={{0,2},{2,4},{4,6},{6,8},{8,10},{10,12},{12,14},{14,0},{1,3},{3,5},... | collective-permute-start | bytes 393224 | tf_op jit(solution)/shard_map/ppermute | solution.py:40
  97.2 13.8 %collective-permute-start.12 = (bf16[256,1280]{1,0:T(8,128)(2,1)S(1)}, bf16[256,1280]{1,0:T(8,128)(2,1)S(1)}, u32[]{:S(2)}, u32[]{:S(2)}) collective-permute-start(bf16[256,1280]{1,0:T(8,128)(2,1)S(1)} %slice.50), channel_id=1, source_target_pairs={{0,16},{16,0},{1,17},{17,1},{2,18},{18,2},{3,19},{19,3},{4,20},{20... | collective-permute-start | bytes 1966088 | tf_op jit(solution)/shard_map/ppermute | solution.py:10
  111.1 12.3 %collective-permute-start.13 = (bf16[256,640]{1,0:T(8,128)(2,1)S(1)}, bf16[256,640]{1,0:T(8,128)(2,1)S(1)}, u32[]{:S(2)}, u32[]{:S(2)}) collective-permute-start(bf16[256,640]{1,0:T(8,128)(2,1)S(1)} %slice.51), channel_id=1, source_target_pairs={{0,1},{1,0},{2,3},{3,2},{4,5},{5,4},{6,7},{7,6},{8,9},{9,8},{10,11... | collective-permute-start | bytes 983048 | tf_op jit(solution)/shard_map/ppermute | solution.py:10
  138.2 6.5 %collective-permute-start.14 = (bf16[64,512]{1,0:T(8,128)(2,1)S(1)}, bf16[64,512]{1,0:T(8,128)(2,1)S(1)}, u32[]{:S(2)}, u32[]{:S(2)}) collective-permute-start(bf16[64,512]{1,0:T(8,128)(2,1)S(1)} %constant_dynamic-slice_fusion), channel_id=1, source_target_pairs={{0,1},{1,0},{2,3},{3,2},{4,5},{5,4},{6,7},{7,6},{8,9},{9,8},{10,11... | collective-permute-start | bytes 196616 | tf_op jit(solution)/shard_map/ppermute | solution.py:10
  145.6 8.7 %collective-permute-start.15 = (bf16[128,256]{1,0:T(8,128)(2,1)S(1)}, bf16[128,256]{1,0:T(8,128)(2,1)S(1)}, u32[]{:S(2)}, u32[]{:S(2)}) collective-permute-start(bf16[128,256]{1,0:T(8,128)(2,1)S(1)} %pad_maximum_fusion.4), channel_id=1, source_target_pairs={{0,16},{16,0},{1,17},{17,1},{2,18},{18,2},{3,19},{19,3},{4,20},{20... | collective-permute-start | bytes 196616 | tf_op jit(solution)/shard_map/ppermute | solution.py:10
Sparse Core Ops, SparseCore 0:
  16.3 73.1 all-gather.1
  93.9 43.4 reduce-scatter.1

commit v2 on v1

v2 whole, which is shorter than its diff:
```python
import jax
import jax.numpy as jnp
from jax import lax
from jax.sharding import Mesh, PartitionSpec as P

SWAP = ((0, 1), (1, 0))


def swap(block, axis):
    return lax.ppermute(block, axis, SWAP)


def in_order(own, kept, got, axis):
    return jnp.concatenate(
        [jnp.where(own == 0, kept, got), jnp.where(own == 0, got, kept)], axis=axis
    )


def exchange(pieces, axes):
    return lax.all_to_all(pieces, axes, split_axis=0, concat_axis=0, tiled=True)


def ring_gather(block, axis):
    size = lax.axis_size(axis)
    me = lax.axis_index(axis)
    up = [(i, (i + 1) % size) for i in range(size)]
    down = [(i, (i - 1) % size) for i in range(size)]
    panel = jnp.zeros((block.shape[0], size) + block.shape[2:], block.dtype)

    def put(panel, block, owner):
        return lax.dynamic_update_slice_in_dim(panel, block, lax.rem(owner + size, size), 1)

    panel = put(panel, block, me)
    rising = falling = block
    for step in range(1, size // 2 + 1):
        rising = lax.ppermute(rising, axis, up)
        panel = put(panel, rising, me - step)
        if 2 * step < size:
            falling = lax.ppermute(falling, axis, down)
            panel = put(panel, falling, me + step)
    return panel


def per_device(inputs, out_grad, weight):
    core = lax.axis_index("core")
    half = lax.axis_index("xh")
    tokens, columns = out_grad.shape
    part = tokens // 2
    features = inputs.shape[1]

    pieces = jnp.broadcast_to(out_grad.reshape(1, 2, part, columns), (2, 2, part, columns))
    pieces = exchange(pieces.reshape(4, part, columns), ("xl", "xh"))
    pieces = pieces.reshape(2, 2, part, columns)
    grads = in_order(half, pieces[:, 0], pieces[:, 1], 2)
    grads, inputs, weight = lax.optimization_barrier((grads, inputs, weight))
    grads = ring_gather(grads[:, None], "z")
    grads = grads.reshape(-1, 2 * columns)

    acts = exchange(inputs.reshape(4, part, features), ("core", "xh"))
    acts = acts.reshape(2, 2 * part, features)
    acts = jnp.concatenate([acts[0], acts[1]], axis=1)
    acts = lax.all_gather(acts, "y", axis=0, tiled=True)

    weights = jnp.concatenate([weight, swap(weight, "xh")], axis=1)
    weights = in_order(core, weights, swap(weights, "core"), 0)

    grads, weights = lax.optimization_barrier((grads, weights))
    partial = jnp.concatenate(
        [
            lax.dot_general(
                grads,
                weights[i * features : (i + 1) * features],
                (((1,), (1,)), ((), ())),
                preferred_element_type=jnp.float32,
            ).astype(jnp.bfloat16)
            for i in range(2)
        ],
        axis=0,
    )

    w_part = lax.dot_general(
        acts, grads, (((0,), (0,)), ((), ())), preferred_element_type=jnp.float32
    )
    given = lax.dynamic_slice_in_dim(w_part, (1 - core) * features, features, 0)
    kept = lax.dynamic_slice_in_dim(w_part, core * features, features, 0)
    w_part = kept + swap(given.astype(jnp.bfloat16), "core")
    kept, given = w_part[:, :columns], w_part[:, columns:].astype(jnp.bfloat16)
    kept, given, partial = lax.optimization_barrier((kept, given, partial))
    w_grad = kept + swap(given, "xh")

    partial = partial.reshape(-1, part, features)
    shares = exchange(partial, ("core", "y", "xh"))
    shares = shares.reshape(2, -1, 2, part, features).astype(jnp.float32)
    input_grad = jnp.sum(shares, axis=1).astype(jnp.bfloat16).reshape(-1, features)
    return (w_grad, input_grad)


def solution(mesh):
    rows, cols = mesh.devices.shape
    split = Mesh(
        mesh.devices.reshape(2, rows // 4, 2, cols // 2, 2), ("xl", "z", "core", "y", "xh")
    )
    row, col = ("xl", "z", "core"), ("y", "xh")
    return jax.shard_map(
        per_device,
        mesh=split,
        in_specs=(P(col, row), P(row, col), P(row, col)),
        out_specs=(P(row, col), P(col, row)),
        check_vma=False,
    )
```

time: 163 us -> 142 us (0.87)
  starting transfers between devices: 75.8 us -> 60.9 us
  waiting for transfers between devices: 57.6 us -> 48.6 us
  local copies, waits for them, and re-layouts: 3.08 us -> 7.25 us
  matrix products: 7.57 us -> 4.65 us
  other arithmetic: 3.39 us -> 5.6 us
    ppermute x9 -> x4, starting transfers between devices: 54.2 us -> 14.7 us  [swap(): return lax.ppermute(block, axis, SWAP)]
    all_gather x1, waiting for transfers between devices: 21.1 us -> 0.02 us  [per_device(): acts = lax.all_gather(acts, 'y', axis=0, tiled=True)]
    all_to_all x0 -> x3, waiting for transfers between devices: none -> 18.7 us  [exchange(): return lax.all_to_all(pieces, axes, split_axis=0, concat_axis=0, tiled=True)]
    all_to_all x0 -> x3, starting transfers between devices: none -> 17.9 us  [exchange(): return lax.all_to_all(pieces, axes, split_axis=0, concat_axis=0, tiled=True)]
    reduce_scatter x1 -> x0, waiting for transfers between devices: 13.1 us -> none  [per_device(): share = lax.psum_scatter(partial, 'y', scatter_dimension=0, tiled=True)]
    ppermute x4, waiting for transfers between devices: 7.61 us -> 16.6 us  [ring_gather(): rising = lax.ppermute(rising, axis, up)]
    ppermute x3, starting transfers between devices: 13.8 us -> 17.7 us  [ring_gather(): falling = lax.ppermute(falling, axis, down)]
    dynamic_update_slice x7 -> x8, local copies, waits for them, and re-layouts: 0.11 us -> 3.15 us  [put(): lax.dynamic_update_slice_in_dim(panel, block, lax.rem(owner + size, size)...]
  transfers between devices with their start and end apart: 18 -> 15, of which waited for: 11 -> 7; matrix products, arithmetic and copies ran while one was open for 4% -> 8% of each run, Pallas kernels for 0% -> 0%
where the time goes in v2:
time: 142 us; the launch traced here: 141 us
  starting transfers between devices  60.9 us (43%)
  waiting for transfers between devices  48.6 us (34%)
  between operations  14.3 us (10%)
  local copies, waits for them, and re-layouts  7.25 us (5%)
  other arithmetic  5.6 us (4%)
  matrix products  4.65 us (3%)
    all_to_all x3, waiting for transfers between devices, exchange(): return lax.all_to_all(pieces, axes, split_axis=0, concat_axis=0, tiled=True)  18.7 us
    all_to_all x3, starting transfers between devices, exchange(): return lax.all_to_all(pieces, axes, split_axis=0, concat_axis=0, tiled=True)  17.9 us
    ppermute x3, starting transfers between devices, ring_gather(): falling = lax.ppermute(falling, axis, down)  17.7 us
    ppermute x4, waiting for transfers between devices, ring_gather(): rising = lax.ppermute(rising, axis, up)  16.6 us
    ppermute x4, starting transfers between devices, swap(): return lax.ppermute(block, axis, SWAP)  14.7 us
    ppermute x4, waiting for transfers between devices, swap(): return lax.ppermute(block, axis, SWAP)  13.3 us
    ppermute x4, starting transfers between devices, ring_gather(): rising = lax.ppermute(rising, axis, up)  10.6 us
    dynamic_update_slice x8, local copies, waits for them, and re-layouts, put(): lax.dynamic_update_slice_in_dim(panel, block, lax.rem(owner + size, size)...  3.15 us
  transfers between devices with their start and end apart: 15, of which 7 were waited for; matrix products, arithmetic and copies ran while one was open for 8% of the time, Pallas kernels for 0%

profile of v2, /device:TPU:1, one launch (start us, length us, event | category | flops | bytes accessed | tf_op | source)
XLA Modules:
  0.0 141.3 jit_solution(4342496791270827332)
XLA Ops:
  7.2 1.7 %broadcast_in_dim.14 = bf16[2,2,64,640]{3,2,1,0:T(8,128)(2,1)} broadcast(bf16[2,64,640]{2,1,0:T(8,128)(2,1)} %bitcast.56), dimensions={1,2,3} | broadcast | bytes 491520 | tf_op jit(solution)/shard_map/broadcast_in_dim | solution.py:51
  8.8 4.8 %all-to-all-start = ((bf16[4,64,640]{2,1,0:T(8,128)(2,1)}), bf16[4,64,640]{2,1,0:T(8,128)(2,1)S(1)}, u32[]{:S(2)}, u32[]{:S(2)}) async-start(bf16[4,64,640]{2,1,0:T(8,128)(2,1)} %bitcast.1), calls=%async_computation | async-start | bytes 655360 | tf_op jit(solution)/shard_map/all_to_all | solution.py:20
  13.7 5.6 %all-to-all-done = bf16[4,64,640]{2,1,0:T(8,128)(2,1)S(1)} async-done(((bf16[4,64,640]{2,1,0:T(8,128)(2,1)}), bf16[4,64,640]{2,1,0:T(8,128)(2,1)S(1)}, u32[]{:S(2)}, u32[]{:S(2)}) %all-to-all-start) | async-done | bytes 327712 | tf_op jit(solution)/shard_map/all_to_all | solution.py:20
  19.3 0.8 pad_maximum_fusion.2
  20.1 4.8 %collective-permute-start = (bf16[2,1,64,1280]{3,2,0,1:T(8,128)(2,1)}, bf16[2,1,64,1280]{3,2,0,1:T(8,128)(2,1)}, u32[]{:S(2)}, u32[]{:S(2)}) collective-permute-start(bf16[2,1,64,1280]{3,2,0,1:T(8,128)(2,1)} %bitcast.11), channel_id=1, source_target_pairs={{0,32},{32,64},{64,96},{96,128},{128,160},{160,192},{192,224},{224... | collective-permute-start | bytes 983048 | tf_op jit(solution)/shard_map/ppermute | solution.py:36
  24.9 8.6 %collective-permute-start.1 = (bf16[2,1,64,1280]{3,2,0,1:T(8,128)(2,1)}, bf16[2,1,64,1280]{3,2,0,1:T(8,128)(2,1)}, u32[]{:S(2)}, u32[]{:S(2)}) collective-permute-start(bf16[2,1,64,1280]{3,2,0,1:T(8,128)(2,1)} %bitcast.11), channel_id=1, source_target_pairs={{0,224},{32,0},{64,32},{96,64},{128,96},{160,128},{192,160},{224,1... | collective-permute-start | bytes 983048 | tf_op jit(solution)/shard_map/ppermute | solution.py:39
  33.5 2.8 %collective-permute-start.7 = (bf16[256,640]{1,0:T(8,128)(2,1)}, bf16[256,640]{1,0:T(8,128)(2,1)}, u32[]{:S(2)}, u32[]{:S(2)}) collective-permute-start(bf16[256,640]{1,0:T(8,128)(2,1)} %param.5), channel_id=1, source_target_pairs={{0,1},{1,0},{2,3},{3,2},{4,5},{5,4},{6,7},{7,6},{8,9},{9,8},{10,11... | collective-permute-start | bytes 983048 | tf_op jit(solution)/shard_map/ppermute | solution.py:10
  36.3 5.8 %all-to-all-start.1 = ((bf16[4,64,256]{2,1,0:T(8,128)(2,1)}), bf16[4,64,256]{2,1,0:T(8,128)(2,1)S(1)}, u32[]{:S(2)}, u32[]{:S(2)}) async-start(bf16[4,64,256]{2,1,0:T(8,128)(2,1)} %bitcast.8), calls=%async_computation.1 | async-start | bytes 262144 | tf_op jit(solution)/shard_map/all_to_all | solution.py:20
  42.1 0.0 all-gather.2.cloned.1.call-start
  42.1 0.2 broadcast_in_dim.15
  42.4 1.0 bitcast_dynamic-update-slice_fusion
  43.4 1.0 constant_dynamic-update-slice_fusion.1
  44.4 3.5 %all-to-all-done.1 = bf16[4,64,256]{2,1,0:T(8,128)(2,1)S(1)} async-done(((bf16[4,64,256]{2,1,0:T(8,128)(2,1)}), bf16[4,64,256]{2,1,0:T(8,128)(2,1)S(1)}, u32[]{:S(2)}, u32[]{:S(2)}) %all-to-all-start.1) | async-done | bytes 131104 | tf_op jit(solution)/shard_map/all_to_all | solution.py:20
  47.9 0.7 pad_maximum_fusion.3
  48.6 0.0 all-gather.2.cloned.1.call-update
  48.6 0.0 collective-permute-done.7
  48.6 1.0 constant_dynamic-update-slice_fusion
  49.7 2.6 %collective-permute-start.8 = (bf16[256,1280]{1,0:T(8,128)(2,1)S(1)}, bf16[256,1280]{1,0:T(8,128)(2,1)S(1)}, u32[]{:S(2)}, u32[]{:S(2)}) collective-permute-start(bf16[256,1280]{1,0:T(8,128)(2,1)S(1)} %constant_dynamic-update-slice_fusion), channel_id=1, source_target_pairs={{0,16},{16,0},{1,17},{17,1},{2,18},{18,2},{3,19},{19,3},{4,20},{20... | collective-permute-start | bytes 1966088 | tf_op jit(solution)/shard_map/ppermute | solution.py:10
  52.3 0.0 collective-permute-done
  52.3 1.9 %collective-permute-start.2 = (bf16[2,1,64,1280]{3,2,0,1:T(8,128)(2,1)}, bf16[2,1,64,1280]{3,2,0,1:T(8,128)(2,1)S(1)}, u32[]{:S(2)}, u32[]{:S(2)}) collective-permute-start(bf16[2,1,64,1280]{3,2,0,1:T(8,128)(2,1)} %collective-permute-done), channel_id=1, source_target_pairs={{0,32},{32,64},{64,96},{96,128},{128,160},{160,192},{192,224},{224... | collective-permute-start | bytes 983048 | tf_op jit(solution)/shard_map/ppermute | solution.py:36
  54.2 0.0 collective-permute-done.1
  54.3 4.6 %collective-permute-start.3 = (bf16[2,1,64,1280]{3,2,0,1:T(8,128)(2,1)}, bf16[2,1,64,1280]{3,2,0,1:T(8,128)(2,1)S(1)}, u32[]{:S(2)}, u32[]{:S(2)}) collective-permute-start(bf16[2,1,64,1280]{3,2,0,1:T(8,128)(2,1)} %collective-permute-done.1), channel_id=1, source_target_pairs={{0,224},{32,0},{64,32},{96,64},{128,96},{160,128},{192,160},{224,1... | collective-permute-start | bytes 983048 | tf_op jit(solution)/shard_map/ppermute | solution.py:39
  58.8 1.0 bitcast_dynamic-update-slice_fusion.7
  59.8 1.0 bitcast_dynamic-update-slice_fusion.6
  60.8 4.1 %collective-permute-done.2 = bf16[2,1,64,1280]{3,2,0,1:T(8,128)(2,1)S(1)} collective-permute-done((bf16[2,1,64,1280]{3,2,0,1:T(8,128)(2,1)}, bf16[2,1,64,1280]{3,2,0,1:T(8,128)(2,1)S(1)}, u32[]{:S(2)}, u32[]{:S(2)}) %collective-permute-start.2) | collective-permute-done | bytes 327712 | tf_op jit(solution)/shard_map/ppermute | solution.py:36
  65.0 1.9 %collective-permute-start.4 = (bf16[2,1,64,1280]{3,2,0,1:T(8,128)(2,1)S(1)}, bf16[2,1,64,1280]{3,2,0,1:T(8,128)(2,1)S(1)}, u32[]{:S(2)}, u32[]{:S(2)}) collective-permute-start(bf16[2,1,64,1280]{3,2,0,1:T(8,128)(2,1)S(1)} %collective-permute-done.2), channel_id=1, source_target_pairs={{0,32},{32,64},{64,96},{96,128},{128,160},{160,192},{192,224},{224... | collective-permute-start | bytes 983048 | tf_op jit(solution)/shard_map/ppermute | solution.py:36
  66.9 0.0 collective-permute-done.3
  66.9 4.6 %collective-permute-start.5 = (bf16[2,1,64,1280]{3,2,0,1:T(8,128)(2,1)S(1)}, bf16[2,1,64,1280]{3,2,0,1:T(8,128)(2,1)S(1)}, u32[]{:S(2)}, u32[]{:S(2)}) collective-permute-start(bf16[2,1,64,1280]{3,2,0,1:T(8,128)(2,1)S(1)} %collective-permute-done.3), channel_id=1, source_target_pairs={{0,224},{32,0},{64,32},{96,64},{128,96},{160,128},{192,160},{224,1... | collective-permute-start | bytes 983048 | tf_op jit(solution)/shard_map/ppermute | solution.py:39
  71.5 5.1 %collective-permute-done.4 = bf16[2,1,64,1280]{3,2,0,1:T(8,128)(2,1)S(1)} collective-permute-done((bf16[2,1,64,1280]{3,2,0,1:T(8,128)(2,1)S(1)}, bf16[2,1,64,1280]{3,2,0,1:T(8,128)(2,1)S(1)}, u32[]{:S(2)}, u32[]{:S(2)}) %collective-permute-start.4) | collective-permute-done | bytes 327712 | tf_op jit(solution)/shard_map/ppermute | solution.py:36
  76.6 1.9 %collective-permute-start.6 = (bf16[2,1,64,1280]{3,2,0,1:T(8,128)(2,1)S(1)}, bf16[2,1,64,1280]{3,2,0,1:T(8,128)(2,1)S(1)}, u32[]{:S(2)}, u32[]{:S(2)}) collective-permute-start(bf16[2,1,64,1280]{3,2,0,1:T(8,128)(2,1)S(1)} %collective-permute-done.4), channel_id=1, source_target_pairs={{0,32},{32,64},{64,96},{96,128},{128,160},{160,192},{192,224},{224... | collective-permute-start | bytes 983048 | tf_op jit(solution)/shard_map/ppermute | solution.py:36
  78.5 0.0 collective-permute-done.8
  78.5 0.1 broadcast_select_fusion.1
  78.7 0.0 collective-permute-done.5
  78.7 1.2 pad_maximum_fusion
  79.9 7.4 %collective-permute-done.6 = bf16[2,1,64,1280]{3,2,0,1:T(8,128)(2,1)S(1)} collective-permute-done((bf16[2,1,64,1280]{3,2,0,1:T(8,128)(2,1)S(1)}, bf16[2,1,64,1280]{3,2,0,1:T(8,128)(2,1)S(1)}, u32[]{:S(2)}, u32[]{:S(2)}) %collective-permute-start.6) | collective-permute-done | bytes 327712 | tf_op jit(solution)/shard_map/ppermute | solution.py:36
  87.3 0.0 all-gather.2.cloned.1.call-done
  87.4 0.0 copy-start
  87.4 2.9 %fusion.5 = f32[512,1280]{1,0:T(8,128)S(1)} fusion(bf16[1024,512]{1,0:T(8,128)(2,1)} %all-gather.2.cloned.1.call-done, bf16[1024,1280]{1,0:T(8,128)(2,1)S(1)} %bitcast.48), kind=kOutput, calls=%fused_computation.29 | convolution fusion | flops 1342177280 | bytes 6291456 | tf_op jit(solution)/shard_map/dot_general | solution.py:81
  90.3 0.1 dynamic-slice_convert_fusion
  90.4 4.4 %collective-permute-start.9 = (bf16[256,1280]{1,0:T(8,128)(2,1)S(1)}, bf16[256,1280]{1,0:T(8,128)(2,1)S(1)}, u32[]{:S(2)}, u32[]{:S(2)}) collective-permute-start(bf16[256,1280]{1,0:T(8,128)(2,1)S(1)} %dynamic-slice_convert_fusion), channel_id=1, source_target_pairs={{0,16},{16,0},{1,17},{17,1},{2,18},{18,2},{3,19},{19,3},{4,20},{20... | collective-permute-start | bytes 1966088 | tf_op jit(solution)/shard_map/ppermute | solution.py:10
  94.8 0.0 copy-done
  94.8 0.9 convolution_convert_fusion.1
  95.7 0.9 convolution_convert_fusion
  96.6 1.1 pad_maximum_fusion.1
  97.6 0.0 collective-permute-done.9
  97.6 0.1 convert_add_fusion
  97.8 7.3 %all-to-all-start.2 = ((bf16[32,64,256]{2,1,0:T(8,128)(2,1)}), bf16[32,64,256]{2,1,0:T(8,128)(2,1)S(1)}, u32[]{:S(2)}, u32[]{:S(2)}) async-start(bf16[32,64,256]{2,1,0:T(8,128)(2,1)} %bitcast.21), calls=%async_computation.2 | async-start | bytes 2097152 | tf_op jit(solution)/shard_map/all_to_all | solution.py:20
  105.1 4.8 %collective-permute-start.10 = (bf16[256,640]{1,0:T(8,128)(2,1)S(1)}, bf16[256,640]{1,0:T(8,128)(2,1)S(1)}, u32[]{:S(2)}, u32[]{:S(2)}) collective-permute-start(bf16[256,640]{1,0:T(8,128)(2,1)S(1)} %slice.50), channel_id=1, source_target_pairs={{0,1},{1,0},{2,3},{3,2},{4,5},{5,4},{6,7},{7,6},{8,9},{9,8},{10,11... | collective-permute-start | bytes 983048 | tf_op jit(solution)/shard_map/ppermute | solution.py:10
  109.9 13.3 %collective-permute-done.10 = bf16[256,640]{1,0:T(8,128)(2,1)S(1)} collective-permute-done((bf16[256,640]{1,0:T(8,128)(2,1)S(1)}, bf16[256,640]{1,0:T(8,128)(2,1)S(1)}, u32[]{:S(2)}, u32[]{:S(2)}) %collective-permute-start.10) | collective-permute-done | bytes 327712 | tf_op jit(solution)/shard_map/ppermute | solution.py:10
  123.2 0.9 convert_add_fusion.1
  124.1 9.5 %all-to-all-done.2 = bf16[32,64,256]{2,1,0:T(8,128)(2,1)S(1)} async-done(((bf16[32,64,256]{2,1,0:T(8,128)(2,1)}), bf16[32,64,256]{2,1,0:T(8,128)(2,1)S(1)}, u32[]{:S(2)}, u32[]{:S(2)}) %all-to-all-start.2) | async-done | bytes 1048608 | tf_op jit(solution)/shard_map/all_to_all | solution.py:20
  133.6 0.8 reduce_sum.12
  (10 shorter events, 0.3 us)
Async XLA Ops:
  8.8 10.4 %all-to-all-start = ((bf16[4,64,640]{2,1,0:T(8,128)(2,1)}), bf16[4,64,640]{2,1,0:T(8,128)(2,1)S(1)}, u32[]{:S(2)}, u32[]{:S(2)}) async-start(bf16[4,64,640]{2,1,0:T(8,128)(2,1)} %bitcast.1), calls=%async_computation | async-start | bytes 655360 | tf_op jit(solution)/shard_map/all_to_all | solution.py:20
  20.1 32.2 %collective-permute-start = (bf16[2,1,64,1280]{3,2,0,1:T(8,128)(2,1)}, bf16[2,1,64,1280]{3,2,0,1:T(8,128)(2,1)}, u32[]{:S(2)}, u32[]{:S(2)}) collective-permute-start(bf16[2,1,64,1280]{3,2,0,1:T(8,128)(2,1)} %bitcast.11), channel_id=1, source_target_pairs={{0,32},{32,64},{64,96},{96,128},{128,160},{160,192},{192,224},{224... | collective-permute-start | bytes 983048 | tf_op jit(solution)/shard_map/ppermute | solution.py:36
  24.9 29.3 %collective-permute-start.1 = (bf16[2,1,64,1280]{3,2,0,1:T(8,128)(2,1)}, bf16[2,1,64,1280]{3,2,0,1:T(8,128)(2,1)}, u32[]{:S(2)}, u32[]{:S(2)}) collective-permute-start(bf16[2,1,64,1280]{3,2,0,1:T(8,128)(2,1)} %bitcast.11), channel_id=1, source_target_pairs={{0,224},{32,0},{64,32},{96,64},{128,96},{160,128},{192,160},{224,1... | collective-permute-start | bytes 983048 | tf_op jit(solution)/shard_map/ppermute | solution.py:39
  33.5 15.1 %collective-permute-start.7 = (bf16[256,640]{1,0:T(8,128)(2,1)}, bf16[256,640]{1,0:T(8,128)(2,1)}, u32[]{:S(2)}, u32[]{:S(2)}) collective-permute-start(bf16[256,640]{1,0:T(8,128)(2,1)} %param.5), channel_id=1, source_target_pairs={{0,1},{1,0},{2,3},{3,2},{4,5},{5,4},{6,7},{7,6},{8,9},{9,8},{10,11... | collective-permute-start | bytes 983048 | tf_op jit(solution)/shard_map/ppermute | solution.py:10
  36.3 11.6 %all-to-all-start.1 = ((bf16[4,64,256]{2,1,0:T(8,128)(2,1)}), bf16[4,64,256]{2,1,0:T(8,128)(2,1)S(1)}, u32[]{:S(2)}, u32[]{:S(2)}) async-start(bf16[4,64,256]{2,1,0:T(8,128)(2,1)} %bitcast.8), calls=%async_computation.1 | async-start | bytes 262144 | tf_op jit(solution)/shard_map/all_to_all | solution.py:20
  42.1 45.3 %all-gather.2.cloned.1.call-start = ((), (), s32[]{:S(2)}) async-start(), calls=%async_computation.3 | async-start | bytes 1179648 | tf_op jit(solution)/shard_map/all_gather | solution.py:62
  49.7 28.9 %collective-permute-start.8 = (bf16[256,1280]{1,0:T(8,128)(2,1)S(1)}, bf16[256,1280]{1,0:T(8,128)(2,1)S(1)}, u32[]{:S(2)}, u32[]{:S(2)}) collective-permute-start(bf16[256,1280]{1,0:T(8,128)(2,1)S(1)} %constant_dynamic-update-slice_fusion), channel_id=1, source_target_pairs={{0,16},{16,0},{1,17},{17,1},{2,18},{18,2},{3,19},{19,3},{4,20},{20... | collective-permute-start | bytes 1966088 | tf_op jit(solution)/shard_map/ppermute | solution.py:10
  52.3 12.6 %collective-permute-start.2 = (bf16[2,1,64,1280]{3,2,0,1:T(8,128)(2,1)}, bf16[2,1,64,1280]{3,2,0,1:T(8,128)(2,1)S(1)}, u32[]{:S(2)}, u32[]{:S(2)}) collective-permute-start(bf16[2,1,64,1280]{3,2,0,1:T(8,128)(2,1)} %collective-permute-done), channel_id=1, source_target_pairs={{0,32},{32,64},{64,96},{96,128},{128,160},{160,192},{192,224},{224... | collective-permute-start | bytes 983048 | tf_op jit(solution)/shard_map/ppermute | solution.py:36
  54.3 12.6 %collective-permute-start.3 = (bf16[2,1,64,1280]{3,2,0,1:T(8,128)(2,1)}, bf16[2,1,64,1280]{3,2,0,1:T(8,128)(2,1)S(1)}, u32[]{:S(2)}, u32[]{:S(2)}) collective-permute-start(bf16[2,1,64,1280]{3,2,0,1:T(8,128)(2,1)} %collective-permute-done.1), channel_id=1, source_target_pairs={{0,224},{32,0},{64,32},{96,64},{128,96},{160,128},{192,160},{224,1... | collective-permute-start | bytes 983048 | tf_op jit(solution)/shard_map/ppermute | solution.py:39
  65.0 11.6 %collective-permute-start.4 = (bf16[2,1,64,1280]{3,2,0,1:T(8,128)(2,1)S(1)}, bf16[2,1,64,1280]{3,2,0,1:T(8,128)(2,1)S(1)}, u32[]{:S(2)}, u32[]{:S(2)}) collective-permute-start(bf16[2,1,64,1280]{3,2,0,1:T(8,128)(2,1)S(1)} %collective-permute-done.2), channel_id=1, source_target_pairs={{0,32},{32,64},{64,96},{96,128},{128,160},{160,192},{192,224},{224... | collective-permute-start | bytes 983048 | tf_op jit(solution)/shard_map/ppermute | solution.py:36
  66.9 11.8 %collective-permute-start.5 = (bf16[2,1,64,1280]{3,2,0,1:T(8,128)(2,1)S(1)}, bf16[2,1,64,1280]{3,2,0,1:T(8,128)(2,1)S(1)}, u32[]{:S(2)}, u32[]{:S(2)}) collective-permute-start(bf16[2,1,64,1280]{3,2,0,1:T(8,128)(2,1)S(1)} %collective-permute-done.3), channel_id=1, source_target_pairs={{0,224},{32,0},{64,32},{96,64},{128,96},{160,128},{192,160},{224,1... | collective-permute-start | bytes 983048 | tf_op jit(solution)/shard_map/ppermute | solution.py:39
  76.6 10.7 %collective-permute-start.6 = (bf16[2,1,64,1280]{3,2,0,1:T(8,128)(2,1)S(1)}, bf16[2,1,64,1280]{3,2,0,1:T(8,128)(2,1)S(1)}, u32[]{:S(2)}, u32[]{:S(2)}) collective-permute-start(bf16[2,1,64,1280]{3,2,0,1:T(8,128)(2,1)S(1)} %collective-permute-done.4), channel_id=1, source_target_pairs={{0,32},{32,64},{64,96},{96,128},{128,160},{160,192},{192,224},{224... | collective-permute-start | bytes 983048 | tf_op jit(solution)/shard_map/ppermute | solution.py:36
  87.4 7.4 %copy-start = (bf16[512,1280]{1,0:T(8,128)(2,1)S(1)}, bf16[512,1280]{1,0:T(8,128)(2,1)}, u32[]{:S(2)}) copy-start(bf16[512,1280]{1,0:T(8,128)(2,1)} %pad_maximum_fusion) | copy-start | bytes 3932164
  90.4 7.3 %collective-permute-start.9 = (bf16[256,1280]{1,0:T(8,128)(2,1)S(1)}, bf16[256,1280]{1,0:T(8,128)(2,1)S(1)}, u32[]{:S(2)}, u32[]{:S(2)}) collective-permute-start(bf16[256,1280]{1,0:T(8,128)(2,1)S(1)} %dynamic-slice_convert_fusion), channel_id=1, source_target_pairs={{0,16},{16,0},{1,17},{17,1},{2,18},{18,2},{3,19},{19,3},{4,20},{20... | collective-permute-start | bytes 1966088 | tf_op jit(solution)/shard_map/ppermute | solution.py:10
  97.8 35.8 %all-to-all-start.2 = ((bf16[32,64,256]{2,1,0:T(8,128)(2,1)}), bf16[32,64,256]{2,1,0:T(8,128)(2,1)S(1)}, u32[]{:S(2)}, u32[]{:S(2)}) async-start(bf16[32,64,256]{2,1,0:T(8,128)(2,1)} %bitcast.21), calls=%async_computation.2 | async-start | bytes 2097152 | tf_op jit(solution)/shard_map/all_to_all | solution.py:20
  105.1 18.1 %collective-permute-start.10 = (bf16[256,640]{1,0:T(8,128)(2,1)S(1)}, bf16[256,640]{1,0:T(8,128)(2,1)S(1)}, u32[]{:S(2)}, u32[]{:S(2)}) collective-permute-start(bf16[256,640]{1,0:T(8,128)(2,1)S(1)} %slice.50), channel_id=1, source_target_pairs={{0,1},{1,0},{2,3},{3,2},{4,5},{5,4},{6,7},{7,6},{8,9},{9,8},{10,11... | collective-permute-start | bytes 983048 | tf_op jit(solution)/shard_map/ppermute | solution.py:10
Sparse Core Ops, SparseCore 0:
  48.7 33.3 all-gather.1

commit v3 on v2

v3 whole, which is shorter than its diff:
```python
import jax
import jax.numpy as jnp
from jax import lax
from jax.sharding import Mesh, PartitionSpec as P

SWAP = ((0, 1), (1, 0))


def swap(block, axis):
    return lax.ppermute(block, axis, SWAP)


def in_order(own, kept, got, axis):
    return jnp.concatenate(
        [jnp.where(own == 0, kept, got), jnp.where(own == 0, got, kept)], axis=axis
    )


def keep_and_give(block, own):
    half = block.shape[0] // 2
    kept = lax.dynamic_slice_in_dim(block, own * half, half, 0)
    given = lax.dynamic_slice_in_dim(block, (1 - own) * half, half, 0)
    return kept, given


def exchange(pieces, axes):
    return lax.all_to_all(pieces, axes, split_axis=0, concat_axis=0, tiled=True)


def ring_gather(block, axis, lanes):
    size = lax.axis_size(axis)
    me = lax.axis_index(axis)
    up = [(i, (i + 1) % size) for i in range(size)]
    down = [(i, (i - 1) % size) for i in range(size)]
    panel = jnp.zeros((block.shape[0], size) + block.shape[1:], block.dtype)

    def put(panel, block, first, owner):
        at = (first, lax.rem(owner + size, size), 0, 0)
        return lax.dynamic_update_slice(panel, block[:, None], at)

    panel = put(panel, block, 0, me)
    step_rows = block.shape[0] // lanes
    rising = [block[i * step_rows : (i + 1) * step_rows] for i in range(lanes)]
    falling = list(rising)
    for step in range(1, size // 2):
        for i in range(lanes):
            rising[i] = lax.ppermute(rising[i], axis, up)
            falling[i] = lax.ppermute(falling[i], axis, down)
            panel = put(panel, rising[i], i * step_rows, me - step)
            panel = put(panel, falling[i], i * step_rows, me + step)
    rising, falling = jnp.concatenate(rising), jnp.concatenate(falling)
    middle = block.shape[0] // 2
    panel = put(panel, lax.ppermute(rising[:middle], axis, up), 0, me + size // 2)
    return put(panel, lax.ppermute(falling[middle:], axis, down), middle, me + size // 2)


def per_device(inputs, out_grad, weight):
    core = lax.axis_index("core")
    half = lax.axis_index("xh")
    tokens, columns = out_grad.shape
    part = tokens // 2
    features = inputs.shape[1]

    pieces = jnp.broadcast_to(out_grad.reshape(1, 2, part, columns), (2, 2, part, columns))
    pieces = pieces.reshape(4, part, columns)
    pieces = exchange(pieces, ("xl", "xh")).reshape(2, 2, part, columns)
    grads = in_order(half, pieces[:, 0], pieces[:, 1], 2)
    grads, inputs, weight = lax.optimization_barrier((grads, inputs, weight))
    grads = ring_gather(grads, "z", 1).reshape(-1, 2 * columns)

    kept, given = keep_and_give(inputs, core)
    acts = jnp.concatenate([kept, swap(given, "core")], axis=1)
    kept, given = keep_and_give(acts, half)
    acts = in_order(half, kept, swap(given, "xh"), 0)
    weights = in_order(core, weight, swap(weight, "core"), 0)
    acts = lax.all_gather(acts, "y", axis=0, tiled=True)
    weights = jnp.concatenate([weights, swap(weights, "xh")], axis=1)

    grads, weights = lax.optimization_barrier((grads, weights))
    partial = jnp.concatenate(
        [
            lax.dot_general(
                grads,
                weights[i * features : (i + 1) * features],
                (((1,), (1,)), ((), ())),
                preferred_element_type=jnp.float32,
            ).astype(jnp.bfloat16)
            for i in range(2)
        ],
        axis=0,
    )
    shares = exchange(partial.reshape(-1, part, features), ("core", "y", "xh"))
    shares = shares.reshape(2, -1, 2, part, features).astype(jnp.float32)
    input_grad = jnp.sum(shares, axis=1).astype(jnp.bfloat16).reshape(-1, features)

    w_part = lax.dot_general(
        acts, grads, (((0,), (0,)), ((), ())), preferred_element_type=jnp.float32
    )
    w_part = w_part[:features] + swap(w_part[features:].astype(jnp.bfloat16), "core")
    w_grad = w_part[:, :columns] + swap(w_part[:, columns:].astype(jnp.bfloat16), "xh")
    return (w_grad, input_grad)


def solution(mesh):
    rows, cols = mesh.devices.shape
    split = Mesh(
        mesh.devices.reshape(2, rows // 4, 2, cols // 2, 2), ("xl", "z", "core", "y", "xh")
    )
    row, col = ("xl", "z", "core"), ("y", "xh")
    return jax.shard_map(
        per_device,
        mesh=split,
        in_specs=(P(col, row), P(row, col), P(row, col)),
        out_specs=(P(row, col), P(col, row)),
        check_vma=False,
    )
```

time: 142 us -> 135 us (0.951)
  waiting for transfers between devices: 48.6 us -> 35.9 us
  starting transfers between devices: 60.9 us -> 69.7 us
  local copies, waits for them, and re-layouts: 7.25 us -> 3.31 us
    all_to_all x3 -> x2, waiting for transfers between devices: 18.7 us -> 8.57 us  [exchange(): return lax.all_to_all(pieces, axes, split_axis=0, concat_axis=0, tiled=True)]
    ppermute x4 -> x6, starting transfers between devices: 14.7 us -> 23.9 us  [swap(): return lax.ppermute(block, axis, SWAP)]
    ppermute x7 -> x8, waiting for transfers between devices: 16.6 us -> 9.18 us  [the longest x3 7.14 us: ring_gather(): rising[i] = lax.ppermute(rising[i], axis, up)]
    ppermute x4 -> x6, waiting for transfers between devices: 13.3 us -> 18.1 us  [swap(): return lax.ppermute(block, axis, SWAP)]
    dynamic_update_slice x8 -> x9, local copies, waits for them, and re-layouts: 3.15 us -> 1.2 us  [put(): return lax.dynamic_update_slice(panel, block[:, None], at)]
    ppermute x7 -> x8, starting transfers between devices: 28.3 us -> 27.9 us  [the longest x3 15.6 us: ring_gather(): falling[i] = lax.ppermute(falling[i], axis, down)]
    all_to_all x3 -> x2, starting transfers between devices: 17.9 us -> 17.9 us  [exchange(): return lax.all_to_all(pieces, axes, split_axis=0, concat_axis=0, tiled=True)]
  transfers between devices with their start and end apart: 15 -> 17, of which waited for: 7 -> 9; matrix products, arithmetic and copies ran while one was open for 8% -> 8% of each run, Pallas kernels for 0% -> 0%
where the time goes in v3:
time: 135 us; the launch traced here: 134 us
  starting transfers between devices  69.7 us (52%)
  waiting for transfers between devices  35.9 us (27%)
  between operations  14.5 us (11%)
  other arithmetic  6.2 us (5%)
  matrix products  4.56 us (3%)
  local copies, waits for them, and re-layouts  3.31 us (2%)
    ppermute x6, starting transfers between devices, swap(): return lax.ppermute(block, axis, SWAP)  23.9 us
    ppermute x6, waiting for transfers between devices, swap(): return lax.ppermute(block, axis, SWAP)  18.1 us
    all_to_all x2, starting transfers between devices, exchange(): return lax.all_to_all(pieces, axes, split_axis=0, concat_axis=0, tiled=True)  17.9 us
    ppermute x3, starting transfers between devices, ring_gather(): falling[i] = lax.ppermute(falling[i], axis, down)  15.6 us
    all_to_all x2, waiting for transfers between devices, exchange(): return lax.all_to_all(pieces, axes, split_axis=0, concat_axis=0, tiled=True)  8.57 us
    ppermute x3, waiting for transfers between devices, ring_gather(): rising[i] = lax.ppermute(rising[i], axis, up)  7.14 us
    ppermute x3, starting transfers between devices, ring_gather(): rising[i] = lax.ppermute(rising[i], axis, up)  5.75 us
    ppermute x1, starting transfers between devices, ring_gather(): lax.ppermute(falling[middle:], axis, down)  4.57 us
  transfers between devices with their start and end apart: 17, of which 9 were waited for; matrix products, arithmetic and copies ran while one was open for 8% of the time, Pallas kernels for 0%

profile of v3, /device:TPU:1, one launch (start us, length us, event | category | flops | bytes accessed | tf_op | source)
XLA Modules:
  0.0 134.1 jit_solution(2870277452509418914)
XLA Ops:
  7.2 0.0 copy-start
  7.2 1.7 %broadcast_in_dim.38 = bf16[2,2,64,640]{3,2,1,0:T(8,128)(2,1)} broadcast(bf16[2,64,640]{2,1,0:T(8,128)(2,1)} %bitcast.65), dimensions={1,2,3} | broadcast | bytes 491520 | tf_op jit(solution)/shard_map/broadcast_in_dim | solution.py:64
  8.9 4.8 %all-to-all-start = ((bf16[4,64,640]{2,1,0:T(8,128)(2,1)}), bf16[4,64,640]{2,1,0:T(8,128)(2,1)S(1)}, u32[]{:S(2)}, u32[]{:S(2)}) async-start(bf16[4,64,640]{2,1,0:T(8,128)(2,1)} %bitcast.1), calls=%async_computation | async-start | bytes 655360 | tf_op jit(solution)/shard_map/all_to_all | solution.py:27
  13.7 0.0 all-gather.2.cloned.1.call-start
  13.7 5.6 %all-to-all-done = bf16[4,64,640]{2,1,0:T(8,128)(2,1)S(1)} async-done(((bf16[4,64,640]{2,1,0:T(8,128)(2,1)}), bf16[4,64,640]{2,1,0:T(8,128)(2,1)S(1)}, u32[]{:S(2)}, u32[]{:S(2)}) %all-to-all-start) | async-done | bytes 327712 | tf_op jit(solution)/shard_map/all_to_all | solution.py:27
  19.4 0.0 copy-done
  19.4 8.5 %collective-permute-start = (bf16[128,256]{1,0:T(8,128)(2,1)S(1)}, bf16[128,256]{1,0:T(8,128)(2,1)S(1)}, u32[]{:S(2)}, u32[]{:S(2)}) collective-permute-start(bf16[128,256]{1,0:T(8,128)(2,1)S(1)} %get-tuple-element.16), channel_id=1, source_target_pairs={{0,16},{16,0},{1,17},{17,1},{2,18},{18,2},{3,19},{19,3},{4,20},{20... | collective-permute-start | bytes 196616 | tf_op jit(solution)/shard_map/ppermute | solution.py:10
  28.0 1.9 %collective-permute-start.2 = (bf16[2,64,1280]{2,1,0:T(8,128)(2,1)S(1)}, bf16[2,64,1280]{2,1,0:T(8,128)(2,1)}, u32[]{:S(2)}, u32[]{:S(2)}) collective-permute-start(bf16[2,64,1280]{2,1,0:T(8,128)(2,1)S(1)} %pad_maximum_fusion.3), channel_id=1, source_target_pairs={{0,32},{32,64},{64,96},{96,128},{128,160},{160,192},{192,224},{224... | collective-permute-start | bytes 983048 | tf_op jit(solution)/shard_map/ppermute | solution.py:47
  30.0 6.5 %collective-permute-start.3 = (bf16[2,64,1280]{2,1,0:T(8,128)(2,1)S(1)}, bf16[2,64,1280]{2,1,0:T(8,128)(2,1)S(1)}, u32[]{:S(2)}, u32[]{:S(2)}) collective-permute-start(bf16[2,64,1280]{2,1,0:T(8,128)(2,1)S(1)} %pad_maximum_fusion.3), channel_id=1, source_target_pairs={{0,224},{32,0},{64,32},{96,64},{128,96},{160,128},{192,160},{224,1... | collective-permute-start | bytes 983048 | tf_op jit(solution)/shard_map/ppermute | solution.py:48
  36.5 2.2 %collective-permute-start.10 = (bf16[256,640]{1,0:T(8,128)(2,1)}, bf16[256,640]{1,0:T(8,128)(2,1)}, u32[]{:S(2)}, u32[]{:S(2)}) collective-permute-start(bf16[256,640]{1,0:T(8,128)(2,1)} %param.5), channel_id=1, source_target_pairs={{0,16},{16,0},{1,17},{17,1},{2,18},{18,2},{3,19},{19,3},{4,20},{20... | collective-permute-start | bytes 983048 | tf_op jit(solution)/shard_map/ppermute | solution.py:10
  38.7 0.0 collective-permute-done
  38.7 3.1 %collective-permute-start.1 = (bf16[64,512]{1,0:T(8,128)(2,1)S(1)}, bf16[64,512]{1,0:T(8,128)(2,1)S(1)}, u32[]{:S(2)}, u32[]{:S(2)}) collective-permute-start(bf16[64,512]{1,0:T(8,128)(2,1)S(1)} %fusion.4), channel_id=1, source_target_pairs={{0,1},{1,0},{2,3},{3,2},{4,5},{5,4},{6,7},{7,6},{8,9},{9,8},{10,11... | collective-permute-start | bytes 196616 | tf_op jit(solution)/shard_map/ppermute | solution.py:10
  41.8 0.2 broadcast_in_dim.39
  42.1 3.5 %collective-permute-done.1 = bf16[64,512]{1,0:T(8,128)(2,1)S(1)} collective-permute-done((bf16[64,512]{1,0:T(8,128)(2,1)S(1)}, bf16[64,512]{1,0:T(8,128)(2,1)S(1)}, u32[]{:S(2)}, u32[]{:S(2)}) %collective-permute-start.1) | collective-permute-done | bytes 65568 | tf_op jit(solution)/shard_map/ppermute | solution.py:10
  45.6 0.7 pad_maximum_fusion.4
  46.3 0.0 all-gather.2.cloned.1.call-update
  46.3 0.0 collective-permute-done.10
  46.3 1.1 broadcast_select_fusion.1
  47.5 0.1 pad_maximum_fusion.2
  47.5 3.1 %collective-permute-start.11 = (bf16[512,640]{1,0:T(8,128)(2,1)S(1)}, bf16[512,640]{1,0:T(8,128)(2,1)S(1)}, u32[]{:S(2)}, u32[]{:S(2)}) collective-permute-start(bf16[512,640]{1,0:T(8,128)(2,1)S(1)} %pad_maximum_fusion.2), channel_id=1, source_target_pairs={{0,1},{1,0},{2,3},{3,2},{4,5},{5,4},{6,7},{7,6},{8,9},{9,8},{10,11... | collective-permute-start | bytes 1966088 | tf_op jit(solution)/shard_map/ppermute | solution.py:10
  50.6 0.0 collective-permute-done.2
  50.6 1.9 %collective-permute-start.4 = (bf16[2,64,1280]{2,1,0:T(8,128)(2,1)}, bf16[2,64,1280]{2,1,0:T(8,128)(2,1)S(1)}, u32[]{:S(2)}, u32[]{:S(2)}) collective-permute-start(bf16[2,64,1280]{2,1,0:T(8,128)(2,1)} %collective-permute-done.2), channel_id=1, source_target_pairs={{0,32},{32,64},{64,96},{96,128},{128,160},{160,192},{192,224},{224... | collective-permute-start | bytes 983048 | tf_op jit(solution)/shard_map/ppermute | solution.py:47
  52.6 0.0 collective-permute-done.3
  52.6 4.6 %collective-permute-start.5 = (bf16[2,64,1280]{2,1,0:T(8,128)(2,1)S(1)}, bf16[2,64,1280]{2,1,0:T(8,128)(2,1)S(1)}, u32[]{:S(2)}, u32[]{:S(2)}) collective-permute-start(bf16[2,64,1280]{2,1,0:T(8,128)(2,1)S(1)} %collective-permute-done.3), channel_id=1, source_target_pairs={{0,224},{32,0},{64,32},{96,64},{128,96},{160,128},{192,160},{224,1... | collective-permute-start | bytes 983048 | tf_op jit(solution)/shard_map/ppermute | solution.py:48
  57.1 1.0 bitcast_dynamic-update-slice_fusion.5
  58.2 3.7 %collective-permute-done.4 = bf16[2,64,1280]{2,1,0:T(8,128)(2,1)S(1)} collective-permute-done((bf16[2,64,1280]{2,1,0:T(8,128)(2,1)}, bf16[2,64,1280]{2,1,0:T(8,128)(2,1)S(1)}, u32[]{:S(2)}, u32[]{:S(2)}) %collective-permute-start.4) | collective-permute-done | bytes 327712 | tf_op jit(solution)/shard_map/ppermute | solution.py:47
  61.8 1.9 %collective-permute-start.6 = (bf16[2,64,1280]{2,1,0:T(8,128)(2,1)S(1)}, bf16[2,64,1280]{2,1,0:T(8,128)(2,1)S(1)}, u32[]{:S(2)}, u32[]{:S(2)}) collective-permute-start(bf16[2,64,1280]{2,1,0:T(8,128)(2,1)S(1)} %collective-permute-done.4), channel_id=1, source_target_pairs={{0,32},{32,64},{64,96},{96,128},{128,160},{160,192},{192,224},{224... | collective-permute-start | bytes 983048 | tf_op jit(solution)/shard_map/ppermute | solution.py:47
  63.8 0.0 collective-permute-done.5
  63.8 4.6 %collective-permute-start.7 = (bf16[2,64,1280]{2,1,0:T(8,128)(2,1)S(1)}, bf16[2,64,1280]{2,1,0:T(8,128)(2,1)S(1)}, u32[]{:S(2)}, u32[]{:S(2)}) collective-permute-start(bf16[2,64,1280]{2,1,0:T(8,128)(2,1)S(1)} %collective-permute-done.5), channel_id=1, source_target_pairs={{0,224},{32,0},{64,32},{96,64},{128,96},{160,128},{192,160},{224,1... | collective-permute-start | bytes 983048 | tf_op jit(solution)/shard_map/ppermute | solution.py:48
  68.4 3.5 %collective-permute-done.6 = bf16[2,64,1280]{2,1,0:T(8,128)(2,1)S(1)} collective-permute-done((bf16[2,64,1280]{2,1,0:T(8,128)(2,1)S(1)}, bf16[2,64,1280]{2,1,0:T(8,128)(2,1)S(1)}, u32[]{:S(2)}, u32[]{:S(2)}) %collective-permute-start.6) | collective-permute-done | bytes 327712 | tf_op jit(solution)/shard_map/ppermute | solution.py:47
  71.9 1.9 %collective-permute-start.8 = (bf16[1,64,1280]{2,1,0:T(8,128)(2,1)S(1)}, bf16[1,64,1280]{2,1,0:T(8,128)(2,1)S(1)}, u32[]{:S(2)}, u32[]{:S(2)}) collective-permute-start(bf16[1,64,1280]{2,1,0:T(8,128)(2,1)S(1)} %slice.44), channel_id=1, source_target_pairs={{0,32},{32,64},{64,96},{96,128},{128,160},{160,192},{192,224},{224... | collective-permute-start | bytes 491528 | tf_op jit(solution)/shard_map/ppermute | solution.py:53
  73.9 0.0 collective-permute-done.7
  73.9 4.6 %collective-permute-start.9 = (bf16[1,64,1280]{2,1,0:T(8,128)(2,1)S(1)}, bf16[1,64,1280]{2,1,0:T(8,128)(2,1)S(1)}, u32[]{:S(2)}, u32[]{:S(2)}) collective-permute-start(bf16[1,64,1280]{2,1,0:T(8,128)(2,1)S(1)} %slice.45), channel_id=1, source_target_pairs={{0,224},{32,0},{64,32},{96,64},{128,96},{160,128},{192,160},{224,1... | collective-permute-start | bytes 491528 | tf_op jit(solution)/shard_map/ppermute | solution.py:54
  78.5 0.0 collective-permute-done.11
  78.6 0.1 pad_maximum_fusion
  78.7 0.5 collective-permute-done.8
  79.2 1.5 %collective-permute-done.9 = bf16[1,64,1280]{2,1,0:T(8,128)(2,1)S(1)} collective-permute-done((bf16[1,64,1280]{2,1,0:T(8,128)(2,1)S(1)}, bf16[1,64,1280]{2,1,0:T(8,128)(2,1)S(1)}, u32[]{:S(2)}, u32[]{:S(2)}) %collective-permute-start.9) | collective-permute-done | bytes 163872 | tf_op jit(solution)/shard_map/ppermute | solution.py:54
  80.7 0.9 convolution_convert_fusion.1
  81.6 0.9 convolution_convert_fusion
  82.5 1.1 pad_maximum_fusion.1
  83.6 13.1 %all-to-all-start.1 = ((bf16[32,64,256]{2,1,0:T(8,128)(2,1)}), bf16[32,64,256]{2,1,0:T(8,128)(2,1)}, u32[]{:S(2)}, u32[]{:S(2)}) async-start(bf16[32,64,256]{2,1,0:T(8,128)(2,1)} %bitcast.62), calls=%async_computation.1 | async-start | bytes 2097152 | tf_op jit(solution)/shard_map/all_to_all | solution.py:27
  96.7 0.0 all-gather.2.cloned.1.call-done
  96.7 2.8 %fusion.6 = f32[512,1280]{1,0:T(8,128)S(1)} fusion(bf16[1024,512]{1,0:T(8,128)(2,1)} %all-gather.2.cloned.1.call-done, bf16[1024,1280]{1,0:T(8,128)(2,1)S(1)} %bitcast.61), kind=kOutput, calls=%fused_computation.38 | convolution fusion | flops 1342177280 | bytes 6291456 | tf_op jit(solution)/shard_map/dot_general | solution.py:96
  99.5 0.1 slice.62
  99.6 2.2 %collective-permute-start.12 = (bf16[256,1280]{1,0:T(8,128)(2,1)S(1)}, bf16[256,1280]{1,0:T(8,128)(2,1)S(1)}, u32[]{:S(2)}, u32[]{:S(2)}) collective-permute-start(bf16[256,1280]{1,0:T(8,128)(2,1)S(1)} %slice.62), channel_id=1, source_target_pairs={{0,16},{16,0},{1,17},{17,1},{2,18},{18,2},{3,19},{19,3},{4,20},{20... | collective-permute-start | bytes 1966088 | tf_op jit(solution)/shard_map/ppermute | solution.py:10
  101.8 1.8 %collective-permute-done.12 = bf16[256,1280]{1,0:T(8,128)(2,1)S(1)} collective-permute-done((bf16[256,1280]{1,0:T(8,128)(2,1)S(1)}, bf16[256,1280]{1,0:T(8,128)(2,1)S(1)}, u32[]{:S(2)}, u32[]{:S(2)}) %collective-permute-start.12) | collective-permute-done | bytes 655392 | tf_op jit(solution)/shard_map/ppermute | solution.py:10
  103.6 0.1 slice_add_fusion
  103.7 4.8 %collective-permute-start.13 = (bf16[256,640]{1,0:T(8,128)(2,1)S(1)}, bf16[256,640]{1,0:T(8,128)(2,1)S(1)}, u32[]{:S(2)}, u32[]{:S(2)}) collective-permute-start(bf16[256,640]{1,0:T(8,128)(2,1)S(1)} %slice.63), channel_id=1, source_target_pairs={{0,1},{1,0},{2,3},{3,2},{4,5},{5,4},{6,7},{7,6},{8,9},{9,8},{10,11... | collective-permute-start | bytes 983048 | tf_op jit(solution)/shard_map/ppermute | solution.py:10
  108.5 12.8 %collective-permute-done.13 = bf16[256,640]{1,0:T(8,128)(2,1)S(1)} collective-permute-done((bf16[256,640]{1,0:T(8,128)(2,1)S(1)}, bf16[256,640]{1,0:T(8,128)(2,1)S(1)}, u32[]{:S(2)}, u32[]{:S(2)}) %collective-permute-start.13) | collective-permute-done | bytes 327712 | tf_op jit(solution)/shard_map/ppermute | solution.py:10
  121.3 0.9 slice_add_fusion.1
  122.2 3.0 %all-to-all-done.1 = bf16[32,64,256]{2,1,0:T(8,128)(2,1)} async-done(((bf16[32,64,256]{2,1,0:T(8,128)(2,1)}), bf16[32,64,256]{2,1,0:T(8,128)(2,1)}, u32[]{:S(2)}, u32[]{:S(2)}) %all-to-all-start.1) | async-done | bytes 1048608 | tf_op jit(solution)/shard_map/all_to_all | solution.py:27
  125.2 2.1 %reduce_sum.12 = bf16[2,2,64,256]{3,2,1,0:T(8,128)(2,1)} reduce(bf16[2,8,2,64,256]{4,3,2,1,0:T(8,128)(2,1)} %bitcast.26, bf16[]{:T(256)} %constant.55.clone.1), dimensions={1}, to_apply=%region_0.1 | reduce | flops 458752 | bytes 1179650 | tf_op jit(solution)/shard_map/reduce_sum | solution.py:94
  (17 shorter events, 0.4 us)
Async XLA Ops:
  7.2 12.2 %copy-start = (bf16[256,256]{1,0:T(8,128)(2,1)S(1)}, bf16[256,256]{1,0:T(8,128)(2,1)}, u32[]{:S(2)}) copy-start(bf16[256,256]{1,0:T(8,128)(2,1)} %param.3) | copy-start | bytes 393220
  8.9 10.4 %all-to-all-start = ((bf16[4,64,640]{2,1,0:T(8,128)(2,1)}), bf16[4,64,640]{2,1,0:T(8,128)(2,1)S(1)}, u32[]{:S(2)}, u32[]{:S(2)}) async-start(bf16[4,64,640]{2,1,0:T(8,128)(2,1)} %bitcast.1), calls=%async_computation | async-start | bytes 655360 | tf_op jit(solution)/shard_map/all_to_all | solution.py:27
  13.7 83.0 %all-gather.2.cloned.1.call-start = ((), (), s32[]{:S(2)}) async-start(), calls=%async_computation.2 | async-start | bytes 1179648 | tf_op jit(solution)/shard_map/all_gather | solution.py:76
  19.4 19.2 %collective-permute-start = (bf16[128,256]{1,0:T(8,128)(2,1)S(1)}, bf16[128,256]{1,0:T(8,128)(2,1)S(1)}, u32[]{:S(2)}, u32[]{:S(2)}) collective-permute-start(bf16[128,256]{1,0:T(8,128)(2,1)S(1)} %get-tuple-element.16), channel_id=1, source_target_pairs={{0,16},{16,0},{1,17},{17,1},{2,18},{18,2},{3,19},{19,3},{4,20},{20... | collective-permute-start | bytes 196616 | tf_op jit(solution)/shard_map/ppermute | solution.py:10
  28.0 22.6 %collective-permute-start.2 = (bf16[2,64,1280]{2,1,0:T(8,128)(2,1)S(1)}, bf16[2,64,1280]{2,1,0:T(8,128)(2,1)}, u32[]{:S(2)}, u32[]{:S(2)}) collective-permute-start(bf16[2,64,1280]{2,1,0:T(8,128)(2,1)S(1)} %pad_maximum_fusion.3), channel_id=1, source_target_pairs={{0,32},{32,64},{64,96},{96,128},{128,160},{160,192},{192,224},{224... | collective-permute-start | bytes 983048 | tf_op jit(solution)/shard_map/ppermute | solution.py:47
  30.0 22.6 %collective-permute-start.3 = (bf16[2,64,1280]{2,1,0:T(8,128)(2,1)S(1)}, bf16[2,64,1280]{2,1,0:T(8,128)(2,1)S(1)}, u32[]{:S(2)}, u32[]{:S(2)}) collective-permute-start(bf16[2,64,1280]{2,1,0:T(8,128)(2,1)S(1)} %pad_maximum_fusion.3), channel_id=1, source_target_pairs={{0,224},{32,0},{64,32},{96,64},{128,96},{160,128},{192,160},{224,1... | collective-permute-start | bytes 983048 | tf_op jit(solution)/shard_map/ppermute | solution.py:48
  36.5 9.8 %collective-permute-start.10 = (bf16[256,640]{1,0:T(8,128)(2,1)}, bf16[256,640]{1,0:T(8,128)(2,1)}, u32[]{:S(2)}, u32[]{:S(2)}) collective-permute-start(bf16[256,640]{1,0:T(8,128)(2,1)} %param.5), channel_id=1, source_target_pairs={{0,16},{16,0},{1,17},{17,1},{2,18},{18,2},{3,19},{19,3},{4,20},{20... | collective-permute-start | bytes 983048 | tf_op jit(solution)/shard_map/ppermute | solution.py:10
  38.7 6.9 %collective-permute-start.1 = (bf16[64,512]{1,0:T(8,128)(2,1)S(1)}, bf16[64,512]{1,0:T(8,128)(2,1)S(1)}, u32[]{:S(2)}, u32[]{:S(2)}) collective-permute-start(bf16[64,512]{1,0:T(8,128)(2,1)S(1)} %fusion.4), channel_id=1, source_target_pairs={{0,1},{1,0},{2,3},{3,2},{4,5},{5,4},{6,7},{7,6},{8,9},{9,8},{10,11... | collective-permute-start | bytes 196616 | tf_op jit(solution)/shard_map/ppermute | solution.py:10
  47.5 31.0 %collective-permute-start.11 = (bf16[512,640]{1,0:T(8,128)(2,1)S(1)}, bf16[512,640]{1,0:T(8,128)(2,1)S(1)}, u32[]{:S(2)}, u32[]{:S(2)}) collective-permute-start(bf16[512,640]{1,0:T(8,128)(2,1)S(1)} %pad_maximum_fusion.2), channel_id=1, source_target_pairs={{0,1},{1,0},{2,3},{3,2},{4,5},{5,4},{6,7},{7,6},{8,9},{9,8},{10,11... | collective-permute-start | bytes 1966088 | tf_op jit(solution)/shard_map/ppermute | solution.py:10
  50.6 11.2 %collective-permute-start.4 = (bf16[2,64,1280]{2,1,0:T(8,128)(2,1)}, bf16[2,64,1280]{2,1,0:T(8,128)(2,1)S(1)}, u32[]{:S(2)}, u32[]{:S(2)}) collective-permute-start(bf16[2,64,1280]{2,1,0:T(8,128)(2,1)} %collective-permute-done.2), channel_id=1, source_target_pairs={{0,32},{32,64},{64,96},{96,128},{128,160},{160,192},{192,224},{224... | collective-permute-start | bytes 983048 | tf_op jit(solution)/shard_map/ppermute | solution.py:47
  52.6 11.2 %collective-permute-start.5 = (bf16[2,64,1280]{2,1,0:T(8,128)(2,1)S(1)}, bf16[2,64,1280]{2,1,0:T(8,128)(2,1)S(1)}, u32[]{:S(2)}, u32[]{:S(2)}) collective-permute-start(bf16[2,64,1280]{2,1,0:T(8,128)(2,1)S(1)} %collective-permute-done.3), channel_id=1, source_target_pairs={{0,224},{32,0},{64,32},{96,64},{128,96},{160,128},{192,160},{224,1... | collective-permute-start | bytes 983048 | tf_op jit(solution)/shard_map/ppermute | solution.py:48
  61.8 10.1 %collective-permute-start.6 = (bf16[2,64,1280]{2,1,0:T(8,128)(2,1)S(1)}, bf16[2,64,1280]{2,1,0:T(8,128)(2,1)S(1)}, u32[]{:S(2)}, u32[]{:S(2)}) collective-permute-start(bf16[2,64,1280]{2,1,0:T(8,128)(2,1)S(1)} %collective-permute-done.4), channel_id=1, source_target_pairs={{0,32},{32,64},{64,96},{96,128},{128,160},{160,192},{192,224},{224... | collective-permute-start | bytes 983048 | tf_op jit(solution)/shard_map/ppermute | solution.py:47
  63.8 10.1 %collective-permute-start.7 = (bf16[2,64,1280]{2,1,0:T(8,128)(2,1)S(1)}, bf16[2,64,1280]{2,1,0:T(8,128)(2,1)S(1)}, u32[]{:S(2)}, u32[]{:S(2)}) collective-permute-start(bf16[2,64,1280]{2,1,0:T(8,128)(2,1)S(1)} %collective-permute-done.5), channel_id=1, source_target_pairs={{0,224},{32,0},{64,32},{96,64},{128,96},{160,128},{192,160},{224,1... | collective-permute-start | bytes 983048 | tf_op jit(solution)/shard_map/ppermute | solution.py:48
  71.9 7.3 %collective-permute-start.8 = (bf16[1,64,1280]{2,1,0:T(8,128)(2,1)S(1)}, bf16[1,64,1280]{2,1,0:T(8,128)(2,1)S(1)}, u32[]{:S(2)}, u32[]{:S(2)}) collective-permute-start(bf16[1,64,1280]{2,1,0:T(8,128)(2,1)S(1)} %slice.44), channel_id=1, source_target_pairs={{0,32},{32,64},{64,96},{96,128},{128,160},{160,192},{192,224},{224... | collective-permute-start | bytes 491528 | tf_op jit(solution)/shard_map/ppermute | solution.py:53
  73.9 6.8 %collective-permute-start.9 = (bf16[1,64,1280]{2,1,0:T(8,128)(2,1)S(1)}, bf16[1,64,1280]{2,1,0:T(8,128)(2,1)S(1)}, u32[]{:S(2)}, u32[]{:S(2)}) collective-permute-start(bf16[1,64,1280]{2,1,0:T(8,128)(2,1)S(1)} %slice.45), channel_id=1, source_target_pairs={{0,224},{32,0},{64,32},{96,64},{128,96},{160,128},{192,160},{224,1... | collective-permute-start | bytes 491528 | tf_op jit(solution)/shard_map/ppermute | solution.py:54
  83.6 41.7 %all-to-all-start.1 = ((bf16[32,64,256]{2,1,0:T(8,128)(2,1)}), bf16[32,64,256]{2,1,0:T(8,128)(2,1)}, u32[]{:S(2)}, u32[]{:S(2)}) async-start(bf16[32,64,256]{2,1,0:T(8,128)(2,1)} %bitcast.62), calls=%async_computation.1 | async-start | bytes 2097152 | tf_op jit(solution)/shard_map/all_to_all | solution.py:27
  99.6 4.0 %collective-permute-start.12 = (bf16[256,1280]{1,0:T(8,128)(2,1)S(1)}, bf16[256,1280]{1,0:T(8,128)(2,1)S(1)}, u32[]{:S(2)}, u32[]{:S(2)}) collective-permute-start(bf16[256,1280]{1,0:T(8,128)(2,1)S(1)} %slice.62), channel_id=1, source_target_pairs={{0,16},{16,0},{1,17},{17,1},{2,18},{18,2},{3,19},{19,3},{4,20},{20... | collective-permute-start | bytes 1966088 | tf_op jit(solution)/shard_map/ppermute | solution.py:10
  103.7 17.6 %collective-permute-start.13 = (bf16[256,640]{1,0:T(8,128)(2,1)S(1)}, bf16[256,640]{1,0:T(8,128)(2,1)S(1)}, u32[]{:S(2)}, u32[]{:S(2)}) collective-permute-start(bf16[256,640]{1,0:T(8,128)(2,1)S(1)} %slice.63), channel_id=1, source_target_pairs={{0,1},{1,0},{2,3},{3,2},{4,5},{5,4},{6,7},{7,6},{8,9},{9,8},{10,11... | collective-permute-start | bytes 983048 | tf_op jit(solution)/shard_map/ppermute | solution.py:10
Sparse Core Ops, SparseCore 0:
  46.4 34.3 all-gather.1

commit v4 on v0

v4 whole, which is shorter than its diff:
```python
import functools

import jax
import jax.numpy as jnp
from jax import lax
from jax.experimental import pallas as pl
from jax.experimental.pallas import tpu as pltpu
from jax.sharding import Mesh, PartitionSpec as P


def swap(block, axis):
    return lax.ppermute(block, axis, ((0, 1), (1, 0)))


def in_order(own, kept, got, axis):
    return jnp.concatenate(
        [jnp.where(own == 0, kept, got), jnp.where(own == 0, got, kept)], axis=axis
    )


def pick(block, index, axis):
    return lax.dynamic_slice_in_dim(block, index, 1, axis)


def exchange(pieces, axes):
    return lax.all_to_all(pieces, axes, split_axis=0, concat_axis=0, tiled=True)


def times(left, right, left_dims, right_dims):
    return lax.dot_general(
        left, right, ((left_dims, right_dims), ((), ())), preferred_element_type=jnp.float32
    )


def project_kernel(part, own_ref, other_ref, weight_ref, out_ref):
    features = out_ref.shape[-1]
    for c, g in enumerate((own_ref, other_ref)):
        for i in range(2):
            w = weight_ref.at[:, i * features : (i + 1) * features]
            acc = times(g[0], w[0], (1,), (1,)) + times(g[1], w[1], (1,), (1,))
            acc = acc.reshape(-1, part, features)
            out_ref[i, :, c * part : (c + 1) * part, :] = acc.astype(out_ref.dtype)


def project(own, other, weights, part):
    _, rows, columns = own.shape
    features = weights.shape[1] // 2
    blocks = rows // part
    steps = 4
    grads_spec = pl.BlockSpec((2, rows // steps, columns), lambda r: (0, r, 0))
    return pl.pallas_call(
        functools.partial(project_kernel, part),
        out_shape=jax.ShapeDtypeStruct((2, blocks, 2 * part, features), own.dtype),
        grid=(steps,),
        in_specs=[grads_spec, grads_spec, pl.BlockSpec(weights.shape, lambda r: (0, 0, 0))],
        out_specs=pl.BlockSpec(
            (2, blocks // steps, 2 * part, features), lambda r: (0, r, 0, 0)
        ),
        compiler_params=pltpu.CompilerParams(vmem_limit_bytes=24 * 2**20),
        cost_estimate=pl.CostEstimate(
            flops=8 * rows * columns * 2 * features,
            bytes_accessed=2 * (2 * own.size + weights.size + 4 * rows * features),
            transcendentals=0,
        ),
    )(own, other, weights)


def per_device(inputs, out_grad, weight):
    core = lax.axis_index("core")
    near = lax.axis_index("xl")
    far = lax.axis_index("xh")
    depth = lax.axis_size("z")
    tokens, columns = out_grad.shape
    features = inputs.shape[1]
    part = tokens // 4

    grads = jnp.broadcast_to(
        out_grad.reshape(2, 2, part, columns).transpose(1, 0, 2, 3)[:, :, None],
        (2, 2, depth, part, columns),
    ).reshape(-1, part, columns)
    grads = exchange(grads, ("xh", "xl", "z")).reshape(2, -1, columns)

    acts = inputs.reshape(2, 2, 2, part, features)
    acts = jnp.concatenate(
        [pick(acts, near, 1), swap(pick(acts, 1 - near, 1), "xl")], axis=4
    )
    acts = in_order(far, pick(acts, far, 2), swap(pick(acts, 1 - far, 2), "xh"), 2)
    acts = jnp.concatenate([pick(acts, core, 0), pick(acts, 1 - core, 0)], axis=0)
    acts = acts.reshape(4 * part, 2 * features)
    weights = in_order(far, weight[None], swap(weight, "xh")[None], 0)
    weights, acts = lax.optimization_barrier((weights, acts))
    weights = in_order(near, weights, swap(weights, "xl"), 1)

    acts = lax.all_gather(acts, "y", axis=0, tiled=True)
    grads, weights = lax.optimization_barrier((grads, weights))
    others = swap(grads, "core")

    partial = project(grads, others, weights, part)
    shares = exchange(partial.reshape(-1, 2 * part, features), ("xl", "y", "xh"))
    shares = shares.reshape(2, -1, 2, 2, part, features).astype(jnp.float32)
    shares = jnp.sum(shares, axis=1).astype(jnp.bfloat16)
    shares = shares.transpose(2, 0, 1, 3, 4)
    shares = in_order(core, shares[:1], shares[1:], 0)
    input_grad = shares.reshape(-1, features)

    acts = acts.reshape(-1, 2, 2 * part, 2 * features)
    w_part = sum(
        times(acts[:, i].reshape(-1, 2 * features), g, (0,), (1,))
        for i, g in enumerate((grads, others))
    )
    w_part = w_part.reshape(2, features, 2, columns)

    def piece(a, b):
        return pick(pick(w_part, a, 0), b, 2).reshape(features, columns)

    w_grad = piece(0, far)
    for a, b in ((1, 0), (0, 1), (1, 1)):
        perm = [(i, i ^ (2 * a + b)) for i in range(4)]
        sent = piece(a, far ^ b).astype(jnp.bfloat16)
        w_grad = w_grad + lax.ppermute(sent, ("xl", "xh"), perm)
    return (w_grad, input_grad)


def solution(mesh):
    rows, cols = mesh.devices.shape
    split = Mesh(
        mesh.devices.reshape(2, rows // 4, 2, cols // 2, 2), ("xl", "z", "core", "y", "xh")
    )
    row, col = ("xl", "z", "core"), ("y", "xh")
    return jax.shard_map(
        per_device,
        mesh=split,
        in_specs=(P(col, row), P(row, col), P(row, col)),
        out_specs=(P(row, col), P(col, row)),
        check_vma=False,
    )
```

time: 401 us -> 136 us (0.34)
  waiting for transfers between devices: 373 us -> 50.1 us
  starting transfers between devices: 0.11 us -> 52 us
  matrix products: 11.5 us -> 1.78 us
  local copies, waits for them, and re-layouts: 0.01 us -> 6.62 us
  other arithmetic: 0 us -> 4.57 us
  Pallas kernels: 0 us -> 4.17 us
    reduce_scatter x1 -> x0, waiting for transfers between devices: 208 us -> none  [per_device(): lax.psum_scatter(lax.dot_general(grad_panel, weight, (((1,), (1,)), ((),...]
    all_gather x2 -> x1, waiting for transfers between devices: 163 us -> 4.54 us  [per_device(): acts = lax.all_gather(acts, 'y', axis=0, tiled=True)]
    ppermute x0 -> x8, waiting for transfers between devices: none -> 45.6 us  [the longest x5 30.5 us: swap(): return lax.ppermute(block, axis, ((0, 1), (1, 0)))]
    ppermute x0 -> x8, starting transfers between devices: none -> 27.8 us  [the longest x5 18.5 us: swap(): return lax.ppermute(block, axis, ((0, 1), (1, 0)))]
    all_to_all x0 -> x2, starting transfers between devices: none -> 24.2 us  [exchange(): return lax.all_to_all(pieces, axes, split_axis=0, concat_axis=0, tiled=True)]
    dot_general x2, matrix products: 11.5 us -> 1.78 us  [times(): lax.dot_general(left, right, ((left_dims, right_dims), ((), ())), preferr...]
    pallas_call x0 -> x1, Pallas kernels: none -> 4.17 us  [project(): pl.pallas_call(functools.partial(project_kernel, part), out_shape=jax.Sha...]
  transfers between devices with their start and end apart: 3 -> 11, of which waited for: 3 -> 9; matrix products, arithmetic and copies ran while one was open for 3% -> 5% of each run, Pallas kernels for 0% -> 3%
where the time goes in v4:
time: 136 us; the launch traced here: 134 us
  starting transfers between devices  52 us (38%)
  waiting for transfers between devices  50.1 us (37%)
  between operations  14.3 us (11%)
  local copies, waits for them, and re-layouts  6.62 us (5%)
  other arithmetic  4.57 us (3%)
  Pallas kernels  4.17 us (3%)
  matrix products  1.78 us (1%)
    ppermute x5, waiting for transfers between devices, swap(): return lax.ppermute(block, axis, ((0, 1), (1, 0)))  30.5 us
    all_to_all x2, starting transfers between devices, exchange(): return lax.all_to_all(pieces, axes, split_axis=0, concat_axis=0, tiled=True)  24.2 us
    ppermute x5, starting transfers between devices, swap(): return lax.ppermute(block, axis, ((0, 1), (1, 0)))  18.5 us
    ppermute x3, waiting for transfers between devices, per_device(): w_grad = w_grad + lax.ppermute(sent, ('xl', 'xh'), perm)  15.1 us
    ppermute x3, starting transfers between devices, per_device(): w_grad = w_grad + lax.ppermute(sent, ('xl', 'xh'), perm)  9.28 us
    all_gather x1, waiting for transfers between devices, per_device(): acts = lax.all_gather(acts, 'y', axis=0, tiled=True)  4.54 us
    pallas_call x1, Pallas kernels, project(): pl.pallas_call(functools.partial(project_kernel, part), out_shape=jax.Sha...  4.17 us
  transfers between devices with their start and end apart: 11, of which 9 were waited for; matrix products, arithmetic and copies ran while one was open for 5% of the time, Pallas kernels for 3%

profile of v4, /device:TPU:1, one launch (start us, length us, event | category | flops | bytes accessed | tf_op | source)
XLA Modules:
  0.0 133.6 jit_solution(9382129568411558509)
XLA Ops:
  7.2 0.9 copy.18
  8.1 1.2 broadcast_in_dim.2
  9.3 0.0 copy-start.3
  9.3 0.0 copy-start.2
  9.3 13.8 %all-to-all-start = ((bf16[32,32,640]{2,1,0:T(8,128)(2,1)}), bf16[32,32,640]{2,1,0:T(8,128)(2,1)S(1)}, u32[]{:S(2)}, u32[]{:S(2)}) async-start(bf16[32,32,640]{2,1,0:T(8,128)(2,1)} %bitcast.9), calls=%async_computation | async-start | bytes 2621440 | tf_op jit(solution)/shard_map/all_to_all | solution.py:26
  23.1 0.0 all-gather.2.cloned.1.call-start
  23.2 0.0 copy-done.3
  23.2 3.1 %collective-permute-start.1 = (bf16[2,1,2,32,256]{4,3,2,0,1:T(8,128)(2,1)S(1)}, bf16[2,1,2,32,256]{4,3,2,0,1:T(8,128)(2,1)S(1)}, u32[]{:S(2)}, u32[]{:S(2)}) collective-permute-start(bf16[2,1,2,32,256]{4,3,2,0,1:T(8,128)(2,1)S(1)} %get-tuple-element.24), channel_id=1, source_target_pairs={{0,256},{256,0},{1,257},{257,1},{2,258},{258,2},{3,259},{259,3},{4... | collective-permute-start | bytes 196616 | tf_op jit(solution)/shard_map/ppermute | solution.py:12
  26.4 2.4 %collective-permute-done.1 = bf16[2,1,2,32,256]{4,3,2,0,1:T(8,128)(2,1)S(1)} collective-permute-done((bf16[2,1,2,32,256]{4,3,2,0,1:T(8,128)(2,1)S(1)}, bf16[2,1,2,32,256]{4,3,2,0,1:T(8,128)(2,1)S(1)}, u32[]{:S(2)}, u32[]{:S(2)}) %collective-permute-start.1) | collective-permute-done | bytes 65568 | tf_op jit(solution)/shard_map/ppermute | solution.py:12
  28.8 4.2 %collective-permute-start.2 = (bf16[2,1,1,32,512]{4,3,2,0,1:T(8,128)(2,1)S(1)}, bf16[2,1,1,32,512]{4,3,2,0,1:T(8,128)(2,1)S(1)}, u32[]{:S(2)}, u32[]{:S(2)}) collective-permute-start(bf16[2,1,1,32,512]{4,3,2,0,1:T(8,128)(2,1)S(1)} %fusion.7), channel_id=1, source_target_pairs={{0,1},{1,0},{2,3},{3,2},{4,5},{5,4},{6,7},{7,6},{8,9},{9,8},{10,11... | collective-permute-start | bytes 196616 | tf_op jit(solution)/shard_map/ppermute | solution.py:12
  33.0 0.0 copy-done.2
  33.0 2.6 %collective-permute-start = (bf16[256,640]{1,0:T(8,128)(2,1)S(1)}, bf16[256,640]{1,0:T(8,128)(2,1)S(1)}, u32[]{:S(2)}, u32[]{:S(2)}) collective-permute-start(bf16[256,640]{1,0:T(8,128)(2,1)S(1)} %copy-done.2), channel_id=1, source_target_pairs={{0,1},{1,0},{2,3},{3,2},{4,5},{5,4},{6,7},{7,6},{8,9},{9,8},{10,11... | collective-permute-start | bytes 983048 | tf_op jit(solution)/shard_map/ppermute | solution.py:12
  35.6 1.5 %collective-permute-done.2 = bf16[2,1,1,32,512]{4,3,2,0,1:T(8,128)(2,1)S(1)} collective-permute-done((bf16[2,1,1,32,512]{4,3,2,0,1:T(8,128)(2,1)S(1)}, bf16[2,1,1,32,512]{4,3,2,0,1:T(8,128)(2,1)S(1)}, u32[]{:S(2)}, u32[]{:S(2)}) %collective-permute-start.2) | collective-permute-done | bytes 65568 | tf_op jit(solution)/shard_map/ppermute | solution.py:12
  37.2 0.7 pad_maximum_fusion.2
  37.9 10.9 %collective-permute-done = bf16[256,640]{1,0:T(8,128)(2,1)S(1)} collective-permute-done((bf16[256,640]{1,0:T(8,128)(2,1)S(1)}, bf16[256,640]{1,0:T(8,128)(2,1)S(1)}, u32[]{:S(2)}, u32[]{:S(2)}) %collective-permute-start) | collective-permute-done | bytes 327712 | tf_op jit(solution)/shard_map/ppermute | solution.py:12
  48.8 0.1 select_bitcast_fusion.1
  48.9 0.1 pad_maximum_fusion.1
  49.0 1.9 %collective-permute-start.3 = (bf16[2,256,640]{2,1,0:T(8,128)(2,1)S(1)}, bf16[2,256,640]{2,1,0:T(8,128)(2,1)S(1)}, u32[]{:S(2)}, u32[]{:S(2)}) collective-permute-start(bf16[2,256,640]{2,1,0:T(8,128)(2,1)S(1)} %pad_maximum_fusion.1), channel_id=1, source_target_pairs={{0,256},{256,0},{1,257},{257,1},{2,258},{258,2},{3,259},{259,3},{4... | collective-permute-start | bytes 1966088 | tf_op jit(solution)/shard_map/ppermute | solution.py:12
  50.9 0.0 all-gather.2.cloned.1.call-update
  50.9 13.0 %collective-permute-done.3 = bf16[2,256,640]{2,1,0:T(8,128)(2,1)S(1)} collective-permute-done((bf16[2,256,640]{2,1,0:T(8,128)(2,1)S(1)}, bf16[2,256,640]{2,1,0:T(8,128)(2,1)S(1)}, u32[]{:S(2)}, u32[]{:S(2)}) %collective-permute-start.3) | collective-permute-done | bytes 655392 | tf_op jit(solution)/shard_map/ppermute | solution.py:12
  63.9 0.1 broadcast_select_fusion.1
  64.1 1.2 pad_maximum_fusion.weight_ref
  65.2 0.0 all-to-all-done
  65.2 6.7 %collective-permute-start.4 = (bf16[2,512,640]{2,1,0:T(8,128)(2,1)S(1)}, bf16[2,512,640]{2,1,0:T(8,128)(2,1)S(1)}, u32[]{:S(2)}, u32[]{:S(2)}) collective-permute-start(bf16[2,512,640]{2,1,0:T(8,128)(2,1)S(1)} %bitcast.42), channel_id=1, source_target_pairs={{0,16},{16,0},{1,17},{17,1},{2,18},{18,2},{3,19},{19,3},{4,20},{20... | collective-permute-start | bytes 3932168 | tf_op jit(solution)/shard_map/ppermute | solution.py:12
  71.9 2.6 %collective-permute-done.4.other_ref = bf16[2,512,640]{2,1,0:T(8,128)(2,1)S(1)} collective-permute-done((bf16[2,512,640]{2,1,0:T(8,128)(2,1)S(1)}, bf16[2,512,640]{2,1,0:T(8,128)(2,1)S(1)}, u32[]{:S(2)}, u32[]{:S(2)}) %collective-permute-start.4) | collective-permute-done | bytes 1310752 | tf_op jit(solution)/shard_map/ppermute | solution.py:12
  74.6 0.0 copy-start
  74.6 1.3 copy-done
  75.9 4.2 %shard_map.50 = bf16[2,16,64,256]{3,2,1,0:T(8,128)(2,1)S(1)} custom-call(bf16[2,512,640]{2,1,0:T(8,128)(2,1)S(1)} %bitcast.43, bf16[2,512,640]{2,1,0:T(8,128)(2,1)S(1)} %collective-permute-done.4.other_ref, bf16[2,512,640]{2,1,0:T(8,128)(2,1)S(1)} %copy-done), custom_call_target="tpu_custom_call" | custom-call | flops 1342177280 | bytes 4980736 | tf_op jit(solution)/shard_map/pallas_call | solution.py:51
  80.1 0.0 copy-start.1
  80.1 1.0 copy-done.1
  81.0 10.3 %all-to-all-start.1 = ((bf16[32,64,256]{2,1,0:T(8,128)(2,1)}), bf16[32,64,256]{2,1,0:T(8,128)(2,1)}, u32[]{:S(2)}, u32[]{:S(2)}) async-start(bf16[32,64,256]{2,1,0:T(8,128)(2,1)} %bitcast.45), calls=%async_computation.1 | async-start | bytes 2097152 | tf_op jit(solution)/shard_map/all_to_all | solution.py:26
  91.4 4.5 %all-gather.2.cloned.1.call-done = bf16[1024,512]{1,0:T(8,128)(2,1)} async-done(((bf16[128,512]{1,0:T(8,128)(2,1)}), bf16[1024,512]{1,0:T(8,128)(2,1)}) %all-gather.2.cloned.1.call-update) | async-done | bytes 1048592 | tf_op jit(solution)/shard_map/all_gather | solution.py:94
  95.9 1.3 fusion.9
  97.2 0.9 fusion.10
  98.1 0.9 convolution_add_fusion
  99.0 0.1 dynamic_slice.47
  99.1 0.1 dynamic_slice.46
  99.2 4.6 %collective-permute-start.6 = (bf16[256,640]{1,0:T(8,128)(2,1)S(1)}, bf16[256,640]{1,0:T(8,128)(2,1)S(1)}, u32[]{:S(2)}, u32[]{:S(2)}) collective-permute-start(bf16[256,640]{1,0:T(8,128)(2,1)S(1)} %fusion.3), channel_id=1, source_target_pairs={{0,1},{1,0},{256,257},{257,256},{2,3},{3,2},{258,259},{259,258},{4... | collective-permute-start | bytes 983048 | tf_op jit(solution)/shard_map/ppermute | solution.py:120
  103.9 0.1 fusion.2
  103.9 2.2 %collective-permute-start.5 = (bf16[256,640]{1,0:T(8,128)(2,1)S(1)}, bf16[256,640]{1,0:T(8,128)(2,1)S(1)}, u32[]{:S(2)}, u32[]{:S(2)}) collective-permute-start(bf16[256,640]{1,0:T(8,128)(2,1)S(1)} %get-tuple-element.14), channel_id=1, source_target_pairs={{0,256},{1,257},{256,0},{257,1},{2,258},{3,259},{258,2},{259,3},{4... | collective-permute-start | bytes 983048 | tf_op jit(solution)/shard_map/ppermute | solution.py:120
  106.1 2.5 %collective-permute-start.7 = (bf16[256,640]{1,0:T(8,128)(2,1)S(1)}, bf16[256,640]{1,0:T(8,128)(2,1)S(1)}, u32[]{:S(2)}, u32[]{:S(2)}) collective-permute-start(bf16[256,640]{1,0:T(8,128)(2,1)S(1)} %get-tuple-element.15), channel_id=1, source_target_pairs={{0,257},{1,256},{256,1},{257,0},{2,259},{3,258},{258,3},{259,2},{4... | collective-permute-start | bytes 983048 | tf_op jit(solution)/shard_map/ppermute | solution.py:120
  108.6 3.4 %collective-permute-done.6 = bf16[256,640]{1,0:T(8,128)(2,1)S(1)} collective-permute-done((bf16[256,640]{1,0:T(8,128)(2,1)S(1)}, bf16[256,640]{1,0:T(8,128)(2,1)S(1)}, u32[]{:S(2)}, u32[]{:S(2)}) %collective-permute-start.6) | collective-permute-done | bytes 327712 | tf_op jit(solution)/shard_map/ppermute | solution.py:120
  112.0 9.2 %collective-permute-done.5 = bf16[256,640]{1,0:T(8,128)(2,1)S(1)} collective-permute-done((bf16[256,640]{1,0:T(8,128)(2,1)S(1)}, bf16[256,640]{1,0:T(8,128)(2,1)S(1)}, u32[]{:S(2)}, u32[]{:S(2)}) %collective-permute-start.5) | collective-permute-done | bytes 327712 | tf_op jit(solution)/shard_map/ppermute | solution.py:120
  121.2 2.4 %collective-permute-done.7 = bf16[256,640]{1,0:T(8,128)(2,1)S(1)} collective-permute-done((bf16[256,640]{1,0:T(8,128)(2,1)S(1)}, bf16[256,640]{1,0:T(8,128)(2,1)S(1)}, u32[]{:S(2)}, u32[]{:S(2)}) %collective-permute-start.7) | collective-permute-done | bytes 327712 | tf_op jit(solution)/shard_map/ppermute | solution.py:120
  123.6 1.0 fusion.1
  124.6 0.0 all-to-all-done.1
  124.6 1.4 %reduce_sum.12 = bf16[2,2,2,32,256]{4,3,2,1,0:T(8,128)(2,1)S(1)} reduce(bf16[2,8,2,2,32,256]{5,4,3,2,1,0:T(8,128)(2,1)} %bitcast.18, bf16[]{:T(256)} %constant.24.clone.1), dimensions={1}, to_apply=%region_0.1 | reduce | flops 458752 | bytes 1179650 | tf_op jit(solution)/shard_map/reduce_sum | solution.py:101
  126.1 0.7 copy.21
  (7 shorter events, 0.1 us)
Async XLA Ops:
  9.3 13.9 %copy-start.3 = (bf16[256,256]{1,0:T(8,128)(2,1)S(1)}, bf16[256,256]{1,0:T(8,128)(2,1)}, u32[]{:S(2)}) copy-start(bf16[256,256]{1,0:T(8,128)(2,1)} %param.3) | copy-start | bytes 393220
  9.3 23.7 %copy-start.2 = (bf16[256,640]{1,0:T(8,128)(2,1)S(1)}, bf16[256,640]{1,0:T(8,128)(2,1)}, u32[]{:S(2)}) copy-start(bf16[256,640]{1,0:T(8,128)(2,1)} %param.5) | copy-start | bytes 983044
  9.3 56.0 %all-to-all-start = ((bf16[32,32,640]{2,1,0:T(8,128)(2,1)}), bf16[32,32,640]{2,1,0:T(8,128)(2,1)S(1)}, u32[]{:S(2)}, u32[]{:S(2)}) async-start(bf16[32,32,640]{2,1,0:T(8,128)(2,1)} %bitcast.9), calls=%async_computation | async-start | bytes 2621440 | tf_op jit(solution)/shard_map/all_to_all | solution.py:26
  23.1 72.8 %all-gather.2.cloned.1.call-start = ((), (), s32[]{:S(2)}) async-start(), calls=%async_computation.2 | async-start | bytes 1179648 | tf_op jit(solution)/shard_map/all_gather | solution.py:94
  23.2 5.6 %collective-permute-start.1 = (bf16[2,1,2,32,256]{4,3,2,0,1:T(8,128)(2,1)S(1)}, bf16[2,1,2,32,256]{4,3,2,0,1:T(8,128)(2,1)S(1)}, u32[]{:S(2)}, u32[]{:S(2)}) collective-permute-start(bf16[2,1,2,32,256]{4,3,2,0,1:T(8,128)(2,1)S(1)} %get-tuple-element.24), channel_id=1, source_target_pairs={{0,256},{256,0},{1,257},{257,1},{2,258},{258,2},{3,259},{259,3},{4... | collective-permute-start | bytes 196616 | tf_op jit(solution)/shard_map/ppermute | solution.py:12
  28.8 8.3 %collective-permute-start.2 = (bf16[2,1,1,32,512]{4,3,2,0,1:T(8,128)(2,1)S(1)}, bf16[2,1,1,32,512]{4,3,2,0,1:T(8,128)(2,1)S(1)}, u32[]{:S(2)}, u32[]{:S(2)}) collective-permute-start(bf16[2,1,1,32,512]{4,3,2,0,1:T(8,128)(2,1)S(1)} %fusion.7), channel_id=1, source_target_pairs={{0,1},{1,0},{2,3},{3,2},{4,5},{5,4},{6,7},{7,6},{8,9},{9,8},{10,11... | collective-permute-start | bytes 196616 | tf_op jit(solution)/shard_map/ppermute | solution.py:12
  33.0 15.8 %collective-permute-start = (bf16[256,640]{1,0:T(8,128)(2,1)S(1)}, bf16[256,640]{1,0:T(8,128)(2,1)S(1)}, u32[]{:S(2)}, u32[]{:S(2)}) collective-permute-start(bf16[256,640]{1,0:T(8,128)(2,1)S(1)} %copy-done.2), channel_id=1, source_target_pairs={{0,1},{1,0},{2,3},{3,2},{4,5},{5,4},{6,7},{7,6},{8,9},{9,8},{10,11... | collective-permute-start | bytes 983048 | tf_op jit(solution)/shard_map/ppermute | solution.py:12
  49.0 15.0 %collective-permute-start.3 = (bf16[2,256,640]{2,1,0:T(8,128)(2,1)S(1)}, bf16[2,256,640]{2,1,0:T(8,128)(2,1)S(1)}, u32[]{:S(2)}, u32[]{:S(2)}) collective-permute-start(bf16[2,256,640]{2,1,0:T(8,128)(2,1)S(1)} %pad_maximum_fusion.1), channel_id=1, source_target_pairs={{0,256},{256,0},{1,257},{257,1},{2,258},{258,2},{3,259},{259,3},{4... | collective-permute-start | bytes 1966088 | tf_op jit(solution)/shard_map/ppermute | solution.py:12
  65.2 9.3 %collective-permute-start.4 = (bf16[2,512,640]{2,1,0:T(8,128)(2,1)S(1)}, bf16[2,512,640]{2,1,0:T(8,128)(2,1)S(1)}, u32[]{:S(2)}, u32[]{:S(2)}) collective-permute-start(bf16[2,512,640]{2,1,0:T(8,128)(2,1)S(1)} %bitcast.42), channel_id=1, source_target_pairs={{0,16},{16,0},{1,17},{17,1},{2,18},{18,2},{3,19},{19,3},{4,20},{20... | collective-permute-start | bytes 3932168 | tf_op jit(solution)/shard_map/ppermute | solution.py:12
  74.6 1.3 copy-start
  80.1 1.0 copy-start.1
  81.0 43.6 %all-to-all-start.1 = ((bf16[32,64,256]{2,1,0:T(8,128)(2,1)}), bf16[32,64,256]{2,1,0:T(8,128)(2,1)}, u32[]{:S(2)}, u32[]{:S(2)}) async-start(bf16[32,64,256]{2,1,0:T(8,128)(2,1)} %bitcast.45), calls=%async_computation.1 | async-start | bytes 2097152 | tf_op jit(solution)/shard_map/all_to_all | solution.py:26
  99.2 12.8 %collective-permute-start.6 = (bf16[256,640]{1,0:T(8,128)(2,1)S(1)}, bf16[256,640]{1,0:T(8,128)(2,1)S(1)}, u32[]{:S(2)}, u32[]{:S(2)}) collective-permute-start(bf16[256,640]{1,0:T(8,128)(2,1)S(1)} %fusion.3), channel_id=1, source_target_pairs={{0,1},{1,0},{256,257},{257,256},{2,3},{3,2},{258,259},{259,258},{4... | collective-permute-start | bytes 983048 | tf_op jit(solution)/shard_map/ppermute | solution.py:120
  103.9 17.3 %collective-permute-start.5 = (bf16[256,640]{1,0:T(8,128)(2,1)S(1)}, bf16[256,640]{1,0:T(8,128)(2,1)S(1)}, u32[]{:S(2)}, u32[]{:S(2)}) collective-permute-start(bf16[256,640]{1,0:T(8,128)(2,1)S(1)} %get-tuple-element.14), channel_id=1, source_target_pairs={{0,256},{1,257},{256,0},{257,1},{2,258},{3,259},{258,2},{259,3},{4... | collective-permute-start | bytes 983048 | tf_op jit(solution)/shard_map/ppermute | solution.py:120
  106.1 17.6 %collective-permute-start.7 = (bf16[256,640]{1,0:T(8,128)(2,1)S(1)}, bf16[256,640]{1,0:T(8,128)(2,1)S(1)}, u32[]{:S(2)}, u32[]{:S(2)}) collective-permute-start(bf16[256,640]{1,0:T(8,128)(2,1)S(1)} %get-tuple-element.15), channel_id=1, source_target_pairs={{0,257},{1,256},{256,1},{257,0},{2,259},{3,258},{258,3},{259,2},{4... | collective-permute-start | bytes 983048 | tf_op jit(solution)/shard_map/ppermute | solution.py:120
Sparse Core Ops, SparseCore 0:
  51.0 44.8 all-gather.1

commit v5 on v0

v5 whole, which is shorter than its diff:
```python
import jax
import jax.numpy as jnp
from jax import lax
from jax.sharding import Mesh, PartitionSpec as P

PAIRS = ((1, 0), (0, 1), (1, 1))


def swap(block, axis):
    return lax.ppermute(block, axis, ((0, 1), (1, 0)))


def to_partner(block, a, b):
    return lax.ppermute(block, ("xl", "xh"), [(i, i ^ (2 * a + b)) for i in range(4)])


def in_order(own, kept, got, axis):
    return jnp.concatenate(
        [jnp.where(own == 0, kept, got), jnp.where(own == 0, got, kept)], axis=axis
    )


def pick(block, index, axis):
    return lax.dynamic_slice_in_dim(block, index, 1, axis)


def exchange(pieces, axes):
    return lax.all_to_all(pieces, axes, split_axis=0, concat_axis=0, tiled=True)


def times(left, right, left_dim, right_dim):
    return lax.dot_general(
        left,
        right,
        (((left_dim,), (right_dim,)), ((), ())),
        preferred_element_type=jnp.float32,
    )


def per_device(inputs, out_grad, weight):
    core = lax.axis_index("core")
    near = lax.axis_index("xl")
    far = lax.axis_index("xh")
    depth = lax.axis_size("z")
    tokens, columns = out_grad.shape
    features = inputs.shape[1]
    part = tokens // 4

    grads = jnp.broadcast_to(
        out_grad.reshape(4, 1, part, columns), (4, depth, part, columns)
    ).reshape(-1, part, columns)
    grads = exchange(grads, ("xl", "xh", "z"))

    acts = lax.all_gather(inputs, "y", axis=0, tiled=False)

    came = {(a, b): to_partner(weight, a, b) for a, b in PAIRS}
    came[0, 0] = weight
    weights = [in_order(far, came[a, 0], came[a, 1], 1) for a in range(2)]
    weights = in_order(near, weights[0], weights[1], 0)
    grads, weights, acts = lax.optimization_barrier((grads, weights, acts))

    acts = acts.reshape(-1, 2, 4, part, features)

    def quarter(a, b):
        rows = pick(acts, 2 * (near ^ a) + (far ^ b), 2)
        rows = jnp.concatenate([pick(rows, core, 1), pick(rows, 1 - core, 1)], axis=1)
        return rows.reshape(-1, 2 * part, features)

    came = {(a, b): to_partner(quarter(a, b), a, b) for a, b in PAIRS}
    came[0, 0] = quarter(0, 0)

    panels = [
        g.reshape(2, 2, depth, 1, part, columns) for g in (grads, swap(grads, "core"))
    ]
    panels = [jnp.concatenate([g[:, 0], g[:, 1]], axis=4) for g in panels]
    panel = jnp.concatenate(panels, axis=2).reshape(-1, 2 * columns)
    partial = [
        times(panel, weights[i * features : (i + 1) * features], 1, 1).astype(jnp.bfloat16)
        for i in range(2)
    ]
    *partial, came, panel = lax.optimization_barrier((*partial, came, panel))
    partial = jnp.concatenate(partial, axis=0).reshape(-1, 2 * part, features)
    shares = exchange(partial, ("xl", "y", "xh"))
    shares = shares.reshape(2, -1, 2, 2, part, features).astype(jnp.float32)
    shares = jnp.sum(shares, axis=1).astype(jnp.bfloat16)
    shares = shares.transpose(2, 0, 1, 3, 4)
    input_grad = in_order(core, shares[:1], shares[1:], 0).reshape(-1, features)

    acts = [jnp.concatenate([came[0, b], came[1, b]], axis=2)[:, None] for b in range(2)]
    acts = in_order(far, acts[0], acts[1], 1).reshape(-1, 2 * features)
    w_part = times(acts, panel, 0, 0)

    def piece(a, b):
        rows = w_part[a * features : (a + 1) * features]
        return lax.dynamic_slice_in_dim(rows, (far ^ b) * columns, columns, 1)

    w_grad = piece(0, 0)
    for a, b in PAIRS:
        w_grad = w_grad + to_partner(piece(a, b).astype(jnp.bfloat16), a, b)
    return (w_grad, input_grad)


def solution(mesh):
    rows, cols = mesh.devices.shape
    split = Mesh(
        mesh.devices.reshape(2, rows // 4, 2, cols // 2, 2), ("xl", "z", "core", "y", "xh")
    )
    row, col = ("xl", "z", "core"), ("y", "xh")
    return jax.shard_map(
        per_device,
        mesh=split,
        in_specs=(P(col, row), P(row, col), P(row, col)),
        out_specs=(P(row, col), P(col, row)),
        check_vma=False,
    )
```

time: 401 us -> 140 us (0.35)
  waiting for transfers between devices: 373 us -> 52.7 us
  starting transfers between devices: 0.11 us -> 55.6 us
  matrix products: 11.5 us -> 3.32 us
  other arithmetic: 0 us -> 6.66 us
  local copies, waits for them, and re-layouts: 0.01 us -> 6 us
    reduce_scatter x1 -> x0, waiting for transfers between devices: 208 us -> none  [per_device(): lax.psum_scatter(lax.dot_general(grad_panel, weight, (((1,), (1,)), ((),...]
    all_gather x2 -> x1, waiting for transfers between devices: 163 us -> 8.27 us  [per_device(): acts = lax.all_gather(inputs, 'y', axis=0, tiled=False)]
    ppermute x0 -> x10, waiting for transfers between devices: none -> 43.7 us  [the longest x9 43.7 us: to_partner(): lax.ppermute(block, ('xl', 'xh'), [(i, i ^ 2 * a + b) for i in range(4)])]
    ppermute x0 -> x10, starting transfers between devices: none -> 34.8 us  [the longest x9 28 us: to_partner(): lax.ppermute(block, ('xl', 'xh'), [(i, i ^ 2 * a + b) for i in range(4)])]
    all_to_all x0 -> x2, starting transfers between devices: none -> 20.8 us  [exchange(): return lax.all_to_all(pieces, axes, split_axis=0, concat_axis=0, tiled=True)]
    dot_general x2 -> x3, matrix products: 11.5 us -> 3.32 us  [times(): lax.dot_general(left, right, (((left_dim,), (right_dim,)), ((), ())), pre...]
  transfers between devices with their start and end apart: 3 -> 13, of which waited for: 3 -> 7; matrix products, arithmetic and copies ran while one was open for 3% -> 7% of each run, Pallas kernels for 0% -> 0%
where the time goes in v5:
time: 140 us; the launch traced here: 139 us
  starting transfers between devices  55.6 us (40%)
  waiting for transfers between devices  52.7 us (38%)
  between operations  14.4 us (10%)
  other arithmetic  6.66 us (5%)
  local copies, waits for them, and re-layouts  6 us (4%)
  matrix products  3.32 us (2%)
    ppermute x9, waiting for transfers between devices, to_partner(): lax.ppermute(block, ('xl', 'xh'), [(i, i ^ 2 * a + b) for i in range(4)])  43.7 us
    ppermute x9, starting transfers between devices, to_partner(): lax.ppermute(block, ('xl', 'xh'), [(i, i ^ 2 * a + b) for i in range(4)])  28 us
    all_to_all x2, starting transfers between devices, exchange(): return lax.all_to_all(pieces, axes, split_axis=0, concat_axis=0, tiled=True)  20.8 us
    all_gather x1, waiting for transfers between devices, per_device(): acts = lax.all_gather(inputs, 'y', axis=0, tiled=False)  8.27 us
    ppermute x1, starting transfers between devices, swap(): return lax.ppermute(block, axis, ((0, 1), (1, 0)))  6.75 us
    dot_general x3, matrix products, times(): lax.dot_general(left, right, (((left_dim,), (right_dim,)), ((), ())), pre...  3.32 us
  transfers between devices with their start and end apart: 13, of which 7 were waited for; matrix products, arithmetic and copies ran while one was open for 7% of the time, Pallas kernels for 0%

profile of v5, /device:TPU:1, one launch (start us, length us, event | category | flops | bytes accessed | tf_op | source)
XLA Modules:
  0.0 138.6 jit_solution(12637390348030665709)
XLA Ops:
  7.2 0.0 copy-start.1
  7.2 2.1 %broadcast_in_dim.10 = bf16[4,8,32,640]{3,2,1,0:T(8,128)(2,1)} broadcast(bf16[4,32,640]{2,1,0:T(8,128)(2,1)} %bitcast.54), dimensions={0,2,3} | broadcast | bytes 1474560 | tf_op jit(solution)/shard_map/broadcast_in_dim | solution.py:49
  9.3 13.7 %all-to-all-start = ((bf16[32,32,640]{2,1,0:T(8,128)(2,1)}), bf16[32,32,640]{2,1,0:T(8,128)(2,1)S(1)}, u32[]{:S(2)}, u32[]{:S(2)}) async-start(bf16[32,32,640]{2,1,0:T(8,128)(2,1)} %bitcast.1), calls=%async_computation | async-start | bytes 2621440 | tf_op jit(solution)/shard_map/all_to_all | solution.py:28
  23.0 0.0 all-gather.3.cloned.1.call-start
  23.1 0.7 all-gather.3.cloned.1.call-update
  23.8 0.0 copy-done.1
  23.8 4.6 %collective-permute-start = (bf16[256,640]{1,0:T(8,128)(2,1)S(1)}, bf16[256,640]{1,0:T(8,128)(2,1)S(1)}, u32[]{:S(2)}, u32[]{:S(2)}) collective-permute-start(bf16[256,640]{1,0:T(8,128)(2,1)S(1)} %copy-done.1), channel_id=1, source_target_pairs={{0,1},{1,0},{256,257},{257,256},{2,3},{3,2},{258,259},{259,258},{4... | collective-permute-start | bytes 983048 | tf_op jit(solution)/shard_map/ppermute | solution.py:14
  28.4 2.8 %collective-permute-start.2 = (bf16[256,640]{1,0:T(8,128)(2,1)S(1)}, bf16[256,640]{1,0:T(8,128)(2,1)S(1)}, u32[]{:S(2)}, u32[]{:S(2)}) collective-permute-start(bf16[256,640]{1,0:T(8,128)(2,1)S(1)} %copy-done.1), channel_id=1, source_target_pairs={{0,257},{1,256},{256,1},{257,0},{2,259},{3,258},{258,3},{259,2},{4... | collective-permute-start | bytes 983048 | tf_op jit(solution)/shard_map/ppermute | solution.py:14
  31.3 1.9 %collective-permute-start.1 = (bf16[256,640]{1,0:T(8,128)(2,1)S(1)}, bf16[256,640]{1,0:T(8,128)(2,1)S(1)}, u32[]{:S(2)}, u32[]{:S(2)}) collective-permute-start(bf16[256,640]{1,0:T(8,128)(2,1)S(1)} %copy-done.1), channel_id=1, source_target_pairs={{0,256},{1,257},{256,0},{257,1},{2,258},{3,259},{258,2},{259,3},{4... | collective-permute-start | bytes 983048 | tf_op jit(solution)/shard_map/ppermute | solution.py:14
  33.2 7.4 %collective-permute-done = bf16[256,640]{1,0:T(8,128)(2,1)S(1)} collective-permute-done((bf16[256,640]{1,0:T(8,128)(2,1)S(1)}, bf16[256,640]{1,0:T(8,128)(2,1)S(1)}, u32[]{:S(2)}, u32[]{:S(2)}) %collective-permute-start) | collective-permute-done | bytes 327712 | tf_op jit(solution)/shard_map/ppermute | solution.py:14
  40.6 0.1 broadcast_select_fusion.7
  40.6 14.1 %collective-permute-done.2 = bf16[256,640]{1,0:T(8,128)(2,1)S(1)} collective-permute-done((bf16[256,640]{1,0:T(8,128)(2,1)S(1)}, bf16[256,640]{1,0:T(8,128)(2,1)S(1)}, u32[]{:S(2)}, u32[]{:S(2)}) %collective-permute-start.2) | collective-permute-done | bytes 327712 | tf_op jit(solution)/shard_map/ppermute | solution.py:14
  54.7 0.0 collective-permute-done.1
  54.7 0.1 broadcast_select_fusion.5
  54.8 0.2 broadcast_select_fusion.1
  55.0 1.1 pad_maximum_fusion
  56.1 8.3 %all-gather.3.cloned.1.call-done = bf16[2048,256]{1,0:T(8,128)(2,1)} async-done(((bf16[256,256]{1,0:T(8,128)(2,1)}), bf16[2048,256]{1,0:T(8,128)(2,1)}) %all-gather.3.cloned.1.call-update) | async-done | bytes 1048592 | tf_op jit(solution)/shard_map/all_gather | solution.py:54
  64.4 0.0 all-to-all-done
  64.4 6.8 %collective-permute-start.3 = (bf16[32,32,640]{2,1,0:T(8,128)(2,1)S(1)}, bf16[32,32,640]{2,1,0:T(8,128)(2,1)S(1)}, u32[]{:S(2)}, u32[]{:S(2)}) collective-permute-start(bf16[32,32,640]{2,1,0:T(8,128)(2,1)S(1)} %all-to-all-done), channel_id=1, source_target_pairs={{0,16},{16,0},{1,17},{17,1},{2,18},{18,2},{3,19},{19,3},{4,20},{20... | collective-permute-start | bytes 3932168 | tf_op jit(solution)/shard_map/ppermute | solution.py:10
  71.2 1.4 constant_dynamic-slice_fusion.1
  72.6 4.4 %collective-permute-start.4 = (bf16[8,64,256]{2,1,0:T(8,128)(2,1)S(1)}, bf16[8,64,256]{2,1,0:T(8,128)(2,1)S(1)}, u32[]{:S(2)}, u32[]{:S(2)}) collective-permute-start(bf16[8,64,256]{2,1,0:T(8,128)(2,1)S(1)} %bitcast.51), channel_id=1, source_target_pairs={{0,1},{1,0},{256,257},{257,256},{2,3},{3,2},{258,259},{259,258},{4... | collective-permute-start | bytes 786440 | tf_op jit(solution)/shard_map/ppermute | solution.py:14
  77.1 2.2 %collective-permute-start.5 = (bf16[8,64,256]{2,1,0:T(8,128)(2,1)S(1)}, bf16[8,64,256]{2,1,0:T(8,128)(2,1)S(1)}, u32[]{:S(2)}, u32[]{:S(2)}) collective-permute-start(bf16[8,64,256]{2,1,0:T(8,128)(2,1)S(1)} %bitcast.52), channel_id=1, source_target_pairs={{0,256},{1,257},{256,0},{257,1},{2,258},{3,259},{258,2},{259,3},{4... | collective-permute-start | bytes 786440 | tf_op jit(solution)/shard_map/ppermute | solution.py:14
  79.4 2.7 %collective-permute-start.6 = (bf16[8,64,256]{2,1,0:T(8,128)(2,1)S(1)}, bf16[8,64,256]{2,1,0:T(8,128)(2,1)S(1)}, u32[]{:S(2)}, u32[]{:S(2)}) collective-permute-start(bf16[8,64,256]{2,1,0:T(8,128)(2,1)S(1)} %bitcast.53), channel_id=1, source_target_pairs={{0,257},{1,256},{256,1},{257,0},{2,259},{3,258},{258,3},{259,2},{4... | collective-permute-start | bytes 786440 | tf_op jit(solution)/shard_map/ppermute | solution.py:14
  82.1 0.1 slice_bitcast_fusion.3
  82.2 0.0 collective-permute-done.3
  82.2 0.1 slice_bitcast_fusion.1
  82.3 0.3 maximum_maximum_fusion
  82.7 0.0 copy-start
  82.7 0.2 copy.21
  82.9 1.1 copy-done
  84.0 0.9 convolution_convert_fusion
  84.9 0.9 convolution_convert_fusion.1
  85.8 0.0 collective-permute-done.4
  85.8 3.7 %collective-permute-done.5 = bf16[8,64,256]{2,1,0:T(8,128)(2,1)S(1)} collective-permute-done((bf16[8,64,256]{2,1,0:T(8,128)(2,1)S(1)}, bf16[8,64,256]{2,1,0:T(8,128)(2,1)S(1)}, u32[]{:S(2)}, u32[]{:S(2)}) %collective-permute-start.5) | collective-permute-done | bytes 262176 | tf_op jit(solution)/shard_map/ppermute | solution.py:14
  89.4 0.3 collective-permute-done.6
  89.8 0.0 copy-start.2
  89.8 1.0 pad_maximum_fusion.2
  90.8 0.0 copy-done.2
  90.8 7.1 %all-to-all-start.1 = ((bf16[32,64,256]{2,1,0:T(8,128)(2,1)}), bf16[32,64,256]{2,1,0:T(8,128)(2,1)}, u32[]{:S(2)}, u32[]{:S(2)}) async-start(bf16[32,64,256]{2,1,0:T(8,128)(2,1)} %bitcast.42), calls=%async_computation.1 | async-start | bytes 2097152 | tf_op jit(solution)/shard_map/all_to_all | solution.py:28
  97.9 1.2 broadcast_select_fusion.3
  99.1 0.1 pad_maximum_fusion.1
  99.2 1.6 %fusion.2 = f32[512,1280]{1,0:T(8,128)S(1)} fusion(bf16[1024,512]{1,0:T(8,128)(2,1)S(1)} %bitcast.43, bf16[1024,1280]{1,0:T(8,128)(2,1)S(1)} %bitcast.40), kind=kOutput, calls=%fused_computation.43 | convolution fusion | flops 1342177280 | bytes 6291456 | tf_op jit(solution)/shard_map/dot_general | solution.py:32
  100.8 0.1 slice.47
  100.8 0.1 slice.46
  101.0 4.6 %collective-permute-start.8 = (bf16[256,640]{1,0:T(8,128)(2,1)S(1)}, bf16[256,640]{1,0:T(8,128)(2,1)S(1)}, u32[]{:S(2)}, u32[]{:S(2)}) collective-permute-start(bf16[256,640]{1,0:T(8,128)(2,1)S(1)} %dynamic-slice_convert_fusion.1), channel_id=1, source_target_pairs={{0,1},{1,0},{256,257},{257,256},{2,3},{3,2},{258,259},{259,258},{4... | collective-permute-start | bytes 983048 | tf_op jit(solution)/shard_map/ppermute | solution.py:14
  105.6 0.1 dynamic-slice_convert_fusion.2
  105.6 2.2 %collective-permute-start.7 = (bf16[256,640]{1,0:T(8,128)(2,1)S(1)}, bf16[256,640]{1,0:T(8,128)(2,1)S(1)}, u32[]{:S(2)}, u32[]{:S(2)}) collective-permute-start(bf16[256,640]{1,0:T(8,128)(2,1)S(1)} %get-tuple-element.38), channel_id=1, source_target_pairs={{0,256},{1,257},{256,0},{257,1},{2,258},{3,259},{258,2},{259,3},{4... | collective-permute-start | bytes 983048 | tf_op jit(solution)/shard_map/ppermute | solution.py:14
  107.8 2.6 %collective-permute-start.9 = (bf16[256,640]{1,0:T(8,128)(2,1)S(1)}, bf16[256,640]{1,0:T(8,128)(2,1)S(1)}, u32[]{:S(2)}, u32[]{:S(2)}) collective-permute-start(bf16[256,640]{1,0:T(8,128)(2,1)S(1)} %get-tuple-element.39), channel_id=1, source_target_pairs={{0,257},{1,256},{256,1},{257,0},{2,259},{3,258},{258,3},{259,2},{4... | collective-permute-start | bytes 983048 | tf_op jit(solution)/shard_map/ppermute | solution.py:14
  110.4 8.9 %collective-permute-done.8 = bf16[256,640]{1,0:T(8,128)(2,1)S(1)} collective-permute-done((bf16[256,640]{1,0:T(8,128)(2,1)S(1)}, bf16[256,640]{1,0:T(8,128)(2,1)S(1)}, u32[]{:S(2)}, u32[]{:S(2)}) %collective-permute-start.8) | collective-permute-done | bytes 327712 | tf_op jit(solution)/shard_map/ppermute | solution.py:14
  119.3 9.4 %collective-permute-done.7 = bf16[256,640]{1,0:T(8,128)(2,1)S(1)} collective-permute-done((bf16[256,640]{1,0:T(8,128)(2,1)S(1)}, bf16[256,640]{1,0:T(8,128)(2,1)S(1)}, u32[]{:S(2)}, u32[]{:S(2)}) %collective-permute-start.7) | collective-permute-done | bytes 327712 | tf_op jit(solution)/shard_map/ppermute | solution.py:14
  128.7 0.0 collective-permute-done.9
  128.7 1.0 convert_add_fusion
  129.7 0.0 all-to-all-done.1
  129.7 1.4 %reduce_sum.12 = bf16[2,2,2,32,256]{4,3,2,1,0:T(8,128)(2,1)S(1)} reduce(bf16[2,8,2,2,32,256]{5,4,3,2,1,0:T(8,128)(2,1)} %bitcast.21, bf16[]{:T(256)} %constant.212.clone.1), dimensions={1}, to_apply=%region_0.1 | reduce | flops 458752 | bytes 1179650 | tf_op jit(solution)/shard_map/reduce_sum | solution.py:85
  131.1 0.7 copy.22
  (7 shorter events, 0.2 us)
Async XLA Ops:
  7.2 16.6 %copy-start.1 = (bf16[256,640]{1,0:T(8,128)(2,1)S(1)}, bf16[256,640]{1,0:T(8,128)(2,1)}, u32[]{:S(2)}) copy-start(bf16[256,640]{1,0:T(8,128)(2,1)} %param.5) | copy-start | bytes 983044
  9.3 55.1 %all-to-all-start = ((bf16[32,32,640]{2,1,0:T(8,128)(2,1)}), bf16[32,32,640]{2,1,0:T(8,128)(2,1)S(1)}, u32[]{:S(2)}, u32[]{:S(2)}) async-start(bf16[32,32,640]{2,1,0:T(8,128)(2,1)} %bitcast.1), calls=%async_computation | async-start | bytes 2621440 | tf_op jit(solution)/shard_map/all_to_all | solution.py:28
  23.0 41.4 %all-gather.3.cloned.1.call-start = ((), (), s32[]{:S(2)}) async-start(), calls=%async_computation.2 | async-start | bytes 1179648 | tf_op jit(solution)/shard_map/all_gather | solution.py:54
  23.8 16.8 %collective-permute-start = (bf16[256,640]{1,0:T(8,128)(2,1)S(1)}, bf16[256,640]{1,0:T(8,128)(2,1)S(1)}, u32[]{:S(2)}, u32[]{:S(2)}) collective-permute-start(bf16[256,640]{1,0:T(8,128)(2,1)S(1)} %copy-done.1), channel_id=1, source_target_pairs={{0,1},{1,0},{256,257},{257,256},{2,3},{3,2},{258,259},{259,258},{4... | collective-permute-start | bytes 983048 | tf_op jit(solution)/shard_map/ppermute | solution.py:14
  28.4 26.2 %collective-permute-start.2 = (bf16[256,640]{1,0:T(8,128)(2,1)S(1)}, bf16[256,640]{1,0:T(8,128)(2,1)S(1)}, u32[]{:S(2)}, u32[]{:S(2)}) collective-permute-start(bf16[256,640]{1,0:T(8,128)(2,1)S(1)} %copy-done.1), channel_id=1, source_target_pairs={{0,257},{1,256},{256,1},{257,0},{2,259},{3,258},{258,3},{259,2},{4... | collective-permute-start | bytes 983048 | tf_op jit(solution)/shard_map/ppermute | solution.py:14
  31.3 23.4 %collective-permute-start.1 = (bf16[256,640]{1,0:T(8,128)(2,1)S(1)}, bf16[256,640]{1,0:T(8,128)(2,1)S(1)}, u32[]{:S(2)}, u32[]{:S(2)}) collective-permute-start(bf16[256,640]{1,0:T(8,128)(2,1)S(1)} %copy-done.1), channel_id=1, source_target_pairs={{0,256},{1,257},{256,0},{257,1},{2,258},{3,259},{258,2},{259,3},{4... | collective-permute-start | bytes 983048 | tf_op jit(solution)/shard_map/ppermute | solution.py:14
  64.4 17.8 %collective-permute-start.3 = (bf16[32,32,640]{2,1,0:T(8,128)(2,1)S(1)}, bf16[32,32,640]{2,1,0:T(8,128)(2,1)S(1)}, u32[]{:S(2)}, u32[]{:S(2)}) collective-permute-start(bf16[32,32,640]{2,1,0:T(8,128)(2,1)S(1)} %all-to-all-done), channel_id=1, source_target_pairs={{0,16},{16,0},{1,17},{17,1},{2,18},{18,2},{3,19},{19,3},{4,20},{20... | collective-permute-start | bytes 3932168 | tf_op jit(solution)/shard_map/ppermute | solution.py:10
  72.6 13.1 %collective-permute-start.4 = (bf16[8,64,256]{2,1,0:T(8,128)(2,1)S(1)}, bf16[8,64,256]{2,1,0:T(8,128)(2,1)S(1)}, u32[]{:S(2)}, u32[]{:S(2)}) collective-permute-start(bf16[8,64,256]{2,1,0:T(8,128)(2,1)S(1)} %bitcast.51), channel_id=1, source_target_pairs={{0,1},{1,0},{256,257},{257,256},{2,3},{3,2},{258,259},{259,258},{4... | collective-permute-start | bytes 786440 | tf_op jit(solution)/shard_map/ppermute | solution.py:14
  77.1 12.3 %collective-permute-start.5 = (bf16[8,64,256]{2,1,0:T(8,128)(2,1)S(1)}, bf16[8,64,256]{2,1,0:T(8,128)(2,1)S(1)}, u32[]{:S(2)}, u32[]{:S(2)}) collective-permute-start(bf16[8,64,256]{2,1,0:T(8,128)(2,1)S(1)} %bitcast.52), channel_id=1, source_target_pairs={{0,256},{1,257},{256,0},{257,1},{2,258},{3,259},{258,2},{259,3},{4... | collective-permute-start | bytes 786440 | tf_op jit(solution)/shard_map/ppermute | solution.py:14
  79.4 10.4 %collective-permute-start.6 = (bf16[8,64,256]{2,1,0:T(8,128)(2,1)S(1)}, bf16[8,64,256]{2,1,0:T(8,128)(2,1)S(1)}, u32[]{:S(2)}, u32[]{:S(2)}) collective-permute-start(bf16[8,64,256]{2,1,0:T(8,128)(2,1)S(1)} %bitcast.53), channel_id=1, source_target_pairs={{0,257},{1,256},{256,1},{257,0},{2,259},{3,258},{258,3},{259,2},{4... | collective-permute-start | bytes 786440 | tf_op jit(solution)/shard_map/ppermute | solution.py:14
  82.7 1.3 copy-start
  89.8 1.1 copy-start.2
  90.8 38.9 %all-to-all-start.1 = ((bf16[32,64,256]{2,1,0:T(8,128)(2,1)}), bf16[32,64,256]{2,1,0:T(8,128)(2,1)}, u32[]{:S(2)}, u32[]{:S(2)}) async-start(bf16[32,64,256]{2,1,0:T(8,128)(2,1)} %bitcast.42), calls=%async_computation.1 | async-start | bytes 2097152 | tf_op jit(solution)/shard_map/all_to_all | solution.py:28
  101.0 18.3 %collective-permute-start.8 = (bf16[256,640]{1,0:T(8,128)(2,1)S(1)}, bf16[256,640]{1,0:T(8,128)(2,1)S(1)}, u32[]{:S(2)}, u32[]{:S(2)}) collective-permute-start(bf16[256,640]{1,0:T(8,128)(2,1)S(1)} %dynamic-slice_convert_fusion.1), channel_id=1, source_target_pairs={{0,1},{1,0},{256,257},{257,256},{2,3},{3,2},{258,259},{259,258},{4... | collective-permute-start | bytes 983048 | tf_op jit(solution)/shard_map/ppermute | solution.py:14
  105.6 23.1 %collective-permute-start.7 = (bf16[256,640]{1,0:T(8,128)(2,1)S(1)}, bf16[256,640]{1,0:T(8,128)(2,1)S(1)}, u32[]{:S(2)}, u32[]{:S(2)}) collective-permute-start(bf16[256,640]{1,0:T(8,128)(2,1)S(1)} %get-tuple-element.38), channel_id=1, source_target_pairs={{0,256},{1,257},{256,0},{257,1},{2,258},{3,259},{258,2},{259,3},{4... | collective-permute-start | bytes 983048 | tf_op jit(solution)/shard_map/ppermute | solution.py:14
  107.8 20.9 %collective-permute-start.9 = (bf16[256,640]{1,0:T(8,128)(2,1)S(1)}, bf16[256,640]{1,0:T(8,128)(2,1)S(1)}, u32[]{:S(2)}, u32[]{:S(2)}) collective-permute-start(bf16[256,640]{1,0:T(8,128)(2,1)S(1)} %get-tuple-element.39), channel_id=1, source_target_pairs={{0,257},{1,256},{256,1},{257,0},{2,259},{3,258},{258,3},{259,2},{4... | collective-permute-start | bytes 983048 | tf_op jit(solution)/shard_map/ppermute | solution.py:14
Sparse Core Ops, SparseCore 0:
  26.0 38.3 all-gather.2

commit v6 on v3

--- a/solution.py
+++ b/solution.py
@@ -14,13 +14,6 @@
     return jnp.concatenate(
         [jnp.where(own == 0, kept, got), jnp.where(own == 0, got, kept)], axis=axis
     )
-
-
-def keep_and_give(block, own):
-    half = block.shape[0] // 2
-    kept = lax.dynamic_slice_in_dim(block, own * half, half, 0)
-    given = lax.dynamic_slice_in_dim(block, (1 - own) * half, half, 0)
-    return kept, given
 
 
 def exchange(pieces, axes):
@@ -62,18 +55,28 @@
     features = inputs.shape[1]
 
     pieces = jnp.broadcast_to(out_grad.reshape(1, 2, part, columns), (2, 2, part, columns))
-    pieces = pieces.reshape(4, part, columns)
-    pieces = exchange(pieces, ("xl", "xh")).reshape(2, 2, part, columns)
+    pieces = exchange(pieces.reshape(4, part, columns), ("xl", "xh"))
+
+    quarters = inputs.reshape(4, part, features)
+
+    def quarter(a, b):
+        return lax.dynamic_index_in_dim(quarters, 2 * (core ^ a) + (half ^ b), 0, False)
+
+    came = {}
+    for a, b in ((1, 0), (0, 1), (1, 1)):
+        partner = [(i, i ^ (2 * a + b)) for i in range(4)]
+        came[a, b] = lax.ppermute(quarter(a, b), ("core", "xh"), partner)
+    came[0, 0] = quarter(0, 0)
+    pieces, came, weight = lax.optimization_barrier((pieces, came, weight))
+    pieces = pieces.reshape(2, 2, part, columns)
     grads = in_order(half, pieces[:, 0], pieces[:, 1], 2)
-    grads, inputs, weight = lax.optimization_barrier((grads, inputs, weight))
+    acts = [jnp.concatenate([came[0, b], came[1, b]], axis=1) for b in range(2)]
+    acts = in_order(half, acts[0], acts[1], 0)
+    grads, acts, weight = lax.optimization_barrier((grads, acts, weight))
     grads = ring_gather(grads, "z", 1).reshape(-1, 2 * columns)
+    acts = lax.all_gather(acts, "y", axis=0, tiled=True)
 
-    kept, given = keep_and_give(inputs, core)
-    acts = jnp.concatenate([kept, swap(given, "core")], axis=1)
-    kept, given = keep_and_give(acts, half)
-    acts = in_order(half, kept, swap(given, "xh"), 0)
     weights = in_order(core, weight, swap(weight, "core"), 0)
-    acts = lax.all_gather(acts, "y", axis=0, tiled=True)
     weights = jnp.concatenate([weights, swap(weights, "xh")], axis=1)
 
     grads, weights = lax.optimization_barrier((grads, weights))

time: 135 us -> 136 us (level)
  waiting for transfers between devices: 35.9 us -> 33.3 us
  starting transfers between devices: 69.7 us -> 72 us
  local copies, waits for them, and re-layouts: 3.31 us -> 5.05 us
    ppermute x0 -> x3, starting transfers between devices: none -> 14.7 us  [per_device(): came[a, b] = lax.ppermute(quarter(a, b), ('core', 'xh'), partner)]
    ppermute x6 -> x4, starting transfers between devices: 23.9 us -> 11.2 us  [swap(): return lax.ppermute(block, axis, SWAP)]
    all_to_all x2, waiting for transfers between devices: 8.57 us -> 2.99 us  [exchange(): return lax.all_to_all(pieces, axes, split_axis=0, concat_axis=0, tiled=True)]
    ppermute x0 -> x3, waiting for transfers between devices: none -> 4.73 us  [per_device(): came[a, b] = lax.ppermute(quarter(a, b), ('core', 'xh'), partner)]
    ppermute x6 -> x4, waiting for transfers between devices: 18.1 us -> 15.9 us  [swap(): return lax.ppermute(block, axis, SWAP)]
  transfers between devices with their start and end apart: 17 -> 18, of which waited for: 9 -> 9; matrix products, arithmetic and copies ran while one was open for 8% -> 8% of each run, Pallas kernels for 0% -> 0%
where the time goes in v6:
time: 136 us
  starting transfers between devices  72 us (53%)
  waiting for transfers between devices  33.3 us (24%)
  between operations  14.4 us (11%)
  other arithmetic  6.17 us (5%)
  local copies, waits for them, and re-layouts  5.05 us (4%)
  matrix products  4.55 us (3%)
    all_to_all x2, starting transfers between devices, exchange(): return lax.all_to_all(pieces, axes, split_axis=0, concat_axis=0, tiled=True)  18.5 us
    ppermute x4, waiting for transfers between devices, swap(): return lax.ppermute(block, axis, SWAP)  15.9 us
    ppermute x3, starting transfers between devices, ring_gather(): falling[i] = lax.ppermute(falling[i], axis, down)  15.3 us
    ppermute x3, starting transfers between devices, per_device(): came[a, b] = lax.ppermute(quarter(a, b), ('core', 'xh'), partner)  14.7 us
    ppermute x4, starting transfers between devices, swap(): return lax.ppermute(block, axis, SWAP)  11.2 us
    ppermute x3, waiting for transfers between devices, ring_gather(): rising[i] = lax.ppermute(rising[i], axis, up)  7.58 us
    ppermute x3, starting transfers between devices, ring_gather(): rising[i] = lax.ppermute(rising[i], axis, up)  5.75 us
    ppermute x3, waiting for transfers between devices, per_device(): came[a, b] = lax.ppermute(quarter(a, b), ('core', 'xh'), partner)  4.73 us
  transfers between devices with their start and end apart: 18, of which 9 were waited for; matrix products, arithmetic and copies ran while one was open for 8% of the time, Pallas kernels for 0%

profile of v6, /device:TPU:1, one launch (start us, length us, event | category | flops | bytes accessed | tf_op | source)
XLA Modules:
  0.0 135.5 jit_solution(5104800548762233825)
XLA Ops:
  7.2 1.7 %broadcast_in_dim.38 = bf16[2,2,64,640]{3,2,1,0:T(8,128)(2,1)} broadcast(bf16[2,64,640]{2,1,0:T(8,128)(2,1)} %bitcast.74), dimensions={1,2,3} | broadcast | bytes 491520 | tf_op jit(solution)/shard_map/broadcast_in_dim | solution.py:57
  8.8 4.8 %all-to-all-start = ((bf16[4,64,640]{2,1,0:T(8,128)(2,1)}), bf16[4,64,640]{2,1,0:T(8,128)(2,1)S(1)}, u32[]{:S(2)}, u32[]{:S(2)}) async-start(bf16[4,64,640]{2,1,0:T(8,128)(2,1)} %bitcast.1), calls=%async_computation | async-start | bytes 655360 | tf_op jit(solution)/shard_map/all_to_all | solution.py:20
  13.7 0.0 all-gather.2.cloned.1.call-start
  13.7 0.8 dynamic-slice_bitcast_fusion
  14.5 4.9 %collective-permute-start = (bf16[64,256]{1,0:T(8,128)(2,1)S(1)}, bf16[64,256]{1,0:T(8,128)(2,1)S(1)}, u32[]{:S(2)}, u32[]{:S(2)}) collective-permute-start(bf16[64,256]{1,0:T(8,128)(2,1)S(1)} %get-tuple-element.30), channel_id=1, source_target_pairs={{0,1},{1,0},{16,17},{17,16},{2,3},{3,2},{18,19},{19,18},{4,5},{5,4... | collective-permute-start | bytes 98312 | tf_op jit(solution)/shard_map/ppermute | solution.py:68
  19.4 7.9 %collective-permute-start.1 = (bf16[64,256]{1,0:T(8,128)(2,1)S(1)}, bf16[64,256]{1,0:T(8,128)(2,1)S(1)}, u32[]{:S(2)}, u32[]{:S(2)}) collective-permute-start(bf16[64,256]{1,0:T(8,128)(2,1)S(1)} %get-tuple-element.29), channel_id=1, source_target_pairs={{0,16},{1,17},{16,0},{17,1},{2,18},{3,19},{18,2},{19,3},{4,20},{5,... | collective-permute-start | bytes 98312 | tf_op jit(solution)/shard_map/ppermute | solution.py:68
  27.3 1.9 %collective-permute-start.2 = (bf16[64,256]{1,0:T(8,128)(2,1)S(1)}, bf16[64,256]{1,0:T(8,128)(2,1)S(1)}, u32[]{:S(2)}, u32[]{:S(2)}) collective-permute-start(bf16[64,256]{1,0:T(8,128)(2,1)S(1)} %get-tuple-element.28), channel_id=1, source_target_pairs={{0,17},{1,16},{16,1},{17,0},{2,19},{3,18},{18,3},{19,2},{4,21},{5,... | collective-permute-start | bytes 98312 | tf_op jit(solution)/shard_map/ppermute | solution.py:68
  29.3 0.0 collective-permute-done
  29.3 0.0 collective-permute-done.1
  29.3 4.7 %collective-permute-done.2 = bf16[64,256]{1,0:T(8,128)(2,1)S(1)} collective-permute-done((bf16[64,256]{1,0:T(8,128)(2,1)S(1)}, bf16[64,256]{1,0:T(8,128)(2,1)S(1)}, u32[]{:S(2)}, u32[]{:S(2)}) %collective-permute-start.2) | collective-permute-done | bytes 32800 | tf_op jit(solution)/shard_map/ppermute | solution.py:68
  34.1 0.0 all-to-all-done
  34.2 0.7 pad_maximum_fusion.4
  34.9 1.9 %collective-permute-start.3 = (bf16[2,64,1280]{2,1,0:T(8,128)(2,1)S(1)}, bf16[2,64,1280]{2,1,0:T(8,128)(2,1)}, u32[]{:S(2)}, u32[]{:S(2)}) collective-permute-start(bf16[2,64,1280]{2,1,0:T(8,128)(2,1)S(1)} %pad_maximum_fusion.3), channel_id=1, source_target_pairs={{0,32},{32,64},{64,96},{96,128},{128,160},{160,192},{192,224},{224... | collective-permute-start | bytes 983048 | tf_op jit(solution)/shard_map/ppermute | solution.py:40
  36.8 6.2 %collective-permute-start.4 = (bf16[2,64,1280]{2,1,0:T(8,128)(2,1)S(1)}, bf16[2,64,1280]{2,1,0:T(8,128)(2,1)}, u32[]{:S(2)}, u32[]{:S(2)}) collective-permute-start(bf16[2,64,1280]{2,1,0:T(8,128)(2,1)S(1)} %pad_maximum_fusion.3), channel_id=1, source_target_pairs={{0,224},{32,0},{64,32},{96,64},{128,96},{160,128},{192,160},{224,1... | collective-permute-start | bytes 983048 | tf_op jit(solution)/shard_map/ppermute | solution.py:41
  43.0 2.2 %collective-permute-start.11 = (bf16[256,640]{1,0:T(8,128)(2,1)}, bf16[256,640]{1,0:T(8,128)(2,1)}, u32[]{:S(2)}, u32[]{:S(2)}) collective-permute-start(bf16[256,640]{1,0:T(8,128)(2,1)} %param.5), channel_id=1, source_target_pairs={{0,16},{16,0},{1,17},{17,1},{2,18},{18,2},{3,19},{19,3},{4,20},{20... | collective-permute-start | bytes 983048 | tf_op jit(solution)/shard_map/ppermute | solution.py:10
  45.2 0.0 all-gather.2.cloned.1.call-update
  45.2 0.2 broadcast_in_dim.39
  45.5 1.3 collective-permute-done.11
  46.8 1.1 broadcast_select_fusion.1
  48.0 0.1 pad_maximum_fusion.2
  48.0 2.0 %collective-permute-start.12 = (bf16[512,640]{1,0:T(8,128)(2,1)S(1)}, bf16[512,640]{1,0:T(8,128)(2,1)S(1)}, u32[]{:S(2)}, u32[]{:S(2)}) collective-permute-start(bf16[512,640]{1,0:T(8,128)(2,1)S(1)} %pad_maximum_fusion.2), channel_id=1, source_target_pairs={{0,1},{1,0},{2,3},{3,2},{4,5},{5,4},{6,7},{7,6},{8,9},{9,8},{10,11... | collective-permute-start | bytes 1966088 | tf_op jit(solution)/shard_map/ppermute | solution.py:10
  50.1 0.0 collective-permute-done.3
  50.1 1.9 %collective-permute-start.5 = (bf16[2,64,1280]{2,1,0:T(8,128)(2,1)}, bf16[2,64,1280]{2,1,0:T(8,128)(2,1)S(1)}, u32[]{:S(2)}, u32[]{:S(2)}) collective-permute-start(bf16[2,64,1280]{2,1,0:T(8,128)(2,1)} %collective-permute-done.3), channel_id=1, source_target_pairs={{0,32},{32,64},{64,96},{96,128},{128,160},{160,192},{192,224},{224... | collective-permute-start | bytes 983048 | tf_op jit(solution)/shard_map/ppermute | solution.py:40
  52.0 0.0 collective-permute-done.4
  52.0 4.6 %collective-permute-start.6 = (bf16[2,64,1280]{2,1,0:T(8,128)(2,1)}, bf16[2,64,1280]{2,1,0:T(8,128)(2,1)S(1)}, u32[]{:S(2)}, u32[]{:S(2)}) collective-permute-start(bf16[2,64,1280]{2,1,0:T(8,128)(2,1)} %collective-permute-done.4), channel_id=1, source_target_pairs={{0,224},{32,0},{64,32},{96,64},{128,96},{160,128},{192,160},{224,1... | collective-permute-start | bytes 983048 | tf_op jit(solution)/shard_map/ppermute | solution.py:41
  56.6 1.0 bitcast_dynamic-update-slice_fusion.5
  57.6 1.0 bitcast_dynamic-update-slice_fusion.4
  58.6 3.4 %collective-permute-done.5 = bf16[2,64,1280]{2,1,0:T(8,128)(2,1)S(1)} collective-permute-done((bf16[2,64,1280]{2,1,0:T(8,128)(2,1)}, bf16[2,64,1280]{2,1,0:T(8,128)(2,1)S(1)}, u32[]{:S(2)}, u32[]{:S(2)}) %collective-permute-start.5) | collective-permute-done | bytes 327712 | tf_op jit(solution)/shard_map/ppermute | solution.py:40
  62.0 1.9 %collective-permute-start.7 = (bf16[2,64,1280]{2,1,0:T(8,128)(2,1)S(1)}, bf16[2,64,1280]{2,1,0:T(8,128)(2,1)S(1)}, u32[]{:S(2)}, u32[]{:S(2)}) collective-permute-start(bf16[2,64,1280]{2,1,0:T(8,128)(2,1)S(1)} %collective-permute-done.5), channel_id=1, source_target_pairs={{0,32},{32,64},{64,96},{96,128},{128,160},{160,192},{192,224},{224... | collective-permute-start | bytes 983048 | tf_op jit(solution)/shard_map/ppermute | solution.py:40
  63.9 0.0 collective-permute-done.6
  63.9 4.6 %collective-permute-start.8 = (bf16[2,64,1280]{2,1,0:T(8,128)(2,1)S(1)}, bf16[2,64,1280]{2,1,0:T(8,128)(2,1)S(1)}, u32[]{:S(2)}, u32[]{:S(2)}) collective-permute-start(bf16[2,64,1280]{2,1,0:T(8,128)(2,1)S(1)} %collective-permute-done.6), channel_id=1, source_target_pairs={{0,224},{32,0},{64,32},{96,64},{128,96},{160,128},{192,160},{224,1... | collective-permute-start | bytes 983048 | tf_op jit(solution)/shard_map/ppermute | solution.py:41
  68.6 4.2 %collective-permute-done.7 = bf16[2,64,1280]{2,1,0:T(8,128)(2,1)S(1)} collective-permute-done((bf16[2,64,1280]{2,1,0:T(8,128)(2,1)S(1)}, bf16[2,64,1280]{2,1,0:T(8,128)(2,1)S(1)}, u32[]{:S(2)}, u32[]{:S(2)}) %collective-permute-start.7) | collective-permute-done | bytes 327712 | tf_op jit(solution)/shard_map/ppermute | solution.py:40
  72.8 1.9 %collective-permute-start.9 = (bf16[1,64,1280]{2,1,0:T(8,128)(2,1)S(1)}, bf16[1,64,1280]{2,1,0:T(8,128)(2,1)S(1)}, u32[]{:S(2)}, u32[]{:S(2)}) collective-permute-start(bf16[1,64,1280]{2,1,0:T(8,128)(2,1)S(1)} %slice.44), channel_id=1, source_target_pairs={{0,32},{32,64},{64,96},{96,128},{128,160},{160,192},{192,224},{224... | collective-permute-start | bytes 491528 | tf_op jit(solution)/shard_map/ppermute | solution.py:46
  74.7 0.0 collective-permute-done.8
  74.7 4.6 %collective-permute-start.10 = (bf16[1,64,1280]{2,1,0:T(8,128)(2,1)S(1)}, bf16[1,64,1280]{2,1,0:T(8,128)(2,1)S(1)}, u32[]{:S(2)}, u32[]{:S(2)}) collective-permute-start(bf16[1,64,1280]{2,1,0:T(8,128)(2,1)S(1)} %slice.45), channel_id=1, source_target_pairs={{0,224},{32,0},{64,32},{96,64},{128,96},{160,128},{192,160},{224,1... | collective-permute-start | bytes 491528 | tf_op jit(solution)/shard_map/ppermute | solution.py:47
  79.4 0.0 collective-permute-done.12
  79.4 0.1 pad_maximum_fusion
  79.5 0.5 collective-permute-done.9
  80.1 1.5 %collective-permute-done.10 = bf16[1,64,1280]{2,1,0:T(8,128)(2,1)S(1)} collective-permute-done((bf16[1,64,1280]{2,1,0:T(8,128)(2,1)S(1)}, bf16[1,64,1280]{2,1,0:T(8,128)(2,1)S(1)}, u32[]{:S(2)}, u32[]{:S(2)}) %collective-permute-start.10) | collective-permute-done | bytes 163872 | tf_op jit(solution)/shard_map/ppermute | solution.py:47
  81.6 0.9 convolution_convert_fusion.1
  82.4 0.9 convolution_convert_fusion
  83.3 1.0 pad_maximum_fusion.1
  84.4 13.7 %all-to-all-start.1 = ((bf16[32,64,256]{2,1,0:T(8,128)(2,1)}), bf16[32,64,256]{2,1,0:T(8,128)(2,1)}, u32[]{:S(2)}, u32[]{:S(2)}) async-start(bf16[32,64,256]{2,1,0:T(8,128)(2,1)} %bitcast.71), calls=%async_computation.1 | async-start | bytes 2097152 | tf_op jit(solution)/shard_map/all_to_all | solution.py:20
  98.1 0.0 all-gather.2.cloned.1.call-done
  98.1 2.8 %fusion.4 = f32[512,1280]{1,0:T(8,128)S(1)} fusion(bf16[1024,512]{1,0:T(8,128)(2,1)} %all-gather.2.cloned.1.call-done, bf16[1024,1280]{1,0:T(8,128)(2,1)S(1)} %bitcast.70), kind=kOutput, calls=%fused_computation.38 | convolution fusion | flops 1342177280 | bytes 6291456 | tf_op jit(solution)/shard_map/dot_general | solution.py:99
  100.9 0.1 slice.62
  101.0 2.2 %collective-permute-start.13 = (bf16[256,1280]{1,0:T(8,128)(2,1)S(1)}, bf16[256,1280]{1,0:T(8,128)(2,1)S(1)}, u32[]{:S(2)}, u32[]{:S(2)}) collective-permute-start(bf16[256,1280]{1,0:T(8,128)(2,1)S(1)} %slice.62), channel_id=1, source_target_pairs={{0,16},{16,0},{1,17},{17,1},{2,18},{18,2},{3,19},{19,3},{4,20},{20... | collective-permute-start | bytes 1966088 | tf_op jit(solution)/shard_map/ppermute | solution.py:10
  103.2 1.8 %collective-permute-done.13 = bf16[256,1280]{1,0:T(8,128)(2,1)S(1)} collective-permute-done((bf16[256,1280]{1,0:T(8,128)(2,1)S(1)}, bf16[256,1280]{1,0:T(8,128)(2,1)S(1)}, u32[]{:S(2)}, u32[]{:S(2)}) %collective-permute-start.13) | collective-permute-done | bytes 655392 | tf_op jit(solution)/shard_map/ppermute | solution.py:10
  105.0 0.1 slice_add_fusion
  105.1 4.8 %collective-permute-start.14 = (bf16[256,640]{1,0:T(8,128)(2,1)S(1)}, bf16[256,640]{1,0:T(8,128)(2,1)S(1)}, u32[]{:S(2)}, u32[]{:S(2)}) collective-permute-start(bf16[256,640]{1,0:T(8,128)(2,1)S(1)} %slice.63), channel_id=1, source_target_pairs={{0,1},{1,0},{2,3},{3,2},{4,5},{5,4},{6,7},{7,6},{8,9},{9,8},{10,11... | collective-permute-start | bytes 983048 | tf_op jit(solution)/shard_map/ppermute | solution.py:10
  109.9 12.8 %collective-permute-done.14 = bf16[256,640]{1,0:T(8,128)(2,1)S(1)} collective-permute-done((bf16[256,640]{1,0:T(8,128)(2,1)S(1)}, bf16[256,640]{1,0:T(8,128)(2,1)S(1)}, u32[]{:S(2)}, u32[]{:S(2)}) %collective-permute-start.14) | collective-permute-done | bytes 327712 | tf_op jit(solution)/shard_map/ppermute | solution.py:10
  122.7 0.9 slice_add_fusion.1
  123.6 3.0 %all-to-all-done.1 = bf16[32,64,256]{2,1,0:T(8,128)(2,1)} async-done(((bf16[32,64,256]{2,1,0:T(8,128)(2,1)}), bf16[32,64,256]{2,1,0:T(8,128)(2,1)}, u32[]{:S(2)}, u32[]{:S(2)}) %all-to-all-start.1) | async-done | bytes 1048608 | tf_op jit(solution)/shard_map/all_to_all | solution.py:20
  126.6 2.1 %reduce_sum.12 = bf16[2,2,64,256]{3,2,1,0:T(8,128)(2,1)} reduce(bf16[2,8,2,64,256]{4,3,2,1,0:T(8,128)(2,1)} %bitcast.31, bf16[]{:T(256)} %constant.61.clone.1), dimensions={1}, to_apply=%region_0.1 | reduce | flops 458752 | bytes 1179650 | tf_op jit(solution)/shard_map/reduce_sum | solution.py:97
  (17 shorter events, 0.3 us)
Async XLA Ops:
  8.8 25.2 %all-to-all-start = ((bf16[4,64,640]{2,1,0:T(8,128)(2,1)}), bf16[4,64,640]{2,1,0:T(8,128)(2,1)S(1)}, u32[]{:S(2)}, u32[]{:S(2)}) async-start(bf16[4,64,640]{2,1,0:T(8,128)(2,1)} %bitcast.1), calls=%async_computation | async-start | bytes 655360 | tf_op jit(solution)/shard_map/all_to_all | solution.py:20
  13.7 84.4 %all-gather.2.cloned.1.call-start = ((), (), s32[]{:S(2)}) async-start(), calls=%async_computation.2 | async-start | bytes 1179648 | tf_op jit(solution)/shard_map/all_gather | solution.py:77
  14.5 14.8 %collective-permute-start = (bf16[64,256]{1,0:T(8,128)(2,1)S(1)}, bf16[64,256]{1,0:T(8,128)(2,1)S(1)}, u32[]{:S(2)}, u32[]{:S(2)}) collective-permute-start(bf16[64,256]{1,0:T(8,128)(2,1)S(1)} %get-tuple-element.30), channel_id=1, source_target_pairs={{0,1},{1,0},{16,17},{17,16},{2,3},{3,2},{18,19},{19,18},{4,5},{5,4... | collective-permute-start | bytes 98312 | tf_op jit(solution)/shard_map/ppermute | solution.py:68
  19.4 9.9 %collective-permute-start.1 = (bf16[64,256]{1,0:T(8,128)(2,1)S(1)}, bf16[64,256]{1,0:T(8,128)(2,1)S(1)}, u32[]{:S(2)}, u32[]{:S(2)}) collective-permute-start(bf16[64,256]{1,0:T(8,128)(2,1)S(1)} %get-tuple-element.29), channel_id=1, source_target_pairs={{0,16},{1,17},{16,0},{17,1},{2,18},{3,19},{18,2},{19,3},{4,20},{5,... | collective-permute-start | bytes 98312 | tf_op jit(solution)/shard_map/ppermute | solution.py:68
  27.3 6.7 %collective-permute-start.2 = (bf16[64,256]{1,0:T(8,128)(2,1)S(1)}, bf16[64,256]{1,0:T(8,128)(2,1)S(1)}, u32[]{:S(2)}, u32[]{:S(2)}) collective-permute-start(bf16[64,256]{1,0:T(8,128)(2,1)S(1)} %get-tuple-element.28), channel_id=1, source_target_pairs={{0,17},{1,16},{16,1},{17,0},{2,19},{3,18},{18,3},{19,2},{4,21},{5,... | collective-permute-start | bytes 98312 | tf_op jit(solution)/shard_map/ppermute | solution.py:68
  34.9 15.2 %collective-permute-start.3 = (bf16[2,64,1280]{2,1,0:T(8,128)(2,1)S(1)}, bf16[2,64,1280]{2,1,0:T(8,128)(2,1)}, u32[]{:S(2)}, u32[]{:S(2)}) collective-permute-start(bf16[2,64,1280]{2,1,0:T(8,128)(2,1)S(1)} %pad_maximum_fusion.3), channel_id=1, source_target_pairs={{0,32},{32,64},{64,96},{96,128},{128,160},{160,192},{192,224},{224... | collective-permute-start | bytes 983048 | tf_op jit(solution)/shard_map/ppermute | solution.py:40
  36.8 15.2 %collective-permute-start.4 = (bf16[2,64,1280]{2,1,0:T(8,128)(2,1)S(1)}, bf16[2,64,1280]{2,1,0:T(8,128)(2,1)}, u32[]{:S(2)}, u32[]{:S(2)}) collective-permute-start(bf16[2,64,1280]{2,1,0:T(8,128)(2,1)S(1)} %pad_maximum_fusion.3), channel_id=1, source_target_pairs={{0,224},{32,0},{64,32},{96,64},{128,96},{160,128},{192,160},{224,1... | collective-permute-start | bytes 983048 | tf_op jit(solution)/shard_map/ppermute | solution.py:41
  43.0 3.9 %collective-permute-start.11 = (bf16[256,640]{1,0:T(8,128)(2,1)}, bf16[256,640]{1,0:T(8,128)(2,1)}, u32[]{:S(2)}, u32[]{:S(2)}) collective-permute-start(bf16[256,640]{1,0:T(8,128)(2,1)} %param.5), channel_id=1, source_target_pairs={{0,16},{16,0},{1,17},{17,1},{2,18},{18,2},{3,19},{19,3},{4,20},{20... | collective-permute-start | bytes 983048 | tf_op jit(solution)/shard_map/ppermute | solution.py:10
  48.0 31.3 %collective-permute-start.12 = (bf16[512,640]{1,0:T(8,128)(2,1)S(1)}, bf16[512,640]{1,0:T(8,128)(2,1)S(1)}, u32[]{:S(2)}, u32[]{:S(2)}) collective-permute-start(bf16[512,640]{1,0:T(8,128)(2,1)S(1)} %pad_maximum_fusion.2), channel_id=1, source_target_pairs={{0,1},{1,0},{2,3},{3,2},{4,5},{5,4},{6,7},{7,6},{8,9},{9,8},{10,11... | collective-permute-start | bytes 1966088 | tf_op jit(solution)/shard_map/ppermute | solution.py:10
  50.1 11.9 %collective-permute-start.5 = (bf16[2,64,1280]{2,1,0:T(8,128)(2,1)}, bf16[2,64,1280]{2,1,0:T(8,128)(2,1)S(1)}, u32[]{:S(2)}, u32[]{:S(2)}) collective-permute-start(bf16[2,64,1280]{2,1,0:T(8,128)(2,1)} %collective-permute-done.3), channel_id=1, source_target_pairs={{0,32},{32,64},{64,96},{96,128},{128,160},{160,192},{192,224},{224... | collective-permute-start | bytes 983048 | tf_op jit(solution)/shard_map/ppermute | solution.py:40
  52.0 11.9 %collective-permute-start.6 = (bf16[2,64,1280]{2,1,0:T(8,128)(2,1)}, bf16[2,64,1280]{2,1,0:T(8,128)(2,1)S(1)}, u32[]{:S(2)}, u32[]{:S(2)}) collective-permute-start(bf16[2,64,1280]{2,1,0:T(8,128)(2,1)} %collective-permute-done.4), channel_id=1, source_target_pairs={{0,224},{32,0},{64,32},{96,64},{128,96},{160,128},{192,160},{224,1... | collective-permute-start | bytes 983048 | tf_op jit(solution)/shard_map/ppermute | solution.py:41
  62.0 10.8 %collective-permute-start.7 = (bf16[2,64,1280]{2,1,0:T(8,128)(2,1)S(1)}, bf16[2,64,1280]{2,1,0:T(8,128)(2,1)S(1)}, u32[]{:S(2)}, u32[]{:S(2)}) collective-permute-start(bf16[2,64,1280]{2,1,0:T(8,128)(2,1)S(1)} %collective-permute-done.5), channel_id=1, source_target_pairs={{0,32},{32,64},{64,96},{96,128},{128,160},{160,192},{192,224},{224... | collective-permute-start | bytes 983048 | tf_op jit(solution)/shard_map/ppermute | solution.py:40
  63.9 10.8 %collective-permute-start.8 = (bf16[2,64,1280]{2,1,0:T(8,128)(2,1)S(1)}, bf16[2,64,1280]{2,1,0:T(8,128)(2,1)S(1)}, u32[]{:S(2)}, u32[]{:S(2)}) collective-permute-start(bf16[2,64,1280]{2,1,0:T(8,128)(2,1)S(1)} %collective-permute-done.6), channel_id=1, source_target_pairs={{0,224},{32,0},{64,32},{96,64},{128,96},{160,128},{192,160},{224,1... | collective-permute-start | bytes 983048 | tf_op jit(solution)/shard_map/ppermute | solution.py:41
  72.8 7.3 %collective-permute-start.9 = (bf16[1,64,1280]{2,1,0:T(8,128)(2,1)S(1)}, bf16[1,64,1280]{2,1,0:T(8,128)(2,1)S(1)}, u32[]{:S(2)}, u32[]{:S(2)}) collective-permute-start(bf16[1,64,1280]{2,1,0:T(8,128)(2,1)S(1)} %slice.44), channel_id=1, source_target_pairs={{0,32},{32,64},{64,96},{96,128},{128,160},{160,192},{192,224},{224... | collective-permute-start | bytes 491528 | tf_op jit(solution)/shard_map/ppermute | solution.py:46
  74.7 6.8 %collective-permute-start.10 = (bf16[1,64,1280]{2,1,0:T(8,128)(2,1)S(1)}, bf16[1,64,1280]{2,1,0:T(8,128)(2,1)S(1)}, u32[]{:S(2)}, u32[]{:S(2)}) collective-permute-start(bf16[1,64,1280]{2,1,0:T(8,128)(2,1)S(1)} %slice.45), channel_id=1, source_target_pairs={{0,224},{32,0},{64,32},{96,64},{128,96},{160,128},{192,160},{224,1... | collective-permute-start | bytes 491528 | tf_op jit(solution)/shard_map/ppermute | solution.py:47
  84.4 42.3 %all-to-all-start.1 = ((bf16[32,64,256]{2,1,0:T(8,128)(2,1)}), bf16[32,64,256]{2,1,0:T(8,128)(2,1)}, u32[]{:S(2)}, u32[]{:S(2)}) async-start(bf16[32,64,256]{2,1,0:T(8,128)(2,1)} %bitcast.71), calls=%async_computation.1 | async-start | bytes 2097152 | tf_op jit(solution)/shard_map/all_to_all | solution.py:20
  101.0 4.0 %collective-permute-start.13 = (bf16[256,1280]{1,0:T(8,128)(2,1)S(1)}, bf16[256,1280]{1,0:T(8,128)(2,1)S(1)}, u32[]{:S(2)}, u32[]{:S(2)}) collective-permute-start(bf16[256,1280]{1,0:T(8,128)(2,1)S(1)} %slice.62), channel_id=1, source_target_pairs={{0,16},{16,0},{1,17},{17,1},{2,18},{18,2},{3,19},{19,3},{4,20},{20... | collective-permute-start | bytes 1966088 | tf_op jit(solution)/shard_map/ppermute | solution.py:10
  105.1 17.6 %collective-permute-start.14 = (bf16[256,640]{1,0:T(8,128)(2,1)S(1)}, bf16[256,640]{1,0:T(8,128)(2,1)S(1)}, u32[]{:S(2)}, u32[]{:S(2)}) collective-permute-start(bf16[256,640]{1,0:T(8,128)(2,1)S(1)} %slice.63), channel_id=1, source_target_pairs={{0,1},{1,0},{2,3},{3,2},{4,5},{5,4},{6,7},{7,6},{8,9},{9,8},{10,11... | collective-permute-start | bytes 983048 | tf_op jit(solution)/shard_map/ppermute | solution.py:10
Sparse Core Ops, SparseCore 0:
  45.3 33.3 all-gather.1

commit v7 on v3

v7 whole, which is shorter than its diff:
```python
import jax
import jax.numpy as jnp
from jax import lax
from jax.sharding import Mesh, PartitionSpec as P

SWAP = ((0, 1), (1, 0))


def swap(block, axis):
    return lax.ppermute(block, axis, SWAP)


def in_order(own, kept, got, axis):
    return jnp.concatenate(
        [jnp.where(own == 0, kept, got), jnp.where(own == 0, got, kept)], axis=axis
    )


def pick(block, index, axis):
    return lax.dynamic_slice_in_dim(block, index, 1, axis)


def exchange(pieces, axes):
    return lax.all_to_all(pieces, axes, split_axis=0, concat_axis=0, tiled=True)


def ring_gather(block, weights):
    core = lax.axis_index("core")
    me = lax.axis_index("z")
    size = lax.axis_size("z")
    sign = 1 - 2 * core
    one_way = [
        (2 * i + c, 2 * ((i + 1 - 2 * c) % size) + c) for i in range(size) for c in range(2)
    ]
    other_way = [(target, source) for source, target in one_way]
    panel = jnp.zeros((block.shape[0], size) + block.shape[1:], block.dtype)

    def put(panel, block, first, steps):
        at = (first, lax.rem(me - sign * steps + size, size), 0, 0)
        return lax.dynamic_update_slice(panel, block[:, None], at)

    panel = put(panel, block, 0, 0)
    one = two = block
    for step in range(1, size // 2):
        one = lax.ppermute(one, ("z", "core"), one_way)
        two = lax.ppermute(two, ("z", "core"), other_way)
        panel = put(panel, one, 0, step)
        panel = put(panel, two, 0, -step)
        if step == min(2, size // 2 - 1):
            one, weights = lax.optimization_barrier((one, weights))
            weights = in_order(core, weights, swap(weights, "core"), 0)
    middle = block.shape[0] // 2
    one = lax.ppermute(one[:middle], ("z", "core"), one_way)
    two = lax.ppermute(two[middle:], ("z", "core"), other_way)
    panel = put(panel, one, 0, size // 2)
    return put(panel, two, middle, size // 2), weights


def per_device(inputs, out_grad, weight):
    core = lax.axis_index("core")
    half = lax.axis_index("xh")
    tokens, columns = out_grad.shape
    part = tokens // 2
    features = inputs.shape[1]

    pieces = jnp.broadcast_to(out_grad.reshape(1, 2, part, columns), (2, 2, part, columns))
    pieces = pieces.reshape(4, part, columns)
    pieces = exchange(pieces, ("xl", "xh"))
    acts = inputs.reshape(2, 2, part, features)
    acts = in_order(half, pick(acts, half, 1), swap(pick(acts, 1 - half, 1), "xh"), 1)
    pieces, acts, weight = lax.optimization_barrier((pieces, acts, weight))
    acts = jnp.concatenate([pick(acts, core, 0), pick(acts, 1 - core, 0)], axis=0)
    acts = lax.all_gather(acts.reshape(2, 2 * part, features), "y", axis=0, tiled=False)

    pieces = pieces.reshape(2, 2, part, columns)
    grads = in_order(half, pieces[:, 0], pieces[:, 1], 2)
    grads, weight = lax.optimization_barrier((grads, weight))
    weights = jnp.concatenate([weight, swap(weight, "xh")], axis=1)
    grads, weights = ring_gather(grads, weights)
    grads = grads.reshape(-1, 2 * columns)

    grads, weights = lax.optimization_barrier((grads, weights))
    partial = [
        lax.dot_general(
            grads,
            weights[i * features : (i + 1) * features],
            (((1,), (1,)), ((), ())),
            preferred_element_type=jnp.float32,
        ).astype(jnp.bfloat16)
        for i in range(2)
    ]
    got = swap(acts[:, 1], "core")
    *partial, got, grads = lax.optimization_barrier((*partial, got, grads))
    acts = jnp.concatenate([acts[:, 0], got], axis=2).reshape(-1, 2 * features)

    partial = jnp.concatenate(partial, axis=0)
    shares = exchange(partial.reshape(-1, part, features), ("core", "y", "xh"))
    shares = shares.reshape(2, -1, 2, part, features).astype(jnp.float32)
    input_grad = jnp.sum(shares, axis=1).astype(jnp.bfloat16).reshape(-1, features)

    w_part = lax.dot_general(
        acts, grads, (((0,), (0,)), ((), ())), preferred_element_type=jnp.float32
    )
    w_part = w_part[:features] + swap(w_part[features:].astype(jnp.bfloat16), "core")
    w_grad = w_part[:, :columns] + swap(w_part[:, columns:].astype(jnp.bfloat16), "xh")
    return (w_grad, input_grad)


def solution(mesh):
    rows, cols = mesh.devices.shape
    split = Mesh(
        mesh.devices.reshape(2, rows // 4, 2, cols // 2, 2), ("xl", "z", "core", "y", "xh")
    )
    row, col = ("xl", "z", "core"), ("y", "xh")
    return jax.shard_map(
        per_device,
        mesh=split,
        in_specs=(P(col, row), P(row, col), P(row, col)),
        out_specs=(P(row, col), P(col, row)),
        check_vma=False,
    )
```

time: 135 us -> 136 us (level)
  waiting for transfers between devices: 35.9 us -> 30 us
  local copies, waits for them, and re-layouts: 3.31 us -> 6.42 us
  other arithmetic: 6.2 us -> 8 us
    all_to_all x2, starting transfers between devices: 17.9 us -> 10.9 us  [exchange(): return lax.all_to_all(pieces, axes, split_axis=0, concat_axis=0, tiled=True)]
    ppermute x8, starting transfers between devices: 27.9 us -> 33.2 us  [the longest x3 20.7 us: ring_gather(): one = lax.ppermute(one, ('z', 'core'), one_way)]
    ppermute x6, waiting for transfers between devices: 18.1 us -> 14.8 us  [swap(): return lax.ppermute(block, axis, SWAP)]
    ppermute x6, starting transfers between devices: 23.9 us -> 26.8 us  [swap(): return lax.ppermute(block, axis, SWAP)]
    concatenate x3, other arithmetic: 1.16 us -> 2.74 us  [the longest x1 1.04 us: per_device(): partial = jnp.concatenate(partial, axis=0)]
    ppermute x8, waiting for transfers between devices: 9.18 us -> 7.67 us  [the longest x1 5.23 us: ring_gather(): two = lax.ppermute(two[middle:], ('z', 'core'), other_way)]
  transfers between devices with their start and end apart: 17 -> 17, of which waited for: 9 -> 6; matrix products, arithmetic and copies ran while one was open for 8% -> 11% of each run, Pallas kernels for 0% -> 0%
where the time goes in v7:
time: 136 us; the launch traced here: 135 us
  starting transfers between devices  71 us (52%)
  waiting for transfers between devices  30 us (22%)
  between operations  14.5 us (11%)
  other arithmetic  8 us (6%)
  local copies, waits for them, and re-layouts  6.42 us (5%)
  matrix products  5.46 us (4%)
    ppermute x6, starting transfers between devices, swap(): return lax.ppermute(block, axis, SWAP)  26.8 us
    ppermute x3, starting transfers between devices, ring_gather(): one = lax.ppermute(one, ('z', 'core'), one_way)  20.7 us
    ppermute x6, waiting for transfers between devices, swap(): return lax.ppermute(block, axis, SWAP)  14.8 us
    all_to_all x2, starting transfers between devices, exchange(): return lax.all_to_all(pieces, axes, split_axis=0, concat_axis=0, tiled=True)  10.9 us
    all_to_all x2, waiting for transfers between devices, exchange(): return lax.all_to_all(pieces, axes, split_axis=0, concat_axis=0, tiled=True)  7.54 us
    ppermute x3, starting transfers between devices, ring_gather(): two = lax.ppermute(two, ('z', 'core'), other_way)  5.76 us
    ppermute x1, waiting for transfers between devices, ring_gather(): two = lax.ppermute(two[middle:], ('z', 'core'), other_way)  5.23 us
    ppermute x1, starting transfers between devices, ring_gather(): one = lax.ppermute(one[:middle], ('z', 'core'), one_way)  4.85 us
  transfers between devices with their start and end apart: 17, of which 6 were waited for; matrix products, arithmetic and copies ran while one was open for 11% of the time, Pallas kernels for 0%

profile of v7, /device:TPU:1, one launch (start us, length us, event | category | flops | bytes accessed | tf_op | source)
XLA Modules:
  0.0 135.4 jit_solution(4083287684767210981)
XLA Ops:
  7.2 0.0 copy-start.1
  7.2 0.9 constant_dynamic-slice_fusion.2
  8.1 5.5 %collective-permute-start = (bf16[2,1,64,256]{3,2,1,0:T(8,128)(2,1)S(1)}, bf16[2,1,64,256]{3,2,1,0:T(8,128)(2,1)S(1)}, u32[]{:S(2)}, u32[]{:S(2)}) collective-permute-start(bf16[2,1,64,256]{3,2,1,0:T(8,128)(2,1)S(1)} %constant_dynamic-slice_fusion.2), channel_id=1, source_target_pairs={{0,1},{1,0},{2,3},{3,2},{4,5},{5,4},{6,7},{7,6},{8,9},{9,8},{10,11... | collective-permute-start | bytes 196616 | tf_op jit(solution)/shard_map/ppermute | solution.py:10
  13.6 1.7 %broadcast_in_dim.38 = bf16[2,2,64,640]{3,2,1,0:T(8,128)(2,1)} broadcast(bf16[2,64,640]{2,1,0:T(8,128)(2,1)} %bitcast.72), dimensions={1,2,3} | broadcast | bytes 491520 | tf_op jit(solution)/shard_map/broadcast_in_dim | solution.py:66
  15.2 3.5 %all-to-all-start = ((bf16[4,64,640]{2,1,0:T(8,128)(2,1)}), bf16[4,64,640]{2,1,0:T(8,128)(2,1)S(1)}, u32[]{:S(2)}, u32[]{:S(2)}) async-start(bf16[4,64,640]{2,1,0:T(8,128)(2,1)} %bitcast.1), calls=%async_computation | async-start | bytes 655360 | tf_op jit(solution)/shard_map/all_to_all | solution.py:24
  18.7 0.0 all-gather.2.cloned.1.call-start
  18.8 0.0 collective-permute-done
  18.8 0.9 broadcast_select_fusion.3
  19.7 4.5 %all-to-all-done = bf16[4,64,640]{2,1,0:T(8,128)(2,1)S(1)} async-done(((bf16[4,64,640]{2,1,0:T(8,128)(2,1)}), bf16[4,64,640]{2,1,0:T(8,128)(2,1)S(1)}, u32[]{:S(2)}, u32[]{:S(2)}) %all-to-all-start) | async-done | bytes 327712 | tf_op jit(solution)/shard_map/all_to_all | solution.py:24
  24.3 11.5 %collective-permute-start.1 = (bf16[2,64,1280]{2,1,0:T(8,128)(2,1)S(1)}, bf16[2,64,1280]{2,1,0:T(8,128)(2,1)}, u32[]{:S(2)}, u32[]{:S(2)}) collective-permute-start(bf16[2,64,1280]{2,1,0:T(8,128)(2,1)S(1)} %pad_maximum_fusion.3), channel_id=1, source_target_pairs={{0,32},{16,240},{32,64},{48,16},{64,96},{80,48},{96,128},{112,80},... | collective-permute-start | bytes 983048 | tf_op jit(solution)/shard_map/ppermute | solution.py:45
  35.9 1.9 %collective-permute-start.2 = (bf16[2,64,1280]{2,1,0:T(8,128)(2,1)S(1)}, bf16[2,64,1280]{2,1,0:T(8,128)(2,1)}, u32[]{:S(2)}, u32[]{:S(2)}) collective-permute-start(bf16[2,64,1280]{2,1,0:T(8,128)(2,1)S(1)} %pad_maximum_fusion.3), channel_id=1, source_target_pairs={{32,0},{240,16},{64,32},{16,48},{96,64},{48,80},{128,96},{80,112},... | collective-permute-start | bytes 983048 | tf_op jit(solution)/shard_map/ppermute | solution.py:46
  37.8 0.0 copy-done.1
  37.8 2.8 %collective-permute-start.5 = (bf16[256,640]{1,0:T(8,128)(2,1)S(1)}, bf16[256,640]{1,0:T(8,128)(2,1)}, u32[]{:S(2)}, u32[]{:S(2)}) collective-permute-start(bf16[256,640]{1,0:T(8,128)(2,1)S(1)} %copy-done.1), channel_id=1, source_target_pairs={{0,1},{1,0},{2,3},{3,2},{4,5},{5,4},{6,7},{7,6},{8,9},{9,8},{10,11... | collective-permute-start | bytes 983048 | tf_op jit(solution)/shard_map/ppermute | solution.py:10
  40.7 0.7 pad_maximum_fusion.5
  41.3 0.0 all-gather.2.cloned.1.call-update
  41.3 0.2 broadcast_in_dim.39
  41.6 0.0 collective-permute-done.1
  41.7 4.6 %collective-permute-start.3 = (bf16[2,64,1280]{2,1,0:T(8,128)(2,1)}, bf16[2,64,1280]{2,1,0:T(8,128)(2,1)S(1)}, u32[]{:S(2)}, u32[]{:S(2)}) collective-permute-start(bf16[2,64,1280]{2,1,0:T(8,128)(2,1)} %collective-permute-done.1), channel_id=1, source_target_pairs={{0,32},{16,240},{32,64},{48,16},{64,96},{80,48},{96,128},{112,80},... | collective-permute-start | bytes 983048 | tf_op jit(solution)/shard_map/ppermute | solution.py:45
  46.2 0.0 collective-permute-done.2
  46.2 1.9 %collective-permute-start.4 = (bf16[2,64,1280]{2,1,0:T(8,128)(2,1)}, bf16[2,64,1280]{2,1,0:T(8,128)(2,1)S(1)}, u32[]{:S(2)}, u32[]{:S(2)}) collective-permute-start(bf16[2,64,1280]{2,1,0:T(8,128)(2,1)} %collective-permute-done.2), channel_id=1, source_target_pairs={{32,0},{240,16},{64,32},{16,48},{96,64},{48,80},{128,96},{80,112},... | collective-permute-start | bytes 983048 | tf_op jit(solution)/shard_map/ppermute | solution.py:46
  48.2 1.0 bitcast_dynamic-update-slice_fusion.5
  49.2 1.0 bitcast_dynamic-update-slice_fusion.4
  50.2 0.0 collective-permute-done.5
  50.2 1.0 pad_maximum_fusion.2
  51.2 0.0 collective-permute-done.3
  51.2 4.6 %collective-permute-start.6 = (bf16[2,64,1280]{2,1,0:T(8,128)(2,1)S(1)}, bf16[2,64,1280]{2,1,0:T(8,128)(2,1)S(1)}, u32[]{:S(2)}, u32[]{:S(2)}) collective-permute-start(bf16[2,64,1280]{2,1,0:T(8,128)(2,1)S(1)} %collective-permute-done.3), channel_id=1, source_target_pairs={{0,32},{16,240},{32,64},{48,16},{64,96},{80,48},{96,128},{112,80},... | collective-permute-start | bytes 983048 | tf_op jit(solution)/shard_map/ppermute | solution.py:45
  55.8 6.2 %collective-permute-start.10 = (bf16[256,1280]{1,0:T(8,128)(2,1)S(1)}, bf16[256,1280]{1,0:T(8,128)(2,1)S(1)}, u32[]{:S(2)}, u32[]{:S(2)}) collective-permute-start(bf16[256,1280]{1,0:T(8,128)(2,1)S(1)} %pad_maximum_fusion.2), channel_id=1, source_target_pairs={{0,16},{16,0},{1,17},{17,1},{2,18},{18,2},{3,19},{19,3},{4,20},{20... | collective-permute-start | bytes 1966088 | tf_op jit(solution)/shard_map/ppermute | solution.py:10
  62.0 0.0 collective-permute-done.4
  62.0 1.9 %collective-permute-start.7 = (bf16[2,64,1280]{2,1,0:T(8,128)(2,1)S(1)}, bf16[2,64,1280]{2,1,0:T(8,128)(2,1)S(1)}, u32[]{:S(2)}, u32[]{:S(2)}) collective-permute-start(bf16[2,64,1280]{2,1,0:T(8,128)(2,1)S(1)} %collective-permute-done.4), channel_id=1, source_target_pairs={{32,0},{240,16},{64,32},{16,48},{96,64},{48,80},{128,96},{80,112},... | collective-permute-start | bytes 983048 | tf_op jit(solution)/shard_map/ppermute | solution.py:46
  64.0 0.0 collective-permute-done.6
  64.1 4.9 %collective-permute-start.8 = (bf16[1,64,1280]{2,1,0:T(8,128)(2,1)S(1)}, bf16[1,64,1280]{2,1,0:T(8,128)(2,1)S(1)}, u32[]{:S(2)}, u32[]{:S(2)}) collective-permute-start(bf16[1,64,1280]{2,1,0:T(8,128)(2,1)S(1)} %slice.53), channel_id=1, source_target_pairs={{0,32},{16,240},{32,64},{48,16},{64,96},{80,48},{96,128},{112,80},... | collective-permute-start | bytes 491528 | tf_op jit(solution)/shard_map/ppermute | solution.py:53
  68.9 2.4 %collective-permute-done.7 = bf16[2,64,1280]{2,1,0:T(8,128)(2,1)S(1)} collective-permute-done((bf16[2,64,1280]{2,1,0:T(8,128)(2,1)S(1)}, bf16[2,64,1280]{2,1,0:T(8,128)(2,1)S(1)}, u32[]{:S(2)}, u32[]{:S(2)}) %collective-permute-start.7) | collective-permute-done | bytes 327712 | tf_op jit(solution)/shard_map/ppermute | solution.py:46
  71.3 1.9 %collective-permute-start.9 = (bf16[1,64,1280]{2,1,0:T(8,128)(2,1)S(1)}, bf16[1,64,1280]{2,1,0:T(8,128)(2,1)S(1)}, u32[]{:S(2)}, u32[]{:S(2)}) collective-permute-start(bf16[1,64,1280]{2,1,0:T(8,128)(2,1)S(1)} %slice.54), channel_id=1, source_target_pairs={{32,0},{240,16},{64,32},{16,48},{96,64},{48,80},{128,96},{80,112},... | collective-permute-start | bytes 491528 | tf_op jit(solution)/shard_map/ppermute | solution.py:54
  73.4 0.0 collective-permute-done.8
  73.4 5.2 %collective-permute-done.9 = bf16[1,64,1280]{2,1,0:T(8,128)(2,1)S(1)} collective-permute-done((bf16[1,64,1280]{2,1,0:T(8,128)(2,1)S(1)}, bf16[1,64,1280]{2,1,0:T(8,128)(2,1)S(1)}, u32[]{:S(2)}, u32[]{:S(2)}) %collective-permute-start.9) | collective-permute-done | bytes 163872 | tf_op jit(solution)/shard_map/ppermute | solution.py:54
  78.6 0.0 collective-permute-done.10
  78.7 0.1 broadcast_select_fusion.1
  78.8 1.1 pad_maximum_fusion
  79.9 0.0 all-gather.2.cloned.1.call-done
  79.9 1.3 fusion.9
  81.2 0.0 copy-start
  81.2 5.4 %collective-permute-start.11 = (bf16[8,128,256]{2,1,0:T(8,128)(2,1)S(1)}, bf16[8,128,256]{2,1,0:T(8,128)(2,1)}, u32[]{:S(2)}, u32[]{:S(2)}) collective-permute-start(bf16[8,128,256]{2,1,0:T(8,128)(2,1)S(1)} %get-tuple-element.31), channel_id=1, source_target_pairs={{0,16},{16,0},{1,17},{17,1},{2,18},{18,2},{3,19},{19,3},{4,20},{20... | collective-permute-start | bytes 1572872 | tf_op jit(solution)/shard_map/ppermute | solution.py:10
  86.6 2.0 %convolution_convert_fusion.1 = bf16[1024,256]{1,0:T(8,128)(2,1)S(1)} fusion(bf16[1024,1280]{1,0:T(8,128)(2,1)S(1)} %bitcast.64, bf16[512,1280]{1,0:T(8,128)(2,1)} %pad_maximum_fusion), kind=kOutput, calls=%fused_computation.4 | convolution fusion | flops 671350784 | bytes 3801088 | tf_op jit(solution)/shard_map/dot_general | solution.py:84
  88.5 0.0 copy-done
  88.5 0.9 convolution_convert_fusion
  89.4 0.0 collective-permute-done.11
  89.4 1.0 pad_maximum_fusion.1
  90.5 7.4 %all-to-all-start.1 = ((bf16[32,64,256]{2,1,0:T(8,128)(2,1)}), bf16[32,64,256]{2,1,0:T(8,128)(2,1)}, u32[]{:S(2)}, u32[]{:S(2)}) async-start(bf16[32,64,256]{2,1,0:T(8,128)(2,1)} %bitcast.67), calls=%async_computation.1 | async-start | bytes 2097152 | tf_op jit(solution)/shard_map/all_to_all | solution.py:24
  97.9 2.6 %fusion = f32[512,1280]{1,0:T(8,128)S(1)} fusion(bf16[1024,1280]{1,0:T(8,128)(2,1)S(1)} %bitcast.66, bf16[1024,256]{1,0:T(8,128)(2,1)} %bitcast.29, bf16[1024,256]{1,0:T(8,128)(2,1)S(1)} %bitcast.70), kind=kOutput, calls=%fused_computation.5 | convolution fusion | flops 1344274432 | bytes 6291456 | tf_op jit(solution)/shard_map/dot_general | solution.py:101
  100.5 0.1 slice.73
  100.6 2.2 %collective-permute-start.12 = (bf16[256,1280]{1,0:T(8,128)(2,1)S(1)}, bf16[256,1280]{1,0:T(8,128)(2,1)S(1)}, u32[]{:S(2)}, u32[]{:S(2)}) collective-permute-start(bf16[256,1280]{1,0:T(8,128)(2,1)S(1)} %slice.73), channel_id=1, source_target_pairs={{0,16},{16,0},{1,17},{17,1},{2,18},{18,2},{3,19},{19,3},{4,20},{20... | collective-permute-start | bytes 1966088 | tf_op jit(solution)/shard_map/ppermute | solution.py:10
  102.8 1.8 %collective-permute-done.12 = bf16[256,1280]{1,0:T(8,128)(2,1)S(1)} collective-permute-done((bf16[256,1280]{1,0:T(8,128)(2,1)S(1)}, bf16[256,1280]{1,0:T(8,128)(2,1)S(1)}, u32[]{:S(2)}, u32[]{:S(2)}) %collective-permute-start.12) | collective-permute-done | bytes 655392 | tf_op jit(solution)/shard_map/ppermute | solution.py:10
  104.6 0.1 slice_add_fusion
  104.8 4.8 %collective-permute-start.13 = (bf16[256,640]{1,0:T(8,128)(2,1)S(1)}, bf16[256,640]{1,0:T(8,128)(2,1)S(1)}, u32[]{:S(2)}, u32[]{:S(2)}) collective-permute-start(bf16[256,640]{1,0:T(8,128)(2,1)S(1)} %slice.74), channel_id=1, source_target_pairs={{0,1},{1,0},{2,3},{3,2},{4,5},{5,4},{6,7},{7,6},{8,9},{9,8},{10,11... | collective-permute-start | bytes 983048 | tf_op jit(solution)/shard_map/ppermute | solution.py:10
  109.6 13.0 %collective-permute-done.13 = bf16[256,640]{1,0:T(8,128)(2,1)S(1)} collective-permute-done((bf16[256,640]{1,0:T(8,128)(2,1)S(1)}, bf16[256,640]{1,0:T(8,128)(2,1)S(1)}, u32[]{:S(2)}, u32[]{:S(2)}) %collective-permute-start.13) | collective-permute-done | bytes 327712 | tf_op jit(solution)/shard_map/ppermute | solution.py:10
  122.6 0.9 slice_add_fusion.1
  123.5 3.0 %all-to-all-done.1 = bf16[32,64,256]{2,1,0:T(8,128)(2,1)} async-done(((bf16[32,64,256]{2,1,0:T(8,128)(2,1)}), bf16[32,64,256]{2,1,0:T(8,128)(2,1)}, u32[]{:S(2)}, u32[]{:S(2)}) %all-to-all-start.1) | async-done | bytes 1048608 | tf_op jit(solution)/shard_map/all_to_all | solution.py:24
  126.5 2.1 %reduce_sum.12 = bf16[2,2,64,256]{3,2,1,0:T(8,128)(2,1)} reduce(bf16[2,8,2,64,256]{4,3,2,1,0:T(8,128)(2,1)} %bitcast.31, bf16[]{:T(256)} %constant.46.clone.1), dimensions={1}, to_apply=%region_0.1 | reduce | flops 458752 | bytes 1179650 | tf_op jit(solution)/shard_map/reduce_sum | solution.py:99
  (15 shorter events, 0.3 us)
Async XLA Ops:
  7.2 30.6 %copy-start.1 = (bf16[256,640]{1,0:T(8,128)(2,1)S(1)}, bf16[256,640]{1,0:T(8,128)(2,1)}, u32[]{:S(2)}) copy-start(bf16[256,640]{1,0:T(8,128)(2,1)} %param.5) | copy-start | bytes 983044
  8.1 10.7 %collective-permute-start = (bf16[2,1,64,256]{3,2,1,0:T(8,128)(2,1)S(1)}, bf16[2,1,64,256]{3,2,1,0:T(8,128)(2,1)S(1)}, u32[]{:S(2)}, u32[]{:S(2)}) collective-permute-start(bf16[2,1,64,256]{3,2,1,0:T(8,128)(2,1)S(1)} %constant_dynamic-slice_fusion.2), channel_id=1, source_target_pairs={{0,1},{1,0},{2,3},{3,2},{4,5},{5,4},{6,7},{7,6},{8,9},{9,8},{10,11... | collective-permute-start | bytes 196616 | tf_op jit(solution)/shard_map/ppermute | solution.py:10
  15.2 9.0 %all-to-all-start = ((bf16[4,64,640]{2,1,0:T(8,128)(2,1)}), bf16[4,64,640]{2,1,0:T(8,128)(2,1)S(1)}, u32[]{:S(2)}, u32[]{:S(2)}) async-start(bf16[4,64,640]{2,1,0:T(8,128)(2,1)} %bitcast.1), calls=%async_computation | async-start | bytes 655360 | tf_op jit(solution)/shard_map/all_to_all | solution.py:24
  18.7 61.2 %all-gather.2.cloned.1.call-start = ((), (), s32[]{:S(2)}) async-start(), calls=%async_computation.2 | async-start | bytes 1179648 | tf_op jit(solution)/shard_map/all_gather | solution.py:73
  24.3 17.3 %collective-permute-start.1 = (bf16[2,64,1280]{2,1,0:T(8,128)(2,1)S(1)}, bf16[2,64,1280]{2,1,0:T(8,128)(2,1)}, u32[]{:S(2)}, u32[]{:S(2)}) collective-permute-start(bf16[2,64,1280]{2,1,0:T(8,128)(2,1)S(1)} %pad_maximum_fusion.3), channel_id=1, source_target_pairs={{0,32},{16,240},{32,64},{48,16},{64,96},{80,48},{96,128},{112,80},... | collective-permute-start | bytes 983048 | tf_op jit(solution)/shard_map/ppermute | solution.py:45
  35.9 10.4 %collective-permute-start.2 = (bf16[2,64,1280]{2,1,0:T(8,128)(2,1)S(1)}, bf16[2,64,1280]{2,1,0:T(8,128)(2,1)}, u32[]{:S(2)}, u32[]{:S(2)}) collective-permute-start(bf16[2,64,1280]{2,1,0:T(8,128)(2,1)S(1)} %pad_maximum_fusion.3), channel_id=1, source_target_pairs={{32,0},{240,16},{64,32},{16,48},{96,64},{48,80},{128,96},{80,112},... | collective-permute-start | bytes 983048 | tf_op jit(solution)/shard_map/ppermute | solution.py:46
  37.8 12.4 %collective-permute-start.5 = (bf16[256,640]{1,0:T(8,128)(2,1)S(1)}, bf16[256,640]{1,0:T(8,128)(2,1)}, u32[]{:S(2)}, u32[]{:S(2)}) collective-permute-start(bf16[256,640]{1,0:T(8,128)(2,1)S(1)} %copy-done.1), channel_id=1, source_target_pairs={{0,1},{1,0},{2,3},{3,2},{4,5},{5,4},{6,7},{7,6},{8,9},{9,8},{10,11... | collective-permute-start | bytes 983048 | tf_op jit(solution)/shard_map/ppermute | solution.py:10
  41.7 9.6 %collective-permute-start.3 = (bf16[2,64,1280]{2,1,0:T(8,128)(2,1)}, bf16[2,64,1280]{2,1,0:T(8,128)(2,1)S(1)}, u32[]{:S(2)}, u32[]{:S(2)}) collective-permute-start(bf16[2,64,1280]{2,1,0:T(8,128)(2,1)} %collective-permute-done.1), channel_id=1, source_target_pairs={{0,32},{16,240},{32,64},{48,16},{64,96},{80,48},{96,128},{112,80},... | collective-permute-start | bytes 983048 | tf_op jit(solution)/shard_map/ppermute | solution.py:45
  46.2 15.8 %collective-permute-start.4 = (bf16[2,64,1280]{2,1,0:T(8,128)(2,1)}, bf16[2,64,1280]{2,1,0:T(8,128)(2,1)S(1)}, u32[]{:S(2)}, u32[]{:S(2)}) collective-permute-start(bf16[2,64,1280]{2,1,0:T(8,128)(2,1)} %collective-permute-done.2), channel_id=1, source_target_pairs={{32,0},{240,16},{64,32},{16,48},{96,64},{48,80},{128,96},{80,112},... | collective-permute-start | bytes 983048 | tf_op jit(solution)/shard_map/ppermute | solution.py:46
  51.2 12.8 %collective-permute-start.6 = (bf16[2,64,1280]{2,1,0:T(8,128)(2,1)S(1)}, bf16[2,64,1280]{2,1,0:T(8,128)(2,1)S(1)}, u32[]{:S(2)}, u32[]{:S(2)}) collective-permute-start(bf16[2,64,1280]{2,1,0:T(8,128)(2,1)S(1)} %collective-permute-done.3), channel_id=1, source_target_pairs={{0,32},{16,240},{32,64},{48,16},{64,96},{80,48},{96,128},{112,80},... | collective-permute-start | bytes 983048 | tf_op jit(solution)/shard_map/ppermute | solution.py:45
  55.8 22.8 %collective-permute-start.10 = (bf16[256,1280]{1,0:T(8,128)(2,1)S(1)}, bf16[256,1280]{1,0:T(8,128)(2,1)S(1)}, u32[]{:S(2)}, u32[]{:S(2)}) collective-permute-start(bf16[256,1280]{1,0:T(8,128)(2,1)S(1)} %pad_maximum_fusion.2), channel_id=1, source_target_pairs={{0,16},{16,0},{1,17},{17,1},{2,18},{18,2},{3,19},{19,3},{4,20},{20... | collective-permute-start | bytes 1966088 | tf_op jit(solution)/shard_map/ppermute | solution.py:10
  62.0 9.3 %collective-permute-start.7 = (bf16[2,64,1280]{2,1,0:T(8,128)(2,1)S(1)}, bf16[2,64,1280]{2,1,0:T(8,128)(2,1)S(1)}, u32[]{:S(2)}, u32[]{:S(2)}) collective-permute-start(bf16[2,64,1280]{2,1,0:T(8,128)(2,1)S(1)} %collective-permute-done.4), channel_id=1, source_target_pairs={{32,0},{240,16},{64,32},{16,48},{96,64},{48,80},{128,96},{80,112},... | collective-permute-start | bytes 983048 | tf_op jit(solution)/shard_map/ppermute | solution.py:46
  64.1 9.3 %collective-permute-start.8 = (bf16[1,64,1280]{2,1,0:T(8,128)(2,1)S(1)}, bf16[1,64,1280]{2,1,0:T(8,128)(2,1)S(1)}, u32[]{:S(2)}, u32[]{:S(2)}) collective-permute-start(bf16[1,64,1280]{2,1,0:T(8,128)(2,1)S(1)} %slice.53), channel_id=1, source_target_pairs={{0,32},{16,240},{32,64},{48,16},{64,96},{80,48},{96,128},{112,80},... | collective-permute-start | bytes 491528 | tf_op jit(solution)/shard_map/ppermute | solution.py:53
  71.3 7.3 %collective-permute-start.9 = (bf16[1,64,1280]{2,1,0:T(8,128)(2,1)S(1)}, bf16[1,64,1280]{2,1,0:T(8,128)(2,1)S(1)}, u32[]{:S(2)}, u32[]{:S(2)}) collective-permute-start(bf16[1,64,1280]{2,1,0:T(8,128)(2,1)S(1)} %slice.54), channel_id=1, source_target_pairs={{32,0},{240,16},{64,32},{16,48},{96,64},{48,80},{128,96},{80,112},... | collective-permute-start | bytes 491528 | tf_op jit(solution)/shard_map/ppermute | solution.py:54
  81.2 7.3 %copy-start = (bf16[512,1280]{1,0:T(8,128)(2,1)S(1)}, bf16[512,1280]{1,0:T(8,128)(2,1)}, u32[]{:S(2)}) copy-start(bf16[512,1280]{1,0:T(8,128)(2,1)} %pad_maximum_fusion) | copy-start | bytes 3932164
  81.2 8.2 %collective-permute-start.11 = (bf16[8,128,256]{2,1,0:T(8,128)(2,1)S(1)}, bf16[8,128,256]{2,1,0:T(8,128)(2,1)}, u32[]{:S(2)}, u32[]{:S(2)}) collective-permute-start(bf16[8,128,256]{2,1,0:T(8,128)(2,1)S(1)} %get-tuple-element.31), channel_id=1, source_target_pairs={{0,16},{16,0},{1,17},{17,1},{2,18},{18,2},{3,19},{19,3},{4,20},{20... | collective-permute-start | bytes 1572872 | tf_op jit(solution)/shard_map/ppermute | solution.py:10
  90.5 36.0 %all-to-all-start.1 = ((bf16[32,64,256]{2,1,0:T(8,128)(2,1)}), bf16[32,64,256]{2,1,0:T(8,128)(2,1)}, u32[]{:S(2)}, u32[]{:S(2)}) async-start(bf16[32,64,256]{2,1,0:T(8,128)(2,1)} %bitcast.67), calls=%async_computation.1 | async-start | bytes 2097152 | tf_op jit(solution)/shard_map/all_to_all | solution.py:24
  100.6 4.0 %collective-permute-start.12 = (bf16[256,1280]{1,0:T(8,128)(2,1)S(1)}, bf16[256,1280]{1,0:T(8,128)(2,1)S(1)}, u32[]{:S(2)}, u32[]{:S(2)}) collective-permute-start(bf16[256,1280]{1,0:T(8,128)(2,1)S(1)} %slice.73), channel_id=1, source_target_pairs={{0,16},{16,0},{1,17},{17,1},{2,18},{18,2},{3,19},{19,3},{4,20},{20... | collective-permute-start | bytes 1966088 | tf_op jit(solution)/shard_map/ppermute | solution.py:10
  104.8 17.8 %collective-permute-start.13 = (bf16[256,640]{1,0:T(8,128)(2,1)S(1)}, bf16[256,640]{1,0:T(8,128)(2,1)S(1)}, u32[]{:S(2)}, u32[]{:S(2)}) collective-permute-start(bf16[256,640]{1,0:T(8,128)(2,1)S(1)} %slice.74), channel_id=1, source_target_pairs={{0,1},{1,0},{2,3},{3,2},{4,5},{5,4},{6,7},{7,6},{8,9},{9,8},{10,11... | collective-permute-start | bytes 983048 | tf_op jit(solution)/shard_map/ppermute | solution.py:10
Sparse Core Ops, SparseCore 0:
  41.5 36.2 all-gather.1

commit v8 on v5

--- a/solution.py
+++ b/solution.py
@@ -37,6 +37,34 @@
     )
 
 
+def ring_gather(block, axis):
+    size = lax.axis_size(axis)
+    me = lax.axis_index(axis)
+    rows = block.shape[0]
+    up = [(i, (i + 1) % size) for i in range(size)]
+    down = [(i, (i - 1) % size) for i in range(size)]
+    panel = jnp.zeros((size * rows,) + block.shape[1:], block.dtype)
+
+    def put(panel, block, owner, first):
+        at = lax.rem(owner + size, size) * rows + first
+        return lax.dynamic_update_slice_in_dim(panel, block, at, 0)
+
+    panel = put(panel, block, me, 0)
+    rising = falling = block
+    for step in range(1, size // 2):
+        rising = lax.ppermute(rising, axis, up)
+        falling = lax.ppermute(falling, axis, down)
+        panel = put(panel, rising, me - step, 0)
+        panel = put(panel, falling, me + step, 0)
+    rising, falling, panel = yield rising, falling, panel
+    middle = rows // 2
+    rising = lax.ppermute(rising[:middle], axis, up)
+    falling = lax.ppermute(falling[middle:], axis, down)
+    rising, falling, panel = yield rising, falling, panel
+    panel = put(panel, rising, me + size // 2, 0)
+    yield put(panel, falling, me + size // 2, middle)
+
+
 def per_device(inputs, out_grad, weight):
     core = lax.axis_index("core")
     near = lax.axis_index("xl")
@@ -51,23 +79,26 @@
     ).reshape(-1, part, columns)
     grads = exchange(grads, ("xl", "xh", "z"))
 
-    acts = lax.all_gather(inputs, "y", axis=0, tiled=False)
+    acts = inputs.reshape(2, 4, part, features)
+    acts = jnp.concatenate([pick(acts, core, 0), pick(acts, 1 - core, 0)], axis=0)
+
+    def quarter(a, b):
+        return pick(acts, 2 * (near ^ a) + (far ^ b), 1).reshape(1, 2, part, features)
+
+    came = {(a, b): to_partner(quarter(a, b), a, b) for a, b in PAIRS}
+    came[0, 0] = quarter(0, 0)
+    rows = [jnp.concatenate([came[0, b], came[1, b]], axis=3) for b in range(2)]
+    acts = in_order(far, rows[0], rows[1], 0).reshape(4 * part, 2 * features)
+    acts, weight = lax.optimization_barrier((acts, weight))
 
     came = {(a, b): to_partner(weight, a, b) for a, b in PAIRS}
     came[0, 0] = weight
     weights = [in_order(far, came[a, 0], came[a, 1], 1) for a in range(2)]
     weights = in_order(near, weights[0], weights[1], 0)
-    grads, weights, acts = lax.optimization_barrier((grads, weights, acts))
-
-    acts = acts.reshape(-1, 2, 4, part, features)
-
-    def quarter(a, b):
-        rows = pick(acts, 2 * (near ^ a) + (far ^ b), 2)
-        rows = jnp.concatenate([pick(rows, core, 1), pick(rows, 1 - core, 1)], axis=1)
-        return rows.reshape(-1, 2 * part, features)
-
-    came = {(a, b): to_partner(quarter(a, b), a, b) for a, b in PAIRS}
-    came[0, 0] = quarter(0, 0)
+    gather = ring_gather(acts, "y")
+    ring = next(gather)
+    grads, weights, *ring = lax.optimization_barrier((grads, weights, *ring))
+    ring = gather.send(ring)
 
     panels = [
         g.reshape(2, 2, depth, 1, part, columns) for g in (grads, swap(grads, "core"))
@@ -78,7 +109,8 @@
         times(panel, weights[i * features : (i + 1) * features], 1, 1).astype(jnp.bfloat16)
         for i in range(2)
     ]
-    *partial, came, panel = lax.optimization_barrier((*partial, came, panel))
+    *partial, panel, ring = lax.optimization_barrier((*partial, panel, ring))
+    acts = gather.send(ring)
     partial = jnp.concatenate(partial, axis=0).reshape(-1, 2 * part, features)
     shares = exchange(partial, ("xl", "y", "xh"))
     shares = shares.reshape(2, -1, 2, 2, part, features).astype(jnp.float32)
@@ -86,8 +118,6 @@
     shares = shares.transpose(2, 0, 1, 3, 4)
     input_grad = in_order(core, shares[:1], shares[1:], 0).reshape(-1, features)
 
-    acts = [jnp.concatenate([came[0, b], came[1, b]], axis=2)[:, None] for b in range(2)]
-    acts = in_order(far, acts[0], acts[1], 1).reshape(-1, 2 * features)
     w_part = times(acts, panel, 0, 0)
 
     def piece(a, b):

time: 140 us -> 129 us (0.921)
  waiting for transfers between devices: 52.7 us -> 25.9 us
  starting transfers between devices: 55.6 us -> 79.2 us
  between operations: 14.4 us -> 1.19 us
  local copies, waits for them, and re-layouts: 6 us -> 11.6 us
    ppermute x0 -> x8, starting transfers between devices: none -> 25.3 us  [the longest x3 14.2 us: ring_gather(): falling = lax.ppermute(falling, axis, down)]
    ppermute x9, waiting for transfers between devices: 43.7 us -> 23.8 us  [to_partner(): lax.ppermute(block, ('xl', 'xh'), [(i, i ^ 2 * a + b) for i in range(4)])]
    all_gather x1 -> x0, waiting for transfers between devices: 8.27 us -> none  [per_device(): acts = lax.all_gather(inputs, 'y', axis=0, tiled=False)]
    dynamic_update_slice x0 -> x9, local copies, waits for them, and re-layouts: none -> 5.9 us  [put(): return lax.dynamic_update_slice_in_dim(panel, block, at, 0)]
    all_to_all x2, starting transfers between devices: 20.8 us -> 18.4 us  [exchange(): return lax.all_to_all(pieces, axes, split_axis=0, concat_axis=0, tiled=True)]
    ppermute x0 -> x8, waiting for transfers between devices: none -> 2.11 us  [the longest x3 2.1 us: ring_gather(): rising = lax.ppermute(rising, axis, up)]
  transfers between devices with their start and end apart: 13 -> 20, of which waited for: 7 -> 4; matrix products, arithmetic and copies ran while one was open for 7% -> 12% of each run, Pallas kernels for 0% -> 0%
where the time goes in v8:
time: 129 us; the launch traced here: 128 us
  starting transfers between devices  79.2 us (61%)
  waiting for transfers between devices  25.9 us (20%)
  local copies, waits for them, and re-layouts  11.6 us (9%)
  other arithmetic  5.37 us (4%)
  matrix products  4.56 us (4%)
    ppermute x9, starting transfers between devices, to_partner(): lax.ppermute(block, ('xl', 'xh'), [(i, i ^ 2 * a + b) for i in range(4)])  27.6 us
    ppermute x9, waiting for transfers between devices, to_partner(): lax.ppermute(block, ('xl', 'xh'), [(i, i ^ 2 * a + b) for i in range(4)])  23.8 us
    all_to_all x2, starting transfers between devices, exchange(): return lax.all_to_all(pieces, axes, split_axis=0, concat_axis=0, tiled=True)  18.4 us
    ppermute x3, starting transfers between devices, ring_gather(): falling = lax.ppermute(falling, axis, down)  14.2 us
    ppermute x1, starting transfers between devices, swap(): return lax.ppermute(block, axis, ((0, 1), (1, 0)))  7.91 us
    dynamic_update_slice x9, local copies, waits for them, and re-layouts, put(): return lax.dynamic_update_slice_in_dim(panel, block, at, 0)  5.9 us
    ppermute x3, starting transfers between devices, ring_gather(): rising = lax.ppermute(rising, axis, up)  5.76 us
    dot_general x3, matrix products, times(): lax.dot_general(left, right, (((left_dim,), (right_dim,)), ((), ())), pre...  4.56 us
  transfers between devices with their start and end apart: 20, of which 4 were waited for; matrix products, arithmetic and copies ran while one was open for 12% of the time, Pallas kernels for 0%

profile of v8, /device:TPU:1, one launch (start us, length us, event | category | flops | bytes accessed | tf_op | source)
XLA Modules:
  0.0 127.9 jit_solution(17676314713205146726)
XLA Ops:
  0.6 2.2 %broadcast_in_dim.11 = bf16[4,8,32,640]{3,2,1,0:T(8,128)(2,1)} broadcast(bf16[4,32,640]{2,1,0:T(8,128)(2,1)} %bitcast.47), dimensions={0,2,3} | broadcast | bytes 1474560 | tf_op jit(solution)/shard_map/broadcast_in_dim | solution.py:77
  2.8 13.7 %all-to-all-start = ((bf16[32,32,640]{2,1,0:T(8,128)(2,1)}), bf16[32,32,640]{2,1,0:T(8,128)(2,1)S(1)}, u32[]{:S(2)}, u32[]{:S(2)}) async-start(bf16[32,32,640]{2,1,0:T(8,128)(2,1)} %bitcast.1), calls=%async_computation | async-start | bytes 2621440 | tf_op jit(solution)/shard_map/all_to_all | solution.py:28
  16.6 4.6 %collective-permute-start.1 = (bf16[1,2,32,256]{3,2,1,0:T(8,128)(2,1)S(1)}, bf16[1,2,32,256]{3,2,1,0:T(8,128)(2,1)S(1)}, u32[]{:S(2)}, u32[]{:S(2)}) collective-permute-start(bf16[1,2,32,256]{3,2,1,0:T(8,128)(2,1)S(1)} %get-tuple-element.46), channel_id=1, source_target_pairs={{0,1},{1,0},{256,257},{257,256},{2,3},{3,2},{258,259},{259,258},{4... | collective-permute-start | bytes 98312 | tf_op jit(solution)/shard_map/ppermute | solution.py:14
  21.3 2.2 %collective-permute-start = (bf16[1,2,32,256]{3,2,1,0:T(8,128)(2,1)S(1)}, bf16[1,2,32,256]{3,2,1,0:T(8,128)(2,1)S(1)}, u32[]{:S(2)}, u32[]{:S(2)}) collective-permute-start(bf16[1,2,32,256]{3,2,1,0:T(8,128)(2,1)S(1)} %get-tuple-element.45), channel_id=1, source_target_pairs={{0,256},{1,257},{256,0},{257,1},{2,258},{3,259},{258,2},{259,3},{4... | collective-permute-start | bytes 98312 | tf_op jit(solution)/shard_map/ppermute | solution.py:14
  23.5 2.5 %collective-permute-start.2 = (bf16[1,2,32,256]{3,2,1,0:T(8,128)(2,1)S(1)}, bf16[1,2,32,256]{3,2,1,0:T(8,128)(2,1)S(1)}, u32[]{:S(2)}, u32[]{:S(2)}) collective-permute-start(bf16[1,2,32,256]{3,2,1,0:T(8,128)(2,1)S(1)} %get-tuple-element.47), channel_id=1, source_target_pairs={{0,257},{1,256},{256,1},{257,0},{2,259},{3,258},{258,3},{259,2},{4... | collective-permute-start | bytes 98312 | tf_op jit(solution)/shard_map/ppermute | solution.py:14
  26.0 0.0 collective-permute-done.1
  26.1 3.9 %collective-permute-done.2 = bf16[1,2,32,256]{3,2,1,0:T(8,128)(2,1)S(1)} collective-permute-done((bf16[1,2,32,256]{3,2,1,0:T(8,128)(2,1)S(1)}, bf16[1,2,32,256]{3,2,1,0:T(8,128)(2,1)S(1)}, u32[]{:S(2)}, u32[]{:S(2)}) %collective-permute-start.2) | collective-permute-done | bytes 32800 | tf_op jit(solution)/shard_map/ppermute | solution.py:14
  30.0 5.1 %collective-permute-start.9 = (bf16[128,512]{1,0:T(8,128)(2,1)S(1)}, bf16[128,512]{1,0:T(8,128)(2,1)S(1)}, u32[]{:S(2)}, u32[]{:S(2)}) collective-permute-start(bf16[128,512]{1,0:T(8,128)(2,1)S(1)} %bitcast.44), channel_id=1, source_target_pairs={{0,14},{2,0},{4,2},{6,4},{8,6},{10,8},{12,10},{14,12},{1,15},{3,1}... | collective-permute-start | bytes 393224 | tf_op jit(solution)/shard_map/ppermute | solution.py:56
  35.1 1.9 %collective-permute-start.6 = (bf16[128,512]{1,0:T(8,128)(2,1)S(1)}, bf16[128,512]{1,0:T(8,128)(2,1)S(1)}, u32[]{:S(2)}, u32[]{:S(2)}) collective-permute-start(bf16[128,512]{1,0:T(8,128)(2,1)S(1)} %bitcast.45), channel_id=1, source_target_pairs={{0,2},{2,4},{4,6},{6,8},{8,10},{10,12},{12,14},{14,0},{1,3},{3,5},... | collective-permute-start | bytes 393224 | tf_op jit(solution)/shard_map/ppermute | solution.py:55
  37.1 1.9 %collective-permute-start.4 = (bf16[256,640]{1,0:T(8,128)(2,1)S(1)}, bf16[256,640]{1,0:T(8,128)(2,1)S(1)}, u32[]{:S(2)}, u32[]{:S(2)}) collective-permute-start(bf16[256,640]{1,0:T(8,128)(2,1)S(1)} %copy-done.1), channel_id=1, source_target_pairs={{0,256},{1,257},{256,0},{257,1},{2,258},{3,259},{258,2},{259,3},{4... | collective-permute-start | bytes 983048 | tf_op jit(solution)/shard_map/ppermute | solution.py:14
  39.0 3.5 %collective-permute-start.5 = (bf16[256,640]{1,0:T(8,128)(2,1)S(1)}, bf16[256,640]{1,0:T(8,128)(2,1)S(1)}, u32[]{:S(2)}, u32[]{:S(2)}) collective-permute-start(bf16[256,640]{1,0:T(8,128)(2,1)S(1)} %copy-done.1), channel_id=1, source_target_pairs={{0,257},{1,256},{256,1},{257,0},{2,259},{3,258},{258,3},{259,2},{4... | collective-permute-start | bytes 983048 | tf_op jit(solution)/shard_map/ppermute | solution.py:14
  42.6 3.5 %collective-permute-start.3 = (bf16[256,640]{1,0:T(8,128)(2,1)S(1)}, bf16[256,640]{1,0:T(8,128)(2,1)S(1)}, u32[]{:S(2)}, u32[]{:S(2)}) collective-permute-start(bf16[256,640]{1,0:T(8,128)(2,1)S(1)} %copy-done.1), channel_id=1, source_target_pairs={{0,1},{1,0},{256,257},{257,256},{2,3},{3,2},{258,259},{259,258},{4... | collective-permute-start | bytes 983048 | tf_op jit(solution)/shard_map/ppermute | solution.py:14
  46.1 1.1 broadcast_in_dim.12
  47.2 0.7 constant_dynamic-update-slice_fusion.10
  47.8 0.0 collective-permute-done.9
  47.8 4.6 %collective-permute-start.10 = (bf16[128,512]{1,0:T(8,128)(2,1)S(1)}, bf16[128,512]{1,0:T(8,128)(2,1)S(1)}, u32[]{:S(2)}, u32[]{:S(2)}) collective-permute-start(bf16[128,512]{1,0:T(8,128)(2,1)S(1)} %collective-permute-done.9), channel_id=1, source_target_pairs={{0,14},{2,0},{4,2},{6,4},{8,6},{10,8},{12,10},{14,12},{1,15},{3,1}... | collective-permute-start | bytes 393224 | tf_op jit(solution)/shard_map/ppermute | solution.py:56
  52.4 0.0 collective-permute-done.6
  52.4 1.9 %collective-permute-start.7 = (bf16[128,512]{1,0:T(8,128)(2,1)S(1)}, bf16[128,512]{1,0:T(8,128)(2,1)S(1)}, u32[]{:S(2)}, u32[]{:S(2)}) collective-permute-start(bf16[128,512]{1,0:T(8,128)(2,1)S(1)} %collective-permute-done.6), channel_id=1, source_target_pairs={{0,2},{2,4},{4,6},{6,8},{8,10},{10,12},{12,14},{14,0},{1,3},{3,5},... | collective-permute-start | bytes 393224 | tf_op jit(solution)/shard_map/ppermute | solution.py:55
  54.3 0.7 constant_dynamic-update-slice_fusion.9
  55.0 0.7 constant_dynamic-update-slice_fusion.8
  55.7 4.6 %collective-permute-start.11 = (bf16[128,512]{1,0:T(8,128)(2,1)S(1)}, bf16[128,512]{1,0:T(8,128)(2,1)S(1)}, u32[]{:S(2)}, u32[]{:S(2)}) collective-permute-start(bf16[128,512]{1,0:T(8,128)(2,1)S(1)} %collective-permute-done.10), channel_id=1, source_target_pairs={{0,14},{2,0},{4,2},{6,4},{8,6},{10,8},{12,10},{14,12},{1,15},{3,1}... | collective-permute-start | bytes 393224 | tf_op jit(solution)/shard_map/ppermute | solution.py:56
  60.2 0.0 collective-permute-done.7
  60.2 1.9 %collective-permute-start.8 = (bf16[128,512]{1,0:T(8,128)(2,1)S(1)}, bf16[128,512]{1,0:T(8,128)(2,1)S(1)}, u32[]{:S(2)}, u32[]{:S(2)}) collective-permute-start(bf16[128,512]{1,0:T(8,128)(2,1)S(1)} %collective-permute-done.7), channel_id=1, source_target_pairs={{0,2},{2,4},{4,6},{6,8},{8,10},{10,12},{12,14},{14,0},{1,3},{3,5},... | collective-permute-start | bytes 393224 | tf_op jit(solution)/shard_map/ppermute | solution.py:55
  62.2 0.7 constant_dynamic-update-slice_fusion.7
  62.8 0.7 constant_dynamic-update-slice_fusion.6
  63.5 0.1 broadcast_select_fusion.5
  63.6 0.0 collective-permute-done.4
  63.6 0.0 collective-permute-done.5
  63.6 0.1 broadcast_select_fusion.3
  63.7 0.2 broadcast_select_fusion.1
  63.9 1.2 pad_maximum_fusion
  65.1 2.1 %collective-permute-done.8 = bf16[128,512]{1,0:T(8,128)(2,1)S(1)} collective-permute-done((bf16[128,512]{1,0:T(8,128)(2,1)S(1)}, bf16[128,512]{1,0:T(8,128)(2,1)S(1)}, u32[]{:S(2)}, u32[]{:S(2)}) %collective-permute-start.8) | collective-permute-done | bytes 131104 | tf_op jit(solution)/shard_map/ppermute | solution.py:55
  67.2 0.7 constant_dynamic-update-slice_fusion.5
  67.8 0.7 constant_dynamic-update-slice_fusion.4
  68.5 0.0 all-to-all-done
  68.5 7.9 %collective-permute-start.12 = (bf16[32,32,640]{2,1,0:T(8,128)(2,1)S(1)}, bf16[32,32,640]{2,1,0:T(8,128)(2,1)S(1)}, u32[]{:S(2)}, u32[]{:S(2)}) collective-permute-start(bf16[32,32,640]{2,1,0:T(8,128)(2,1)S(1)} %all-to-all-done), channel_id=1, source_target_pairs={{0,16},{16,0},{1,17},{17,1},{2,18},{18,2},{3,19},{19,3},{4,20},{20... | collective-permute-start | bytes 3932168 | tf_op jit(solution)/shard_map/ppermute | solution.py:10
  76.4 1.9 %collective-permute-start.14 = (bf16[64,512]{1,0:T(8,128)(2,1)S(1)}, bf16[64,512]{1,0:T(8,128)(2,1)S(1)}, u32[]{:S(2)}, u32[]{:S(2)}) collective-permute-start(bf16[64,512]{1,0:T(8,128)(2,1)S(1)} %slice.45), channel_id=1, source_target_pairs={{0,14},{2,0},{4,2},{6,4},{8,6},{10,8},{12,10},{14,12},{1,15},{3,1}... | collective-permute-start | bytes 196616 | tf_op jit(solution)/shard_map/ppermute | solution.py:62
  78.4 3.4 %collective-permute-start.13 = (bf16[64,512]{1,0:T(8,128)(2,1)S(1)}, bf16[64,512]{1,0:T(8,128)(2,1)S(1)}, u32[]{:S(2)}, u32[]{:S(2)}) collective-permute-start(bf16[64,512]{1,0:T(8,128)(2,1)S(1)} %slice.44), channel_id=1, source_target_pairs={{0,2},{2,4},{4,6},{6,8},{8,10},{10,12},{12,14},{14,0},{1,3},{3,5},... | collective-permute-start | bytes 196616 | tf_op jit(solution)/shard_map/ppermute | solution.py:61
  81.7 0.1 slice_bitcast_fusion.3
  81.9 0.1 slice_bitcast_fusion.1
  82.0 0.3 maximum_maximum_fusion
  82.4 0.2 copy.21
  82.6 1.1 copy-done
  83.7 0.9 convolution_convert_fusion
  84.5 0.9 convolution_convert_fusion.1
  85.4 0.0 collective-permute-done.14
  85.5 1.0 pad_maximum_fusion.1
  86.5 4.7 %all-to-all-start.1 = ((bf16[32,64,256]{2,1,0:T(8,128)(2,1)}), bf16[32,64,256]{2,1,0:T(8,128)(2,1)}, u32[]{:S(2)}, u32[]{:S(2)}) async-start(bf16[32,64,256]{2,1,0:T(8,128)(2,1)} %bitcast.41), calls=%async_computation.1 | async-start | bytes 2097152 | tf_op jit(solution)/shard_map/all_to_all | solution.py:28
  91.2 0.6 constant_dynamic-update-slice_fusion.3
  91.8 0.6 constant_dynamic-update-slice_fusion.2
  92.5 2.8 %fusion.10 = f32[512,1280]{1,0:T(8,128)S(1)} fusion(bf16[1024,512]{1,0:T(8,128)(2,1)} %constant_dynamic-update-slice_fusion.2, bf16[1024,1280]{1,0:T(8,128)(2,1)S(1)} %bitcast.39), kind=kOutput, calls=%fused_computation.59 | convolution fusion | flops 1342177280 | bytes 6291456 | tf_op jit(solution)/shard_map/dot_general | solution.py:32
  95.3 0.1 slice.55
  95.3 0.1 slice.54
  95.5 4.5 %collective-permute-start.16 = (bf16[256,640]{1,0:T(8,128)(2,1)S(1)}, bf16[256,640]{1,0:T(8,128)(2,1)S(1)}, u32[]{:S(2)}, u32[]{:S(2)}) collective-permute-start(bf16[256,640]{1,0:T(8,128)(2,1)S(1)} %dynamic-slice_convert_fusion.1), channel_id=1, source_target_pairs={{0,1},{1,0},{256,257},{257,256},{2,3},{3,2},{258,259},{259,258},{4... | collective-permute-start | bytes 983048 | tf_op jit(solution)/shard_map/ppermute | solution.py:14
  100.0 0.1 dynamic-slice_convert_fusion.2
  100.0 2.3 %collective-permute-start.15 = (bf16[256,640]{1,0:T(8,128)(2,1)S(1)}, bf16[256,640]{1,0:T(8,128)(2,1)S(1)}, u32[]{:S(2)}, u32[]{:S(2)}) collective-permute-start(bf16[256,640]{1,0:T(8,128)(2,1)S(1)} %get-tuple-element.34), channel_id=1, source_target_pairs={{0,256},{1,257},{256,0},{257,1},{2,258},{3,259},{258,2},{259,3},{4... | collective-permute-start | bytes 983048 | tf_op jit(solution)/shard_map/ppermute | solution.py:14
  102.3 2.5 %collective-permute-start.17 = (bf16[256,640]{1,0:T(8,128)(2,1)S(1)}, bf16[256,640]{1,0:T(8,128)(2,1)S(1)}, u32[]{:S(2)}, u32[]{:S(2)}) collective-permute-start(bf16[256,640]{1,0:T(8,128)(2,1)S(1)} %get-tuple-element.35), channel_id=1, source_target_pairs={{0,257},{1,256},{256,1},{257,0},{2,259},{3,258},{258,3},{259,2},{4... | collective-permute-start | bytes 983048 | tf_op jit(solution)/shard_map/ppermute | solution.py:14
  104.9 10.9 %collective-permute-done.16 = bf16[256,640]{1,0:T(8,128)(2,1)S(1)} collective-permute-done((bf16[256,640]{1,0:T(8,128)(2,1)S(1)}, bf16[256,640]{1,0:T(8,128)(2,1)S(1)}, u32[]{:S(2)}, u32[]{:S(2)}) %collective-permute-start.16) | collective-permute-done | bytes 327712 | tf_op jit(solution)/shard_map/ppermute | solution.py:14
  115.8 9.0 %collective-permute-done.15 = bf16[256,640]{1,0:T(8,128)(2,1)S(1)} collective-permute-done((bf16[256,640]{1,0:T(8,128)(2,1)S(1)}, bf16[256,640]{1,0:T(8,128)(2,1)S(1)}, u32[]{:S(2)}, u32[]{:S(2)}) %collective-permute-start.15) | collective-permute-done | bytes 327712 | tf_op jit(solution)/shard_map/ppermute | solution.py:14
  124.8 0.0 collective-permute-done.17
  124.8 1.0 convert_add_fusion
  125.7 0.0 all-to-all-done.1
  125.7 1.4 %reduce_sum.12 = bf16[2,2,2,32,256]{4,3,2,1,0:T(8,128)(2,1)S(1)} reduce(bf16[2,8,2,2,32,256]{5,4,3,2,1,0:T(8,128)(2,1)} %bitcast.16, bf16[]{:T(256)} %constant.62.clone.1), dimensions={1}, to_apply=%region_0.1 | reduce | flops 458752 | bytes 1179650 | tf_op jit(solution)/shard_map/reduce_sum | solution.py:117
  127.2 0.7 copy.22
  (22 shorter events, 0.2 us)
Async XLA Ops:
  0.6 15.9 %copy-start.2 = (bf16[256,256]{1,0:T(8,128)(2,1)S(1)}, bf16[256,256]{1,0:T(8,128)(2,1)}, u32[]{:S(2)}) copy-start(bf16[256,256]{1,0:T(8,128)(2,1)} %param.3) | copy-start | bytes 393220
  0.6 36.5 %copy-start.1 = (bf16[256,640]{1,0:T(8,128)(2,1)S(1)}, bf16[256,640]{1,0:T(8,128)(2,1)}, u32[]{:S(2)}) copy-start(bf16[256,640]{1,0:T(8,128)(2,1)} %param.5) | copy-start | bytes 983044
  2.8 65.7 %all-to-all-start = ((bf16[32,32,640]{2,1,0:T(8,128)(2,1)}), bf16[32,32,640]{2,1,0:T(8,128)(2,1)S(1)}, u32[]{:S(2)}, u32[]{:S(2)}) async-start(bf16[32,32,640]{2,1,0:T(8,128)(2,1)} %bitcast.1), calls=%async_computation | async-start | bytes 2621440 | tf_op jit(solution)/shard_map/all_to_all | solution.py:28
  16.6 9.4 %collective-permute-start.1 = (bf16[1,2,32,256]{3,2,1,0:T(8,128)(2,1)S(1)}, bf16[1,2,32,256]{3,2,1,0:T(8,128)(2,1)S(1)}, u32[]{:S(2)}, u32[]{:S(2)}) collective-permute-start(bf16[1,2,32,256]{3,2,1,0:T(8,128)(2,1)S(1)} %get-tuple-element.46), channel_id=1, source_target_pairs={{0,1},{1,0},{256,257},{257,256},{2,3},{3,2},{258,259},{259,258},{4... | collective-permute-start | bytes 98312 | tf_op jit(solution)/shard_map/ppermute | solution.py:14
  21.3 8.7 %collective-permute-start = (bf16[1,2,32,256]{3,2,1,0:T(8,128)(2,1)S(1)}, bf16[1,2,32,256]{3,2,1,0:T(8,128)(2,1)S(1)}, u32[]{:S(2)}, u32[]{:S(2)}) collective-permute-start(bf16[1,2,32,256]{3,2,1,0:T(8,128)(2,1)S(1)} %get-tuple-element.45), channel_id=1, source_target_pairs={{0,256},{1,257},{256,0},{257,1},{2,258},{3,259},{258,2},{259,3},{4... | collective-permute-start | bytes 98312 | tf_op jit(solution)/shard_map/ppermute | solution.py:14
  23.5 6.4 %collective-permute-start.2 = (bf16[1,2,32,256]{3,2,1,0:T(8,128)(2,1)S(1)}, bf16[1,2,32,256]{3,2,1,0:T(8,128)(2,1)S(1)}, u32[]{:S(2)}, u32[]{:S(2)}) collective-permute-start(bf16[1,2,32,256]{3,2,1,0:T(8,128)(2,1)S(1)} %get-tuple-element.47), channel_id=1, source_target_pairs={{0,257},{1,256},{256,1},{257,0},{2,259},{3,258},{258,3},{259,2},{4... | collective-permute-start | bytes 98312 | tf_op jit(solution)/shard_map/ppermute | solution.py:14
  30.0 17.8 %collective-permute-start.9 = (bf16[128,512]{1,0:T(8,128)(2,1)S(1)}, bf16[128,512]{1,0:T(8,128)(2,1)S(1)}, u32[]{:S(2)}, u32[]{:S(2)}) collective-permute-start(bf16[128,512]{1,0:T(8,128)(2,1)S(1)} %bitcast.44), channel_id=1, source_target_pairs={{0,14},{2,0},{4,2},{6,4},{8,6},{10,8},{12,10},{14,12},{1,15},{3,1}... | collective-permute-start | bytes 393224 | tf_op jit(solution)/shard_map/ppermute | solution.py:56
  35.1 17.3 %collective-permute-start.6 = (bf16[128,512]{1,0:T(8,128)(2,1)S(1)}, bf16[128,512]{1,0:T(8,128)(2,1)S(1)}, u32[]{:S(2)}, u32[]{:S(2)}) collective-permute-start(bf16[128,512]{1,0:T(8,128)(2,1)S(1)} %bitcast.45), channel_id=1, source_target_pairs={{0,2},{2,4},{4,6},{6,8},{8,10},{10,12},{12,14},{14,0},{1,3},{3,5},... | collective-permute-start | bytes 393224 | tf_op jit(solution)/shard_map/ppermute | solution.py:55
  37.1 26.5 %collective-permute-start.4 = (bf16[256,640]{1,0:T(8,128)(2,1)S(1)}, bf16[256,640]{1,0:T(8,128)(2,1)S(1)}, u32[]{:S(2)}, u32[]{:S(2)}) collective-permute-start(bf16[256,640]{1,0:T(8,128)(2,1)S(1)} %copy-done.1), channel_id=1, source_target_pairs={{0,256},{1,257},{256,0},{257,1},{2,258},{3,259},{258,2},{259,3},{4... | collective-permute-start | bytes 983048 | tf_op jit(solution)/shard_map/ppermute | solution.py:14
  39.0 24.6 %collective-permute-start.5 = (bf16[256,640]{1,0:T(8,128)(2,1)S(1)}, bf16[256,640]{1,0:T(8,128)(2,1)S(1)}, u32[]{:S(2)}, u32[]{:S(2)}) collective-permute-start(bf16[256,640]{1,0:T(8,128)(2,1)S(1)} %copy-done.1), channel_id=1, source_target_pairs={{0,257},{1,256},{256,1},{257,0},{2,259},{3,258},{258,3},{259,2},{4... | collective-permute-start | bytes 983048 | tf_op jit(solution)/shard_map/ppermute | solution.py:14
  42.6 21.0 %collective-permute-start.3 = (bf16[256,640]{1,0:T(8,128)(2,1)S(1)}, bf16[256,640]{1,0:T(8,128)(2,1)S(1)}, u32[]{:S(2)}, u32[]{:S(2)}) collective-permute-start(bf16[256,640]{1,0:T(8,128)(2,1)S(1)} %copy-done.1), channel_id=1, source_target_pairs={{0,1},{1,0},{256,257},{257,256},{2,3},{3,2},{258,259},{259,258},{4... | collective-permute-start | bytes 983048 | tf_op jit(solution)/shard_map/ppermute | solution.py:14
  47.8 7.8 %collective-permute-start.10 = (bf16[128,512]{1,0:T(8,128)(2,1)S(1)}, bf16[128,512]{1,0:T(8,128)(2,1)S(1)}, u32[]{:S(2)}, u32[]{:S(2)}) collective-permute-start(bf16[128,512]{1,0:T(8,128)(2,1)S(1)} %collective-permute-done.9), channel_id=1, source_target_pairs={{0,14},{2,0},{4,2},{6,4},{8,6},{10,8},{12,10},{14,12},{1,15},{3,1}... | collective-permute-start | bytes 393224 | tf_op jit(solution)/shard_map/ppermute | solution.py:56
  52.4 7.8 %collective-permute-start.7 = (bf16[128,512]{1,0:T(8,128)(2,1)S(1)}, bf16[128,512]{1,0:T(8,128)(2,1)S(1)}, u32[]{:S(2)}, u32[]{:S(2)}) collective-permute-start(bf16[128,512]{1,0:T(8,128)(2,1)S(1)} %collective-permute-done.6), channel_id=1, source_target_pairs={{0,2},{2,4},{4,6},{6,8},{8,10},{10,12},{12,14},{14,0},{1,3},{3,5},... | collective-permute-start | bytes 393224 | tf_op jit(solution)/shard_map/ppermute | solution.py:55
  55.7 12.2 %collective-permute-start.11 = (bf16[128,512]{1,0:T(8,128)(2,1)S(1)}, bf16[128,512]{1,0:T(8,128)(2,1)S(1)}, u32[]{:S(2)}, u32[]{:S(2)}) collective-permute-start(bf16[128,512]{1,0:T(8,128)(2,1)S(1)} %collective-permute-done.10), channel_id=1, source_target_pairs={{0,14},{2,0},{4,2},{6,4},{8,6},{10,8},{12,10},{14,12},{1,15},{3,1}... | collective-permute-start | bytes 393224 | tf_op jit(solution)/shard_map/ppermute | solution.py:56
  60.2 6.9 %collective-permute-start.8 = (bf16[128,512]{1,0:T(8,128)(2,1)S(1)}, bf16[128,512]{1,0:T(8,128)(2,1)S(1)}, u32[]{:S(2)}, u32[]{:S(2)}) collective-permute-start(bf16[128,512]{1,0:T(8,128)(2,1)S(1)} %collective-permute-done.7), channel_id=1, source_target_pairs={{0,2},{2,4},{4,6},{6,8},{8,10},{10,12},{12,14},{14,0},{1,3},{3,5},... | collective-permute-start | bytes 393224 | tf_op jit(solution)/shard_map/ppermute | solution.py:55
  68.5 13.4 %collective-permute-start.12 = (bf16[32,32,640]{2,1,0:T(8,128)(2,1)S(1)}, bf16[32,32,640]{2,1,0:T(8,128)(2,1)S(1)}, u32[]{:S(2)}, u32[]{:S(2)}) collective-permute-start(bf16[32,32,640]{2,1,0:T(8,128)(2,1)S(1)} %all-to-all-done), channel_id=1, source_target_pairs={{0,16},{16,0},{1,17},{17,1},{2,18},{18,2},{3,19},{19,3},{4,20},{20... | collective-permute-start | bytes 3932168 | tf_op jit(solution)/shard_map/ppermute | solution.py:10
  76.4 9.0 %collective-permute-start.14 = (bf16[64,512]{1,0:T(8,128)(2,1)S(1)}, bf16[64,512]{1,0:T(8,128)(2,1)S(1)}, u32[]{:S(2)}, u32[]{:S(2)}) collective-permute-start(bf16[64,512]{1,0:T(8,128)(2,1)S(1)} %slice.45), channel_id=1, source_target_pairs={{0,14},{2,0},{4,2},{6,4},{8,6},{10,8},{12,10},{14,12},{1,15},{3,1}... | collective-permute-start | bytes 196616 | tf_op jit(solution)/shard_map/ppermute | solution.py:62
  78.4 7.1 %collective-permute-start.13 = (bf16[64,512]{1,0:T(8,128)(2,1)S(1)}, bf16[64,512]{1,0:T(8,128)(2,1)S(1)}, u32[]{:S(2)}, u32[]{:S(2)}) collective-permute-start(bf16[64,512]{1,0:T(8,128)(2,1)S(1)} %slice.44), channel_id=1, source_target_pairs={{0,2},{2,4},{4,6},{6,8},{8,10},{10,12},{12,14},{14,0},{1,3},{3,5},... | collective-permute-start | bytes 196616 | tf_op jit(solution)/shard_map/ppermute | solution.py:61
  82.3 1.3 %copy-start = (bf16[512,1280]{1,0:T(8,128)(2,1)S(1)}, bf16[512,1280]{1,0:T(8,128)(2,1)}, u32[]{:S(2)}) copy-start(bf16[512,1280]{1,0:T(8,128)(2,1)} %pad_maximum_fusion) | copy-start | bytes 3932164
  86.5 39.2 %all-to-all-start.1 = ((bf16[32,64,256]{2,1,0:T(8,128)(2,1)}), bf16[32,64,256]{2,1,0:T(8,128)(2,1)}, u32[]{:S(2)}, u32[]{:S(2)}) async-start(bf16[32,64,256]{2,1,0:T(8,128)(2,1)} %bitcast.41), calls=%async_computation.1 | async-start | bytes 2097152 | tf_op jit(solution)/shard_map/all_to_all | solution.py:28
  95.5 20.3 %collective-permute-start.16 = (bf16[256,640]{1,0:T(8,128)(2,1)S(1)}, bf16[256,640]{1,0:T(8,128)(2,1)S(1)}, u32[]{:S(2)}, u32[]{:S(2)}) collective-permute-start(bf16[256,640]{1,0:T(8,128)(2,1)S(1)} %dynamic-slice_convert_fusion.1), channel_id=1, source_target_pairs={{0,1},{1,0},{256,257},{257,256},{2,3},{3,2},{258,259},{259,258},{4... | collective-permute-start | bytes 983048 | tf_op jit(solution)/shard_map/ppermute | solution.py:14
  100.0 24.7 %collective-permute-start.15 = (bf16[256,640]{1,0:T(8,128)(2,1)S(1)}, bf16[256,640]{1,0:T(8,128)(2,1)S(1)}, u32[]{:S(2)}, u32[]{:S(2)}) collective-permute-start(bf16[256,640]{1,0:T(8,128)(2,1)S(1)} %get-tuple-element.34), channel_id=1, source_target_pairs={{0,256},{1,257},{256,0},{257,1},{2,258},{3,259},{258,2},{259,3},{4... | collective-permute-start | bytes 983048 | tf_op jit(solution)/shard_map/ppermute | solution.py:14
  102.3 22.4 %collective-permute-start.17 = (bf16[256,640]{1,0:T(8,128)(2,1)S(1)}, bf16[256,640]{1,0:T(8,128)(2,1)S(1)}, u32[]{:S(2)}, u32[]{:S(2)}) collective-permute-start(bf16[256,640]{1,0:T(8,128)(2,1)S(1)} %get-tuple-element.35), channel_id=1, source_target_pairs={{0,257},{1,256},{256,1},{257,0},{2,259},{3,258},{258,3},{259,2},{4... | collective-permute-start | bytes 983048 | tf_op jit(solution)/shard_map/ppermute | solution.py:14

commit v9 on v8

--- a/solution.py
+++ b/solution.py
@@ -74,11 +74,6 @@
     features = inputs.shape[1]
     part = tokens // 4
 
-    grads = jnp.broadcast_to(
-        out_grad.reshape(4, 1, part, columns), (4, depth, part, columns)
-    ).reshape(-1, part, columns)
-    grads = exchange(grads, ("xl", "xh", "z"))
-
     acts = inputs.reshape(2, 4, part, features)
     acts = jnp.concatenate([pick(acts, core, 0), pick(acts, 1 - core, 0)], axis=0)
 
@@ -89,7 +84,12 @@
     came[0, 0] = quarter(0, 0)
     rows = [jnp.concatenate([came[0, b], came[1, b]], axis=3) for b in range(2)]
     acts = in_order(far, rows[0], rows[1], 0).reshape(4 * part, 2 * features)
-    acts, weight = lax.optimization_barrier((acts, weight))
+    acts, out_grad, weight = lax.optimization_barrier((acts, out_grad, weight))
+
+    grads = jnp.broadcast_to(
+        out_grad.reshape(4, 1, part, columns), (4, depth, part, columns)
+    ).reshape(-1, part, columns)
+    grads = exchange(grads, ("xl", "xh", "z"))
 
     came = {(a, b): to_partner(weight, a, b) for a, b in PAIRS}
     came[0, 0] = weight

time: 129 us -> 129 us (level)
    ppermute x9, starting transfers between devices: 27.6 us -> 29 us  [to_partner(): lax.ppermute(block, ('xl', 'xh'), [(i, i ^ 2 * a + b) for i in range(4)])]
    all_to_all x2, starting transfers between devices: 18.4 us -> 17.1 us  [exchange(): return lax.all_to_all(pieces, axes, split_axis=0, concat_axis=0, tiled=True)]
  transfers between devices with their start and end apart: 20 -> 20, of which waited for: 4 -> 5; matrix products, arithmetic and copies ran while one was open for 12% -> 12% of each run, Pallas kernels for 0% -> 0%
where the time goes in v9:
time: 129 us; the launch traced here: 128 us
  starting transfers between devices  79 us (61%)
  waiting for transfers between devices  25.9 us (20%)
  local copies, waits for them, and re-layouts  12.4 us (10%)
  other arithmetic  5.34 us (4%)
  matrix products  4.56 us (4%)
    ppermute x9, starting transfers between devices, to_partner(): lax.ppermute(block, ('xl', 'xh'), [(i, i ^ 2 * a + b) for i in range(4)])  29 us
    ppermute x9, waiting for transfers between devices, to_partner(): lax.ppermute(block, ('xl', 'xh'), [(i, i ^ 2 * a + b) for i in range(4)])  24.2 us
    all_to_all x2, starting transfers between devices, exchange(): return lax.all_to_all(pieces, axes, split_axis=0, concat_axis=0, tiled=True)  17.1 us
    ppermute x3, starting transfers between devices, ring_gather(): falling = lax.ppermute(falling, axis, down)  14.2 us
    ppermute x1, starting transfers between devices, swap(): return lax.ppermute(block, axis, ((0, 1), (1, 0)))  7.62 us
    dynamic_update_slice x9, local copies, waits for them, and re-layouts, put(): return lax.dynamic_update_slice_in_dim(panel, block, at, 0)  5.84 us
    ppermute x3, starting transfers between devices, ring_gather(): rising = lax.ppermute(rising, axis, up)  5.76 us
    dot_general x3, matrix products, times(): lax.dot_general(left, right, (((left_dim,), (right_dim,)), ((), ())), pre...  4.56 us
  transfers between devices with their start and end apart: 20, of which 5 were waited for; matrix products, arithmetic and copies ran while one was open for 12% of the time, Pallas kernels for 0%

profile of v9, /device:TPU:1, one launch (start us, length us, event | category | flops | bytes accessed | tf_op | source)
XLA Modules:
  0.0 128.3 jit_solution(9733746686608204697)
XLA Ops:
  0.7 0.9 constant_dynamic-slice_fusion
  1.5 0.0 copy-start.1
  1.6 5.6 %collective-permute-start.1 = (bf16[1,2,32,256]{3,2,1,0:T(8,128)(2,1)S(1)}, bf16[1,2,32,256]{3,2,1,0:T(8,128)(2,1)S(1)}, u32[]{:S(2)}, u32[]{:S(2)}) collective-permute-start(bf16[1,2,32,256]{3,2,1,0:T(8,128)(2,1)S(1)} %get-tuple-element.48), channel_id=1, source_target_pairs={{0,1},{1,0},{256,257},{257,256},{2,3},{3,2},{258,259},{259,258},{4... | collective-permute-start | bytes 98312 | tf_op jit(solution)/shard_map/ppermute | solution.py:14
  7.2 2.2 %collective-permute-start = (bf16[1,2,32,256]{3,2,1,0:T(8,128)(2,1)S(1)}, bf16[1,2,32,256]{3,2,1,0:T(8,128)(2,1)S(1)}, u32[]{:S(2)}, u32[]{:S(2)}) collective-permute-start(bf16[1,2,32,256]{3,2,1,0:T(8,128)(2,1)S(1)} %get-tuple-element.47), channel_id=1, source_target_pairs={{0,256},{1,257},{256,0},{257,1},{2,258},{3,259},{258,2},{259,3},{4... | collective-permute-start | bytes 98312 | tf_op jit(solution)/shard_map/ppermute | solution.py:14
  9.4 2.5 %collective-permute-start.2 = (bf16[1,2,32,256]{3,2,1,0:T(8,128)(2,1)S(1)}, bf16[1,2,32,256]{3,2,1,0:T(8,128)(2,1)S(1)}, u32[]{:S(2)}, u32[]{:S(2)}) collective-permute-start(bf16[1,2,32,256]{3,2,1,0:T(8,128)(2,1)S(1)} %get-tuple-element.49), channel_id=1, source_target_pairs={{0,257},{1,256},{256,1},{257,0},{2,259},{3,258},{258,3},{259,2},{4... | collective-permute-start | bytes 98312 | tf_op jit(solution)/shard_map/ppermute | solution.py:14
  11.9 0.0 collective-permute-done.1
  11.9 3.6 %collective-permute-done.2 = bf16[1,2,32,256]{3,2,1,0:T(8,128)(2,1)S(1)} collective-permute-done((bf16[1,2,32,256]{3,2,1,0:T(8,128)(2,1)S(1)}, bf16[1,2,32,256]{3,2,1,0:T(8,128)(2,1)S(1)}, u32[]{:S(2)}, u32[]{:S(2)}) %collective-permute-start.2) | collective-permute-done | bytes 32800 | tf_op jit(solution)/shard_map/ppermute | solution.py:14
  15.6 0.0 collective-permute-done
  15.6 2.1 %broadcast_in_dim.11 = bf16[4,8,32,640]{3,2,1,0:T(8,128)(2,1)} broadcast(bf16[4,32,640]{2,1,0:T(8,128)(2,1)} %bitcast.47), dimensions={0,2,3} | broadcast | bytes 1474560 | tf_op jit(solution)/shard_map/broadcast_in_dim | solution.py:89
  17.8 10.4 %all-to-all-start = ((bf16[32,32,640]{2,1,0:T(8,128)(2,1)}), bf16[32,32,640]{2,1,0:T(8,128)(2,1)S(1)}, u32[]{:S(2)}, u32[]{:S(2)}) async-start(bf16[32,32,640]{2,1,0:T(8,128)(2,1)} %bitcast.7), calls=%async_computation | async-start | bytes 2621440 | tf_op jit(solution)/shard_map/all_to_all | solution.py:28
  28.2 5.1 %collective-permute-start.9 = (bf16[128,512]{1,0:T(8,128)(2,1)S(1)}, bf16[128,512]{1,0:T(8,128)(2,1)S(1)}, u32[]{:S(2)}, u32[]{:S(2)}) collective-permute-start(bf16[128,512]{1,0:T(8,128)(2,1)S(1)} %bitcast.44), channel_id=1, source_target_pairs={{0,14},{2,0},{4,2},{6,4},{8,6},{10,8},{12,10},{14,12},{1,15},{3,1}... | collective-permute-start | bytes 393224 | tf_op jit(solution)/shard_map/ppermute | solution.py:56
  33.3 1.9 %collective-permute-start.6 = (bf16[128,512]{1,0:T(8,128)(2,1)S(1)}, bf16[128,512]{1,0:T(8,128)(2,1)S(1)}, u32[]{:S(2)}, u32[]{:S(2)}) collective-permute-start(bf16[128,512]{1,0:T(8,128)(2,1)S(1)} %bitcast.45), channel_id=1, source_target_pairs={{0,2},{2,4},{4,6},{6,8},{8,10},{10,12},{12,14},{14,0},{1,3},{3,5},... | collective-permute-start | bytes 393224 | tf_op jit(solution)/shard_map/ppermute | solution.py:55
  35.3 3.1 %collective-permute-start.4 = (bf16[256,640]{1,0:T(8,128)(2,1)S(1)}, bf16[256,640]{1,0:T(8,128)(2,1)S(1)}, u32[]{:S(2)}, u32[]{:S(2)}) collective-permute-start(bf16[256,640]{1,0:T(8,128)(2,1)S(1)} %copy-done.1), channel_id=1, source_target_pairs={{0,256},{1,257},{256,0},{257,1},{2,258},{3,259},{258,2},{259,3},{4... | collective-permute-start | bytes 983048 | tf_op jit(solution)/shard_map/ppermute | solution.py:14
  38.4 3.7 %collective-permute-start.5 = (bf16[256,640]{1,0:T(8,128)(2,1)S(1)}, bf16[256,640]{1,0:T(8,128)(2,1)S(1)}, u32[]{:S(2)}, u32[]{:S(2)}) collective-permute-start(bf16[256,640]{1,0:T(8,128)(2,1)S(1)} %copy-done.1), channel_id=1, source_target_pairs={{0,257},{1,256},{256,1},{257,0},{2,259},{3,258},{258,3},{259,2},{4... | collective-permute-start | bytes 983048 | tf_op jit(solution)/shard_map/ppermute | solution.py:14
  42.1 2.6 %collective-permute-start.3 = (bf16[256,640]{1,0:T(8,128)(2,1)S(1)}, bf16[256,640]{1,0:T(8,128)(2,1)S(1)}, u32[]{:S(2)}, u32[]{:S(2)}) collective-permute-start(bf16[256,640]{1,0:T(8,128)(2,1)S(1)} %copy-done.1), channel_id=1, source_target_pairs={{0,1},{1,0},{256,257},{257,256},{2,3},{3,2},{258,259},{259,258},{4... | collective-permute-start | bytes 983048 | tf_op jit(solution)/shard_map/ppermute | solution.py:14
  44.7 1.1 broadcast_in_dim.12
  45.8 0.7 constant_dynamic-update-slice_fusion.10
  46.4 0.0 collective-permute-done.9
  46.4 4.6 %collective-permute-start.10 = (bf16[128,512]{1,0:T(8,128)(2,1)S(1)}, bf16[128,512]{1,0:T(8,128)(2,1)S(1)}, u32[]{:S(2)}, u32[]{:S(2)}) collective-permute-start(bf16[128,512]{1,0:T(8,128)(2,1)S(1)} %collective-permute-done.9), channel_id=1, source_target_pairs={{0,14},{2,0},{4,2},{6,4},{8,6},{10,8},{12,10},{14,12},{1,15},{3,1}... | collective-permute-start | bytes 393224 | tf_op jit(solution)/shard_map/ppermute | solution.py:56
  51.0 1.9 %collective-permute-start.7 = (bf16[128,512]{1,0:T(8,128)(2,1)S(1)}, bf16[128,512]{1,0:T(8,128)(2,1)S(1)}, u32[]{:S(2)}, u32[]{:S(2)}) collective-permute-start(bf16[128,512]{1,0:T(8,128)(2,1)S(1)} %collective-permute-done.6), channel_id=1, source_target_pairs={{0,2},{2,4},{4,6},{6,8},{8,10},{10,12},{12,14},{14,0},{1,3},{3,5},... | collective-permute-start | bytes 393224 | tf_op jit(solution)/shard_map/ppermute | solution.py:55
  53.0 0.7 constant_dynamic-update-slice_fusion.9
  53.6 0.7 constant_dynamic-update-slice_fusion.8
  54.3 0.0 collective-permute-done.10
  54.3 4.5 %collective-permute-start.11 = (bf16[128,512]{1,0:T(8,128)(2,1)S(1)}, bf16[128,512]{1,0:T(8,128)(2,1)S(1)}, u32[]{:S(2)}, u32[]{:S(2)}) collective-permute-start(bf16[128,512]{1,0:T(8,128)(2,1)S(1)} %collective-permute-done.10), channel_id=1, source_target_pairs={{0,14},{2,0},{4,2},{6,4},{8,6},{10,8},{12,10},{14,12},{1,15},{3,1}... | collective-permute-start | bytes 393224 | tf_op jit(solution)/shard_map/ppermute | solution.py:56
  58.8 0.0 collective-permute-done.7
  58.8 1.9 %collective-permute-start.8 = (bf16[128,512]{1,0:T(8,128)(2,1)S(1)}, bf16[128,512]{1,0:T(8,128)(2,1)S(1)}, u32[]{:S(2)}, u32[]{:S(2)}) collective-permute-start(bf16[128,512]{1,0:T(8,128)(2,1)S(1)} %collective-permute-done.7), channel_id=1, source_target_pairs={{0,2},{2,4},{4,6},{6,8},{8,10},{10,12},{12,14},{14,0},{1,3},{3,5},... | collective-permute-start | bytes 393224 | tf_op jit(solution)/shard_map/ppermute | solution.py:55
  60.8 0.7 constant_dynamic-update-slice_fusion.7
  61.4 0.7 constant_dynamic-update-slice_fusion.6
  62.1 0.7 collective-permute-done.3
  62.8 0.1 broadcast_select_fusion.5
  62.9 0.0 collective-permute-done.4
  62.9 0.0 collective-permute-done.5
  62.9 0.1 broadcast_select_fusion.3
  63.0 0.2 broadcast_select_fusion.1
  63.2 1.1 pad_maximum_fusion
  64.4 1.7 %collective-permute-done.8 = bf16[128,512]{1,0:T(8,128)(2,1)S(1)} collective-permute-done((bf16[128,512]{1,0:T(8,128)(2,1)S(1)}, bf16[128,512]{1,0:T(8,128)(2,1)S(1)}, u32[]{:S(2)}, u32[]{:S(2)}) %collective-permute-start.8) | collective-permute-done | bytes 131104 | tf_op jit(solution)/shard_map/ppermute | solution.py:55
  66.1 0.7 constant_dynamic-update-slice_fusion.5
  66.7 0.7 constant_dynamic-update-slice_fusion.4
  67.4 7.6 %collective-permute-start.12 = (bf16[32,32,640]{2,1,0:T(8,128)(2,1)S(1)}, bf16[32,32,640]{2,1,0:T(8,128)(2,1)S(1)}, u32[]{:S(2)}, u32[]{:S(2)}) collective-permute-start(bf16[32,32,640]{2,1,0:T(8,128)(2,1)S(1)} %all-to-all-done), channel_id=1, source_target_pairs={{0,16},{16,0},{1,17},{17,1},{2,18},{18,2},{3,19},{19,3},{4,20},{20... | collective-permute-start | bytes 3932168 | tf_op jit(solution)/shard_map/ppermute | solution.py:10
  75.0 1.9 %collective-permute-start.14 = (bf16[64,512]{1,0:T(8,128)(2,1)S(1)}, bf16[64,512]{1,0:T(8,128)(2,1)S(1)}, u32[]{:S(2)}, u32[]{:S(2)}) collective-permute-start(bf16[64,512]{1,0:T(8,128)(2,1)S(1)} %slice.45), channel_id=1, source_target_pairs={{0,14},{2,0},{4,2},{6,4},{8,6},{10,8},{12,10},{14,12},{1,15},{3,1}... | collective-permute-start | bytes 196616 | tf_op jit(solution)/shard_map/ppermute | solution.py:62
  77.0 3.4 %collective-permute-start.13 = (bf16[64,512]{1,0:T(8,128)(2,1)S(1)}, bf16[64,512]{1,0:T(8,128)(2,1)S(1)}, u32[]{:S(2)}, u32[]{:S(2)}) collective-permute-start(bf16[64,512]{1,0:T(8,128)(2,1)S(1)} %slice.44), channel_id=1, source_target_pairs={{0,2},{2,4},{4,6},{6,8},{8,10},{10,12},{12,14},{14,0},{1,3},{3,5},... | collective-permute-start | bytes 196616 | tf_op jit(solution)/shard_map/ppermute | solution.py:61
  80.3 0.1 slice_bitcast_fusion.3
  80.5 0.1 slice_bitcast_fusion.1
  80.6 0.3 maximum_maximum_fusion
  81.0 0.2 copy.21
  81.2 1.1 copy-done
  82.3 0.9 convolution_convert_fusion
  83.1 0.9 convolution_convert_fusion.1
  84.1 1.0 pad_maximum_fusion.1
  85.1 6.6 %all-to-all-start.1 = ((bf16[32,64,256]{2,1,0:T(8,128)(2,1)}), bf16[32,64,256]{2,1,0:T(8,128)(2,1)}, u32[]{:S(2)}, u32[]{:S(2)}) async-start(bf16[32,64,256]{2,1,0:T(8,128)(2,1)} %bitcast.41), calls=%async_computation.1 | async-start | bytes 2097152 | tf_op jit(solution)/shard_map/all_to_all | solution.py:28
  91.8 0.6 constant_dynamic-update-slice_fusion.3
  92.4 0.6 constant_dynamic-update-slice_fusion.2
  93.0 2.8 %fusion.10 = f32[512,1280]{1,0:T(8,128)S(1)} fusion(bf16[1024,512]{1,0:T(8,128)(2,1)} %constant_dynamic-update-slice_fusion.2, bf16[1024,1280]{1,0:T(8,128)(2,1)S(1)} %bitcast.39), kind=kOutput, calls=%fused_computation.59 | convolution fusion | flops 1342177280 | bytes 6291456 | tf_op jit(solution)/shard_map/dot_general | solution.py:32
  95.8 0.1 slice.55
  95.9 0.1 slice.54
  96.0 4.6 %collective-permute-start.16 = (bf16[256,640]{1,0:T(8,128)(2,1)S(1)}, bf16[256,640]{1,0:T(8,128)(2,1)S(1)}, u32[]{:S(2)}, u32[]{:S(2)}) collective-permute-start(bf16[256,640]{1,0:T(8,128)(2,1)S(1)} %dynamic-slice_convert_fusion.1), channel_id=1, source_target_pairs={{0,1},{1,0},{256,257},{257,256},{2,3},{3,2},{258,259},{259,258},{4... | collective-permute-start | bytes 983048 | tf_op jit(solution)/shard_map/ppermute | solution.py:14
  100.6 0.1 dynamic-slice_convert_fusion.2
  100.7 2.2 %collective-permute-start.15 = (bf16[256,640]{1,0:T(8,128)(2,1)S(1)}, bf16[256,640]{1,0:T(8,128)(2,1)S(1)}, u32[]{:S(2)}, u32[]{:S(2)}) collective-permute-start(bf16[256,640]{1,0:T(8,128)(2,1)S(1)} %get-tuple-element.36), channel_id=1, source_target_pairs={{0,256},{1,257},{256,0},{257,1},{2,258},{3,259},{258,2},{259,3},{4... | collective-permute-start | bytes 983048 | tf_op jit(solution)/shard_map/ppermute | solution.py:14
  102.9 2.6 %collective-permute-start.17 = (bf16[256,640]{1,0:T(8,128)(2,1)S(1)}, bf16[256,640]{1,0:T(8,128)(2,1)S(1)}, u32[]{:S(2)}, u32[]{:S(2)}) collective-permute-start(bf16[256,640]{1,0:T(8,128)(2,1)S(1)} %get-tuple-element.37), channel_id=1, source_target_pairs={{0,257},{1,256},{256,1},{257,0},{2,259},{3,258},{258,3},{259,2},{4... | collective-permute-start | bytes 983048 | tf_op jit(solution)/shard_map/ppermute | solution.py:14
  105.4 10.7 %collective-permute-done.16 = bf16[256,640]{1,0:T(8,128)(2,1)S(1)} collective-permute-done((bf16[256,640]{1,0:T(8,128)(2,1)S(1)}, bf16[256,640]{1,0:T(8,128)(2,1)S(1)}, u32[]{:S(2)}, u32[]{:S(2)}) %collective-permute-start.16) | collective-permute-done | bytes 327712 | tf_op jit(solution)/shard_map/ppermute | solution.py:14
  116.2 9.0 %collective-permute-done.15 = bf16[256,640]{1,0:T(8,128)(2,1)S(1)} collective-permute-done((bf16[256,640]{1,0:T(8,128)(2,1)S(1)}, bf16[256,640]{1,0:T(8,128)(2,1)S(1)}, u32[]{:S(2)}, u32[]{:S(2)}) %collective-permute-start.15) | collective-permute-done | bytes 327712 | tf_op jit(solution)/shard_map/ppermute | solution.py:14
  125.2 1.0 convert_add_fusion
  126.2 1.4 %reduce_sum.12 = bf16[2,2,2,32,256]{4,3,2,1,0:T(8,128)(2,1)S(1)} reduce(bf16[2,8,2,2,32,256]{5,4,3,2,1,0:T(8,128)(2,1)} %bitcast.16, bf16[]{:T(256)} %constant.62.clone.1), dimensions={1}, to_apply=%region_0.1 | reduce | flops 458752 | bytes 1179650 | tf_op jit(solution)/shard_map/reduce_sum | solution.py:117
  127.6 0.7 copy.22
  (20 shorter events, 0.2 us)
Async XLA Ops:
  1.5 33.7 %copy-start.1 = (bf16[256,640]{1,0:T(8,128)(2,1)S(1)}, bf16[256,640]{1,0:T(8,128)(2,1)}, u32[]{:S(2)}) copy-start(bf16[256,640]{1,0:T(8,128)(2,1)} %param.5) | copy-start | bytes 983044
  1.6 10.3 %collective-permute-start.1 = (bf16[1,2,32,256]{3,2,1,0:T(8,128)(2,1)S(1)}, bf16[1,2,32,256]{3,2,1,0:T(8,128)(2,1)S(1)}, u32[]{:S(2)}, u32[]{:S(2)}) collective-permute-start(bf16[1,2,32,256]{3,2,1,0:T(8,128)(2,1)S(1)} %get-tuple-element.48), channel_id=1, source_target_pairs={{0,1},{1,0},{256,257},{257,256},{2,3},{3,2},{258,259},{259,258},{4... | collective-permute-start | bytes 98312 | tf_op jit(solution)/shard_map/ppermute | solution.py:14
  7.2 8.4 %collective-permute-start = (bf16[1,2,32,256]{3,2,1,0:T(8,128)(2,1)S(1)}, bf16[1,2,32,256]{3,2,1,0:T(8,128)(2,1)S(1)}, u32[]{:S(2)}, u32[]{:S(2)}) collective-permute-start(bf16[1,2,32,256]{3,2,1,0:T(8,128)(2,1)S(1)} %get-tuple-element.47), channel_id=1, source_target_pairs={{0,256},{1,257},{256,0},{257,1},{2,258},{3,259},{258,2},{259,3},{4... | collective-permute-start | bytes 98312 | tf_op jit(solution)/shard_map/ppermute | solution.py:14
  9.4 6.1 %collective-permute-start.2 = (bf16[1,2,32,256]{3,2,1,0:T(8,128)(2,1)S(1)}, bf16[1,2,32,256]{3,2,1,0:T(8,128)(2,1)S(1)}, u32[]{:S(2)}, u32[]{:S(2)}) collective-permute-start(bf16[1,2,32,256]{3,2,1,0:T(8,128)(2,1)S(1)} %get-tuple-element.49), channel_id=1, source_target_pairs={{0,257},{1,256},{256,1},{257,0},{2,259},{3,258},{258,3},{259,2},{4... | collective-permute-start | bytes 98312 | tf_op jit(solution)/shard_map/ppermute | solution.py:14
  17.8 49.6 %all-to-all-start = ((bf16[32,32,640]{2,1,0:T(8,128)(2,1)}), bf16[32,32,640]{2,1,0:T(8,128)(2,1)S(1)}, u32[]{:S(2)}, u32[]{:S(2)}) async-start(bf16[32,32,640]{2,1,0:T(8,128)(2,1)} %bitcast.7), calls=%async_computation | async-start | bytes 2621440 | tf_op jit(solution)/shard_map/all_to_all | solution.py:28
  28.2 18.2 %collective-permute-start.9 = (bf16[128,512]{1,0:T(8,128)(2,1)S(1)}, bf16[128,512]{1,0:T(8,128)(2,1)S(1)}, u32[]{:S(2)}, u32[]{:S(2)}) collective-permute-start(bf16[128,512]{1,0:T(8,128)(2,1)S(1)} %bitcast.44), channel_id=1, source_target_pairs={{0,14},{2,0},{4,2},{6,4},{8,6},{10,8},{12,10},{14,12},{1,15},{3,1}... | collective-permute-start | bytes 393224 | tf_op jit(solution)/shard_map/ppermute | solution.py:56
  33.3 17.7 %collective-permute-start.6 = (bf16[128,512]{1,0:T(8,128)(2,1)S(1)}, bf16[128,512]{1,0:T(8,128)(2,1)S(1)}, u32[]{:S(2)}, u32[]{:S(2)}) collective-permute-start(bf16[128,512]{1,0:T(8,128)(2,1)S(1)} %bitcast.45), channel_id=1, source_target_pairs={{0,2},{2,4},{4,6},{6,8},{8,10},{10,12},{12,14},{14,0},{1,3},{3,5},... | collective-permute-start | bytes 393224 | tf_op jit(solution)/shard_map/ppermute | solution.py:55
  35.3 27.6 %collective-permute-start.4 = (bf16[256,640]{1,0:T(8,128)(2,1)S(1)}, bf16[256,640]{1,0:T(8,128)(2,1)S(1)}, u32[]{:S(2)}, u32[]{:S(2)}) collective-permute-start(bf16[256,640]{1,0:T(8,128)(2,1)S(1)} %copy-done.1), channel_id=1, source_target_pairs={{0,256},{1,257},{256,0},{257,1},{2,258},{3,259},{258,2},{259,3},{4... | collective-permute-start | bytes 983048 | tf_op jit(solution)/shard_map/ppermute | solution.py:14
  38.4 24.5 %collective-permute-start.5 = (bf16[256,640]{1,0:T(8,128)(2,1)S(1)}, bf16[256,640]{1,0:T(8,128)(2,1)S(1)}, u32[]{:S(2)}, u32[]{:S(2)}) collective-permute-start(bf16[256,640]{1,0:T(8,128)(2,1)S(1)} %copy-done.1), channel_id=1, source_target_pairs={{0,257},{1,256},{256,1},{257,0},{2,259},{3,258},{258,3},{259,2},{4... | collective-permute-start | bytes 983048 | tf_op jit(solution)/shard_map/ppermute | solution.py:14
  42.1 20.7 %collective-permute-start.3 = (bf16[256,640]{1,0:T(8,128)(2,1)S(1)}, bf16[256,640]{1,0:T(8,128)(2,1)S(1)}, u32[]{:S(2)}, u32[]{:S(2)}) collective-permute-start(bf16[256,640]{1,0:T(8,128)(2,1)S(1)} %copy-done.1), channel_id=1, source_target_pairs={{0,1},{1,0},{256,257},{257,256},{2,3},{3,2},{258,259},{259,258},{4... | collective-permute-start | bytes 983048 | tf_op jit(solution)/shard_map/ppermute | solution.py:14
  46.4 7.8 %collective-permute-start.10 = (bf16[128,512]{1,0:T(8,128)(2,1)S(1)}, bf16[128,512]{1,0:T(8,128)(2,1)S(1)}, u32[]{:S(2)}, u32[]{:S(2)}) collective-permute-start(bf16[128,512]{1,0:T(8,128)(2,1)S(1)} %collective-permute-done.9), channel_id=1, source_target_pairs={{0,14},{2,0},{4,2},{6,4},{8,6},{10,8},{12,10},{14,12},{1,15},{3,1}... | collective-permute-start | bytes 393224 | tf_op jit(solution)/shard_map/ppermute | solution.py:56
  51.0 7.8 %collective-permute-start.7 = (bf16[128,512]{1,0:T(8,128)(2,1)S(1)}, bf16[128,512]{1,0:T(8,128)(2,1)S(1)}, u32[]{:S(2)}, u32[]{:S(2)}) collective-permute-start(bf16[128,512]{1,0:T(8,128)(2,1)S(1)} %collective-permute-done.6), channel_id=1, source_target_pairs={{0,2},{2,4},{4,6},{6,8},{8,10},{10,12},{12,14},{14,0},{1,3},{3,5},... | collective-permute-start | bytes 393224 | tf_op jit(solution)/shard_map/ppermute | solution.py:55
  54.3 12.4 %collective-permute-start.11 = (bf16[128,512]{1,0:T(8,128)(2,1)S(1)}, bf16[128,512]{1,0:T(8,128)(2,1)S(1)}, u32[]{:S(2)}, u32[]{:S(2)}) collective-permute-start(bf16[128,512]{1,0:T(8,128)(2,1)S(1)} %collective-permute-done.10), channel_id=1, source_target_pairs={{0,14},{2,0},{4,2},{6,4},{8,6},{10,8},{12,10},{14,12},{1,15},{3,1}... | collective-permute-start | bytes 393224 | tf_op jit(solution)/shard_map/ppermute | solution.py:56
  58.8 7.2 %collective-permute-start.8 = (bf16[128,512]{1,0:T(8,128)(2,1)S(1)}, bf16[128,512]{1,0:T(8,128)(2,1)S(1)}, u32[]{:S(2)}, u32[]{:S(2)}) collective-permute-start(bf16[128,512]{1,0:T(8,128)(2,1)S(1)} %collective-permute-done.7), channel_id=1, source_target_pairs={{0,2},{2,4},{4,6},{6,8},{8,10},{10,12},{12,14},{14,0},{1,3},{3,5},... | collective-permute-start | bytes 393224 | tf_op jit(solution)/shard_map/ppermute | solution.py:55
  67.4 13.1 %collective-permute-start.12 = (bf16[32,32,640]{2,1,0:T(8,128)(2,1)S(1)}, bf16[32,32,640]{2,1,0:T(8,128)(2,1)S(1)}, u32[]{:S(2)}, u32[]{:S(2)}) collective-permute-start(bf16[32,32,640]{2,1,0:T(8,128)(2,1)S(1)} %all-to-all-done), channel_id=1, source_target_pairs={{0,16},{16,0},{1,17},{17,1},{2,18},{18,2},{3,19},{19,3},{4,20},{20... | collective-permute-start | bytes 3932168 | tf_op jit(solution)/shard_map/ppermute | solution.py:10
  75.0 9.0 %collective-permute-start.14 = (bf16[64,512]{1,0:T(8,128)(2,1)S(1)}, bf16[64,512]{1,0:T(8,128)(2,1)S(1)}, u32[]{:S(2)}, u32[]{:S(2)}) collective-permute-start(bf16[64,512]{1,0:T(8,128)(2,1)S(1)} %slice.45), channel_id=1, source_target_pairs={{0,14},{2,0},{4,2},{6,4},{8,6},{10,8},{12,10},{14,12},{1,15},{3,1}... | collective-permute-start | bytes 196616 | tf_op jit(solution)/shard_map/ppermute | solution.py:62
  77.0 7.1 %collective-permute-start.13 = (bf16[64,512]{1,0:T(8,128)(2,1)S(1)}, bf16[64,512]{1,0:T(8,128)(2,1)S(1)}, u32[]{:S(2)}, u32[]{:S(2)}) collective-permute-start(bf16[64,512]{1,0:T(8,128)(2,1)S(1)} %slice.44), channel_id=1, source_target_pairs={{0,2},{2,4},{4,6},{6,8},{8,10},{10,12},{12,14},{14,0},{1,3},{3,5},... | collective-permute-start | bytes 196616 | tf_op jit(solution)/shard_map/ppermute | solution.py:61
  80.9 1.3 %copy-start = (bf16[512,1280]{1,0:T(8,128)(2,1)S(1)}, bf16[512,1280]{1,0:T(8,128)(2,1)}, u32[]{:S(2)}) copy-start(bf16[512,1280]{1,0:T(8,128)(2,1)} %pad_maximum_fusion) | copy-start | bytes 3932164
  85.1 41.1 %all-to-all-start.1 = ((bf16[32,64,256]{2,1,0:T(8,128)(2,1)}), bf16[32,64,256]{2,1,0:T(8,128)(2,1)}, u32[]{:S(2)}, u32[]{:S(2)}) async-start(bf16[32,64,256]{2,1,0:T(8,128)(2,1)} %bitcast.41), calls=%async_computation.1 | async-start | bytes 2097152 | tf_op jit(solution)/shard_map/all_to_all | solution.py:28
  96.0 20.1 %collective-permute-start.16 = (bf16[256,640]{1,0:T(8,128)(2,1)S(1)}, bf16[256,640]{1,0:T(8,128)(2,1)S(1)}, u32[]{:S(2)}, u32[]{:S(2)}) collective-permute-start(bf16[256,640]{1,0:T(8,128)(2,1)S(1)} %dynamic-slice_convert_fusion.1), channel_id=1, source_target_pairs={{0,1},{1,0},{256,257},{257,256},{2,3},{3,2},{258,259},{259,258},{4... | collective-permute-start | bytes 983048 | tf_op jit(solution)/shard_map/ppermute | solution.py:14
  100.7 24.5 %collective-permute-start.15 = (bf16[256,640]{1,0:T(8,128)(2,1)S(1)}, bf16[256,640]{1,0:T(8,128)(2,1)S(1)}, u32[]{:S(2)}, u32[]{:S(2)}) collective-permute-start(bf16[256,640]{1,0:T(8,128)(2,1)S(1)} %get-tuple-element.36), channel_id=1, source_target_pairs={{0,256},{1,257},{256,0},{257,1},{2,258},{3,259},{258,2},{259,3},{4... | collective-permute-start | bytes 983048 | tf_op jit(solution)/shard_map/ppermute | solution.py:14
  102.9 22.3 %collective-permute-start.17 = (bf16[256,640]{1,0:T(8,128)(2,1)S(1)}, bf16[256,640]{1,0:T(8,128)(2,1)S(1)}, u32[]{:S(2)}, u32[]{:S(2)}) collective-permute-start(bf16[256,640]{1,0:T(8,128)(2,1)S(1)} %get-tuple-element.37), channel_id=1, source_target_pairs={{0,257},{1,256},{256,1},{257,0},{2,259},{3,258},{258,3},{259,2},{4... | collective-permute-start | bytes 983048 | tf_op jit(solution)/shard_map/ppermute | solution.py:14

commit v10 on v9

--- a/solution.py
+++ b/solution.py
@@ -43,26 +43,21 @@
     rows = block.shape[0]
     up = [(i, (i + 1) % size) for i in range(size)]
     down = [(i, (i - 1) % size) for i in range(size)]
-    panel = jnp.zeros((size * rows,) + block.shape[1:], block.dtype)
-
-    def put(panel, block, owner, first):
-        at = lax.rem(owner + size, size) * rows + first
-        return lax.dynamic_update_slice_in_dim(panel, block, at, 0)
-
-    panel = put(panel, block, me, 0)
-    rising = falling = block
-    for step in range(1, size // 2):
-        rising = lax.ppermute(rising, axis, up)
-        falling = lax.ppermute(falling, axis, down)
-        panel = put(panel, rising, me - step, 0)
-        panel = put(panel, falling, me + step, 0)
-    rising, falling, panel = yield rising, falling, panel
+    rising, falling = [block], [block]
+    for _ in range(1, size // 2):
+        rising.append(lax.ppermute(rising[-1], axis, up))
+        falling.append(lax.ppermute(falling[-1], axis, down))
+    rising, falling = yield rising, falling
     middle = rows // 2
-    rising = lax.ppermute(rising[:middle], axis, up)
-    falling = lax.ppermute(falling[middle:], axis, down)
-    rising, falling, panel = yield rising, falling, panel
-    panel = put(panel, rising, me + size // 2, 0)
-    yield put(panel, falling, me + size // 2, middle)
+    far = (
+        lax.ppermute(rising[-1][:middle], axis, up),
+        lax.ppermute(falling[-1][middle:], axis, down),
+    )
+    rising, falling, far = yield rising, falling, far
+    blocks = falling[:] + list(far) + rising[:0:-1]
+    panel = jnp.concatenate(blocks + blocks[:-1], axis=0)
+    first = lax.rem(size - me, size) * rows
+    yield lax.dynamic_slice_in_dim(panel, first, size * rows, 0)
 
 
 def per_device(inputs, out_grad, weight):
@@ -97,7 +92,7 @@
     weights = in_order(near, weights[0], weights[1], 0)
     gather = ring_gather(acts, "y")
     ring = next(gather)
-    grads, weights, *ring = lax.optimization_barrier((grads, weights, *ring))
+    grads, weights, ring = lax.optimization_barrier((grads, weights, ring))
     ring = gather.send(ring)
 
     panels = [

time: 129 us -> 124 us (0.961)
  local copies, waits for them, and re-layouts: 12.4 us -> 6.61 us
    dynamic_update_slice x9 -> x0, local copies, waits for them, and re-layouts: 5.84 us -> none  [put(): return lax.dynamic_update_slice_in_dim(panel, block, at, 0)]
    ppermute x9, waiting for transfers between devices: 24.2 us -> 26.4 us  [to_partner(): lax.ppermute(block, ('xl', 'xh'), [(i, i ^ 2 * a + b) for i in range(4)])]
    ppermute x8, waiting for transfers between devices: 1.7 us -> 0.03 us  [the longest x3 0.02 us: ring_gather(): rising.append(lax.ppermute(rising[-1], axis, up))]
  transfers between devices with their start and end apart: 20 -> 20, of which waited for: 5 -> 4; matrix products, arithmetic and copies ran while one was open for 12% -> 7% of each run, Pallas kernels for 0% -> 0%
where the time goes in v10:
time: 124 us; the launch traced here: 122 us
  starting transfers between devices  79.1 us (64%)
  waiting for transfers between devices  26.5 us (21%)
  local copies, waits for them, and re-layouts  6.61 us (5%)
  other arithmetic  5.34 us (4%)
  matrix products  3.34 us (3%)
  between operations  1.25 us (1%)
    ppermute x9, starting transfers between devices, to_partner(): lax.ppermute(block, ('xl', 'xh'), [(i, i ^ 2 * a + b) for i in range(4)])  28.9 us
    ppermute x9, waiting for transfers between devices, to_partner(): lax.ppermute(block, ('xl', 'xh'), [(i, i ^ 2 * a + b) for i in range(4)])  26.4 us
    all_to_all x2, starting transfers between devices, exchange(): return lax.all_to_all(pieces, axes, split_axis=0, concat_axis=0, tiled=True)  17.1 us
    ppermute x3, starting transfers between devices, ring_gather(): falling.append(lax.ppermute(falling[-1], axis, down))  14.9 us
    ppermute x1, starting transfers between devices, swap(): return lax.ppermute(block, axis, ((0, 1), (1, 0)))  7.21 us
    ppermute x3, starting transfers between devices, ring_gather(): rising.append(lax.ppermute(rising[-1], axis, up))  5.76 us
    dot_general x3, matrix products, times(): lax.dot_general(left, right, (((left_dim,), (right_dim,)), ((), ())), pre...  3.34 us
    ppermute x1, starting transfers between devices, ring_gather(): lax.ppermute(falling[-1][middle:], axis, down)  2.76 us
  transfers between devices with their start and end apart: 20, of which 4 were waited for; matrix products, arithmetic and copies ran while one was open for 7% of the time, Pallas kernels for 0%

profile of v10, /device:TPU:1, one launch (start us, length us, event | category | flops | bytes accessed | tf_op | source)
XLA Modules:
  0.0 122.1 jit_solution(1923176088670271279)
XLA Ops:
  0.7 0.9 constant_dynamic-slice_fusion
  1.6 5.5 %collective-permute-start.1 = (bf16[1,2,32,256]{3,2,1,0:T(8,128)(2,1)S(1)}, bf16[1,2,32,256]{3,2,1,0:T(8,128)(2,1)S(1)}, u32[]{:S(2)}, u32[]{:S(2)}) collective-permute-start(bf16[1,2,32,256]{3,2,1,0:T(8,128)(2,1)S(1)} %get-tuple-element.68), channel_id=1, source_target_pairs={{0,1},{1,0},{256,257},{257,256},{2,3},{3,2},{258,259},{259,258},{4... | collective-permute-start | bytes 98312 | tf_op jit(solution)/shard_map/ppermute | solution.py:14
  7.1 2.2 %collective-permute-start = (bf16[1,2,32,256]{3,2,1,0:T(8,128)(2,1)S(1)}, bf16[1,2,32,256]{3,2,1,0:T(8,128)(2,1)S(1)}, u32[]{:S(2)}, u32[]{:S(2)}) collective-permute-start(bf16[1,2,32,256]{3,2,1,0:T(8,128)(2,1)S(1)} %get-tuple-element.67), channel_id=1, source_target_pairs={{0,256},{1,257},{256,0},{257,1},{2,258},{3,259},{258,2},{259,3},{4... | collective-permute-start | bytes 98312 | tf_op jit(solution)/shard_map/ppermute | solution.py:14
  9.3 2.5 %collective-permute-start.2 = (bf16[1,2,32,256]{3,2,1,0:T(8,128)(2,1)S(1)}, bf16[1,2,32,256]{3,2,1,0:T(8,128)(2,1)S(1)}, u32[]{:S(2)}, u32[]{:S(2)}) collective-permute-start(bf16[1,2,32,256]{3,2,1,0:T(8,128)(2,1)S(1)} %get-tuple-element.69), channel_id=1, source_target_pairs={{0,257},{1,256},{256,1},{257,0},{2,259},{3,258},{258,3},{259,2},{4... | collective-permute-start | bytes 98312 | tf_op jit(solution)/shard_map/ppermute | solution.py:14
  11.8 0.0 collective-permute-done.1
  11.8 3.6 %collective-permute-done.2 = bf16[1,2,32,256]{3,2,1,0:T(8,128)(2,1)S(1)} collective-permute-done((bf16[1,2,32,256]{3,2,1,0:T(8,128)(2,1)S(1)}, bf16[1,2,32,256]{3,2,1,0:T(8,128)(2,1)S(1)}, u32[]{:S(2)}, u32[]{:S(2)}) %collective-permute-start.2) | collective-permute-done | bytes 32800 | tf_op jit(solution)/shard_map/ppermute | solution.py:14
  15.4 0.0 collective-permute-done
  15.5 0.0 copy-start.1
  15.5 2.2 %broadcast_in_dim.8 = bf16[4,8,32,640]{3,2,1,0:T(8,128)(2,1)} broadcast(bf16[4,32,640]{2,1,0:T(8,128)(2,1)} %bitcast.47), dimensions={0,2,3} | broadcast | bytes 1474560 | tf_op jit(solution)/shard_map/broadcast_in_dim | solution.py:84
  17.7 10.4 %all-to-all-start = ((bf16[32,32,640]{2,1,0:T(8,128)(2,1)}), bf16[32,32,640]{2,1,0:T(8,128)(2,1)S(1)}, u32[]{:S(2)}, u32[]{:S(2)}) async-start(bf16[32,32,640]{2,1,0:T(8,128)(2,1)} %bitcast.7), calls=%async_computation | async-start | bytes 2621440 | tf_op jit(solution)/shard_map/all_to_all | solution.py:28
  28.1 0.0 copy-done.1
  28.1 4.6 %collective-permute-start.3 = (bf16[256,640]{1,0:T(8,128)(2,1)S(1)}, bf16[256,640]{1,0:T(8,128)(2,1)S(1)}, u32[]{:S(2)}, u32[]{:S(2)}) collective-permute-start(bf16[256,640]{1,0:T(8,128)(2,1)S(1)} %copy-done.1), channel_id=1, source_target_pairs={{0,1},{1,0},{256,257},{257,256},{2,3},{3,2},{258,259},{259,258},{4... | collective-permute-start | bytes 983048 | tf_op jit(solution)/shard_map/ppermute | solution.py:14
  32.8 5.1 %collective-permute-start.9 = (bf16[128,512]{1,0:T(8,128)(2,1)S(1)}, bf16[128,512]{1,0:T(8,128)(2,1)S(1)}, u32[]{:S(2)}, u32[]{:S(2)}) collective-permute-start(bf16[128,512]{1,0:T(8,128)(2,1)S(1)} %bitcast.42), channel_id=1, source_target_pairs={{0,14},{2,0},{4,2},{6,4},{8,6},{10,8},{12,10},{14,12},{1,15},{3,1}... | collective-permute-start | bytes 393224 | tf_op jit(solution)/shard_map/ppermute | solution.py:49
  37.9 1.9 %collective-permute-start.6 = (bf16[128,512]{1,0:T(8,128)(2,1)S(1)}, bf16[128,512]{1,0:T(8,128)(2,1)}, u32[]{:S(2)}, u32[]{:S(2)}) collective-permute-start(bf16[128,512]{1,0:T(8,128)(2,1)S(1)} %bitcast.43), channel_id=1, source_target_pairs={{0,2},{2,4},{4,6},{6,8},{8,10},{10,12},{12,14},{14,0},{1,3},{3,5},... | collective-permute-start | bytes 393224 | tf_op jit(solution)/shard_map/ppermute | solution.py:48
  39.8 0.0 collective-permute-done.9
  39.8 5.3 %collective-permute-start.10 = (bf16[128,512]{1,0:T(8,128)(2,1)S(1)}, bf16[128,512]{1,0:T(8,128)(2,1)S(1)}, u32[]{:S(2)}, u32[]{:S(2)}) collective-permute-start(bf16[128,512]{1,0:T(8,128)(2,1)S(1)} %collective-permute-done.9), channel_id=1, source_target_pairs={{0,14},{2,0},{4,2},{6,4},{8,6},{10,8},{12,10},{14,12},{1,15},{3,1}... | collective-permute-start | bytes 393224 | tf_op jit(solution)/shard_map/ppermute | solution.py:49
  45.1 0.0 collective-permute-done.6
  45.1 1.9 %collective-permute-start.7 = (bf16[128,512]{1,0:T(8,128)(2,1)}, bf16[128,512]{1,0:T(8,128)(2,1)S(1)}, u32[]{:S(2)}, u32[]{:S(2)}) collective-permute-start(bf16[128,512]{1,0:T(8,128)(2,1)} %collective-permute-done.6), channel_id=1, source_target_pairs={{0,2},{2,4},{4,6},{6,8},{8,10},{10,12},{12,14},{14,0},{1,3},{3,5},... | collective-permute-start | bytes 393224 | tf_op jit(solution)/shard_map/ppermute | solution.py:48
  47.0 2.2 %collective-permute-start.4 = (bf16[256,640]{1,0:T(8,128)(2,1)S(1)}, bf16[256,640]{1,0:T(8,128)(2,1)S(1)}, u32[]{:S(2)}, u32[]{:S(2)}) collective-permute-start(bf16[256,640]{1,0:T(8,128)(2,1)S(1)} %copy-done.1), channel_id=1, source_target_pairs={{0,256},{1,257},{256,0},{257,1},{2,258},{3,259},{258,2},{259,3},{4... | collective-permute-start | bytes 983048 | tf_op jit(solution)/shard_map/ppermute | solution.py:14
  49.3 2.5 %collective-permute-start.5 = (bf16[256,640]{1,0:T(8,128)(2,1)S(1)}, bf16[256,640]{1,0:T(8,128)(2,1)S(1)}, u32[]{:S(2)}, u32[]{:S(2)}) collective-permute-start(bf16[256,640]{1,0:T(8,128)(2,1)S(1)} %copy-done.1), channel_id=1, source_target_pairs={{0,257},{1,256},{256,1},{257,0},{2,259},{3,258},{258,3},{259,2},{4... | collective-permute-start | bytes 983048 | tf_op jit(solution)/shard_map/ppermute | solution.py:14
  51.8 0.0 collective-permute-done.10
  51.8 4.6 %collective-permute-start.11 = (bf16[128,512]{1,0:T(8,128)(2,1)S(1)}, bf16[128,512]{1,0:T(8,128)(2,1)S(1)}, u32[]{:S(2)}, u32[]{:S(2)}) collective-permute-start(bf16[128,512]{1,0:T(8,128)(2,1)S(1)} %collective-permute-done.10), channel_id=1, source_target_pairs={{0,14},{2,0},{4,2},{6,4},{8,6},{10,8},{12,10},{14,12},{1,15},{3,1}... | collective-permute-start | bytes 393224 | tf_op jit(solution)/shard_map/ppermute | solution.py:49
  56.4 0.0 collective-permute-done.7
  56.4 1.9 %collective-permute-start.8 = (bf16[128,512]{1,0:T(8,128)(2,1)S(1)}, bf16[128,512]{1,0:T(8,128)(2,1)S(1)}, u32[]{:S(2)}, u32[]{:S(2)}) collective-permute-start(bf16[128,512]{1,0:T(8,128)(2,1)S(1)} %collective-permute-done.7), channel_id=1, source_target_pairs={{0,2},{2,4},{4,6},{6,8},{8,10},{10,12},{12,14},{14,0},{1,3},{3,5},... | collective-permute-start | bytes 393224 | tf_op jit(solution)/shard_map/ppermute | solution.py:48
  58.3 0.0 collective-permute-done.3
  58.3 0.1 broadcast_select_fusion.5
  58.4 0.0 collective-permute-done.4
  58.4 4.5 %collective-permute-done.5 = bf16[256,640]{1,0:T(8,128)(2,1)S(1)} collective-permute-done((bf16[256,640]{1,0:T(8,128)(2,1)S(1)}, bf16[256,640]{1,0:T(8,128)(2,1)S(1)}, u32[]{:S(2)}, u32[]{:S(2)}) %collective-permute-start.5) | collective-permute-done | bytes 327712 | tf_op jit(solution)/shard_map/ppermute | solution.py:14
  62.9 0.1 broadcast_select_fusion.3
  63.0 0.2 broadcast_select_fusion.1
  63.2 1.1 pad_maximum_fusion
  64.4 0.0 collective-permute-done.11
  64.4 0.0 collective-permute-done.8
  64.4 0.0 all-to-all-done
  64.4 7.2 %collective-permute-start.12 = (bf16[32,32,640]{2,1,0:T(8,128)(2,1)S(1)}, bf16[32,32,640]{2,1,0:T(8,128)(2,1)S(1)}, u32[]{:S(2)}, u32[]{:S(2)}) collective-permute-start(bf16[32,32,640]{2,1,0:T(8,128)(2,1)S(1)} %all-to-all-done), channel_id=1, source_target_pairs={{0,16},{16,0},{1,17},{17,1},{2,18},{18,2},{3,19},{19,3},{4,20},{20... | collective-permute-start | bytes 3932168 | tf_op jit(solution)/shard_map/ppermute | solution.py:10
  71.7 2.8 %collective-permute-start.14 = (bf16[64,512]{1,0:T(8,128)(2,1)S(1)}, bf16[64,512]{1,0:T(8,128)(2,1)S(1)}, u32[]{:S(2)}, u32[]{:S(2)}) collective-permute-start(bf16[64,512]{1,0:T(8,128)(2,1)S(1)} %slice.45), channel_id=1, source_target_pairs={{0,14},{2,0},{4,2},{6,4},{8,6},{10,8},{12,10},{14,12},{1,15},{3,1}... | collective-permute-start | bytes 196616 | tf_op jit(solution)/shard_map/ppermute | solution.py:54
  74.4 2.5 %collective-permute-start.13 = (bf16[64,512]{1,0:T(8,128)(2,1)S(1)}, bf16[64,512]{1,0:T(8,128)(2,1)S(1)}, u32[]{:S(2)}, u32[]{:S(2)}) collective-permute-start(bf16[64,512]{1,0:T(8,128)(2,1)S(1)} %slice.44), channel_id=1, source_target_pairs={{0,2},{2,4},{4,6},{6,8},{8,10},{10,12},{12,14},{14,0},{1,3},{3,5},... | collective-permute-start | bytes 196616 | tf_op jit(solution)/shard_map/ppermute | solution.py:53
  76.9 0.1 slice_bitcast_fusion.3
  77.1 0.0 collective-permute-done.12
  77.1 0.1 slice_bitcast_fusion.1
  77.2 0.3 maximum_maximum_fusion
  77.6 0.2 copy.21
  77.8 1.1 copy-done
  78.9 0.9 convolution_convert_fusion
  79.8 0.9 convolution_convert_fusion.1
  80.6 0.0 collective-permute-done.14
  80.6 0.0 collective-permute-done.13
  80.7 1.0 pad_maximum_fusion.1
  81.7 6.7 %all-to-all-start.1 = ((bf16[32,64,256]{2,1,0:T(8,128)(2,1)}), bf16[32,64,256]{2,1,0:T(8,128)(2,1)}, u32[]{:S(2)}, u32[]{:S(2)}) async-start(bf16[32,64,256]{2,1,0:T(8,128)(2,1)} %bitcast.40), calls=%async_computation.1 | async-start | bytes 2097152 | tf_op jit(solution)/shard_map/all_to_all | solution.py:28
  88.5 0.9 constant_dynamic-update-slice_fusion.10
  89.6 1.6 %fusion = f32[512,1280]{1,0:T(8,128)S(1)} fusion(bf16[1024,1280]{1,0:T(8,128)(2,1)S(1)} %bitcast.38, bf16[1920,512]{1,0:T(8,128)(2,1)S(1)} %constant_dynamic-update-slice_fusion.2, s32[]{:T(128)S(6)} %select_n.118), kind=kOutput, calls=%fused_computation.5 | convolution fusion | flops 1342177280 | bytes 6291460 | tf_op jit(solution)/shard_map/dot_general | solution.py:32
  91.1 0.1 slice.55
  91.2 0.1 slice.54
  91.4 4.6 %collective-permute-start.16 = (bf16[256,640]{1,0:T(8,128)(2,1)S(1)}, bf16[256,640]{1,0:T(8,128)(2,1)S(1)}, u32[]{:S(2)}, u32[]{:S(2)}) collective-permute-start(bf16[256,640]{1,0:T(8,128)(2,1)S(1)} %dynamic-slice_convert_fusion.1), channel_id=1, source_target_pairs={{0,1},{1,0},{256,257},{257,256},{2,3},{3,2},{258,259},{259,258},{4... | collective-permute-start | bytes 983048 | tf_op jit(solution)/shard_map/ppermute | solution.py:14
  95.9 0.1 dynamic-slice_convert_fusion.2
  96.0 2.2 %collective-permute-start.15 = (bf16[256,640]{1,0:T(8,128)(2,1)S(1)}, bf16[256,640]{1,0:T(8,128)(2,1)S(1)}, u32[]{:S(2)}, u32[]{:S(2)}) collective-permute-start(bf16[256,640]{1,0:T(8,128)(2,1)S(1)} %get-tuple-element.56), channel_id=1, source_target_pairs={{0,256},{1,257},{256,0},{257,1},{2,258},{3,259},{258,2},{259,3},{4... | collective-permute-start | bytes 983048 | tf_op jit(solution)/shard_map/ppermute | solution.py:14
  98.2 2.6 %collective-permute-start.17 = (bf16[256,640]{1,0:T(8,128)(2,1)S(1)}, bf16[256,640]{1,0:T(8,128)(2,1)S(1)}, u32[]{:S(2)}, u32[]{:S(2)}) collective-permute-start(bf16[256,640]{1,0:T(8,128)(2,1)S(1)} %get-tuple-element.57), channel_id=1, source_target_pairs={{0,257},{1,256},{256,1},{257,0},{2,259},{3,258},{258,3},{259,2},{4... | collective-permute-start | bytes 983048 | tf_op jit(solution)/shard_map/ppermute | solution.py:14
  100.8 8.6 %collective-permute-done.16 = bf16[256,640]{1,0:T(8,128)(2,1)S(1)} collective-permute-done((bf16[256,640]{1,0:T(8,128)(2,1)S(1)}, bf16[256,640]{1,0:T(8,128)(2,1)S(1)}, u32[]{:S(2)}, u32[]{:S(2)}) %collective-permute-start.16) | collective-permute-done | bytes 327712 | tf_op jit(solution)/shard_map/ppermute | solution.py:14
  109.4 9.7 %collective-permute-done.15 = bf16[256,640]{1,0:T(8,128)(2,1)S(1)} collective-permute-done((bf16[256,640]{1,0:T(8,128)(2,1)S(1)}, bf16[256,640]{1,0:T(8,128)(2,1)S(1)}, u32[]{:S(2)}, u32[]{:S(2)}) %collective-permute-start.15) | collective-permute-done | bytes 327712 | tf_op jit(solution)/shard_map/ppermute | solution.py:14
  119.0 0.0 collective-permute-done.17
  119.1 1.0 convert_add_fusion
  120.0 0.0 all-to-all-done.1
  120.0 1.4 %reduce_sum.12 = bf16[2,2,2,32,256]{4,3,2,1,0:T(8,128)(2,1)S(1)} reduce(bf16[2,8,2,2,32,256]{5,4,3,2,1,0:T(8,128)(2,1)} %bitcast.16, bf16[]{:T(256)} %constant.41.clone.1), dimensions={1}, to_apply=%region_0.1 | reduce | flops 458752 | bytes 1179650 | tf_op jit(solution)/shard_map/reduce_sum | solution.py:112
  121.5 0.7 copy.22
  (27 shorter events, 0.3 us)
Async XLA Ops:
  1.6 10.2 %collective-permute-start.1 = (bf16[1,2,32,256]{3,2,1,0:T(8,128)(2,1)S(1)}, bf16[1,2,32,256]{3,2,1,0:T(8,128)(2,1)S(1)}, u32[]{:S(2)}, u32[]{:S(2)}) collective-permute-start(bf16[1,2,32,256]{3,2,1,0:T(8,128)(2,1)S(1)} %get-tuple-element.68), channel_id=1, source_target_pairs={{0,1},{1,0},{256,257},{257,256},{2,3},{3,2},{258,259},{259,258},{4... | collective-permute-start | bytes 98312 | tf_op jit(solution)/shard_map/ppermute | solution.py:14
  7.1 8.4 %collective-permute-start = (bf16[1,2,32,256]{3,2,1,0:T(8,128)(2,1)S(1)}, bf16[1,2,32,256]{3,2,1,0:T(8,128)(2,1)S(1)}, u32[]{:S(2)}, u32[]{:S(2)}) collective-permute-start(bf16[1,2,32,256]{3,2,1,0:T(8,128)(2,1)S(1)} %get-tuple-element.67), channel_id=1, source_target_pairs={{0,256},{1,257},{256,0},{257,1},{2,258},{3,259},{258,2},{259,3},{4... | collective-permute-start | bytes 98312 | tf_op jit(solution)/shard_map/ppermute | solution.py:14
  9.3 6.1 %collective-permute-start.2 = (bf16[1,2,32,256]{3,2,1,0:T(8,128)(2,1)S(1)}, bf16[1,2,32,256]{3,2,1,0:T(8,128)(2,1)S(1)}, u32[]{:S(2)}, u32[]{:S(2)}) collective-permute-start(bf16[1,2,32,256]{3,2,1,0:T(8,128)(2,1)S(1)} %get-tuple-element.69), channel_id=1, source_target_pairs={{0,257},{1,256},{256,1},{257,0},{2,259},{3,258},{258,3},{259,2},{4... | collective-permute-start | bytes 98312 | tf_op jit(solution)/shard_map/ppermute | solution.py:14
  15.5 12.6 %copy-start.1 = (bf16[256,640]{1,0:T(8,128)(2,1)S(1)}, bf16[256,640]{1,0:T(8,128)(2,1)}, u32[]{:S(2)}) copy-start(bf16[256,640]{1,0:T(8,128)(2,1)} %param.5) | copy-start | bytes 983044
  17.7 46.7 %all-to-all-start = ((bf16[32,32,640]{2,1,0:T(8,128)(2,1)}), bf16[32,32,640]{2,1,0:T(8,128)(2,1)S(1)}, u32[]{:S(2)}, u32[]{:S(2)}) async-start(bf16[32,32,640]{2,1,0:T(8,128)(2,1)} %bitcast.7), calls=%async_computation | async-start | bytes 2621440 | tf_op jit(solution)/shard_map/all_to_all | solution.py:28
  28.1 30.2 %collective-permute-start.3 = (bf16[256,640]{1,0:T(8,128)(2,1)S(1)}, bf16[256,640]{1,0:T(8,128)(2,1)S(1)}, u32[]{:S(2)}, u32[]{:S(2)}) collective-permute-start(bf16[256,640]{1,0:T(8,128)(2,1)S(1)} %copy-done.1), channel_id=1, source_target_pairs={{0,1},{1,0},{256,257},{257,256},{2,3},{3,2},{258,259},{259,258},{4... | collective-permute-start | bytes 983048 | tf_op jit(solution)/shard_map/ppermute | solution.py:14
  32.8 7.0 %collective-permute-start.9 = (bf16[128,512]{1,0:T(8,128)(2,1)S(1)}, bf16[128,512]{1,0:T(8,128)(2,1)S(1)}, u32[]{:S(2)}, u32[]{:S(2)}) collective-permute-start(bf16[128,512]{1,0:T(8,128)(2,1)S(1)} %bitcast.42), channel_id=1, source_target_pairs={{0,14},{2,0},{4,2},{6,4},{8,6},{10,8},{12,10},{14,12},{1,15},{3,1}... | collective-permute-start | bytes 393224 | tf_op jit(solution)/shard_map/ppermute | solution.py:49
  37.9 7.2 %collective-permute-start.6 = (bf16[128,512]{1,0:T(8,128)(2,1)S(1)}, bf16[128,512]{1,0:T(8,128)(2,1)}, u32[]{:S(2)}, u32[]{:S(2)}) collective-permute-start(bf16[128,512]{1,0:T(8,128)(2,1)S(1)} %bitcast.43), channel_id=1, source_target_pairs={{0,2},{2,4},{4,6},{6,8},{8,10},{10,12},{12,14},{14,0},{1,3},{3,5},... | collective-permute-start | bytes 393224 | tf_op jit(solution)/shard_map/ppermute | solution.py:48
  39.8 11.9 %collective-permute-start.10 = (bf16[128,512]{1,0:T(8,128)(2,1)S(1)}, bf16[128,512]{1,0:T(8,128)(2,1)S(1)}, u32[]{:S(2)}, u32[]{:S(2)}) collective-permute-start(bf16[128,512]{1,0:T(8,128)(2,1)S(1)} %collective-permute-done.9), channel_id=1, source_target_pairs={{0,14},{2,0},{4,2},{6,4},{8,6},{10,8},{12,10},{14,12},{1,15},{3,1}... | collective-permute-start | bytes 393224 | tf_op jit(solution)/shard_map/ppermute | solution.py:49
  45.1 11.3 %collective-permute-start.7 = (bf16[128,512]{1,0:T(8,128)(2,1)}, bf16[128,512]{1,0:T(8,128)(2,1)S(1)}, u32[]{:S(2)}, u32[]{:S(2)}) collective-permute-start(bf16[128,512]{1,0:T(8,128)(2,1)} %collective-permute-done.6), channel_id=1, source_target_pairs={{0,2},{2,4},{4,6},{6,8},{8,10},{10,12},{12,14},{14,0},{1,3},{3,5},... | collective-permute-start | bytes 393224 | tf_op jit(solution)/shard_map/ppermute | solution.py:48
  47.0 11.4 %collective-permute-start.4 = (bf16[256,640]{1,0:T(8,128)(2,1)S(1)}, bf16[256,640]{1,0:T(8,128)(2,1)S(1)}, u32[]{:S(2)}, u32[]{:S(2)}) collective-permute-start(bf16[256,640]{1,0:T(8,128)(2,1)S(1)} %copy-done.1), channel_id=1, source_target_pairs={{0,256},{1,257},{256,0},{257,1},{2,258},{3,259},{258,2},{259,3},{4... | collective-permute-start | bytes 983048 | tf_op jit(solution)/shard_map/ppermute | solution.py:14
  49.3 13.7 %collective-permute-start.5 = (bf16[256,640]{1,0:T(8,128)(2,1)S(1)}, bf16[256,640]{1,0:T(8,128)(2,1)S(1)}, u32[]{:S(2)}, u32[]{:S(2)}) collective-permute-start(bf16[256,640]{1,0:T(8,128)(2,1)S(1)} %copy-done.1), channel_id=1, source_target_pairs={{0,257},{1,256},{256,1},{257,0},{2,259},{3,258},{258,3},{259,2},{4... | collective-permute-start | bytes 983048 | tf_op jit(solution)/shard_map/ppermute | solution.py:14
  51.8 12.6 %collective-permute-start.11 = (bf16[128,512]{1,0:T(8,128)(2,1)S(1)}, bf16[128,512]{1,0:T(8,128)(2,1)S(1)}, u32[]{:S(2)}, u32[]{:S(2)}) collective-permute-start(bf16[128,512]{1,0:T(8,128)(2,1)S(1)} %collective-permute-done.10), channel_id=1, source_target_pairs={{0,14},{2,0},{4,2},{6,4},{8,6},{10,8},{12,10},{14,12},{1,15},{3,1}... | collective-permute-start | bytes 393224 | tf_op jit(solution)/shard_map/ppermute | solution.py:49
  56.4 8.0 %collective-permute-start.8 = (bf16[128,512]{1,0:T(8,128)(2,1)S(1)}, bf16[128,512]{1,0:T(8,128)(2,1)S(1)}, u32[]{:S(2)}, u32[]{:S(2)}) collective-permute-start(bf16[128,512]{1,0:T(8,128)(2,1)S(1)} %collective-permute-done.7), channel_id=1, source_target_pairs={{0,2},{2,4},{4,6},{6,8},{8,10},{10,12},{12,14},{14,0},{1,3},{3,5},... | collective-permute-start | bytes 393224 | tf_op jit(solution)/shard_map/ppermute | solution.py:48
  64.4 12.7 %collective-permute-start.12 = (bf16[32,32,640]{2,1,0:T(8,128)(2,1)S(1)}, bf16[32,32,640]{2,1,0:T(8,128)(2,1)S(1)}, u32[]{:S(2)}, u32[]{:S(2)}) collective-permute-start(bf16[32,32,640]{2,1,0:T(8,128)(2,1)S(1)} %all-to-all-done), channel_id=1, source_target_pairs={{0,16},{16,0},{1,17},{17,1},{2,18},{18,2},{3,19},{19,3},{4,20},{20... | collective-permute-start | bytes 3932168 | tf_op jit(solution)/shard_map/ppermute | solution.py:10
  71.7 9.0 %collective-permute-start.14 = (bf16[64,512]{1,0:T(8,128)(2,1)S(1)}, bf16[64,512]{1,0:T(8,128)(2,1)S(1)}, u32[]{:S(2)}, u32[]{:S(2)}) collective-permute-start(bf16[64,512]{1,0:T(8,128)(2,1)S(1)} %slice.45), channel_id=1, source_target_pairs={{0,14},{2,0},{4,2},{6,4},{8,6},{10,8},{12,10},{14,12},{1,15},{3,1}... | collective-permute-start | bytes 196616 | tf_op jit(solution)/shard_map/ppermute | solution.py:54
  74.4 6.2 %collective-permute-start.13 = (bf16[64,512]{1,0:T(8,128)(2,1)S(1)}, bf16[64,512]{1,0:T(8,128)(2,1)S(1)}, u32[]{:S(2)}, u32[]{:S(2)}) collective-permute-start(bf16[64,512]{1,0:T(8,128)(2,1)S(1)} %slice.44), channel_id=1, source_target_pairs={{0,2},{2,4},{4,6},{6,8},{8,10},{10,12},{12,14},{14,0},{1,3},{3,5},... | collective-permute-start | bytes 196616 | tf_op jit(solution)/shard_map/ppermute | solution.py:53
  77.6 1.3 %copy-start = (bf16[512,1280]{1,0:T(8,128)(2,1)S(1)}, bf16[512,1280]{1,0:T(8,128)(2,1)}, u32[]{:S(2)}) copy-start(bf16[512,1280]{1,0:T(8,128)(2,1)} %pad_maximum_fusion) | copy-start | bytes 3932164
  81.7 38.3 %all-to-all-start.1 = ((bf16[32,64,256]{2,1,0:T(8,128)(2,1)}), bf16[32,64,256]{2,1,0:T(8,128)(2,1)}, u32[]{:S(2)}, u32[]{:S(2)}) async-start(bf16[32,64,256]{2,1,0:T(8,128)(2,1)} %bitcast.40), calls=%async_computation.1 | async-start | bytes 2097152 | tf_op jit(solution)/shard_map/all_to_all | solution.py:28
  91.4 18.0 %collective-permute-start.16 = (bf16[256,640]{1,0:T(8,128)(2,1)S(1)}, bf16[256,640]{1,0:T(8,128)(2,1)S(1)}, u32[]{:S(2)}, u32[]{:S(2)}) collective-permute-start(bf16[256,640]{1,0:T(8,128)(2,1)S(1)} %dynamic-slice_convert_fusion.1), channel_id=1, source_target_pairs={{0,1},{1,0},{256,257},{257,256},{2,3},{3,2},{258,259},{259,258},{4... | collective-permute-start | bytes 983048 | tf_op jit(solution)/shard_map/ppermute | solution.py:14
  96.0 23.0 %collective-permute-start.15 = (bf16[256,640]{1,0:T(8,128)(2,1)S(1)}, bf16[256,640]{1,0:T(8,128)(2,1)S(1)}, u32[]{:S(2)}, u32[]{:S(2)}) collective-permute-start(bf16[256,640]{1,0:T(8,128)(2,1)S(1)} %get-tuple-element.56), channel_id=1, source_target_pairs={{0,256},{1,257},{256,0},{257,1},{2,258},{3,259},{258,2},{259,3},{4... | collective-permute-start | bytes 983048 | tf_op jit(solution)/shard_map/ppermute | solution.py:14
  98.2 20.8 %collective-permute-start.17 = (bf16[256,640]{1,0:T(8,128)(2,1)S(1)}, bf16[256,640]{1,0:T(8,128)(2,1)S(1)}, u32[]{:S(2)}, u32[]{:S(2)}) collective-permute-start(bf16[256,640]{1,0:T(8,128)(2,1)S(1)} %get-tuple-element.57), channel_id=1, source_target_pairs={{0,257},{1,256},{256,1},{257,0},{2,259},{3,258},{258,3},{259,2},{4... | collective-permute-start | bytes 983048 | tf_op jit(solution)/shard_map/ppermute | solution.py:14

commit v11 on v10

--- a/solution.py
+++ b/solution.py
@@ -48,13 +48,9 @@
         rising.append(lax.ppermute(rising[-1], axis, up))
         falling.append(lax.ppermute(falling[-1], axis, down))
     rising, falling = yield rising, falling
-    middle = rows // 2
-    far = (
-        lax.ppermute(rising[-1][:middle], axis, up),
-        lax.ppermute(falling[-1][middle:], axis, down),
-    )
+    far = lax.ppermute(rising[-1], axis, up)
     rising, falling, far = yield rising, falling, far
-    blocks = falling[:] + list(far) + rising[:0:-1]
+    blocks = falling + [far] + rising[:0:-1]
     panel = jnp.concatenate(blocks + blocks[:-1], axis=0)
     first = lax.rem(size - me, size) * rows
     yield lax.dynamic_slice_in_dim(panel, first, size * rows, 0)
@@ -88,22 +84,22 @@
 
     came = {(a, b): to_partner(weight, a, b) for a, b in PAIRS}
     came[0, 0] = weight
-    weights = [in_order(far, came[a, 0], came[a, 1], 1) for a in range(2)]
-    weights = in_order(near, weights[0], weights[1], 0)
     gather = ring_gather(acts, "y")
     ring = next(gather)
-    grads, weights, ring = lax.optimization_barrier((grads, weights, ring))
+    grads, came, ring = lax.optimization_barrier((grads, came, ring))
     ring = gather.send(ring)
+    weights = [in_order(far, came[a, 0], came[a, 1], 1) for a in range(2)]
+    weights = [
+        jnp.where(near == 0, weights[0], weights[1]),
+        jnp.where(near == 0, weights[1], weights[0]),
+    ]
 
     panels = [
         g.reshape(2, 2, depth, 1, part, columns) for g in (grads, swap(grads, "core"))
     ]
     panels = [jnp.concatenate([g[:, 0], g[:, 1]], axis=4) for g in panels]
     panel = jnp.concatenate(panels, axis=2).reshape(-1, 2 * columns)
-    partial = [
-        times(panel, weights[i * features : (i + 1) * features], 1, 1).astype(jnp.bfloat16)
-        for i in range(2)
-    ]
+    partial = [times(panel, w, 1, 1).astype(jnp.bfloat16) for w in weights]
     *partial, panel, ring = lax.optimization_barrier((*partial, panel, ring))
     acts = gather.send(ring)
     partial = jnp.concatenate(partial, axis=0).reshape(-1, 2 * part, features)

time: 124 us -> 124 us (level)
  waiting for transfers between devices: 26.5 us -> 32 us
  starting transfers between devices: 79.1 us -> 75.5 us
  other arithmetic: 5.34 us -> 3.97 us
    ppermute x2 -> x1, waiting for transfers between devices: 0.01 us -> 3.28 us  [ring_gather(): far = lax.ppermute(rising[-1], axis, up)]
    ppermute x2 -> x1, starting transfers between devices: 5.28 us -> 2.05 us  [ring_gather(): far = lax.ppermute(rising[-1], axis, up)]
    ppermute x9, waiting for transfers between devices: 26.4 us -> 28.2 us  [to_partner(): lax.ppermute(block, ('xl', 'xh'), [(i, i ^ 2 * a + b) for i in range(4)])]
  transfers between devices with their start and end apart: 20 -> 19, of which waited for: 4 -> 7; matrix products, arithmetic and copies ran while one was open for 7% -> 5% of each run, Pallas kernels for 0% -> 0%
where the time goes in v11:
time: 124 us; the launch traced here: 122 us
  starting transfers between devices  75.5 us (61%)
  waiting for transfers between devices  32 us (26%)
  local copies, waits for them, and re-layouts  6.23 us (5%)
  other arithmetic  3.97 us (3%)
  matrix products  3.38 us (3%)
  between operations  1.27 us (1%)
    ppermute x9, starting transfers between devices, to_partner(): lax.ppermute(block, ('xl', 'xh'), [(i, i ^ 2 * a + b) for i in range(4)])  29.1 us
    ppermute x9, waiting for transfers between devices, to_partner(): lax.ppermute(block, ('xl', 'xh'), [(i, i ^ 2 * a + b) for i in range(4)])  28.2 us
    all_to_all x2, starting transfers between devices, exchange(): return lax.all_to_all(pieces, axes, split_axis=0, concat_axis=0, tiled=True)  17.2 us
    ppermute x3, starting transfers between devices, ring_gather(): falling.append(lax.ppermute(falling[-1], axis, down))  14.9 us
    ppermute x1, starting transfers between devices, swap(): return lax.ppermute(block, axis, ((0, 1), (1, 0)))  6.47 us
    ppermute x3, starting transfers between devices, ring_gather(): rising.append(lax.ppermute(rising[-1], axis, up))  5.75 us
    dot_general x3, matrix products, times(): lax.dot_general(left, right, (((left_dim,), (right_dim,)), ((), ())), pre...  3.38 us
    ppermute x1, waiting for transfers between devices, ring_gather(): far = lax.ppermute(rising[-1], axis, up)  3.28 us
  transfers between devices with their start and end apart: 19, of which 7 were waited for; matrix products, arithmetic and copies ran while one was open for 5% of the time, Pallas kernels for 0%

profile of v11, /device:TPU:1, one launch (start us, length us, event | category | flops | bytes accessed | tf_op | source)
XLA Modules:
  0.0 122.3 jit_solution(18030973720262062711)
XLA Ops:
  0.7 0.9 constant_dynamic-slice_fusion
  1.6 5.5 %collective-permute-start.1 = (bf16[1,2,32,256]{3,2,1,0:T(8,128)(2,1)S(1)}, bf16[1,2,32,256]{3,2,1,0:T(8,128)(2,1)S(1)}, u32[]{:S(2)}, u32[]{:S(2)}) collective-permute-start(bf16[1,2,32,256]{3,2,1,0:T(8,128)(2,1)S(1)} %get-tuple-element.70), channel_id=1, source_target_pairs={{0,1},{1,0},{256,257},{257,256},{2,3},{3,2},{258,259},{259,258},{4... | collective-permute-start | bytes 98312 | tf_op jit(solution)/shard_map/ppermute | solution.py:14
  7.1 2.2 %collective-permute-start = (bf16[1,2,32,256]{3,2,1,0:T(8,128)(2,1)S(1)}, bf16[1,2,32,256]{3,2,1,0:T(8,128)(2,1)S(1)}, u32[]{:S(2)}, u32[]{:S(2)}) collective-permute-start(bf16[1,2,32,256]{3,2,1,0:T(8,128)(2,1)S(1)} %get-tuple-element.69), channel_id=1, source_target_pairs={{0,256},{1,257},{256,0},{257,1},{2,258},{3,259},{258,2},{259,3},{4... | collective-permute-start | bytes 98312 | tf_op jit(solution)/shard_map/ppermute | solution.py:14
  9.3 2.5 %collective-permute-start.2 = (bf16[1,2,32,256]{3,2,1,0:T(8,128)(2,1)S(1)}, bf16[1,2,32,256]{3,2,1,0:T(8,128)(2,1)S(1)}, u32[]{:S(2)}, u32[]{:S(2)}) collective-permute-start(bf16[1,2,32,256]{3,2,1,0:T(8,128)(2,1)S(1)} %get-tuple-element.71), channel_id=1, source_target_pairs={{0,257},{1,256},{256,1},{257,0},{2,259},{3,258},{258,3},{259,2},{4... | collective-permute-start | bytes 98312 | tf_op jit(solution)/shard_map/ppermute | solution.py:14
  11.8 0.0 collective-permute-done.1
  11.8 3.6 %collective-permute-done.2 = bf16[1,2,32,256]{3,2,1,0:T(8,128)(2,1)S(1)} collective-permute-done((bf16[1,2,32,256]{3,2,1,0:T(8,128)(2,1)S(1)}, bf16[1,2,32,256]{3,2,1,0:T(8,128)(2,1)S(1)}, u32[]{:S(2)}, u32[]{:S(2)}) %collective-permute-start.2) | collective-permute-done | bytes 32800 | tf_op jit(solution)/shard_map/ppermute | solution.py:14
  15.4 0.0 collective-permute-done
  15.5 0.0 copy-start
  15.5 2.2 %broadcast_in_dim.8 = bf16[4,8,32,640]{3,2,1,0:T(8,128)(2,1)} broadcast(bf16[4,32,640]{2,1,0:T(8,128)(2,1)} %bitcast.47), dimensions={0,2,3} | broadcast | bytes 1474560 | tf_op jit(solution)/shard_map/broadcast_in_dim | solution.py:80
  17.7 10.4 %all-to-all-start = ((bf16[32,32,640]{2,1,0:T(8,128)(2,1)}), bf16[32,32,640]{2,1,0:T(8,128)(2,1)S(1)}, u32[]{:S(2)}, u32[]{:S(2)}) async-start(bf16[32,32,640]{2,1,0:T(8,128)(2,1)} %bitcast.7), calls=%async_computation | async-start | bytes 2621440 | tf_op jit(solution)/shard_map/all_to_all | solution.py:28
  28.1 5.1 %collective-permute-start.9 = (bf16[128,512]{1,0:T(8,128)(2,1)S(1)}, bf16[128,512]{1,0:T(8,128)(2,1)S(1)}, u32[]{:S(2)}, u32[]{:S(2)}) collective-permute-start(bf16[128,512]{1,0:T(8,128)(2,1)S(1)} %bitcast.42), channel_id=1, source_target_pairs={{0,14},{2,0},{4,2},{6,4},{8,6},{10,8},{12,10},{14,12},{1,15},{3,1}... | collective-permute-start | bytes 393224 | tf_op jit(solution)/shard_map/ppermute | solution.py:49
  33.2 1.9 %collective-permute-start.6 = (bf16[128,512]{1,0:T(8,128)(2,1)S(1)}, bf16[128,512]{1,0:T(8,128)(2,1)}, u32[]{:S(2)}, u32[]{:S(2)}) collective-permute-start(bf16[128,512]{1,0:T(8,128)(2,1)S(1)} %bitcast.43), channel_id=1, source_target_pairs={{0,2},{2,4},{4,6},{6,8},{8,10},{10,12},{12,14},{14,0},{1,3},{3,5},... | collective-permute-start | bytes 393224 | tf_op jit(solution)/shard_map/ppermute | solution.py:48
  35.1 0.0 copy-done
  35.1 4.4 %collective-permute-start.5 = (bf16[256,640]{1,0:T(8,128)(2,1)S(1)}, bf16[256,640]{1,0:T(8,128)(2,1)S(1)}, u32[]{:S(2)}, u32[]{:S(2)}) collective-permute-start(bf16[256,640]{1,0:T(8,128)(2,1)S(1)} %copy-done), channel_id=1, source_target_pairs={{0,257},{1,256},{256,1},{257,0},{2,259},{3,258},{258,3},{259,2},{4... | collective-permute-start | bytes 983048 | tf_op jit(solution)/shard_map/ppermute | solution.py:14
  39.5 1.9 %collective-permute-start.4 = (bf16[256,640]{1,0:T(8,128)(2,1)S(1)}, bf16[256,640]{1,0:T(8,128)(2,1)S(1)}, u32[]{:S(2)}, u32[]{:S(2)}) collective-permute-start(bf16[256,640]{1,0:T(8,128)(2,1)S(1)} %copy-done), channel_id=1, source_target_pairs={{0,256},{1,257},{256,0},{257,1},{2,258},{3,259},{258,2},{259,3},{4... | collective-permute-start | bytes 983048 | tf_op jit(solution)/shard_map/ppermute | solution.py:14
  41.5 3.3 %collective-permute-start.3 = (bf16[256,640]{1,0:T(8,128)(2,1)S(1)}, bf16[256,640]{1,0:T(8,128)(2,1)S(1)}, u32[]{:S(2)}, u32[]{:S(2)}) collective-permute-start(bf16[256,640]{1,0:T(8,128)(2,1)S(1)} %copy-done), channel_id=1, source_target_pairs={{0,1},{1,0},{256,257},{257,256},{2,3},{3,2},{258,259},{259,258},{4... | collective-permute-start | bytes 983048 | tf_op jit(solution)/shard_map/ppermute | solution.py:14
  44.8 0.0 collective-permute-done.9
  44.8 4.6 %collective-permute-start.10 = (bf16[128,512]{1,0:T(8,128)(2,1)S(1)}, bf16[128,512]{1,0:T(8,128)(2,1)S(1)}, u32[]{:S(2)}, u32[]{:S(2)}) collective-permute-start(bf16[128,512]{1,0:T(8,128)(2,1)S(1)} %collective-permute-done.9), channel_id=1, source_target_pairs={{0,14},{2,0},{4,2},{6,4},{8,6},{10,8},{12,10},{14,12},{1,15},{3,1}... | collective-permute-start | bytes 393224 | tf_op jit(solution)/shard_map/ppermute | solution.py:49
  49.3 0.0 collective-permute-done.6
  49.4 1.9 %collective-permute-start.7 = (bf16[128,512]{1,0:T(8,128)(2,1)}, bf16[128,512]{1,0:T(8,128)(2,1)S(1)}, u32[]{:S(2)}, u32[]{:S(2)}) collective-permute-start(bf16[128,512]{1,0:T(8,128)(2,1)} %collective-permute-done.6), channel_id=1, source_target_pairs={{0,2},{2,4},{4,6},{6,8},{8,10},{10,12},{12,14},{14,0},{1,3},{3,5},... | collective-permute-start | bytes 393224 | tf_op jit(solution)/shard_map/ppermute | solution.py:48
  51.3 0.0 collective-permute-done.10
  51.3 5.2 %collective-permute-start.11 = (bf16[128,512]{1,0:T(8,128)(2,1)S(1)}, bf16[128,512]{1,0:T(8,128)(2,1)S(1)}, u32[]{:S(2)}, u32[]{:S(2)}) collective-permute-start(bf16[128,512]{1,0:T(8,128)(2,1)S(1)} %collective-permute-done.10), channel_id=1, source_target_pairs={{0,14},{2,0},{4,2},{6,4},{8,6},{10,8},{12,10},{14,12},{1,15},{3,1}... | collective-permute-start | bytes 393224 | tf_op jit(solution)/shard_map/ppermute | solution.py:49
  56.6 0.2 collective-permute-done.7
  56.8 1.9 %collective-permute-start.8 = (bf16[128,512]{1,0:T(8,128)(2,1)S(1)}, bf16[128,512]{1,0:T(8,128)(2,1)S(1)}, u32[]{:S(2)}, u32[]{:S(2)}) collective-permute-start(bf16[128,512]{1,0:T(8,128)(2,1)S(1)} %collective-permute-done.7), channel_id=1, source_target_pairs={{0,2},{2,4},{4,6},{6,8},{8,10},{10,12},{12,14},{14,0},{1,3},{3,5},... | collective-permute-start | bytes 393224 | tf_op jit(solution)/shard_map/ppermute | solution.py:48
  58.7 0.0 collective-permute-done.5
  58.7 0.0 copy-start.2
  58.7 0.0 collective-permute-done.4
  58.7 0.0 copy-start.4
  58.7 6.0 %collective-permute-done.3 = bf16[256,640]{1,0:T(8,128)(2,1)S(1)} collective-permute-done((bf16[256,640]{1,0:T(8,128)(2,1)S(1)}, bf16[256,640]{1,0:T(8,128)(2,1)S(1)}, u32[]{:S(2)}, u32[]{:S(2)}) %collective-permute-start.3) | collective-permute-done | bytes 327712 | tf_op jit(solution)/shard_map/ppermute | solution.py:14
  64.7 0.0 collective-permute-done.11
  64.7 0.0 collective-permute-done.8
  64.7 0.0 copy-done.2
  64.8 0.7 copy-done.6
  65.5 0.0 all-to-all-done
  65.5 6.5 %collective-permute-start.12 = (bf16[32,32,640]{2,1,0:T(8,128)(2,1)S(1)}, bf16[32,32,640]{2,1,0:T(8,128)(2,1)S(1)}, u32[]{:S(2)}, u32[]{:S(2)}) collective-permute-start(bf16[32,32,640]{2,1,0:T(8,128)(2,1)S(1)} %all-to-all-done), channel_id=1, source_target_pairs={{0,16},{16,0},{1,17},{17,1},{2,18},{18,2},{3,19},{19,3},{4,20},{20... | collective-permute-start | bytes 3932168 | tf_op jit(solution)/shard_map/ppermute | solution.py:10
  72.0 0.0 copy-start.1
  72.0 0.0 copy-start.5
  72.0 2.1 %collective-permute-start.13 = (bf16[128,512]{1,0:T(8,128)(2,1)S(1)}, bf16[128,512]{1,0:T(8,128)(2,1)S(1)}, u32[]{:S(2)}, u32[]{:S(2)}) collective-permute-start(bf16[128,512]{1,0:T(8,128)(2,1)S(1)} %collective-permute-done.8), channel_id=1, source_target_pairs={{0,2},{2,4},{4,6},{6,8},{8,10},{10,12},{12,14},{14,0},{1,3},{3,5},... | collective-permute-start | bytes 393224 | tf_op jit(solution)/shard_map/ppermute | solution.py:51
  74.1 0.1 slice_bitcast_fusion.3
  74.2 0.1 broadcast_select_fusion.1
  74.4 0.2 collective-permute-done.12
  74.6 0.1 slice_bitcast_fusion.1
  74.7 0.3 maximum_maximum_fusion
  75.0 0.2 copy.21
  75.3 0.9 convolution_convert_fusion
  76.2 0.9 convolution_convert_fusion.1
  77.1 3.3 %collective-permute-done.13 = bf16[128,512]{1,0:T(8,128)(2,1)S(1)} collective-permute-done((bf16[128,512]{1,0:T(8,128)(2,1)S(1)}, bf16[128,512]{1,0:T(8,128)(2,1)S(1)}, u32[]{:S(2)}, u32[]{:S(2)}) %collective-permute-start.13) | collective-permute-done | bytes 131104 | tf_op jit(solution)/shard_map/ppermute | solution.py:51
  80.4 1.0 pad_maximum_fusion
  81.4 6.8 %all-to-all-start.1 = ((bf16[32,64,256]{2,1,0:T(8,128)(2,1)}), bf16[32,64,256]{2,1,0:T(8,128)(2,1)}, u32[]{:S(2)}, u32[]{:S(2)}) async-start(bf16[32,64,256]{2,1,0:T(8,128)(2,1)} %bitcast.40), calls=%async_computation.1 | async-start | bytes 2097152 | tf_op jit(solution)/shard_map/all_to_all | solution.py:28
  88.3 0.9 constant_dynamic-update-slice_fusion.9
  89.4 1.6 %fusion = f32[512,1280]{1,0:T(8,128)S(1)} fusion(bf16[1024,1280]{1,0:T(8,128)(2,1)S(1)} %bitcast.38, bf16[1920,512]{1,0:T(8,128)(2,1)S(1)} %constant_dynamic-update-slice_fusion.2, s32[]{:T(128)S(6)} %select_n.118), kind=kOutput, calls=%fused_computation.4 | convolution fusion | flops 1342177280 | bytes 6291460 | tf_op jit(solution)/shard_map/dot_general | solution.py:32
  91.0 0.1 slice.39
  91.1 0.1 slice.38
  91.2 4.6 %collective-permute-start.15 = (bf16[256,640]{1,0:T(8,128)(2,1)S(1)}, bf16[256,640]{1,0:T(8,128)(2,1)S(1)}, u32[]{:S(2)}, u32[]{:S(2)}) collective-permute-start(bf16[256,640]{1,0:T(8,128)(2,1)S(1)} %dynamic-slice_convert_fusion.1), channel_id=1, source_target_pairs={{0,1},{1,0},{256,257},{257,256},{2,3},{3,2},{258,259},{259,258},{4... | collective-permute-start | bytes 983048 | tf_op jit(solution)/shard_map/ppermute | solution.py:14
  95.8 0.1 dynamic-slice_convert_fusion.2
  95.8 2.2 %collective-permute-start.14 = (bf16[256,640]{1,0:T(8,128)(2,1)S(1)}, bf16[256,640]{1,0:T(8,128)(2,1)S(1)}, u32[]{:S(2)}, u32[]{:S(2)}) collective-permute-start(bf16[256,640]{1,0:T(8,128)(2,1)S(1)} %get-tuple-element.58), channel_id=1, source_target_pairs={{0,256},{1,257},{256,0},{257,1},{2,258},{3,259},{258,2},{259,3},{4... | collective-permute-start | bytes 983048 | tf_op jit(solution)/shard_map/ppermute | solution.py:14
  98.1 2.6 %collective-permute-start.16 = (bf16[256,640]{1,0:T(8,128)(2,1)S(1)}, bf16[256,640]{1,0:T(8,128)(2,1)S(1)}, u32[]{:S(2)}, u32[]{:S(2)}) collective-permute-start(bf16[256,640]{1,0:T(8,128)(2,1)S(1)} %get-tuple-element.59), channel_id=1, source_target_pairs={{0,257},{1,256},{256,1},{257,0},{2,259},{3,258},{258,3},{259,2},{4... | collective-permute-start | bytes 983048 | tf_op jit(solution)/shard_map/ppermute | solution.py:14
  100.6 9.6 %collective-permute-done.15 = bf16[256,640]{1,0:T(8,128)(2,1)S(1)} collective-permute-done((bf16[256,640]{1,0:T(8,128)(2,1)S(1)}, bf16[256,640]{1,0:T(8,128)(2,1)S(1)}, u32[]{:S(2)}, u32[]{:S(2)}) %collective-permute-start.15) | collective-permute-done | bytes 327712 | tf_op jit(solution)/shard_map/ppermute | solution.py:14
  110.2 9.0 %collective-permute-done.14 = bf16[256,640]{1,0:T(8,128)(2,1)S(1)} collective-permute-done((bf16[256,640]{1,0:T(8,128)(2,1)S(1)}, bf16[256,640]{1,0:T(8,128)(2,1)S(1)}, u32[]{:S(2)}, u32[]{:S(2)}) %collective-permute-start.14) | collective-permute-done | bytes 327712 | tf_op jit(solution)/shard_map/ppermute | solution.py:14
  119.2 0.0 collective-permute-done.16
  119.2 1.0 convert_add_fusion
  120.2 0.0 all-to-all-done.1
  120.2 1.4 %reduce_sum.12 = bf16[2,2,2,32,256]{4,3,2,1,0:T(8,128)(2,1)S(1)} reduce(bf16[2,8,2,2,32,256]{5,4,3,2,1,0:T(8,128)(2,1)} %bitcast.16, bf16[]{:T(256)} %constant.41.clone.1), dimensions={1}, to_apply=%region_0.1 | reduce | flops 458752 | bytes 1179650 | tf_op jit(solution)/shard_map/reduce_sum | solution.py:108
  121.7 0.7 copy.22
  (30 shorter events, 0.3 us)
Async XLA Ops:
  1.6 10.2 %collective-permute-start.1 = (bf16[1,2,32,256]{3,2,1,0:T(8,128)(2,1)S(1)}, bf16[1,2,32,256]{3,2,1,0:T(8,128)(2,1)S(1)}, u32[]{:S(2)}, u32[]{:S(2)}) collective-permute-start(bf16[1,2,32,256]{3,2,1,0:T(8,128)(2,1)S(1)} %get-tuple-element.70), channel_id=1, source_target_pairs={{0,1},{1,0},{256,257},{257,256},{2,3},{3,2},{258,259},{259,258},{4... | collective-permute-start | bytes 98312 | tf_op jit(solution)/shard_map/ppermute | solution.py:14
  7.1 8.4 %collective-permute-start = (bf16[1,2,32,256]{3,2,1,0:T(8,128)(2,1)S(1)}, bf16[1,2,32,256]{3,2,1,0:T(8,128)(2,1)S(1)}, u32[]{:S(2)}, u32[]{:S(2)}) collective-permute-start(bf16[1,2,32,256]{3,2,1,0:T(8,128)(2,1)S(1)} %get-tuple-element.69), channel_id=1, source_target_pairs={{0,256},{1,257},{256,0},{257,1},{2,258},{3,259},{258,2},{259,3},{4... | collective-permute-start | bytes 98312 | tf_op jit(solution)/shard_map/ppermute | solution.py:14
  9.3 6.1 %collective-permute-start.2 = (bf16[1,2,32,256]{3,2,1,0:T(8,128)(2,1)S(1)}, bf16[1,2,32,256]{3,2,1,0:T(8,128)(2,1)S(1)}, u32[]{:S(2)}, u32[]{:S(2)}) collective-permute-start(bf16[1,2,32,256]{3,2,1,0:T(8,128)(2,1)S(1)} %get-tuple-element.71), channel_id=1, source_target_pairs={{0,257},{1,256},{256,1},{257,0},{2,259},{3,258},{258,3},{259,2},{4... | collective-permute-start | bytes 98312 | tf_op jit(solution)/shard_map/ppermute | solution.py:14
  15.5 19.6 %copy-start = (bf16[256,640]{1,0:T(8,128)(2,1)S(1)}, bf16[256,640]{1,0:T(8,128)(2,1)}, u32[]{:S(2)}) copy-start(bf16[256,640]{1,0:T(8,128)(2,1)} %param.5) | copy-start | bytes 983044
  17.7 47.8 %all-to-all-start = ((bf16[32,32,640]{2,1,0:T(8,128)(2,1)}), bf16[32,32,640]{2,1,0:T(8,128)(2,1)S(1)}, u32[]{:S(2)}, u32[]{:S(2)}) async-start(bf16[32,32,640]{2,1,0:T(8,128)(2,1)} %bitcast.7), calls=%async_computation | async-start | bytes 2621440 | tf_op jit(solution)/shard_map/all_to_all | solution.py:28
  28.1 16.7 %collective-permute-start.9 = (bf16[128,512]{1,0:T(8,128)(2,1)S(1)}, bf16[128,512]{1,0:T(8,128)(2,1)S(1)}, u32[]{:S(2)}, u32[]{:S(2)}) collective-permute-start(bf16[128,512]{1,0:T(8,128)(2,1)S(1)} %bitcast.42), channel_id=1, source_target_pairs={{0,14},{2,0},{4,2},{6,4},{8,6},{10,8},{12,10},{14,12},{1,15},{3,1}... | collective-permute-start | bytes 393224 | tf_op jit(solution)/shard_map/ppermute | solution.py:49
  33.2 16.1 %collective-permute-start.6 = (bf16[128,512]{1,0:T(8,128)(2,1)S(1)}, bf16[128,512]{1,0:T(8,128)(2,1)}, u32[]{:S(2)}, u32[]{:S(2)}) collective-permute-start(bf16[128,512]{1,0:T(8,128)(2,1)S(1)} %bitcast.43), channel_id=1, source_target_pairs={{0,2},{2,4},{4,6},{6,8},{8,10},{10,12},{12,14},{14,0},{1,3},{3,5},... | collective-permute-start | bytes 393224 | tf_op jit(solution)/shard_map/ppermute | solution.py:48
  35.1 23.6 %collective-permute-start.5 = (bf16[256,640]{1,0:T(8,128)(2,1)S(1)}, bf16[256,640]{1,0:T(8,128)(2,1)S(1)}, u32[]{:S(2)}, u32[]{:S(2)}) collective-permute-start(bf16[256,640]{1,0:T(8,128)(2,1)S(1)} %copy-done), channel_id=1, source_target_pairs={{0,257},{1,256},{256,1},{257,0},{2,259},{3,258},{258,3},{259,2},{4... | collective-permute-start | bytes 983048 | tf_op jit(solution)/shard_map/ppermute | solution.py:14
  39.5 19.2 %collective-permute-start.4 = (bf16[256,640]{1,0:T(8,128)(2,1)S(1)}, bf16[256,640]{1,0:T(8,128)(2,1)S(1)}, u32[]{:S(2)}, u32[]{:S(2)}) collective-permute-start(bf16[256,640]{1,0:T(8,128)(2,1)S(1)} %copy-done), channel_id=1, source_target_pairs={{0,256},{1,257},{256,0},{257,1},{2,258},{3,259},{258,2},{259,3},{4... | collective-permute-start | bytes 983048 | tf_op jit(solution)/shard_map/ppermute | solution.py:14
  41.5 23.3 %collective-permute-start.3 = (bf16[256,640]{1,0:T(8,128)(2,1)S(1)}, bf16[256,640]{1,0:T(8,128)(2,1)S(1)}, u32[]{:S(2)}, u32[]{:S(2)}) collective-permute-start(bf16[256,640]{1,0:T(8,128)(2,1)S(1)} %copy-done), channel_id=1, source_target_pairs={{0,1},{1,0},{256,257},{257,256},{2,3},{3,2},{258,259},{259,258},{4... | collective-permute-start | bytes 983048 | tf_op jit(solution)/shard_map/ppermute | solution.py:14
  44.8 6.5 %collective-permute-start.10 = (bf16[128,512]{1,0:T(8,128)(2,1)S(1)}, bf16[128,512]{1,0:T(8,128)(2,1)S(1)}, u32[]{:S(2)}, u32[]{:S(2)}) collective-permute-start(bf16[128,512]{1,0:T(8,128)(2,1)S(1)} %collective-permute-done.9), channel_id=1, source_target_pairs={{0,14},{2,0},{4,2},{6,4},{8,6},{10,8},{12,10},{14,12},{1,15},{3,1}... | collective-permute-start | bytes 393224 | tf_op jit(solution)/shard_map/ppermute | solution.py:49
  49.4 7.4 %collective-permute-start.7 = (bf16[128,512]{1,0:T(8,128)(2,1)}, bf16[128,512]{1,0:T(8,128)(2,1)S(1)}, u32[]{:S(2)}, u32[]{:S(2)}) collective-permute-start(bf16[128,512]{1,0:T(8,128)(2,1)} %collective-permute-done.6), channel_id=1, source_target_pairs={{0,2},{2,4},{4,6},{6,8},{8,10},{10,12},{12,14},{14,0},{1,3},{3,5},... | collective-permute-start | bytes 393224 | tf_op jit(solution)/shard_map/ppermute | solution.py:48
  51.3 13.4 %collective-permute-start.11 = (bf16[128,512]{1,0:T(8,128)(2,1)S(1)}, bf16[128,512]{1,0:T(8,128)(2,1)S(1)}, u32[]{:S(2)}, u32[]{:S(2)}) collective-permute-start(bf16[128,512]{1,0:T(8,128)(2,1)S(1)} %collective-permute-done.10), channel_id=1, source_target_pairs={{0,14},{2,0},{4,2},{6,4},{8,6},{10,8},{12,10},{14,12},{1,15},{3,1}... | collective-permute-start | bytes 393224 | tf_op jit(solution)/shard_map/ppermute | solution.py:49
  56.8 8.0 %collective-permute-start.8 = (bf16[128,512]{1,0:T(8,128)(2,1)S(1)}, bf16[128,512]{1,0:T(8,128)(2,1)S(1)}, u32[]{:S(2)}, u32[]{:S(2)}) collective-permute-start(bf16[128,512]{1,0:T(8,128)(2,1)S(1)} %collective-permute-done.7), channel_id=1, source_target_pairs={{0,2},{2,4},{4,6},{6,8},{8,10},{10,12},{12,14},{14,0},{1,3},{3,5},... | collective-permute-start | bytes 393224 | tf_op jit(solution)/shard_map/ppermute | solution.py:48
  58.7 6.0 %copy-start.2 = (bf16[256,640]{1,0:T(8,128)(2,1)}, bf16[256,640]{1,0:T(8,128)(2,1)S(1)}, u32[]{:S(2)}) copy-start(bf16[256,640]{1,0:T(8,128)(2,1)S(1)} %collective-permute-done.5) | copy-start | bytes 983044
  58.7 6.0 %copy-start.4 = (bf16[256,640]{1,0:T(8,128)(2,1)}, bf16[256,640]{1,0:T(8,128)(2,1)S(1)}, u32[]{:S(2)}) copy-start(bf16[256,640]{1,0:T(8,128)(2,1)S(1)} %collective-permute-done.4) | copy-start | bytes 983044
  64.7 0.7 copy-start.6
  65.5 9.1 %collective-permute-start.12 = (bf16[32,32,640]{2,1,0:T(8,128)(2,1)S(1)}, bf16[32,32,640]{2,1,0:T(8,128)(2,1)S(1)}, u32[]{:S(2)}, u32[]{:S(2)}) collective-permute-start(bf16[32,32,640]{2,1,0:T(8,128)(2,1)S(1)} %all-to-all-done), channel_id=1, source_target_pairs={{0,16},{16,0},{1,17},{17,1},{2,18},{18,2},{3,19},{19,3},{4,20},{20... | collective-permute-start | bytes 3932168 | tf_op jit(solution)/shard_map/ppermute | solution.py:10
  72.0 2.2 %copy-start.1 = (bf16[256,640]{1,0:T(8,128)(2,1)S(1)}, bf16[256,640]{1,0:T(8,128)(2,1)}, u32[]{:S(2)}) copy-start(bf16[256,640]{1,0:T(8,128)(2,1)} %param.5) | copy-start | bytes 983044
  72.0 2.2 %copy-start.3 = (bf16[256,640]{1,0:T(8,128)(2,1)S(1)}, bf16[256,640]{1,0:T(8,128)(2,1)}, u32[]{:S(2)}) copy-start(bf16[256,640]{1,0:T(8,128)(2,1)} %copy-done.2) | copy-start | bytes 983044
  72.0 2.2 %copy-start.5 = (bf16[256,640]{1,0:T(8,128)(2,1)S(1)}, bf16[256,640]{1,0:T(8,128)(2,1)}, u32[]{:S(2)}) copy-start(bf16[256,640]{1,0:T(8,128)(2,1)} %copy-done.4) | copy-start | bytes 983044
  72.0 2.2 %copy-start.7 = (bf16[256,640]{1,0:T(8,128)(2,1)S(1)}, bf16[256,640]{1,0:T(8,128)(2,1)}, u32[]{:S(2)}) copy-start(bf16[256,640]{1,0:T(8,128)(2,1)} %copy-done.6) | copy-start | bytes 983044
  72.0 8.4 %collective-permute-start.13 = (bf16[128,512]{1,0:T(8,128)(2,1)S(1)}, bf16[128,512]{1,0:T(8,128)(2,1)S(1)}, u32[]{:S(2)}, u32[]{:S(2)}) collective-permute-start(bf16[128,512]{1,0:T(8,128)(2,1)S(1)} %collective-permute-done.8), channel_id=1, source_target_pairs={{0,2},{2,4},{4,6},{6,8},{8,10},{10,12},{12,14},{14,0},{1,3},{3,5},... | collective-permute-start | bytes 393224 | tf_op jit(solution)/shard_map/ppermute | solution.py:51
  81.4 38.8 %all-to-all-start.1 = ((bf16[32,64,256]{2,1,0:T(8,128)(2,1)}), bf16[32,64,256]{2,1,0:T(8,128)(2,1)}, u32[]{:S(2)}, u32[]{:S(2)}) async-start(bf16[32,64,256]{2,1,0:T(8,128)(2,1)} %bitcast.40), calls=%async_computation.1 | async-start | bytes 2097152 | tf_op jit(solution)/shard_map/all_to_all | solution.py:28
  91.2 19.0 %collective-permute-start.15 = (bf16[256,640]{1,0:T(8,128)(2,1)S(1)}, bf16[256,640]{1,0:T(8,128)(2,1)S(1)}, u32[]{:S(2)}, u32[]{:S(2)}) collective-permute-start(bf16[256,640]{1,0:T(8,128)(2,1)S(1)} %dynamic-slice_convert_fusion.1), channel_id=1, source_target_pairs={{0,1},{1,0},{256,257},{257,256},{2,3},{3,2},{258,259},{259,258},{4... | collective-permute-start | bytes 983048 | tf_op jit(solution)/shard_map/ppermute | solution.py:14
  95.8 23.4 %collective-permute-start.14 = (bf16[256,640]{1,0:T(8,128)(2,1)S(1)}, bf16[256,640]{1,0:T(8,128)(2,1)S(1)}, u32[]{:S(2)}, u32[]{:S(2)}) collective-permute-start(bf16[256,640]{1,0:T(8,128)(2,1)S(1)} %get-tuple-element.58), channel_id=1, source_target_pairs={{0,256},{1,257},{256,0},{257,1},{2,258},{3,259},{258,2},{259,3},{4... | collective-permute-start | bytes 983048 | tf_op jit(solution)/shard_map/ppermute | solution.py:14
  98.1 21.2 %collective-permute-start.16 = (bf16[256,640]{1,0:T(8,128)(2,1)S(1)}, bf16[256,640]{1,0:T(8,128)(2,1)S(1)}, u32[]{:S(2)}, u32[]{:S(2)}) collective-permute-start(bf16[256,640]{1,0:T(8,128)(2,1)S(1)} %get-tuple-element.59), channel_id=1, source_target_pairs={{0,257},{1,256},{256,1},{257,0},{2,259},{3,258},{258,3},{259,2},{4... | collective-permute-start | bytes 983048 | tf_op jit(solution)/shard_map/ppermute | solution.py:14

commit v12 on v11

--- a/solution.py
+++ b/solution.py
@@ -65,6 +65,11 @@
     features = inputs.shape[1]
     part = tokens // 4
 
+    grads = jnp.broadcast_to(
+        out_grad.reshape(4, 1, part, columns), (4, depth, part, columns)
+    ).reshape(-1, part, columns)
+    grads = exchange(grads, ("xl", "xh", "z"))
+
     acts = inputs.reshape(2, 4, part, features)
     acts = jnp.concatenate([pick(acts, core, 0), pick(acts, 1 - core, 0)], axis=0)
 
@@ -75,12 +80,7 @@
     came[0, 0] = quarter(0, 0)
     rows = [jnp.concatenate([came[0, b], came[1, b]], axis=3) for b in range(2)]
     acts = in_order(far, rows[0], rows[1], 0).reshape(4 * part, 2 * features)
-    acts, out_grad, weight = lax.optimization_barrier((acts, out_grad, weight))
-
-    grads = jnp.broadcast_to(
-        out_grad.reshape(4, 1, part, columns), (4, depth, part, columns)
-    ).reshape(-1, part, columns)
-    grads = exchange(grads, ("xl", "xh", "z"))
+    acts, weight = lax.optimization_barrier((acts, weight))
 
     came = {(a, b): to_partner(weight, a, b) for a, b in PAIRS}
     came[0, 0] = weight

time: 124 us -> 124 us (level)
  starting transfers between devices: 75.5 us -> 77.7 us
  local copies, waits for them, and re-layouts: 6.23 us -> 4.65 us
    ppermute x9, waiting for transfers between devices: 28.2 us -> 22.1 us  [to_partner(): lax.ppermute(block, ('xl', 'xh'), [(i, i ^ 2 * a + b) for i in range(4)])]
    ppermute x3, waiting for transfers between devices: 0.24 us -> 5.15 us  [ring_gather(): rising.append(lax.ppermute(rising[-1], axis, up))]
    ppermute x1, starting transfers between devices: 6.47 us -> 8.22 us  [swap(): return lax.ppermute(block, axis, ((0, 1), (1, 0)))]
    all_to_all x2, starting transfers between devices: 17.2 us -> 18.5 us  [exchange(): return lax.all_to_all(pieces, axes, split_axis=0, concat_axis=0, tiled=True)]
where the time goes in v12:
time: 124 us; the launch traced here: 122 us
  starting transfers between devices  77.7 us (63%)
  waiting for transfers between devices  30.8 us (25%)
  local copies, waits for them, and re-layouts  4.65 us (4%)
  other arithmetic  3.97 us (3%)
  matrix products  3.38 us (3%)
  between operations  1.3 us (1%)
    ppermute x9, starting transfers between devices, to_partner(): lax.ppermute(block, ('xl', 'xh'), [(i, i ^ 2 * a + b) for i in range(4)])  28.3 us
    ppermute x9, waiting for transfers between devices, to_partner(): lax.ppermute(block, ('xl', 'xh'), [(i, i ^ 2 * a + b) for i in range(4)])  22.1 us
    all_to_all x2, starting transfers between devices, exchange(): return lax.all_to_all(pieces, axes, split_axis=0, concat_axis=0, tiled=True)  18.5 us
    ppermute x3, starting transfers between devices, ring_gather(): falling.append(lax.ppermute(falling[-1], axis, down))  14.9 us
    ppermute x1, starting transfers between devices, swap(): return lax.ppermute(block, axis, ((0, 1), (1, 0)))  8.22 us
    ppermute x3, starting transfers between devices, ring_gather(): rising.append(lax.ppermute(rising[-1], axis, up))  5.75 us
    ppermute x3, waiting for transfers between devices, ring_gather(): rising.append(lax.ppermute(rising[-1], axis, up))  5.15 us
    dot_general x3, matrix products, times(): lax.dot_general(left, right, (((left_dim,), (right_dim,)), ((), ())), pre...  3.38 us
  transfers between devices with their start and end apart: 19, of which 7 were waited for; matrix products, arithmetic and copies ran while one was open for 5% of the time, Pallas kernels for 0%

profile of v12, /device:TPU:1, one launch (start us, length us, event | category | flops | bytes accessed | tf_op | source)
XLA Modules:
  0.0 121.8 jit_solution(3074293102848256902)
XLA Ops:
  0.6 0.0 copy-start.8
  0.6 2.1 %broadcast_in_dim.8 = bf16[4,8,32,640]{3,2,1,0:T(8,128)(2,1)} broadcast(bf16[4,32,640]{2,1,0:T(8,128)(2,1)} %bitcast.47), dimensions={0,2,3} | broadcast | bytes 1474560 | tf_op jit(solution)/shard_map/broadcast_in_dim | solution.py:68
  2.8 13.8 %all-to-all-start = ((bf16[32,32,640]{2,1,0:T(8,128)(2,1)}), bf16[32,32,640]{2,1,0:T(8,128)(2,1)S(1)}, u32[]{:S(2)}, u32[]{:S(2)}) async-start(bf16[32,32,640]{2,1,0:T(8,128)(2,1)} %bitcast.1), calls=%async_computation | async-start | bytes 2621440 | tf_op jit(solution)/shard_map/all_to_all | solution.py:28
  16.7 0.0 copy-done.8
  16.7 4.6 %collective-permute-start.1 = (bf16[1,2,32,256]{3,2,1,0:T(8,128)(2,1)S(1)}, bf16[1,2,32,256]{3,2,1,0:T(8,128)(2,1)S(1)}, u32[]{:S(2)}, u32[]{:S(2)}) collective-permute-start(bf16[1,2,32,256]{3,2,1,0:T(8,128)(2,1)S(1)} %get-tuple-element.68), channel_id=1, source_target_pairs={{0,1},{1,0},{256,257},{257,256},{2,3},{3,2},{258,259},{259,258},{4... | collective-permute-start | bytes 98312 | tf_op jit(solution)/shard_map/ppermute | solution.py:14
  21.4 2.2 %collective-permute-start = (bf16[1,2,32,256]{3,2,1,0:T(8,128)(2,1)S(1)}, bf16[1,2,32,256]{3,2,1,0:T(8,128)(2,1)S(1)}, u32[]{:S(2)}, u32[]{:S(2)}) collective-permute-start(bf16[1,2,32,256]{3,2,1,0:T(8,128)(2,1)S(1)} %get-tuple-element.67), channel_id=1, source_target_pairs={{0,256},{1,257},{256,0},{257,1},{2,258},{3,259},{258,2},{259,3},{4... | collective-permute-start | bytes 98312 | tf_op jit(solution)/shard_map/ppermute | solution.py:14
  23.6 2.5 %collective-permute-start.2 = (bf16[1,2,32,256]{3,2,1,0:T(8,128)(2,1)S(1)}, bf16[1,2,32,256]{3,2,1,0:T(8,128)(2,1)S(1)}, u32[]{:S(2)}, u32[]{:S(2)}) collective-permute-start(bf16[1,2,32,256]{3,2,1,0:T(8,128)(2,1)S(1)} %get-tuple-element.69), channel_id=1, source_target_pairs={{0,257},{1,256},{256,1},{257,0},{2,259},{3,258},{258,3},{259,2},{4... | collective-permute-start | bytes 98312 | tf_op jit(solution)/shard_map/ppermute | solution.py:14
  26.1 0.0 collective-permute-done.1
  26.1 3.9 %collective-permute-done.2 = bf16[1,2,32,256]{3,2,1,0:T(8,128)(2,1)S(1)} collective-permute-done((bf16[1,2,32,256]{3,2,1,0:T(8,128)(2,1)S(1)}, bf16[1,2,32,256]{3,2,1,0:T(8,128)(2,1)S(1)}, u32[]{:S(2)}, u32[]{:S(2)}) %collective-permute-start.2) | collective-permute-done | bytes 32800 | tf_op jit(solution)/shard_map/ppermute | solution.py:14
  30.0 0.0 collective-permute-done
  30.1 5.1 %collective-permute-start.9 = (bf16[128,512]{1,0:T(8,128)(2,1)S(1)}, bf16[128,512]{1,0:T(8,128)(2,1)S(1)}, u32[]{:S(2)}, u32[]{:S(2)}) collective-permute-start(bf16[128,512]{1,0:T(8,128)(2,1)S(1)} %bitcast.42), channel_id=1, source_target_pairs={{0,14},{2,0},{4,2},{6,4},{8,6},{10,8},{12,10},{14,12},{1,15},{3,1}... | collective-permute-start | bytes 393224 | tf_op jit(solution)/shard_map/ppermute | solution.py:49
  35.2 1.9 %collective-permute-start.6 = (bf16[128,512]{1,0:T(8,128)(2,1)S(1)}, bf16[128,512]{1,0:T(8,128)(2,1)}, u32[]{:S(2)}, u32[]{:S(2)}) collective-permute-start(bf16[128,512]{1,0:T(8,128)(2,1)S(1)} %bitcast.43), channel_id=1, source_target_pairs={{0,2},{2,4},{4,6},{6,8},{8,10},{10,12},{12,14},{14,0},{1,3},{3,5},... | collective-permute-start | bytes 393224 | tf_op jit(solution)/shard_map/ppermute | solution.py:48
  37.1 0.0 copy-done
  37.1 3.5 %collective-permute-start.5 = (bf16[256,640]{1,0:T(8,128)(2,1)S(1)}, bf16[256,640]{1,0:T(8,128)(2,1)S(1)}, u32[]{:S(2)}, u32[]{:S(2)}) collective-permute-start(bf16[256,640]{1,0:T(8,128)(2,1)S(1)} %copy-done), channel_id=1, source_target_pairs={{0,257},{1,256},{256,1},{257,0},{2,259},{3,258},{258,3},{259,2},{4... | collective-permute-start | bytes 983048 | tf_op jit(solution)/shard_map/ppermute | solution.py:14
  40.7 1.9 %collective-permute-start.4 = (bf16[256,640]{1,0:T(8,128)(2,1)S(1)}, bf16[256,640]{1,0:T(8,128)(2,1)S(1)}, u32[]{:S(2)}, u32[]{:S(2)}) collective-permute-start(bf16[256,640]{1,0:T(8,128)(2,1)S(1)} %copy-done), channel_id=1, source_target_pairs={{0,256},{1,257},{256,0},{257,1},{2,258},{3,259},{258,2},{259,3},{4... | collective-permute-start | bytes 983048 | tf_op jit(solution)/shard_map/ppermute | solution.py:14
  42.6 4.2 %collective-permute-start.3 = (bf16[256,640]{1,0:T(8,128)(2,1)S(1)}, bf16[256,640]{1,0:T(8,128)(2,1)S(1)}, u32[]{:S(2)}, u32[]{:S(2)}) collective-permute-start(bf16[256,640]{1,0:T(8,128)(2,1)S(1)} %copy-done), channel_id=1, source_target_pairs={{0,1},{1,0},{256,257},{257,256},{2,3},{3,2},{258,259},{259,258},{4... | collective-permute-start | bytes 983048 | tf_op jit(solution)/shard_map/ppermute | solution.py:14
  46.8 0.0 collective-permute-done.9
  46.8 4.6 %collective-permute-start.10 = (bf16[128,512]{1,0:T(8,128)(2,1)S(1)}, bf16[128,512]{1,0:T(8,128)(2,1)S(1)}, u32[]{:S(2)}, u32[]{:S(2)}) collective-permute-start(bf16[128,512]{1,0:T(8,128)(2,1)S(1)} %collective-permute-done.9), channel_id=1, source_target_pairs={{0,14},{2,0},{4,2},{6,4},{8,6},{10,8},{12,10},{14,12},{1,15},{3,1}... | collective-permute-start | bytes 393224 | tf_op jit(solution)/shard_map/ppermute | solution.py:49
  51.3 0.0 collective-permute-done.6
  51.4 1.9 %collective-permute-start.7 = (bf16[128,512]{1,0:T(8,128)(2,1)}, bf16[128,512]{1,0:T(8,128)(2,1)S(1)}, u32[]{:S(2)}, u32[]{:S(2)}) collective-permute-start(bf16[128,512]{1,0:T(8,128)(2,1)} %collective-permute-done.6), channel_id=1, source_target_pairs={{0,2},{2,4},{4,6},{6,8},{8,10},{10,12},{12,14},{14,0},{1,3},{3,5},... | collective-permute-start | bytes 393224 | tf_op jit(solution)/shard_map/ppermute | solution.py:48
  53.3 0.0 collective-permute-done.10
  53.3 5.2 %collective-permute-start.11 = (bf16[128,512]{1,0:T(8,128)(2,1)S(1)}, bf16[128,512]{1,0:T(8,128)(2,1)S(1)}, u32[]{:S(2)}, u32[]{:S(2)}) collective-permute-start(bf16[128,512]{1,0:T(8,128)(2,1)S(1)} %collective-permute-done.10), channel_id=1, source_target_pairs={{0,14},{2,0},{4,2},{6,4},{8,6},{10,8},{12,10},{14,12},{1,15},{3,1}... | collective-permute-start | bytes 393224 | tf_op jit(solution)/shard_map/ppermute | solution.py:49
  58.5 0.2 collective-permute-done.7
  58.8 1.9 %collective-permute-start.8 = (bf16[128,512]{1,0:T(8,128)(2,1)S(1)}, bf16[128,512]{1,0:T(8,128)(2,1)S(1)}, u32[]{:S(2)}, u32[]{:S(2)}) collective-permute-start(bf16[128,512]{1,0:T(8,128)(2,1)S(1)} %collective-permute-done.7), channel_id=1, source_target_pairs={{0,2},{2,4},{4,6},{6,8},{8,10},{10,12},{12,14},{14,0},{1,3},{3,5},... | collective-permute-start | bytes 393224 | tf_op jit(solution)/shard_map/ppermute | solution.py:48
  60.7 0.0 collective-permute-done.5
  60.7 0.0 copy-start.2
  60.7 0.0 collective-permute-done.4
  60.7 0.0 copy-start.4
  60.7 0.0 collective-permute-done.3
  60.8 0.0 collective-permute-done.11
  60.8 4.9 %collective-permute-done.8 = bf16[128,512]{1,0:T(8,128)(2,1)S(1)} collective-permute-done((bf16[128,512]{1,0:T(8,128)(2,1)S(1)}, bf16[128,512]{1,0:T(8,128)(2,1)S(1)}, u32[]{:S(2)}, u32[]{:S(2)}) %collective-permute-start.8) | collective-permute-done | bytes 131104 | tf_op jit(solution)/shard_map/ppermute | solution.py:48
  65.7 0.0 copy-done.4
  65.7 0.0 all-to-all-done
  65.7 8.2 %collective-permute-start.12 = (bf16[32,32,640]{2,1,0:T(8,128)(2,1)S(1)}, bf16[32,32,640]{2,1,0:T(8,128)(2,1)S(1)}, u32[]{:S(2)}, u32[]{:S(2)}) collective-permute-start(bf16[32,32,640]{2,1,0:T(8,128)(2,1)S(1)} %all-to-all-done), channel_id=1, source_target_pairs={{0,16},{16,0},{1,17},{17,1},{2,18},{18,2},{3,19},{19,3},{4,20},{20... | collective-permute-start | bytes 3932168 | tf_op jit(solution)/shard_map/ppermute | solution.py:10
  74.0 0.0 copy-start.1
  74.0 0.0 copy-start.3
  74.0 0.0 copy-start.5
  74.0 2.1 %collective-permute-start.13 = (bf16[128,512]{1,0:T(8,128)(2,1)S(1)}, bf16[128,512]{1,0:T(8,128)(2,1)S(1)}, u32[]{:S(2)}, u32[]{:S(2)}) collective-permute-start(bf16[128,512]{1,0:T(8,128)(2,1)S(1)} %collective-permute-done.8), channel_id=1, source_target_pairs={{0,2},{2,4},{4,6},{6,8},{8,10},{10,12},{12,14},{14,0},{1,3},{3,5},... | collective-permute-start | bytes 393224 | tf_op jit(solution)/shard_map/ppermute | solution.py:51
  76.1 0.1 slice_bitcast_fusion.3
  76.2 0.1 broadcast_select_fusion.1
  76.4 0.2 collective-permute-done.12
  76.6 0.1 slice_bitcast_fusion.1
  76.7 0.3 maximum_maximum_fusion
  77.0 0.2 copy.21
  77.3 0.9 convolution_convert_fusion
  78.2 0.9 convolution_convert_fusion.1
  79.1 3.3 %collective-permute-done.13 = bf16[128,512]{1,0:T(8,128)(2,1)S(1)} collective-permute-done((bf16[128,512]{1,0:T(8,128)(2,1)S(1)}, bf16[128,512]{1,0:T(8,128)(2,1)S(1)}, u32[]{:S(2)}, u32[]{:S(2)}) %collective-permute-start.13) | collective-permute-done | bytes 131104 | tf_op jit(solution)/shard_map/ppermute | solution.py:51
  82.4 1.0 pad_maximum_fusion
  83.4 4.7 %all-to-all-start.1 = ((bf16[32,64,256]{2,1,0:T(8,128)(2,1)}), bf16[32,64,256]{2,1,0:T(8,128)(2,1)}, u32[]{:S(2)}, u32[]{:S(2)}) async-start(bf16[32,64,256]{2,1,0:T(8,128)(2,1)} %bitcast.40), calls=%async_computation.1 | async-start | bytes 2097152 | tf_op jit(solution)/shard_map/all_to_all | solution.py:28
  88.2 0.9 constant_dynamic-update-slice_fusion.9
  89.2 1.6 %fusion = f32[512,1280]{1,0:T(8,128)S(1)} fusion(bf16[1024,1280]{1,0:T(8,128)(2,1)S(1)} %bitcast.38, bf16[1920,512]{1,0:T(8,128)(2,1)S(1)} %constant_dynamic-update-slice_fusion.2, s32[]{:T(128)S(6)} %select_n.118), kind=kOutput, calls=%fused_computation.4 | convolution fusion | flops 1342177280 | bytes 6291460 | tf_op jit(solution)/shard_map/dot_general | solution.py:32
  90.8 0.1 slice.39
  90.9 0.1 slice.38
  91.0 4.5 %collective-permute-start.15 = (bf16[256,640]{1,0:T(8,128)(2,1)S(1)}, bf16[256,640]{1,0:T(8,128)(2,1)S(1)}, u32[]{:S(2)}, u32[]{:S(2)}) collective-permute-start(bf16[256,640]{1,0:T(8,128)(2,1)S(1)} %dynamic-slice_convert_fusion.1), channel_id=1, source_target_pairs={{0,1},{1,0},{256,257},{257,256},{2,3},{3,2},{258,259},{259,258},{4... | collective-permute-start | bytes 983048 | tf_op jit(solution)/shard_map/ppermute | solution.py:14
  95.5 0.1 dynamic-slice_convert_fusion.2
  95.6 2.3 %collective-permute-start.14 = (bf16[256,640]{1,0:T(8,128)(2,1)S(1)}, bf16[256,640]{1,0:T(8,128)(2,1)S(1)}, u32[]{:S(2)}, u32[]{:S(2)}) collective-permute-start(bf16[256,640]{1,0:T(8,128)(2,1)S(1)} %get-tuple-element.56), channel_id=1, source_target_pairs={{0,256},{1,257},{256,0},{257,1},{2,258},{3,259},{258,2},{259,3},{4... | collective-permute-start | bytes 983048 | tf_op jit(solution)/shard_map/ppermute | solution.py:14
  97.9 2.5 %collective-permute-start.16 = (bf16[256,640]{1,0:T(8,128)(2,1)S(1)}, bf16[256,640]{1,0:T(8,128)(2,1)S(1)}, u32[]{:S(2)}, u32[]{:S(2)}) collective-permute-start(bf16[256,640]{1,0:T(8,128)(2,1)S(1)} %get-tuple-element.57), channel_id=1, source_target_pairs={{0,257},{1,256},{256,1},{257,0},{2,259},{3,258},{258,3},{259,2},{4... | collective-permute-start | bytes 983048 | tf_op jit(solution)/shard_map/ppermute | solution.py:14
  100.5 8.4 %collective-permute-done.15 = bf16[256,640]{1,0:T(8,128)(2,1)S(1)} collective-permute-done((bf16[256,640]{1,0:T(8,128)(2,1)S(1)}, bf16[256,640]{1,0:T(8,128)(2,1)S(1)}, u32[]{:S(2)}, u32[]{:S(2)}) %collective-permute-start.15) | collective-permute-done | bytes 327712 | tf_op jit(solution)/shard_map/ppermute | solution.py:14
  108.8 9.9 %collective-permute-done.14 = bf16[256,640]{1,0:T(8,128)(2,1)S(1)} collective-permute-done((bf16[256,640]{1,0:T(8,128)(2,1)S(1)}, bf16[256,640]{1,0:T(8,128)(2,1)S(1)}, u32[]{:S(2)}, u32[]{:S(2)}) %collective-permute-start.14) | collective-permute-done | bytes 327712 | tf_op jit(solution)/shard_map/ppermute | solution.py:14
  118.7 0.0 collective-permute-done.16
  118.7 1.0 convert_add_fusion
  119.7 0.0 all-to-all-done.1
  119.7 1.4 %reduce_sum.12 = bf16[2,2,2,32,256]{4,3,2,1,0:T(8,128)(2,1)S(1)} reduce(bf16[2,8,2,2,32,256]{5,4,3,2,1,0:T(8,128)(2,1)} %bitcast.16, bf16[]{:T(256)} %constant.41.clone.1), dimensions={1}, to_apply=%region_0.1 | reduce | flops 458752 | bytes 1179650 | tf_op jit(solution)/shard_map/reduce_sum | solution.py:108
  121.1 0.7 copy.22
  (32 shorter events, 0.3 us)
Async XLA Ops:
  0.6 16.0 %copy-start.8 = (bf16[256,256]{1,0:T(8,128)(2,1)S(1)}, bf16[256,256]{1,0:T(8,128)(2,1)}, u32[]{:S(2)}) copy-start(bf16[256,256]{1,0:T(8,128)(2,1)} %param.3) | copy-start | bytes 393220
  2.8 34.4 %copy-start = (bf16[256,640]{1,0:T(8,128)(2,1)S(1)}, bf16[256,640]{1,0:T(8,128)(2,1)}, u32[]{:S(2)}) copy-start(bf16[256,640]{1,0:T(8,128)(2,1)} %param.5) | copy-start | bytes 983044
  2.8 62.9 %all-to-all-start = ((bf16[32,32,640]{2,1,0:T(8,128)(2,1)}), bf16[32,32,640]{2,1,0:T(8,128)(2,1)S(1)}, u32[]{:S(2)}, u32[]{:S(2)}) async-start(bf16[32,32,640]{2,1,0:T(8,128)(2,1)} %bitcast.1), calls=%async_computation | async-start | bytes 2621440 | tf_op jit(solution)/shard_map/all_to_all | solution.py:28
  16.7 9.4 %collective-permute-start.1 = (bf16[1,2,32,256]{3,2,1,0:T(8,128)(2,1)S(1)}, bf16[1,2,32,256]{3,2,1,0:T(8,128)(2,1)S(1)}, u32[]{:S(2)}, u32[]{:S(2)}) collective-permute-start(bf16[1,2,32,256]{3,2,1,0:T(8,128)(2,1)S(1)} %get-tuple-element.68), channel_id=1, source_target_pairs={{0,1},{1,0},{256,257},{257,256},{2,3},{3,2},{258,259},{259,258},{4... | collective-permute-start | bytes 98312 | tf_op jit(solution)/shard_map/ppermute | solution.py:14
  21.4 8.7 %collective-permute-start = (bf16[1,2,32,256]{3,2,1,0:T(8,128)(2,1)S(1)}, bf16[1,2,32,256]{3,2,1,0:T(8,128)(2,1)S(1)}, u32[]{:S(2)}, u32[]{:S(2)}) collective-permute-start(bf16[1,2,32,256]{3,2,1,0:T(8,128)(2,1)S(1)} %get-tuple-element.67), channel_id=1, source_target_pairs={{0,256},{1,257},{256,0},{257,1},{2,258},{3,259},{258,2},{259,3},{4... | collective-permute-start | bytes 98312 | tf_op jit(solution)/shard_map/ppermute | solution.py:14
  23.6 6.4 %collective-permute-start.2 = (bf16[1,2,32,256]{3,2,1,0:T(8,128)(2,1)S(1)}, bf16[1,2,32,256]{3,2,1,0:T(8,128)(2,1)S(1)}, u32[]{:S(2)}, u32[]{:S(2)}) collective-permute-start(bf16[1,2,32,256]{3,2,1,0:T(8,128)(2,1)S(1)} %get-tuple-element.69), channel_id=1, source_target_pairs={{0,257},{1,256},{256,1},{257,0},{2,259},{3,258},{258,3},{259,2},{4... | collective-permute-start | bytes 98312 | tf_op jit(solution)/shard_map/ppermute | solution.py:14
  30.1 16.7 %collective-permute-start.9 = (bf16[128,512]{1,0:T(8,128)(2,1)S(1)}, bf16[128,512]{1,0:T(8,128)(2,1)S(1)}, u32[]{:S(2)}, u32[]{:S(2)}) collective-permute-start(bf16[128,512]{1,0:T(8,128)(2,1)S(1)} %bitcast.42), channel_id=1, source_target_pairs={{0,14},{2,0},{4,2},{6,4},{8,6},{10,8},{12,10},{14,12},{1,15},{3,1}... | collective-permute-start | bytes 393224 | tf_op jit(solution)/shard_map/ppermute | solution.py:49
  35.2 16.1 %collective-permute-start.6 = (bf16[128,512]{1,0:T(8,128)(2,1)S(1)}, bf16[128,512]{1,0:T(8,128)(2,1)}, u32[]{:S(2)}, u32[]{:S(2)}) collective-permute-start(bf16[128,512]{1,0:T(8,128)(2,1)S(1)} %bitcast.43), channel_id=1, source_target_pairs={{0,2},{2,4},{4,6},{6,8},{8,10},{10,12},{12,14},{14,0},{1,3},{3,5},... | collective-permute-start | bytes 393224 | tf_op jit(solution)/shard_map/ppermute | solution.py:48
  37.1 23.6 %collective-permute-start.5 = (bf16[256,640]{1,0:T(8,128)(2,1)S(1)}, bf16[256,640]{1,0:T(8,128)(2,1)S(1)}, u32[]{:S(2)}, u32[]{:S(2)}) collective-permute-start(bf16[256,640]{1,0:T(8,128)(2,1)S(1)} %copy-done), channel_id=1, source_target_pairs={{0,257},{1,256},{256,1},{257,0},{2,259},{3,258},{258,3},{259,2},{4... | collective-permute-start | bytes 983048 | tf_op jit(solution)/shard_map/ppermute | solution.py:14
  40.7 20.1 %collective-permute-start.4 = (bf16[256,640]{1,0:T(8,128)(2,1)S(1)}, bf16[256,640]{1,0:T(8,128)(2,1)S(1)}, u32[]{:S(2)}, u32[]{:S(2)}) collective-permute-start(bf16[256,640]{1,0:T(8,128)(2,1)S(1)} %copy-done), channel_id=1, source_target_pairs={{0,256},{1,257},{256,0},{257,1},{2,258},{3,259},{258,2},{259,3},{4... | collective-permute-start | bytes 983048 | tf_op jit(solution)/shard_map/ppermute | solution.py:14
  42.6 18.2 %collective-permute-start.3 = (bf16[256,640]{1,0:T(8,128)(2,1)S(1)}, bf16[256,640]{1,0:T(8,128)(2,1)S(1)}, u32[]{:S(2)}, u32[]{:S(2)}) collective-permute-start(bf16[256,640]{1,0:T(8,128)(2,1)S(1)} %copy-done), channel_id=1, source_target_pairs={{0,1},{1,0},{256,257},{257,256},{2,3},{3,2},{258,259},{259,258},{4... | collective-permute-start | bytes 983048 | tf_op jit(solution)/shard_map/ppermute | solution.py:14
  46.8 6.5 %collective-permute-start.10 = (bf16[128,512]{1,0:T(8,128)(2,1)S(1)}, bf16[128,512]{1,0:T(8,128)(2,1)S(1)}, u32[]{:S(2)}, u32[]{:S(2)}) collective-permute-start(bf16[128,512]{1,0:T(8,128)(2,1)S(1)} %collective-permute-done.9), channel_id=1, source_target_pairs={{0,14},{2,0},{4,2},{6,4},{8,6},{10,8},{12,10},{14,12},{1,15},{3,1}... | collective-permute-start | bytes 393224 | tf_op jit(solution)/shard_map/ppermute | solution.py:49
  51.4 7.4 %collective-permute-start.7 = (bf16[128,512]{1,0:T(8,128)(2,1)}, bf16[128,512]{1,0:T(8,128)(2,1)S(1)}, u32[]{:S(2)}, u32[]{:S(2)}) collective-permute-start(bf16[128,512]{1,0:T(8,128)(2,1)} %collective-permute-done.6), channel_id=1, source_target_pairs={{0,2},{2,4},{4,6},{6,8},{8,10},{10,12},{12,14},{14,0},{1,3},{3,5},... | collective-permute-start | bytes 393224 | tf_op jit(solution)/shard_map/ppermute | solution.py:48
  53.3 7.5 %collective-permute-start.11 = (bf16[128,512]{1,0:T(8,128)(2,1)S(1)}, bf16[128,512]{1,0:T(8,128)(2,1)S(1)}, u32[]{:S(2)}, u32[]{:S(2)}) collective-permute-start(bf16[128,512]{1,0:T(8,128)(2,1)S(1)} %collective-permute-done.10), channel_id=1, source_target_pairs={{0,14},{2,0},{4,2},{6,4},{8,6},{10,8},{12,10},{14,12},{1,15},{3,1}... | collective-permute-start | bytes 393224 | tf_op jit(solution)/shard_map/ppermute | solution.py:49
  58.8 6.9 %collective-permute-start.8 = (bf16[128,512]{1,0:T(8,128)(2,1)S(1)}, bf16[128,512]{1,0:T(8,128)(2,1)S(1)}, u32[]{:S(2)}, u32[]{:S(2)}) collective-permute-start(bf16[128,512]{1,0:T(8,128)(2,1)S(1)} %collective-permute-done.7), channel_id=1, source_target_pairs={{0,2},{2,4},{4,6},{6,8},{8,10},{10,12},{12,14},{14,0},{1,3},{3,5},... | collective-permute-start | bytes 393224 | tf_op jit(solution)/shard_map/ppermute | solution.py:48
  60.7 5.0 %copy-start.2 = (bf16[256,640]{1,0:T(8,128)(2,1)}, bf16[256,640]{1,0:T(8,128)(2,1)S(1)}, u32[]{:S(2)}) copy-start(bf16[256,640]{1,0:T(8,128)(2,1)S(1)} %collective-permute-done.5) | copy-start | bytes 983044
  60.7 5.0 %copy-start.4 = (bf16[256,640]{1,0:T(8,128)(2,1)}, bf16[256,640]{1,0:T(8,128)(2,1)S(1)}, u32[]{:S(2)}) copy-start(bf16[256,640]{1,0:T(8,128)(2,1)S(1)} %collective-permute-done.4) | copy-start | bytes 983044
  60.8 4.9 %copy-start.6 = (bf16[256,640]{1,0:T(8,128)(2,1)}, bf16[256,640]{1,0:T(8,128)(2,1)S(1)}, u32[]{:S(2)}) copy-start(bf16[256,640]{1,0:T(8,128)(2,1)S(1)} %collective-permute-done.3) | copy-start | bytes 983044
  65.7 10.9 %collective-permute-start.12 = (bf16[32,32,640]{2,1,0:T(8,128)(2,1)S(1)}, bf16[32,32,640]{2,1,0:T(8,128)(2,1)S(1)}, u32[]{:S(2)}, u32[]{:S(2)}) collective-permute-start(bf16[32,32,640]{2,1,0:T(8,128)(2,1)S(1)} %all-to-all-done), channel_id=1, source_target_pairs={{0,16},{16,0},{1,17},{17,1},{2,18},{18,2},{3,19},{19,3},{4,20},{20... | collective-permute-start | bytes 3932168 | tf_op jit(solution)/shard_map/ppermute | solution.py:10
  74.0 2.2 %copy-start.1 = (bf16[256,640]{1,0:T(8,128)(2,1)S(1)}, bf16[256,640]{1,0:T(8,128)(2,1)}, u32[]{:S(2)}) copy-start(bf16[256,640]{1,0:T(8,128)(2,1)} %param.5) | copy-start | bytes 983044
  74.0 2.2 %copy-start.3 = (bf16[256,640]{1,0:T(8,128)(2,1)S(1)}, bf16[256,640]{1,0:T(8,128)(2,1)}, u32[]{:S(2)}) copy-start(bf16[256,640]{1,0:T(8,128)(2,1)} %copy-done.2) | copy-start | bytes 983044
  74.0 2.2 %copy-start.5 = (bf16[256,640]{1,0:T(8,128)(2,1)S(1)}, bf16[256,640]{1,0:T(8,128)(2,1)}, u32[]{:S(2)}) copy-start(bf16[256,640]{1,0:T(8,128)(2,1)} %copy-done.4) | copy-start | bytes 983044
  74.0 2.2 %copy-start.7 = (bf16[256,640]{1,0:T(8,128)(2,1)S(1)}, bf16[256,640]{1,0:T(8,128)(2,1)}, u32[]{:S(2)}) copy-start(bf16[256,640]{1,0:T(8,128)(2,1)} %copy-done.6) | copy-start | bytes 983044
  74.0 8.4 %collective-permute-start.13 = (bf16[128,512]{1,0:T(8,128)(2,1)S(1)}, bf16[128,512]{1,0:T(8,128)(2,1)S(1)}, u32[]{:S(2)}, u32[]{:S(2)}) collective-permute-start(bf16[128,512]{1,0:T(8,128)(2,1)S(1)} %collective-permute-done.8), channel_id=1, source_target_pairs={{0,2},{2,4},{4,6},{6,8},{8,10},{10,12},{12,14},{14,0},{1,3},{3,5},... | collective-permute-start | bytes 393224 | tf_op jit(solution)/shard_map/ppermute | solution.py:51
  83.4 36.3 %all-to-all-start.1 = ((bf16[32,64,256]{2,1,0:T(8,128)(2,1)}), bf16[32,64,256]{2,1,0:T(8,128)(2,1)}, u32[]{:S(2)}, u32[]{:S(2)}) async-start(bf16[32,64,256]{2,1,0:T(8,128)(2,1)} %bitcast.40), calls=%async_computation.1 | async-start | bytes 2097152 | tf_op jit(solution)/shard_map/all_to_all | solution.py:28
  91.0 17.8 %collective-permute-start.15 = (bf16[256,640]{1,0:T(8,128)(2,1)S(1)}, bf16[256,640]{1,0:T(8,128)(2,1)S(1)}, u32[]{:S(2)}, u32[]{:S(2)}) collective-permute-start(bf16[256,640]{1,0:T(8,128)(2,1)S(1)} %dynamic-slice_convert_fusion.1), channel_id=1, source_target_pairs={{0,1},{1,0},{256,257},{257,256},{2,3},{3,2},{258,259},{259,258},{4... | collective-permute-start | bytes 983048 | tf_op jit(solution)/shard_map/ppermute | solution.py:14
  95.6 23.1 %collective-permute-start.14 = (bf16[256,640]{1,0:T(8,128)(2,1)S(1)}, bf16[256,640]{1,0:T(8,128)(2,1)S(1)}, u32[]{:S(2)}, u32[]{:S(2)}) collective-permute-start(bf16[256,640]{1,0:T(8,128)(2,1)S(1)} %get-tuple-element.56), channel_id=1, source_target_pairs={{0,256},{1,257},{256,0},{257,1},{2,258},{3,259},{258,2},{259,3},{4... | collective-permute-start | bytes 983048 | tf_op jit(solution)/shard_map/ppermute | solution.py:14
  97.9 20.8 %collective-permute-start.16 = (bf16[256,640]{1,0:T(8,128)(2,1)S(1)}, bf16[256,640]{1,0:T(8,128)(2,1)S(1)}, u32[]{:S(2)}, u32[]{:S(2)}) collective-permute-start(bf16[256,640]{1,0:T(8,128)(2,1)S(1)} %get-tuple-element.57), channel_id=1, source_target_pairs={{0,257},{1,256},{256,1},{257,0},{2,259},{3,258},{258,3},{259,2},{4... | collective-permute-start | bytes 983048 | tf_op jit(solution)/shard_map/ppermute | solution.py:14

commit v13 on v12

--- a/solution.py
+++ b/solution.py
@@ -80,18 +80,17 @@
     came[0, 0] = quarter(0, 0)
     rows = [jnp.concatenate([came[0, b], came[1, b]], axis=3) for b in range(2)]
     acts = in_order(far, rows[0], rows[1], 0).reshape(4 * part, 2 * features)
+    weight = in_order(far, weight, swap(weight, "xh"), 1)
     acts, weight = lax.optimization_barrier((acts, weight))
 
-    came = {(a, b): to_partner(weight, a, b) for a, b in PAIRS}
-    came[0, 0] = weight
+    partner = swap(weight, "xl")
     gather = ring_gather(acts, "y")
     ring = next(gather)
-    grads, came, ring = lax.optimization_barrier((grads, came, ring))
+    grads, weight, partner, ring = lax.optimization_barrier((grads, weight, partner, ring))
     ring = gather.send(ring)
-    weights = [in_order(far, came[a, 0], came[a, 1], 1) for a in range(2)]
     weights = [
-        jnp.where(near == 0, weights[0], weights[1]),
-        jnp.where(near == 0, weights[1], weights[0]),
+        jnp.where(near == 0, weight, partner),
+        jnp.where(near == 0, partner, weight),
     ]
 
     panels = [

time: 124 us -> 138 us (1.11)
  waiting for transfers between devices: 30.8 us -> 42.2 us
  local copies, waits for them, and re-layouts: 4.65 us -> 7.91 us
    ppermute x1 -> x3, waiting for transfers between devices: 0.21 us -> 13.4 us  [swap(): return lax.ppermute(block, axis, ((0, 1), (1, 0)))]
    ppermute x9 -> x6, starting transfers between devices: 28.3 us -> 18.7 us  [to_partner(): lax.ppermute(block, ('xl', 'xh'), [(i, i ^ 2 * a + b) for i in range(4)])]
    ppermute x1 -> x3, starting transfers between devices: 8.22 us -> 16.6 us  [swap(): return lax.ppermute(block, axis, ((0, 1), (1, 0)))]
    unnamed x33 -> x43, local copies, waits for them, and re-layouts: 1.11 us -> 4.36 us
    ppermute x9 -> x6, waiting for transfers between devices: 22.1 us -> 19.9 us  [to_partner(): lax.ppermute(block, ('xl', 'xh'), [(i, i ^ 2 * a + b) for i in range(4)])]
    all_to_all x2, starting transfers between devices: 18.5 us -> 20.2 us  [exchange(): return lax.all_to_all(pieces, axes, split_axis=0, concat_axis=0, tiled=True)]
  transfers between devices with their start and end apart: 19 -> 18, of which waited for: 7 -> 8; matrix products, arithmetic and copies ran while one was open for 5% -> 6% of each run, Pallas kernels for 0% -> 0%
where the time goes in v13:
time: 138 us; the launch traced here: 137 us
  starting transfers between devices  78.2 us (57%)
  waiting for transfers between devices  42.2 us (31%)
  local copies, waits for them, and re-layouts  7.91 us (6%)
  other arithmetic  3.97 us (3%)
  matrix products  3.35 us (2%)
    all_to_all x2, starting transfers between devices, exchange(): return lax.all_to_all(pieces, axes, split_axis=0, concat_axis=0, tiled=True)  20.2 us
    ppermute x6, waiting for transfers between devices, to_partner(): lax.ppermute(block, ('xl', 'xh'), [(i, i ^ 2 * a + b) for i in range(4)])  19.9 us
    ppermute x6, starting transfers between devices, to_partner(): lax.ppermute(block, ('xl', 'xh'), [(i, i ^ 2 * a + b) for i in range(4)])  18.7 us
    ppermute x3, starting transfers between devices, swap(): return lax.ppermute(block, axis, ((0, 1), (1, 0)))  16.6 us
    ppermute x3, starting transfers between devices, ring_gather(): falling.append(lax.ppermute(falling[-1], axis, down))  15 us
    ppermute x3, waiting for transfers between devices, swap(): return lax.ppermute(block, axis, ((0, 1), (1, 0)))  13.4 us
    ppermute x3, starting transfers between devices, ring_gather(): rising.append(lax.ppermute(rising[-1], axis, up))  5.75 us
    ppermute x3, waiting for transfers between devices, ring_gather(): rising.append(lax.ppermute(rising[-1], axis, up))  5.61 us
  transfers between devices with their start and end apart: 18, of which 8 were waited for; matrix products, arithmetic and copies ran while one was open for 6% of the time, Pallas kernels for 0%

profile of v13, /device:TPU:1, one launch (start us, length us, event | category | flops | bytes accessed | tf_op | source)
XLA Modules:
  0.0 136.9 jit_solution(4453792228100139588)
XLA Ops:
  0.6 2.1 %broadcast_in_dim.8 = bf16[4,8,32,640]{3,2,1,0:T(8,128)(2,1)} broadcast(bf16[4,32,640]{2,1,0:T(8,128)(2,1)} %bitcast.47), dimensions={0,2,3} | broadcast | bytes 1474560 | tf_op jit(solution)/shard_map/broadcast_in_dim | solution.py:68
  2.8 13.8 %all-to-all-start = ((bf16[32,32,640]{2,1,0:T(8,128)(2,1)}), bf16[32,32,640]{2,1,0:T(8,128)(2,1)S(1)}, u32[]{:S(2)}, u32[]{:S(2)}) async-start(bf16[32,32,640]{2,1,0:T(8,128)(2,1)} %bitcast.1), calls=%async_computation | async-start | bytes 2621440 | tf_op jit(solution)/shard_map/all_to_all | solution.py:28
  16.7 4.6 %collective-permute-start.1 = (bf16[1,2,32,256]{3,2,1,0:T(8,128)(2,1)S(1)}, bf16[1,2,32,256]{3,2,1,0:T(8,128)(2,1)S(1)}, u32[]{:S(2)}, u32[]{:S(2)}) collective-permute-start(bf16[1,2,32,256]{3,2,1,0:T(8,128)(2,1)S(1)} %get-tuple-element.62), channel_id=1, source_target_pairs={{0,1},{1,0},{256,257},{257,256},{2,3},{3,2},{258,259},{259,258},{4... | collective-permute-start | bytes 98312 | tf_op jit(solution)/shard_map/ppermute | solution.py:14
  21.4 2.2 %collective-permute-start = (bf16[1,2,32,256]{3,2,1,0:T(8,128)(2,1)S(1)}, bf16[1,2,32,256]{3,2,1,0:T(8,128)(2,1)S(1)}, u32[]{:S(2)}, u32[]{:S(2)}) collective-permute-start(bf16[1,2,32,256]{3,2,1,0:T(8,128)(2,1)S(1)} %get-tuple-element.61), channel_id=1, source_target_pairs={{0,256},{1,257},{256,0},{257,1},{2,258},{3,259},{258,2},{259,3},{4... | collective-permute-start | bytes 98312 | tf_op jit(solution)/shard_map/ppermute | solution.py:14
  23.6 2.5 %collective-permute-start.2 = (bf16[1,2,32,256]{3,2,1,0:T(8,128)(2,1)S(1)}, bf16[1,2,32,256]{3,2,1,0:T(8,128)(2,1)S(1)}, u32[]{:S(2)}, u32[]{:S(2)}) collective-permute-start(bf16[1,2,32,256]{3,2,1,0:T(8,128)(2,1)S(1)} %get-tuple-element.63), channel_id=1, source_target_pairs={{0,257},{1,256},{256,1},{257,0},{2,259},{3,258},{258,3},{259,2},{4... | collective-permute-start | bytes 98312 | tf_op jit(solution)/shard_map/ppermute | solution.py:14
  26.1 4.3 %collective-permute-start.3 = (bf16[256,640]{1,0:T(8,128)(2,1)S(1)}, bf16[256,640]{1,0:T(8,128)(2,1)S(1)}, u32[]{:S(2)}, u32[]{:S(2)}) collective-permute-start(bf16[256,640]{1,0:T(8,128)(2,1)S(1)} %copy-done.8), channel_id=1, source_target_pairs={{0,1},{1,0},{2,3},{3,2},{4,5},{5,4},{6,7},{7,6},{8,9},{9,8},{10,11... | collective-permute-start | bytes 983048 | tf_op jit(solution)/shard_map/ppermute | solution.py:10
  30.4 0.0 collective-permute-done.1
  30.4 0.0 collective-permute-done.2
  30.5 0.0 collective-permute-done
  30.5 12.8 %collective-permute-done.3 = bf16[256,640]{1,0:T(8,128)(2,1)S(1)} collective-permute-done((bf16[256,640]{1,0:T(8,128)(2,1)S(1)}, bf16[256,640]{1,0:T(8,128)(2,1)S(1)}, u32[]{:S(2)}, u32[]{:S(2)}) %collective-permute-start.3) | collective-permute-done | bytes 327712 | tf_op jit(solution)/shard_map/ppermute | solution.py:10
  43.3 0.1 broadcast_select_fusion.1
  43.4 0.1 pad_maximum_fusion.1
  43.4 1.9 %collective-permute-start.4 = (bf16[256,1280]{1,0:T(8,128)(2,1)S(1)}, bf16[256,1280]{1,0:T(8,128)(2,1)S(1)}, u32[]{:S(2)}, u32[]{:S(2)}) collective-permute-start(bf16[256,1280]{1,0:T(8,128)(2,1)S(1)} %pad_maximum_fusion.1), channel_id=1, source_target_pairs={{0,256},{256,0},{1,257},{257,1},{2,258},{258,2},{3,259},{259,3},{4... | collective-permute-start | bytes 1966088 | tf_op jit(solution)/shard_map/ppermute | solution.py:10
  45.4 5.1 %collective-permute-start.8 = (bf16[128,512]{1,0:T(8,128)(2,1)S(1)}, bf16[128,512]{1,0:T(8,128)(2,1)S(1)}, u32[]{:S(2)}, u32[]{:S(2)}) collective-permute-start(bf16[128,512]{1,0:T(8,128)(2,1)S(1)} %bitcast.42), channel_id=1, source_target_pairs={{0,14},{2,0},{4,2},{6,4},{8,6},{10,8},{12,10},{14,12},{1,15},{3,1}... | collective-permute-start | bytes 393224 | tf_op jit(solution)/shard_map/ppermute | solution.py:49
  50.5 1.9 %collective-permute-start.5 = (bf16[128,512]{1,0:T(8,128)(2,1)S(1)}, bf16[128,512]{1,0:T(8,128)(2,1)S(1)}, u32[]{:S(2)}, u32[]{:S(2)}) collective-permute-start(bf16[128,512]{1,0:T(8,128)(2,1)S(1)} %bitcast.43), channel_id=1, source_target_pairs={{0,2},{2,4},{4,6},{6,8},{8,10},{10,12},{12,14},{14,0},{1,3},{3,5},... | collective-permute-start | bytes 393224 | tf_op jit(solution)/shard_map/ppermute | solution.py:48
  52.4 0.0 collective-permute-done.8
  52.4 5.0 %collective-permute-start.9 = (bf16[128,512]{1,0:T(8,128)(2,1)S(1)}, bf16[128,512]{1,0:T(8,128)(2,1)S(1)}, u32[]{:S(2)}, u32[]{:S(2)}) collective-permute-start(bf16[128,512]{1,0:T(8,128)(2,1)S(1)} %collective-permute-done.8), channel_id=1, source_target_pairs={{0,14},{2,0},{4,2},{6,4},{8,6},{10,8},{12,10},{14,12},{1,15},{3,1}... | collective-permute-start | bytes 393224 | tf_op jit(solution)/shard_map/ppermute | solution.py:49
  57.4 0.0 collective-permute-done.5
  57.4 1.9 %collective-permute-start.6 = (bf16[128,512]{1,0:T(8,128)(2,1)S(1)}, bf16[128,512]{1,0:T(8,128)(2,1)S(1)}, u32[]{:S(2)}, u32[]{:S(2)}) collective-permute-start(bf16[128,512]{1,0:T(8,128)(2,1)S(1)} %collective-permute-done.5), channel_id=1, source_target_pairs={{0,2},{2,4},{4,6},{6,8},{8,10},{10,12},{12,14},{14,0},{1,3},{3,5},... | collective-permute-start | bytes 393224 | tf_op jit(solution)/shard_map/ppermute | solution.py:48
  59.3 0.0 collective-permute-done.9
  59.3 0.0 copy-start.2
  59.4 4.9 %collective-permute-start.10 = (bf16[128,512]{1,0:T(8,128)(2,1)S(1)}, bf16[128,512]{1,0:T(8,128)(2,1)S(1)}, u32[]{:S(2)}, u32[]{:S(2)}) collective-permute-start(bf16[128,512]{1,0:T(8,128)(2,1)S(1)} %collective-permute-done.9), channel_id=1, source_target_pairs={{0,14},{2,0},{4,2},{6,4},{8,6},{10,8},{12,10},{14,12},{1,15},{3,1}... | collective-permute-start | bytes 393224 | tf_op jit(solution)/shard_map/ppermute | solution.py:49
  64.3 0.1 collective-permute-done.6
  64.4 1.9 %collective-permute-start.7 = (bf16[128,512]{1,0:T(8,128)(2,1)S(1)}, bf16[128,512]{1,0:T(8,128)(2,1)}, u32[]{:S(2)}, u32[]{:S(2)}) collective-permute-start(bf16[128,512]{1,0:T(8,128)(2,1)S(1)} %collective-permute-done.6), channel_id=1, source_target_pairs={{0,2},{2,4},{4,6},{6,8},{8,10},{10,12},{12,14},{14,0},{1,3},{3,5},... | collective-permute-start | bytes 393224 | tf_op jit(solution)/shard_map/ppermute | solution.py:48
  66.3 0.8 collective-permute-done.10
  67.2 5.5 %collective-permute-done.7 = bf16[128,512]{1,0:T(8,128)(2,1)} collective-permute-done((bf16[128,512]{1,0:T(8,128)(2,1)S(1)}, bf16[128,512]{1,0:T(8,128)(2,1)}, u32[]{:S(2)}, u32[]{:S(2)}) %collective-permute-start.7) | collective-permute-done | bytes 131104 | tf_op jit(solution)/shard_map/ppermute | solution.py:48
  72.7 0.0 collective-permute-done.4
  72.7 0.0 copy-start.12
  72.7 0.8 copy-done.12
  73.5 0.0 all-to-all-done
  73.5 10.4 %collective-permute-start.11 = (bf16[32,32,640]{2,1,0:T(8,128)(2,1)S(1)}, bf16[32,32,640]{2,1,0:T(8,128)(2,1)S(1)}, u32[]{:S(2)}, u32[]{:S(2)}) collective-permute-start(bf16[32,32,640]{2,1,0:T(8,128)(2,1)S(1)} %all-to-all-done), channel_id=1, source_target_pairs={{0,16},{16,0},{1,17},{17,1},{2,18},{18,2},{3,19},{19,3},{4,20},{20... | collective-permute-start | bytes 3932168 | tf_op jit(solution)/shard_map/ppermute | solution.py:10
  84.0 1.9 %collective-permute-start.12 = (bf16[128,512]{1,0:T(8,128)(2,1)}, bf16[128,512]{1,0:T(8,128)(2,1)S(1)}, u32[]{:S(2)}, u32[]{:S(2)}) collective-permute-start(bf16[128,512]{1,0:T(8,128)(2,1)} %collective-permute-done.7), channel_id=1, source_target_pairs={{0,2},{2,4},{4,6},{6,8},{8,10},{10,12},{12,14},{14,0},{1,3},{3,5},... | collective-permute-start | bytes 393224 | tf_op jit(solution)/shard_map/ppermute | solution.py:51
  85.9 0.1 slice_bitcast_fusion.3
  86.1 0.6 collective-permute-done.11
  86.6 0.1 slice_bitcast_fusion.1
  86.7 0.3 maximum_maximum_fusion
  87.1 0.0 copy-start.13
  87.1 0.2 copy.21
  87.3 0.9 copy-done.13
  88.2 0.9 convolution_convert_fusion
  89.1 0.9 convolution_convert_fusion.1
  90.0 0.0 copy-start.3
  90.0 2.5 %collective-permute-done.12 = bf16[128,512]{1,0:T(8,128)(2,1)S(1)} collective-permute-done((bf16[128,512]{1,0:T(8,128)(2,1)}, bf16[128,512]{1,0:T(8,128)(2,1)S(1)}, u32[]{:S(2)}, u32[]{:S(2)}) %collective-permute-start.12) | collective-permute-done | bytes 131104 | tf_op jit(solution)/shard_map/ppermute | solution.py:51
  92.4 0.7 copy-done.6
  93.1 1.0 pad_maximum_fusion
  94.1 6.3 %all-to-all-start.1 = ((bf16[32,64,256]{2,1,0:T(8,128)(2,1)}), bf16[32,64,256]{2,1,0:T(8,128)(2,1)}, u32[]{:S(2)}, u32[]{:S(2)}) async-start(bf16[32,64,256]{2,1,0:T(8,128)(2,1)} %bitcast.40), calls=%async_computation.1 | async-start | bytes 2097152 | tf_op jit(solution)/shard_map/all_to_all | solution.py:28
  100.5 0.0 copy-done.3
  100.6 0.9 constant_dynamic-update-slice_fusion.11
  101.5 0.0 copy-done.1
  101.7 0.9 constant_dynamic-update-slice_fusion.3
  102.6 1.6 %fusion = f32[512,1280]{1,0:T(8,128)S(1)} fusion(bf16[1024,1280]{1,0:T(8,128)(2,1)S(1)} %bitcast.38, bf16[1920,512]{1,0:T(8,128)(2,1)S(1)} %constant_dynamic-update-slice_fusion.2, s32[]{:T(128)S(6)} %select_n.108), kind=kOutput, calls=%fused_computation.4 | convolution fusion | flops 1342177280 | bytes 6291460 | tf_op jit(solution)/shard_map/dot_general | solution.py:32
  104.2 0.1 slice.39
  104.3 0.1 slice.38
  104.4 4.6 %collective-permute-start.14 = (bf16[256,640]{1,0:T(8,128)(2,1)S(1)}, bf16[256,640]{1,0:T(8,128)(2,1)S(1)}, u32[]{:S(2)}, u32[]{:S(2)}) collective-permute-start(bf16[256,640]{1,0:T(8,128)(2,1)S(1)} %dynamic-slice_convert_fusion.1), channel_id=1, source_target_pairs={{0,1},{1,0},{256,257},{257,256},{2,3},{3,2},{258,259},{259,258},{4... | collective-permute-start | bytes 983048 | tf_op jit(solution)/shard_map/ppermute | solution.py:14
  109.0 0.1 dynamic-slice_convert_fusion.2
  109.1 2.2 %collective-permute-start.13 = (bf16[256,640]{1,0:T(8,128)(2,1)S(1)}, bf16[256,640]{1,0:T(8,128)(2,1)S(1)}, u32[]{:S(2)}, u32[]{:S(2)}) collective-permute-start(bf16[256,640]{1,0:T(8,128)(2,1)S(1)} %get-tuple-element.52), channel_id=1, source_target_pairs={{0,256},{1,257},{256,0},{257,1},{2,258},{3,259},{258,2},{259,3},{4... | collective-permute-start | bytes 983048 | tf_op jit(solution)/shard_map/ppermute | solution.py:14
  111.3 2.6 %collective-permute-start.15 = (bf16[256,640]{1,0:T(8,128)(2,1)S(1)}, bf16[256,640]{1,0:T(8,128)(2,1)S(1)}, u32[]{:S(2)}, u32[]{:S(2)}) collective-permute-start(bf16[256,640]{1,0:T(8,128)(2,1)S(1)} %get-tuple-element.53), channel_id=1, source_target_pairs={{0,257},{1,256},{256,1},{257,0},{2,259},{3,258},{258,3},{259,2},{4... | collective-permute-start | bytes 983048 | tf_op jit(solution)/shard_map/ppermute | solution.py:14
  113.9 9.3 %collective-permute-done.14 = bf16[256,640]{1,0:T(8,128)(2,1)S(1)} collective-permute-done((bf16[256,640]{1,0:T(8,128)(2,1)S(1)}, bf16[256,640]{1,0:T(8,128)(2,1)S(1)}, u32[]{:S(2)}, u32[]{:S(2)}) %collective-permute-start.14) | collective-permute-done | bytes 327712 | tf_op jit(solution)/shard_map/ppermute | solution.py:14
  123.2 10.6 %collective-permute-done.13 = bf16[256,640]{1,0:T(8,128)(2,1)S(1)} collective-permute-done((bf16[256,640]{1,0:T(8,128)(2,1)S(1)}, bf16[256,640]{1,0:T(8,128)(2,1)S(1)}, u32[]{:S(2)}, u32[]{:S(2)}) %collective-permute-start.13) | collective-permute-done | bytes 327712 | tf_op jit(solution)/shard_map/ppermute | solution.py:14
  133.8 0.0 collective-permute-done.15
  133.8 1.0 convert_add_fusion
  134.7 0.0 all-to-all-done.1
  134.7 1.4 %reduce_sum.12 = bf16[2,2,2,32,256]{4,3,2,1,0:T(8,128)(2,1)S(1)} reduce(bf16[2,8,2,2,32,256]{5,4,3,2,1,0:T(8,128)(2,1)} %bitcast.16, bf16[]{:T(256)} %constant.41.clone.1), dimensions={1}, to_apply=%region_0.1 | reduce | flops 458752 | bytes 1179650 | tf_op jit(solution)/shard_map/reduce_sum | solution.py:107
  136.2 0.7 copy.22
  (41 shorter events, 0.3 us)
Async XLA Ops:
  0.6 16.0 %copy-start.9 = (bf16[256,256]{1,0:T(8,128)(2,1)S(1)}, bf16[256,256]{1,0:T(8,128)(2,1)}, u32[]{:S(2)}) copy-start(bf16[256,256]{1,0:T(8,128)(2,1)} %param.3) | copy-start | bytes 393220
  2.8 23.3 %copy-start.8 = (bf16[256,640]{1,0:T(8,128)(2,1)S(1)}, bf16[256,640]{1,0:T(8,128)(2,1)}, u32[]{:S(2)}) copy-start(bf16[256,640]{1,0:T(8,128)(2,1)} %param.5) | copy-start | bytes 983044
  2.8 70.7 %all-to-all-start = ((bf16[32,32,640]{2,1,0:T(8,128)(2,1)}), bf16[32,32,640]{2,1,0:T(8,128)(2,1)S(1)}, u32[]{:S(2)}, u32[]{:S(2)}) async-start(bf16[32,32,640]{2,1,0:T(8,128)(2,1)} %bitcast.1), calls=%async_computation | async-start | bytes 2621440 | tf_op jit(solution)/shard_map/all_to_all | solution.py:28
  16.7 13.7 %collective-permute-start.1 = (bf16[1,2,32,256]{3,2,1,0:T(8,128)(2,1)S(1)}, bf16[1,2,32,256]{3,2,1,0:T(8,128)(2,1)S(1)}, u32[]{:S(2)}, u32[]{:S(2)}) collective-permute-start(bf16[1,2,32,256]{3,2,1,0:T(8,128)(2,1)S(1)} %get-tuple-element.62), channel_id=1, source_target_pairs={{0,1},{1,0},{256,257},{257,256},{2,3},{3,2},{258,259},{259,258},{4... | collective-permute-start | bytes 98312 | tf_op jit(solution)/shard_map/ppermute | solution.py:14
  21.4 9.1 %collective-permute-start = (bf16[1,2,32,256]{3,2,1,0:T(8,128)(2,1)S(1)}, bf16[1,2,32,256]{3,2,1,0:T(8,128)(2,1)S(1)}, u32[]{:S(2)}, u32[]{:S(2)}) collective-permute-start(bf16[1,2,32,256]{3,2,1,0:T(8,128)(2,1)S(1)} %get-tuple-element.61), channel_id=1, source_target_pairs={{0,256},{1,257},{256,0},{257,1},{2,258},{3,259},{258,2},{259,3},{4... | collective-permute-start | bytes 98312 | tf_op jit(solution)/shard_map/ppermute | solution.py:14
  23.6 6.8 %collective-permute-start.2 = (bf16[1,2,32,256]{3,2,1,0:T(8,128)(2,1)S(1)}, bf16[1,2,32,256]{3,2,1,0:T(8,128)(2,1)S(1)}, u32[]{:S(2)}, u32[]{:S(2)}) collective-permute-start(bf16[1,2,32,256]{3,2,1,0:T(8,128)(2,1)S(1)} %get-tuple-element.63), channel_id=1, source_target_pairs={{0,257},{1,256},{256,1},{257,0},{2,259},{3,258},{258,3},{259,2},{4... | collective-permute-start | bytes 98312 | tf_op jit(solution)/shard_map/ppermute | solution.py:14
  26.1 17.2 %collective-permute-start.3 = (bf16[256,640]{1,0:T(8,128)(2,1)S(1)}, bf16[256,640]{1,0:T(8,128)(2,1)S(1)}, u32[]{:S(2)}, u32[]{:S(2)}) collective-permute-start(bf16[256,640]{1,0:T(8,128)(2,1)S(1)} %copy-done.8), channel_id=1, source_target_pairs={{0,1},{1,0},{2,3},{3,2},{4,5},{5,4},{6,7},{7,6},{8,9},{9,8},{10,11... | collective-permute-start | bytes 983048 | tf_op jit(solution)/shard_map/ppermute | solution.py:10
  43.4 29.2 %collective-permute-start.4 = (bf16[256,1280]{1,0:T(8,128)(2,1)S(1)}, bf16[256,1280]{1,0:T(8,128)(2,1)S(1)}, u32[]{:S(2)}, u32[]{:S(2)}) collective-permute-start(bf16[256,1280]{1,0:T(8,128)(2,1)S(1)} %pad_maximum_fusion.1), channel_id=1, source_target_pairs={{0,256},{256,0},{1,257},{257,1},{2,258},{258,2},{3,259},{259,3},{4... | collective-permute-start | bytes 1966088 | tf_op jit(solution)/shard_map/ppermute | solution.py:10
  45.4 7.0 %collective-permute-start.8 = (bf16[128,512]{1,0:T(8,128)(2,1)S(1)}, bf16[128,512]{1,0:T(8,128)(2,1)S(1)}, u32[]{:S(2)}, u32[]{:S(2)}) collective-permute-start(bf16[128,512]{1,0:T(8,128)(2,1)S(1)} %bitcast.42), channel_id=1, source_target_pairs={{0,14},{2,0},{4,2},{6,4},{8,6},{10,8},{12,10},{14,12},{1,15},{3,1}... | collective-permute-start | bytes 393224 | tf_op jit(solution)/shard_map/ppermute | solution.py:49
  50.5 6.9 %collective-permute-start.5 = (bf16[128,512]{1,0:T(8,128)(2,1)S(1)}, bf16[128,512]{1,0:T(8,128)(2,1)S(1)}, u32[]{:S(2)}, u32[]{:S(2)}) collective-permute-start(bf16[128,512]{1,0:T(8,128)(2,1)S(1)} %bitcast.43), channel_id=1, source_target_pairs={{0,2},{2,4},{4,6},{6,8},{8,10},{10,12},{12,14},{14,0},{1,3},{3,5},... | collective-permute-start | bytes 393224 | tf_op jit(solution)/shard_map/ppermute | solution.py:48
  52.4 6.9 %collective-permute-start.9 = (bf16[128,512]{1,0:T(8,128)(2,1)S(1)}, bf16[128,512]{1,0:T(8,128)(2,1)S(1)}, u32[]{:S(2)}, u32[]{:S(2)}) collective-permute-start(bf16[128,512]{1,0:T(8,128)(2,1)S(1)} %collective-permute-done.8), channel_id=1, source_target_pairs={{0,14},{2,0},{4,2},{6,4},{8,6},{10,8},{12,10},{14,12},{1,15},{3,1}... | collective-permute-start | bytes 393224 | tf_op jit(solution)/shard_map/ppermute | solution.py:49
  57.4 15.3 %copy-start.10 = (bf16[128,512]{1,0:T(8,128)(2,1)}, bf16[128,512]{1,0:T(8,128)(2,1)S(1)}, u32[]{:S(2)}) copy-start(bf16[128,512]{1,0:T(8,128)(2,1)S(1)} %collective-permute-done.5) | copy-start | bytes 393220
  57.4 7.0 %collective-permute-start.6 = (bf16[128,512]{1,0:T(8,128)(2,1)S(1)}, bf16[128,512]{1,0:T(8,128)(2,1)S(1)}, u32[]{:S(2)}, u32[]{:S(2)}) collective-permute-start(bf16[128,512]{1,0:T(8,128)(2,1)S(1)} %collective-permute-done.5), channel_id=1, source_target_pairs={{0,2},{2,4},{4,6},{6,8},{8,10},{10,12},{12,14},{14,0},{1,3},{3,5},... | collective-permute-start | bytes 393224 | tf_op jit(solution)/shard_map/ppermute | solution.py:48
  59.3 13.3 %copy-start.2 = (bf16[128,512]{1,0:T(8,128)(2,1)}, bf16[128,512]{1,0:T(8,128)(2,1)S(1)}, u32[]{:S(2)}) copy-start(bf16[128,512]{1,0:T(8,128)(2,1)S(1)} %collective-permute-done.9) | copy-start | bytes 393220
  59.4 7.8 %collective-permute-start.10 = (bf16[128,512]{1,0:T(8,128)(2,1)S(1)}, bf16[128,512]{1,0:T(8,128)(2,1)S(1)}, u32[]{:S(2)}, u32[]{:S(2)}) collective-permute-start(bf16[128,512]{1,0:T(8,128)(2,1)S(1)} %collective-permute-done.9), channel_id=1, source_target_pairs={{0,14},{2,0},{4,2},{6,4},{8,6},{10,8},{12,10},{14,12},{1,15},{3,1}... | collective-permute-start | bytes 393224 | tf_op jit(solution)/shard_map/ppermute | solution.py:49
  64.4 8.2 %copy-start = (bf16[128,512]{1,0:T(8,128)(2,1)}, bf16[128,512]{1,0:T(8,128)(2,1)S(1)}, u32[]{:S(2)}) copy-start(bf16[128,512]{1,0:T(8,128)(2,1)S(1)} %collective-permute-done.6) | copy-start | bytes 393220
  64.4 8.2 %collective-permute-start.7 = (bf16[128,512]{1,0:T(8,128)(2,1)S(1)}, bf16[128,512]{1,0:T(8,128)(2,1)}, u32[]{:S(2)}, u32[]{:S(2)}) collective-permute-start(bf16[128,512]{1,0:T(8,128)(2,1)S(1)} %collective-permute-done.6), channel_id=1, source_target_pairs={{0,2},{2,4},{4,6},{6,8},{8,10},{10,12},{12,14},{14,0},{1,3},{3,5},... | collective-permute-start | bytes 393224 | tf_op jit(solution)/shard_map/ppermute | solution.py:48
  67.2 5.5 %copy-start.4 = (bf16[128,512]{1,0:T(8,128)(2,1)}, bf16[128,512]{1,0:T(8,128)(2,1)S(1)}, u32[]{:S(2)}) copy-start(bf16[128,512]{1,0:T(8,128)(2,1)S(1)} %collective-permute-done.10) | copy-start | bytes 393220
  72.7 0.8 copy-start.12
  73.5 13.1 %collective-permute-start.11 = (bf16[32,32,640]{2,1,0:T(8,128)(2,1)S(1)}, bf16[32,32,640]{2,1,0:T(8,128)(2,1)S(1)}, u32[]{:S(2)}, u32[]{:S(2)}) collective-permute-start(bf16[32,32,640]{2,1,0:T(8,128)(2,1)S(1)} %all-to-all-done), channel_id=1, source_target_pairs={{0,16},{16,0},{1,17},{17,1},{2,18},{18,2},{3,19},{19,3},{4,20},{20... | collective-permute-start | bytes 3932168 | tf_op jit(solution)/shard_map/ppermute | solution.py:10
  84.0 8.4 %collective-permute-start.12 = (bf16[128,512]{1,0:T(8,128)(2,1)}, bf16[128,512]{1,0:T(8,128)(2,1)S(1)}, u32[]{:S(2)}, u32[]{:S(2)}) collective-permute-start(bf16[128,512]{1,0:T(8,128)(2,1)} %collective-permute-done.7), channel_id=1, source_target_pairs={{0,2},{2,4},{4,6},{6,8},{8,10},{10,12},{12,14},{14,0},{1,3},{3,5},... | collective-permute-start | bytes 393224 | tf_op jit(solution)/shard_map/ppermute | solution.py:51
  87.1 1.1 copy-start.13
  90.0 10.6 %copy-start.3 = (bf16[128,512]{1,0:T(8,128)(2,1)S(1)}, bf16[128,512]{1,0:T(8,128)(2,1)}, u32[]{:S(2)}) copy-start(bf16[128,512]{1,0:T(8,128)(2,1)} %copy-done.2) | copy-start | bytes 393220
  92.4 0.7 copy-start.6
  94.1 6.4 %copy-start.5 = (bf16[128,512]{1,0:T(8,128)(2,1)S(1)}, bf16[128,512]{1,0:T(8,128)(2,1)}, u32[]{:S(2)}) copy-start(bf16[128,512]{1,0:T(8,128)(2,1)} %copy-done.4) | copy-start | bytes 393220
  94.1 6.5 %copy-start.7 = (bf16[128,512]{1,0:T(8,128)(2,1)S(1)}, bf16[128,512]{1,0:T(8,128)(2,1)}, u32[]{:S(2)}) copy-start(bf16[128,512]{1,0:T(8,128)(2,1)} %copy-done.6) | copy-start | bytes 393220
  94.1 7.4 %copy-start.1 = (bf16[128,512]{1,0:T(8,128)(2,1)S(1)}, bf16[128,512]{1,0:T(8,128)(2,1)}, u32[]{:S(2)}) copy-start(bf16[128,512]{1,0:T(8,128)(2,1)} %copy-done) | copy-start | bytes 393220
  94.1 7.4 %copy-start.11 = (bf16[128,512]{1,0:T(8,128)(2,1)S(1)}, bf16[128,512]{1,0:T(8,128)(2,1)}, u32[]{:S(2)}) copy-start(bf16[128,512]{1,0:T(8,128)(2,1)} %copy-done.10) | copy-start | bytes 393220
  94.1 40.6 %all-to-all-start.1 = ((bf16[32,64,256]{2,1,0:T(8,128)(2,1)}), bf16[32,64,256]{2,1,0:T(8,128)(2,1)}, u32[]{:S(2)}, u32[]{:S(2)}) async-start(bf16[32,64,256]{2,1,0:T(8,128)(2,1)} %bitcast.40), calls=%async_computation.1 | async-start | bytes 2097152 | tf_op jit(solution)/shard_map/all_to_all | solution.py:28
  104.4 18.7 %collective-permute-start.14 = (bf16[256,640]{1,0:T(8,128)(2,1)S(1)}, bf16[256,640]{1,0:T(8,128)(2,1)S(1)}, u32[]{:S(2)}, u32[]{:S(2)}) collective-permute-start(bf16[256,640]{1,0:T(8,128)(2,1)S(1)} %dynamic-slice_convert_fusion.1), channel_id=1, source_target_pairs={{0,1},{1,0},{256,257},{257,256},{2,3},{3,2},{258,259},{259,258},{4... | collective-permute-start | bytes 983048 | tf_op jit(solution)/shard_map/ppermute | solution.py:14
  109.1 24.7 %collective-permute-start.13 = (bf16[256,640]{1,0:T(8,128)(2,1)S(1)}, bf16[256,640]{1,0:T(8,128)(2,1)S(1)}, u32[]{:S(2)}, u32[]{:S(2)}) collective-permute-start(bf16[256,640]{1,0:T(8,128)(2,1)S(1)} %get-tuple-element.52), channel_id=1, source_target_pairs={{0,256},{1,257},{256,0},{257,1},{2,258},{3,259},{258,2},{259,3},{4... | collective-permute-start | bytes 983048 | tf_op jit(solution)/shard_map/ppermute | solution.py:14
  111.3 22.5 %collective-permute-start.15 = (bf16[256,640]{1,0:T(8,128)(2,1)S(1)}, bf16[256,640]{1,0:T(8,128)(2,1)S(1)}, u32[]{:S(2)}, u32[]{:S(2)}) collective-permute-start(bf16[256,640]{1,0:T(8,128)(2,1)S(1)} %get-tuple-element.53), channel_id=1, source_target_pairs={{0,257},{1,256},{256,1},{257,0},{2,259},{3,258},{258,3},{259,2},{4... | collective-permute-start | bytes 983048 | tf_op jit(solution)/shard_map/ppermute | solution.py:14

commit v14 on v12

--- a/solution.py
+++ b/solution.py
@@ -48,9 +48,13 @@
         rising.append(lax.ppermute(rising[-1], axis, up))
         falling.append(lax.ppermute(falling[-1], axis, down))
     rising, falling = yield rising, falling
-    far = lax.ppermute(rising[-1], axis, up)
+    middle = rows // 2
+    far = (
+        lax.ppermute(rising[-1][:middle], axis, up),
+        lax.ppermute(falling[-1][middle:], axis, down),
+    )
     rising, falling, far = yield rising, falling, far
-    blocks = falling + [far] + rising[:0:-1]
+    blocks = falling + list(far) + rising[:0:-1]
     panel = jnp.concatenate(blocks + blocks[:-1], axis=0)
     first = lax.rem(size - me, size) * rows
     yield lax.dynamic_slice_in_dim(panel, first, size * rows, 0)

time: 124 us -> 124 us (level)
  starting transfers between devices: 77.7 us -> 81.1 us
  waiting for transfers between devices: 30.8 us -> 28 us
    ppermute x1 -> x2, starting transfers between devices: 2.05 us -> 5.41 us  [the longest x1 3.36 us: ring_gather(): lax.ppermute(rising[-1][:middle], axis, up)]
    ppermute x1 -> x2, waiting for transfers between devices: 3.29 us -> 0.63 us  [the longest x1 0.63 us: ring_gather(): lax.ppermute(rising[-1][:middle], axis, up)]
  transfers between devices with their start and end apart: 19 -> 20, of which waited for: 7 -> 6; matrix products, arithmetic and copies ran while one was open for 5% -> 5% of each run, Pallas kernels for 0% -> 0%
where the time goes in v14:
time: 124 us; the launch traced here: 122 us
  starting transfers between devices  81.1 us (65%)
  waiting for transfers between devices  28 us (23%)
  local copies, waits for them, and re-layouts  4.67 us (4%)
  other arithmetic  3.95 us (3%)
  matrix products  3.38 us (3%)
  between operations  1.35 us (1%)
    ppermute x9, starting transfers between devices, to_partner(): lax.ppermute(block, ('xl', 'xh'), [(i, i ^ 2 * a + b) for i in range(4)])  28.3 us
    ppermute x9, waiting for transfers between devices, to_partner(): lax.ppermute(block, ('xl', 'xh'), [(i, i ^ 2 * a + b) for i in range(4)])  22.2 us
    all_to_all x2, starting transfers between devices, exchange(): return lax.all_to_all(pieces, axes, split_axis=0, concat_axis=0, tiled=True)  18.5 us
    ppermute x3, starting transfers between devices, ring_gather(): falling.append(lax.ppermute(falling[-1], axis, down))  14.9 us
    ppermute x1, starting transfers between devices, swap(): return lax.ppermute(block, axis, ((0, 1), (1, 0)))  8.22 us
    ppermute x3, starting transfers between devices, ring_gather(): rising.append(lax.ppermute(rising[-1], axis, up))  5.75 us
    ppermute x3, waiting for transfers between devices, ring_gather(): rising.append(lax.ppermute(rising[-1], axis, up))  5.15 us
    dot_general x3, matrix products, times(): lax.dot_general(left, right, (((left_dim,), (right_dim,)), ((), ())), pre...  3.38 us
  transfers between devices with their start and end apart: 20, of which 6 were waited for; matrix products, arithmetic and copies ran while one was open for 5% of the time, Pallas kernels for 0%

profile of v14, /device:TPU:1, one launch (start us, length us, event | category | flops | bytes accessed | tf_op | source)
XLA Modules:
  0.0 122.4 jit_solution(10255505278363337919)
XLA Ops:
  0.6 0.0 copy-start.8
  0.6 2.1 %broadcast_in_dim.8 = bf16[4,8,32,640]{3,2,1,0:T(8,128)(2,1)} broadcast(bf16[4,32,640]{2,1,0:T(8,128)(2,1)} %bitcast.47), dimensions={0,2,3} | broadcast | bytes 1474560 | tf_op jit(solution)/shard_map/broadcast_in_dim | solution.py:72
  2.8 13.8 %all-to-all-start = ((bf16[32,32,640]{2,1,0:T(8,128)(2,1)}), bf16[32,32,640]{2,1,0:T(8,128)(2,1)S(1)}, u32[]{:S(2)}, u32[]{:S(2)}) async-start(bf16[32,32,640]{2,1,0:T(8,128)(2,1)} %bitcast.1), calls=%async_computation | async-start | bytes 2621440 | tf_op jit(solution)/shard_map/all_to_all | solution.py:28
  16.7 0.0 copy-done.8
  16.7 4.6 %collective-permute-start.1 = (bf16[1,2,32,256]{3,2,1,0:T(8,128)(2,1)S(1)}, bf16[1,2,32,256]{3,2,1,0:T(8,128)(2,1)S(1)}, u32[]{:S(2)}, u32[]{:S(2)}) collective-permute-start(bf16[1,2,32,256]{3,2,1,0:T(8,128)(2,1)S(1)} %get-tuple-element.70), channel_id=1, source_target_pairs={{0,1},{1,0},{256,257},{257,256},{2,3},{3,2},{258,259},{259,258},{4... | collective-permute-start | bytes 98312 | tf_op jit(solution)/shard_map/ppermute | solution.py:14
  21.4 2.2 %collective-permute-start = (bf16[1,2,32,256]{3,2,1,0:T(8,128)(2,1)S(1)}, bf16[1,2,32,256]{3,2,1,0:T(8,128)(2,1)S(1)}, u32[]{:S(2)}, u32[]{:S(2)}) collective-permute-start(bf16[1,2,32,256]{3,2,1,0:T(8,128)(2,1)S(1)} %get-tuple-element.69), channel_id=1, source_target_pairs={{0,256},{1,257},{256,0},{257,1},{2,258},{3,259},{258,2},{259,3},{4... | collective-permute-start | bytes 98312 | tf_op jit(solution)/shard_map/ppermute | solution.py:14
  23.6 2.5 %collective-permute-start.2 = (bf16[1,2,32,256]{3,2,1,0:T(8,128)(2,1)S(1)}, bf16[1,2,32,256]{3,2,1,0:T(8,128)(2,1)S(1)}, u32[]{:S(2)}, u32[]{:S(2)}) collective-permute-start(bf16[1,2,32,256]{3,2,1,0:T(8,128)(2,1)S(1)} %get-tuple-element.71), channel_id=1, source_target_pairs={{0,257},{1,256},{256,1},{257,0},{2,259},{3,258},{258,3},{259,2},{4... | collective-permute-start | bytes 98312 | tf_op jit(solution)/shard_map/ppermute | solution.py:14
  26.1 0.0 collective-permute-done.1
  26.2 3.9 %collective-permute-done.2 = bf16[1,2,32,256]{3,2,1,0:T(8,128)(2,1)S(1)} collective-permute-done((bf16[1,2,32,256]{3,2,1,0:T(8,128)(2,1)S(1)}, bf16[1,2,32,256]{3,2,1,0:T(8,128)(2,1)S(1)}, u32[]{:S(2)}, u32[]{:S(2)}) %collective-permute-start.2) | collective-permute-done | bytes 32800 | tf_op jit(solution)/shard_map/ppermute | solution.py:14
  30.1 0.0 collective-permute-done
  30.1 5.1 %collective-permute-start.9 = (bf16[128,512]{1,0:T(8,128)(2,1)S(1)}, bf16[128,512]{1,0:T(8,128)(2,1)S(1)}, u32[]{:S(2)}, u32[]{:S(2)}) collective-permute-start(bf16[128,512]{1,0:T(8,128)(2,1)S(1)} %bitcast.42), channel_id=1, source_target_pairs={{0,14},{2,0},{4,2},{6,4},{8,6},{10,8},{12,10},{14,12},{1,15},{3,1}... | collective-permute-start | bytes 393224 | tf_op jit(solution)/shard_map/ppermute | solution.py:49
  35.2 1.9 %collective-permute-start.6 = (bf16[128,512]{1,0:T(8,128)(2,1)S(1)}, bf16[128,512]{1,0:T(8,128)(2,1)}, u32[]{:S(2)}, u32[]{:S(2)}) collective-permute-start(bf16[128,512]{1,0:T(8,128)(2,1)S(1)} %bitcast.43), channel_id=1, source_target_pairs={{0,2},{2,4},{4,6},{6,8},{8,10},{10,12},{12,14},{14,0},{1,3},{3,5},... | collective-permute-start | bytes 393224 | tf_op jit(solution)/shard_map/ppermute | solution.py:48
  37.2 3.5 %collective-permute-start.5 = (bf16[256,640]{1,0:T(8,128)(2,1)S(1)}, bf16[256,640]{1,0:T(8,128)(2,1)S(1)}, u32[]{:S(2)}, u32[]{:S(2)}) collective-permute-start(bf16[256,640]{1,0:T(8,128)(2,1)S(1)} %copy-done), channel_id=1, source_target_pairs={{0,257},{1,256},{256,1},{257,0},{2,259},{3,258},{258,3},{259,2},{4... | collective-permute-start | bytes 983048 | tf_op jit(solution)/shard_map/ppermute | solution.py:14
  40.7 1.9 %collective-permute-start.4 = (bf16[256,640]{1,0:T(8,128)(2,1)S(1)}, bf16[256,640]{1,0:T(8,128)(2,1)S(1)}, u32[]{:S(2)}, u32[]{:S(2)}) collective-permute-start(bf16[256,640]{1,0:T(8,128)(2,1)S(1)} %copy-done), channel_id=1, source_target_pairs={{0,256},{1,257},{256,0},{257,1},{2,258},{3,259},{258,2},{259,3},{4... | collective-permute-start | bytes 983048 | tf_op jit(solution)/shard_map/ppermute | solution.py:14
  42.6 4.2 %collective-permute-start.3 = (bf16[256,640]{1,0:T(8,128)(2,1)S(1)}, bf16[256,640]{1,0:T(8,128)(2,1)S(1)}, u32[]{:S(2)}, u32[]{:S(2)}) collective-permute-start(bf16[256,640]{1,0:T(8,128)(2,1)S(1)} %copy-done), channel_id=1, source_target_pairs={{0,1},{1,0},{256,257},{257,256},{2,3},{3,2},{258,259},{259,258},{4... | collective-permute-start | bytes 983048 | tf_op jit(solution)/shard_map/ppermute | solution.py:14
  46.8 0.0 collective-permute-done.9
  46.8 4.6 %collective-permute-start.10 = (bf16[128,512]{1,0:T(8,128)(2,1)S(1)}, bf16[128,512]{1,0:T(8,128)(2,1)S(1)}, u32[]{:S(2)}, u32[]{:S(2)}) collective-permute-start(bf16[128,512]{1,0:T(8,128)(2,1)S(1)} %collective-permute-done.9), channel_id=1, source_target_pairs={{0,14},{2,0},{4,2},{6,4},{8,6},{10,8},{12,10},{14,12},{1,15},{3,1}... | collective-permute-start | bytes 393224 | tf_op jit(solution)/shard_map/ppermute | solution.py:49
  51.3 0.0 collective-permute-done.6
  51.4 1.9 %collective-permute-start.7 = (bf16[128,512]{1,0:T(8,128)(2,1)}, bf16[128,512]{1,0:T(8,128)(2,1)S(1)}, u32[]{:S(2)}, u32[]{:S(2)}) collective-permute-start(bf16[128,512]{1,0:T(8,128)(2,1)} %collective-permute-done.6), channel_id=1, source_target_pairs={{0,2},{2,4},{4,6},{6,8},{8,10},{10,12},{12,14},{14,0},{1,3},{3,5},... | collective-permute-start | bytes 393224 | tf_op jit(solution)/shard_map/ppermute | solution.py:48
  53.3 0.0 collective-permute-done.10
  53.3 5.2 %collective-permute-start.11 = (bf16[128,512]{1,0:T(8,128)(2,1)S(1)}, bf16[128,512]{1,0:T(8,128)(2,1)S(1)}, u32[]{:S(2)}, u32[]{:S(2)}) collective-permute-start(bf16[128,512]{1,0:T(8,128)(2,1)S(1)} %collective-permute-done.10), channel_id=1, source_target_pairs={{0,14},{2,0},{4,2},{6,4},{8,6},{10,8},{12,10},{14,12},{1,15},{3,1}... | collective-permute-start | bytes 393224 | tf_op jit(solution)/shard_map/ppermute | solution.py:49
  58.6 0.2 collective-permute-done.7
  58.8 1.9 %collective-permute-start.8 = (bf16[128,512]{1,0:T(8,128)(2,1)S(1)}, bf16[128,512]{1,0:T(8,128)(2,1)S(1)}, u32[]{:S(2)}, u32[]{:S(2)}) collective-permute-start(bf16[128,512]{1,0:T(8,128)(2,1)S(1)} %collective-permute-done.7), channel_id=1, source_target_pairs={{0,2},{2,4},{4,6},{6,8},{8,10},{10,12},{12,14},{14,0},{1,3},{3,5},... | collective-permute-start | bytes 393224 | tf_op jit(solution)/shard_map/ppermute | solution.py:48
  60.7 0.0 collective-permute-done.5
  60.7 0.0 collective-permute-done.4
  60.7 0.0 copy-start.4
  60.7 0.0 collective-permute-done.3
  60.8 0.0 collective-permute-done.11
  60.8 4.9 %collective-permute-done.8 = bf16[128,512]{1,0:T(8,128)(2,1)S(1)} collective-permute-done((bf16[128,512]{1,0:T(8,128)(2,1)S(1)}, bf16[128,512]{1,0:T(8,128)(2,1)S(1)}, u32[]{:S(2)}, u32[]{:S(2)}) %collective-permute-start.8) | collective-permute-done | bytes 131104 | tf_op jit(solution)/shard_map/ppermute | solution.py:48
  65.7 0.0 copy-done.2
  65.7 0.0 copy-done.6
  65.7 0.0 all-to-all-done
  65.7 8.2 %collective-permute-start.12 = (bf16[32,32,640]{2,1,0:T(8,128)(2,1)S(1)}, bf16[32,32,640]{2,1,0:T(8,128)(2,1)S(1)}, u32[]{:S(2)}, u32[]{:S(2)}) collective-permute-start(bf16[32,32,640]{2,1,0:T(8,128)(2,1)S(1)} %all-to-all-done), channel_id=1, source_target_pairs={{0,16},{16,0},{1,17},{17,1},{2,18},{18,2},{3,19},{19,3},{4,20},{20... | collective-permute-start | bytes 3932168 | tf_op jit(solution)/shard_map/ppermute | solution.py:10
  74.0 0.0 copy-start.1
  74.0 0.0 copy-start.5
  74.0 2.1 %collective-permute-start.14 = (bf16[64,512]{1,0:T(8,128)(2,1)S(1)}, bf16[64,512]{1,0:T(8,128)(2,1)S(1)}, u32[]{:S(2)}, u32[]{:S(2)}) collective-permute-start(bf16[64,512]{1,0:T(8,128)(2,1)S(1)} %slice.37), channel_id=1, source_target_pairs={{0,14},{2,0},{4,2},{6,4},{8,6},{10,8},{12,10},{14,12},{1,15},{3,1}... | collective-permute-start | bytes 196616 | tf_op jit(solution)/shard_map/ppermute | solution.py:54
  76.1 3.4 %collective-permute-start.13 = (bf16[64,512]{1,0:T(8,128)(2,1)S(1)}, bf16[64,512]{1,0:T(8,128)(2,1)S(1)}, u32[]{:S(2)}, u32[]{:S(2)}) collective-permute-start(bf16[64,512]{1,0:T(8,128)(2,1)S(1)} %slice.36), channel_id=1, source_target_pairs={{0,2},{2,4},{4,6},{6,8},{8,10},{10,12},{12,14},{14,0},{1,3},{3,5},... | collective-permute-start | bytes 196616 | tf_op jit(solution)/shard_map/ppermute | solution.py:53
  79.5 0.1 slice_bitcast_fusion.3
  79.6 0.1 broadcast_select_fusion.1
  79.8 0.0 collective-permute-done.12
  79.8 0.1 slice_bitcast_fusion.1
  79.9 0.3 maximum_maximum_fusion
  80.2 0.2 copy.21
  80.5 0.9 convolution_convert_fusion
  81.4 0.9 convolution_convert_fusion.1
  82.3 0.0 collective-permute-done.14
  82.3 0.6 collective-permute-done.13
  82.9 1.0 pad_maximum_fusion
  83.9 4.7 %all-to-all-start.1 = ((bf16[32,64,256]{2,1,0:T(8,128)(2,1)}), bf16[32,64,256]{2,1,0:T(8,128)(2,1)}, u32[]{:S(2)}, u32[]{:S(2)}) async-start(bf16[32,64,256]{2,1,0:T(8,128)(2,1)} %bitcast.40), calls=%async_computation.1 | async-start | bytes 2097152 | tf_op jit(solution)/shard_map/all_to_all | solution.py:28
  88.8 0.9 constant_dynamic-update-slice_fusion.10
  89.8 1.6 %fusion = f32[512,1280]{1,0:T(8,128)S(1)} fusion(bf16[1024,1280]{1,0:T(8,128)(2,1)S(1)} %bitcast.38, bf16[1920,512]{1,0:T(8,128)(2,1)S(1)} %constant_dynamic-update-slice_fusion.2, s32[]{:T(128)S(6)} %select_n.118), kind=kOutput, calls=%fused_computation.4 | convolution fusion | flops 1342177280 | bytes 6291460 | tf_op jit(solution)/shard_map/dot_general | solution.py:32
  91.4 0.1 slice.47
  91.5 0.1 slice.46
  91.6 4.5 %collective-permute-start.16 = (bf16[256,640]{1,0:T(8,128)(2,1)S(1)}, bf16[256,640]{1,0:T(8,128)(2,1)S(1)}, u32[]{:S(2)}, u32[]{:S(2)}) collective-permute-start(bf16[256,640]{1,0:T(8,128)(2,1)S(1)} %dynamic-slice_convert_fusion.1), channel_id=1, source_target_pairs={{0,1},{1,0},{256,257},{257,256},{2,3},{3,2},{258,259},{259,258},{4... | collective-permute-start | bytes 983048 | tf_op jit(solution)/shard_map/ppermute | solution.py:14
  96.1 0.1 dynamic-slice_convert_fusion.2
  96.2 2.3 %collective-permute-start.15 = (bf16[256,640]{1,0:T(8,128)(2,1)S(1)}, bf16[256,640]{1,0:T(8,128)(2,1)S(1)}, u32[]{:S(2)}, u32[]{:S(2)}) collective-permute-start(bf16[256,640]{1,0:T(8,128)(2,1)S(1)} %get-tuple-element.58), channel_id=1, source_target_pairs={{0,256},{1,257},{256,0},{257,1},{2,258},{3,259},{258,2},{259,3},{4... | collective-permute-start | bytes 983048 | tf_op jit(solution)/shard_map/ppermute | solution.py:14
  98.5 2.5 %collective-permute-start.17 = (bf16[256,640]{1,0:T(8,128)(2,1)S(1)}, bf16[256,640]{1,0:T(8,128)(2,1)S(1)}, u32[]{:S(2)}, u32[]{:S(2)}) collective-permute-start(bf16[256,640]{1,0:T(8,128)(2,1)S(1)} %get-tuple-element.59), channel_id=1, source_target_pairs={{0,257},{1,256},{256,1},{257,0},{2,259},{3,258},{258,3},{259,2},{4... | collective-permute-start | bytes 983048 | tf_op jit(solution)/shard_map/ppermute | solution.py:14
  101.0 8.4 %collective-permute-done.16 = bf16[256,640]{1,0:T(8,128)(2,1)S(1)} collective-permute-done((bf16[256,640]{1,0:T(8,128)(2,1)S(1)}, bf16[256,640]{1,0:T(8,128)(2,1)S(1)}, u32[]{:S(2)}, u32[]{:S(2)}) %collective-permute-start.16) | collective-permute-done | bytes 327712 | tf_op jit(solution)/shard_map/ppermute | solution.py:14
  109.4 9.9 %collective-permute-done.15 = bf16[256,640]{1,0:T(8,128)(2,1)S(1)} collective-permute-done((bf16[256,640]{1,0:T(8,128)(2,1)S(1)}, bf16[256,640]{1,0:T(8,128)(2,1)S(1)}, u32[]{:S(2)}, u32[]{:S(2)}) %collective-permute-start.15) | collective-permute-done | bytes 327712 | tf_op jit(solution)/shard_map/ppermute | solution.py:14
  119.3 0.0 collective-permute-done.17
  119.3 1.0 convert_add_fusion
  120.3 0.0 all-to-all-done.1
  120.3 1.4 %reduce_sum.12 = bf16[2,2,2,32,256]{4,3,2,1,0:T(8,128)(2,1)S(1)} reduce(bf16[2,8,2,2,32,256]{5,4,3,2,1,0:T(8,128)(2,1)} %bitcast.16, bf16[]{:T(256)} %constant.41.clone.1), dimensions={1}, to_apply=%region_0.1 | reduce | flops 458752 | bytes 1179650 | tf_op jit(solution)/shard_map/reduce_sum | solution.py:112
  121.7 0.7 copy.22
  (38 shorter events, 0.4 us)
Async XLA Ops:
  0.6 16.0 %copy-start.8 = (bf16[256,256]{1,0:T(8,128)(2,1)S(1)}, bf16[256,256]{1,0:T(8,128)(2,1)}, u32[]{:S(2)}) copy-start(bf16[256,256]{1,0:T(8,128)(2,1)} %param.3) | copy-start | bytes 393220
  2.8 34.4 %copy-start = (bf16[256,640]{1,0:T(8,128)(2,1)S(1)}, bf16[256,640]{1,0:T(8,128)(2,1)}, u32[]{:S(2)}) copy-start(bf16[256,640]{1,0:T(8,128)(2,1)} %param.5) | copy-start | bytes 983044
  2.8 62.9 %all-to-all-start = ((bf16[32,32,640]{2,1,0:T(8,128)(2,1)}), bf16[32,32,640]{2,1,0:T(8,128)(2,1)S(1)}, u32[]{:S(2)}, u32[]{:S(2)}) async-start(bf16[32,32,640]{2,1,0:T(8,128)(2,1)} %bitcast.1), calls=%async_computation | async-start | bytes 2621440 | tf_op jit(solution)/shard_map/all_to_all | solution.py:28
  16.7 9.4 %collective-permute-start.1 = (bf16[1,2,32,256]{3,2,1,0:T(8,128)(2,1)S(1)}, bf16[1,2,32,256]{3,2,1,0:T(8,128)(2,1)S(1)}, u32[]{:S(2)}, u32[]{:S(2)}) collective-permute-start(bf16[1,2,32,256]{3,2,1,0:T(8,128)(2,1)S(1)} %get-tuple-element.70), channel_id=1, source_target_pairs={{0,1},{1,0},{256,257},{257,256},{2,3},{3,2},{258,259},{259,258},{4... | collective-permute-start | bytes 98312 | tf_op jit(solution)/shard_map/ppermute | solution.py:14
  21.4 8.7 %collective-permute-start = (bf16[1,2,32,256]{3,2,1,0:T(8,128)(2,1)S(1)}, bf16[1,2,32,256]{3,2,1,0:T(8,128)(2,1)S(1)}, u32[]{:S(2)}, u32[]{:S(2)}) collective-permute-start(bf16[1,2,32,256]{3,2,1,0:T(8,128)(2,1)S(1)} %get-tuple-element.69), channel_id=1, source_target_pairs={{0,256},{1,257},{256,0},{257,1},{2,258},{3,259},{258,2},{259,3},{4... | collective-permute-start | bytes 98312 | tf_op jit(solution)/shard_map/ppermute | solution.py:14
  23.6 6.4 %collective-permute-start.2 = (bf16[1,2,32,256]{3,2,1,0:T(8,128)(2,1)S(1)}, bf16[1,2,32,256]{3,2,1,0:T(8,128)(2,1)S(1)}, u32[]{:S(2)}, u32[]{:S(2)}) collective-permute-start(bf16[1,2,32,256]{3,2,1,0:T(8,128)(2,1)S(1)} %get-tuple-element.71), channel_id=1, source_target_pairs={{0,257},{1,256},{256,1},{257,0},{2,259},{3,258},{258,3},{259,2},{4... | collective-permute-start | bytes 98312 | tf_op jit(solution)/shard_map/ppermute | solution.py:14
  30.1 16.7 %collective-permute-start.9 = (bf16[128,512]{1,0:T(8,128)(2,1)S(1)}, bf16[128,512]{1,0:T(8,128)(2,1)S(1)}, u32[]{:S(2)}, u32[]{:S(2)}) collective-permute-start(bf16[128,512]{1,0:T(8,128)(2,1)S(1)} %bitcast.42), channel_id=1, source_target_pairs={{0,14},{2,0},{4,2},{6,4},{8,6},{10,8},{12,10},{14,12},{1,15},{3,1}... | collective-permute-start | bytes 393224 | tf_op jit(solution)/shard_map/ppermute | solution.py:49
  35.2 16.1 %collective-permute-start.6 = (bf16[128,512]{1,0:T(8,128)(2,1)S(1)}, bf16[128,512]{1,0:T(8,128)(2,1)}, u32[]{:S(2)}, u32[]{:S(2)}) collective-permute-start(bf16[128,512]{1,0:T(8,128)(2,1)S(1)} %bitcast.43), channel_id=1, source_target_pairs={{0,2},{2,4},{4,6},{6,8},{8,10},{10,12},{12,14},{14,0},{1,3},{3,5},... | collective-permute-start | bytes 393224 | tf_op jit(solution)/shard_map/ppermute | solution.py:48
  37.2 23.6 %collective-permute-start.5 = (bf16[256,640]{1,0:T(8,128)(2,1)S(1)}, bf16[256,640]{1,0:T(8,128)(2,1)S(1)}, u32[]{:S(2)}, u32[]{:S(2)}) collective-permute-start(bf16[256,640]{1,0:T(8,128)(2,1)S(1)} %copy-done), channel_id=1, source_target_pairs={{0,257},{1,256},{256,1},{257,0},{2,259},{3,258},{258,3},{259,2},{4... | collective-permute-start | bytes 983048 | tf_op jit(solution)/shard_map/ppermute | solution.py:14
  40.7 20.1 %collective-permute-start.4 = (bf16[256,640]{1,0:T(8,128)(2,1)S(1)}, bf16[256,640]{1,0:T(8,128)(2,1)S(1)}, u32[]{:S(2)}, u32[]{:S(2)}) collective-permute-start(bf16[256,640]{1,0:T(8,128)(2,1)S(1)} %copy-done), channel_id=1, source_target_pairs={{0,256},{1,257},{256,0},{257,1},{2,258},{3,259},{258,2},{259,3},{4... | collective-permute-start | bytes 983048 | tf_op jit(solution)/shard_map/ppermute | solution.py:14
  42.6 18.2 %collective-permute-start.3 = (bf16[256,640]{1,0:T(8,128)(2,1)S(1)}, bf16[256,640]{1,0:T(8,128)(2,1)S(1)}, u32[]{:S(2)}, u32[]{:S(2)}) collective-permute-start(bf16[256,640]{1,0:T(8,128)(2,1)S(1)} %copy-done), channel_id=1, source_target_pairs={{0,1},{1,0},{256,257},{257,256},{2,3},{3,2},{258,259},{259,258},{4... | collective-permute-start | bytes 983048 | tf_op jit(solution)/shard_map/ppermute | solution.py:14
  46.8 6.5 %collective-permute-start.10 = (bf16[128,512]{1,0:T(8,128)(2,1)S(1)}, bf16[128,512]{1,0:T(8,128)(2,1)S(1)}, u32[]{:S(2)}, u32[]{:S(2)}) collective-permute-start(bf16[128,512]{1,0:T(8,128)(2,1)S(1)} %collective-permute-done.9), channel_id=1, source_target_pairs={{0,14},{2,0},{4,2},{6,4},{8,6},{10,8},{12,10},{14,12},{1,15},{3,1}... | collective-permute-start | bytes 393224 | tf_op jit(solution)/shard_map/ppermute | solution.py:49
  51.4 7.4 %collective-permute-start.7 = (bf16[128,512]{1,0:T(8,128)(2,1)}, bf16[128,512]{1,0:T(8,128)(2,1)S(1)}, u32[]{:S(2)}, u32[]{:S(2)}) collective-permute-start(bf16[128,512]{1,0:T(8,128)(2,1)} %collective-permute-done.6), channel_id=1, source_target_pairs={{0,2},{2,4},{4,6},{6,8},{8,10},{10,12},{12,14},{14,0},{1,3},{3,5},... | collective-permute-start | bytes 393224 | tf_op jit(solution)/shard_map/ppermute | solution.py:48
  53.3 7.5 %collective-permute-start.11 = (bf16[128,512]{1,0:T(8,128)(2,1)S(1)}, bf16[128,512]{1,0:T(8,128)(2,1)S(1)}, u32[]{:S(2)}, u32[]{:S(2)}) collective-permute-start(bf16[128,512]{1,0:T(8,128)(2,1)S(1)} %collective-permute-done.10), channel_id=1, source_target_pairs={{0,14},{2,0},{4,2},{6,4},{8,6},{10,8},{12,10},{14,12},{1,15},{3,1}... | collective-permute-start | bytes 393224 | tf_op jit(solution)/shard_map/ppermute | solution.py:49
  58.8 6.9 %collective-permute-start.8 = (bf16[128,512]{1,0:T(8,128)(2,1)S(1)}, bf16[128,512]{1,0:T(8,128)(2,1)S(1)}, u32[]{:S(2)}, u32[]{:S(2)}) collective-permute-start(bf16[128,512]{1,0:T(8,128)(2,1)S(1)} %collective-permute-done.7), channel_id=1, source_target_pairs={{0,2},{2,4},{4,6},{6,8},{8,10},{10,12},{12,14},{14,0},{1,3},{3,5},... | collective-permute-start | bytes 393224 | tf_op jit(solution)/shard_map/ppermute | solution.py:48
  60.7 5.0 %copy-start.2 = (bf16[256,640]{1,0:T(8,128)(2,1)}, bf16[256,640]{1,0:T(8,128)(2,1)S(1)}, u32[]{:S(2)}) copy-start(bf16[256,640]{1,0:T(8,128)(2,1)S(1)} %collective-permute-done.5) | copy-start | bytes 983044
  60.7 5.0 %copy-start.4 = (bf16[256,640]{1,0:T(8,128)(2,1)}, bf16[256,640]{1,0:T(8,128)(2,1)S(1)}, u32[]{:S(2)}) copy-start(bf16[256,640]{1,0:T(8,128)(2,1)S(1)} %collective-permute-done.4) | copy-start | bytes 983044
  60.8 4.9 %copy-start.6 = (bf16[256,640]{1,0:T(8,128)(2,1)}, bf16[256,640]{1,0:T(8,128)(2,1)S(1)}, u32[]{:S(2)}) copy-start(bf16[256,640]{1,0:T(8,128)(2,1)S(1)} %collective-permute-done.3) | copy-start | bytes 983044
  65.7 14.1 %collective-permute-start.12 = (bf16[32,32,640]{2,1,0:T(8,128)(2,1)S(1)}, bf16[32,32,640]{2,1,0:T(8,128)(2,1)S(1)}, u32[]{:S(2)}, u32[]{:S(2)}) collective-permute-start(bf16[32,32,640]{2,1,0:T(8,128)(2,1)S(1)} %all-to-all-done), channel_id=1, source_target_pairs={{0,16},{16,0},{1,17},{17,1},{2,18},{18,2},{3,19},{19,3},{4,20},{20... | collective-permute-start | bytes 3932168 | tf_op jit(solution)/shard_map/ppermute | solution.py:10
  74.0 5.6 %copy-start.1 = (bf16[256,640]{1,0:T(8,128)(2,1)S(1)}, bf16[256,640]{1,0:T(8,128)(2,1)}, u32[]{:S(2)}) copy-start(bf16[256,640]{1,0:T(8,128)(2,1)} %param.5) | copy-start | bytes 983044
  74.0 5.6 %copy-start.3 = (bf16[256,640]{1,0:T(8,128)(2,1)S(1)}, bf16[256,640]{1,0:T(8,128)(2,1)}, u32[]{:S(2)}) copy-start(bf16[256,640]{1,0:T(8,128)(2,1)} %copy-done.2) | copy-start | bytes 983044
  74.0 5.6 %copy-start.5 = (bf16[256,640]{1,0:T(8,128)(2,1)S(1)}, bf16[256,640]{1,0:T(8,128)(2,1)}, u32[]{:S(2)}) copy-start(bf16[256,640]{1,0:T(8,128)(2,1)} %copy-done.4) | copy-start | bytes 983044
  74.0 5.6 %copy-start.7 = (bf16[256,640]{1,0:T(8,128)(2,1)S(1)}, bf16[256,640]{1,0:T(8,128)(2,1)}, u32[]{:S(2)}) copy-start(bf16[256,640]{1,0:T(8,128)(2,1)} %copy-done.6) | copy-start | bytes 983044
  74.0 8.2 %collective-permute-start.14 = (bf16[64,512]{1,0:T(8,128)(2,1)S(1)}, bf16[64,512]{1,0:T(8,128)(2,1)S(1)}, u32[]{:S(2)}, u32[]{:S(2)}) collective-permute-start(bf16[64,512]{1,0:T(8,128)(2,1)S(1)} %slice.37), channel_id=1, source_target_pairs={{0,14},{2,0},{4,2},{6,4},{8,6},{10,8},{12,10},{14,12},{1,15},{3,1}... | collective-permute-start | bytes 196616 | tf_op jit(solution)/shard_map/ppermute | solution.py:54
  76.1 6.8 %collective-permute-start.13 = (bf16[64,512]{1,0:T(8,128)(2,1)S(1)}, bf16[64,512]{1,0:T(8,128)(2,1)S(1)}, u32[]{:S(2)}, u32[]{:S(2)}) collective-permute-start(bf16[64,512]{1,0:T(8,128)(2,1)S(1)} %slice.36), channel_id=1, source_target_pairs={{0,2},{2,4},{4,6},{6,8},{8,10},{10,12},{12,14},{14,0},{1,3},{3,5},... | collective-permute-start | bytes 196616 | tf_op jit(solution)/shard_map/ppermute | solution.py:53
  83.9 36.3 %all-to-all-start.1 = ((bf16[32,64,256]{2,1,0:T(8,128)(2,1)}), bf16[32,64,256]{2,1,0:T(8,128)(2,1)}, u32[]{:S(2)}, u32[]{:S(2)}) async-start(bf16[32,64,256]{2,1,0:T(8,128)(2,1)} %bitcast.40), calls=%async_computation.1 | async-start | bytes 2097152 | tf_op jit(solution)/shard_map/all_to_all | solution.py:28
  91.6 17.8 %collective-permute-start.16 = (bf16[256,640]{1,0:T(8,128)(2,1)S(1)}, bf16[256,640]{1,0:T(8,128)(2,1)S(1)}, u32[]{:S(2)}, u32[]{:S(2)}) collective-permute-start(bf16[256,640]{1,0:T(8,128)(2,1)S(1)} %dynamic-slice_convert_fusion.1), channel_id=1, source_target_pairs={{0,1},{1,0},{256,257},{257,256},{2,3},{3,2},{258,259},{259,258},{4... | collective-permute-start | bytes 983048 | tf_op jit(solution)/shard_map/ppermute | solution.py:14
  96.2 23.1 %collective-permute-start.15 = (bf16[256,640]{1,0:T(8,128)(2,1)S(1)}, bf16[256,640]{1,0:T(8,128)(2,1)S(1)}, u32[]{:S(2)}, u32[]{:S(2)}) collective-permute-start(bf16[256,640]{1,0:T(8,128)(2,1)S(1)} %get-tuple-element.58), channel_id=1, source_target_pairs={{0,256},{1,257},{256,0},{257,1},{2,258},{3,259},{258,2},{259,3},{4... | collective-permute-start | bytes 983048 | tf_op jit(solution)/shard_map/ppermute | solution.py:14
  98.5 20.8 %collective-permute-start.17 = (bf16[256,640]{1,0:T(8,128)(2,1)S(1)}, bf16[256,640]{1,0:T(8,128)(2,1)S(1)}, u32[]{:S(2)}, u32[]{:S(2)}) collective-permute-start(bf16[256,640]{1,0:T(8,128)(2,1)S(1)} %get-tuple-element.59), channel_id=1, source_target_pairs={{0,257},{1,256},{256,1},{257,0},{2,259},{3,258},{258,3},{259,2},{4... | collective-permute-start | bytes 983048 | tf_op jit(solution)/shard_map/ppermute | solution.py:14
